TPU v7x, 32 devices: a whole 2x2x4 slice. The times are simulated.
32 devices in a mesh: groups: 2 (over y), lat: 4 (over z), lev: 4 (over x, core).
Axes of the slice: x: 2, y: 2, z: 4, core: 2. Of those that a mesh axis runs over, the one named last changes fastest.
Arguments:
- tracers: float32 [8, 8, 144, 1152], P(None, 'lev', ('groups', 'lat')), parts along dimension 2, may hold values from -1 to 8
- wind_x: float32 [8, 144, 1152], P('lev', ('groups', 'lat')), parts along dimension 1, may hold values from -0.9 to 0.9
- wind_y: float32 [8, 144, 1152], P('lev', ('groups', 'lat')), parts along dimension 1, may hold values from -0.9 to 0.9
- level_counts: int32 [4], replicated, may hold values from 1 to 2, 6 in all
- source_level: int32 [6, 144, 1152], P(None, ('groups', 'lat'), 'lev'), parts along dimension 1, may hold values from 0 to 2, as said below
- remap_weight: float32 [4, 6, 144, 1152], P(None, None, ('groups', 'lat'), 'lev'), parts along dimension 2, may hold values from 0.05 to 0.6
Outputs:
- remapped: float32 [8, 6, 144, 1152], P(None, None, ('groups', 'lat'), 'lev'), parts along dimension 2
There are 2 independent parts, one for each index of `groups`. A program takes and returns all parts, laid end to end along the dimension named above; an argument that names none is the same for every part. Nothing has to cross between parts.
Inputs may be any that keep to these rules, and one draw needn't show every extreme that they name: `level_counts`: the counts sum to 6. source_level[k] lies between max(k - 3, 0) and min(k, 2).
All inputs are finite; a program needn't handle non-finite values.
Results may differ from a plain program's by a relative error of at most 0.0003.
Values sent between devices are 32-bit elements; how exact they have to be, the bound alone decides.
No kernel may reach another device: no remote copies, remote signals or barrier semaphores. Data moves between devices by JAX's collectives and lax.ppermute only.
A program may use at most 64 MiB of HBM per device.

v0:
```python
import jax
import jax.numpy as jnp
from jax import lax
from jax.sharding import PartitionSpec as P

SUBSTEPS = 2
TAPS = 4


def shifted_2(value, axis, steps):
    count = lax.axis_size(axis)
    leading, last = (max(0, -steps), min(count, count - steps))
    return lax.ppermute(value, axis, [(source, source + steps) for source in range(leading, last)])


def extended(cells, sides, width):
    for axis, dim in sides:
        count = lax.axis_size(axis)
        ends = count - 1
        head = lax.slice_in_dim(cells, 0, width, axis=dim)
        tail = lax.slice_in_dim(cells, cells.shape[dim] - width, cells.shape[dim], axis=dim)
        cells = jnp.concatenate(
            [
                lax.ppermute(tail, axis, [(i, (i + 1) % count) for i in range(ends)]),
                cells,
                lax.ppermute(head, axis, [((i + 1) % count, i) for i in range(ends)]),
            ],
            axis=dim,
        )
    return cells


def cut(array, start, stop, axis):
    return lax.slice_in_dim(array, start, stop, axis=axis)


def ppm_fluxes(ext, courant, axis):
    cells = ext.shape[axis] - 6
    faces = courant.shape[axis - 1]
    inter = 7.0 / 12.0 * (
        cut(ext, 1, cells + 4, axis) + cut(ext, 2, cells + 5, axis)
    ) - 1.0 / 12.0 * (cut(ext, 0, cells + 3, axis) + cut(ext, 3, cells + 6, axis))
    left = cut(inter, 0, cells + 2, axis)
    right = cut(inter, 1, cells + 3, axis)
    center = cut(ext, 2, cells + 4, axis)
    slope = right - left
    curve = 6.0 * (center - 0.5 * (left + right))
    speed = courant[None]
    upper = cut(right, 0, faces, axis) - 0.5 * speed * (
        cut(slope, 0, faces, axis) - (1.0 - speed * (2.0 / 3.0)) * cut(curve, 0, faces, axis)
    )
    lower = cut(left, 1, faces + 1, axis) - 0.5 * speed * (
        cut(slope, 1, faces + 1, axis)
        + (1.0 + speed * (2.0 / 3.0)) * cut(curve, 1, faces + 1, axis)
    )
    return speed * jnp.where(speed > 0, upper, lower)


def lat_step(ext, faces):
    flux = ppm_fluxes(ext, faces, 2)
    cells = ext.shape[2] - 6
    return cut(ext, 3, cells + 3, 2) - (cut(flux, 1, cells + 1, 2) - cut(flux, 0, cells, 2))


def lon_step(field, wind):
    ext = jnp.concatenate([field[..., -3:], field, field[..., :3]], axis=3)
    flux = ppm_fluxes(ext, wind, 3)
    return field - (jnp.roll(flux, -1, axis=3) - flux)


def select_taps(padded, offsets, weights, count):
    shifted = [cut(padded, 3 + step, 3 + step + count, 1) for step in range(-3, TAPS)]
    total = jnp.zeros(shifted[0].shape, jnp.float32)
    for tap in range(TAPS):
        picked = shifted[tap]
        for lower in range(-2, 1):
            picked = jnp.where((offsets == lower)[None], shifted[tap + lower + 3], picked)
        total = total + weights[tap][None] * picked
    return total


def shards(tracers, wind_x, wind_y, level_counts, source_level, remap_weight):
    depth = tracers.shape[1]
    rows = tracers.shape[2]
    band = lax.axis_index("lat")
    global_face = band * rows + jnp.arange(rows, dtype=jnp.int32)
    face_mask = (global_face != 0).astype(jnp.float32)[None, :, None]
    south_faces = wind_y * face_mask
    north = shifted_2(south_faces[:, :1], "lat", -1)
    faces_y = jnp.concatenate([south_faces, north], axis=1)
    state = tracers
    for step in range(SUBSTEPS):
        ext = extended(state, (("lat", 2),), 3)
        state = lon_step(lat_step(ext, faces_y), wind_x)
    starts = jnp.cumsum(level_counts) - level_counts
    total_levels = source_level.shape[0]
    level_ids = jnp.arange(total_levels, dtype=jnp.int32)
    columns = lax.all_to_all(state, "lev", split_axis=3, concat_axis=1, tiled=True)
    owner = jnp.sum((starts[:, None] <= level_ids[None]).astype(jnp.int32), axis=0) - 1
    table = owner * depth + level_ids - jnp.take(starts, owner)
    compact = jnp.take(columns, table, axis=1)
    padded = jnp.pad(compact, ((0, 0), (3, TAPS - 1), (0, 0), (0, 0)), mode="edge")
    offsets = source_level - level_ids[:, None, None]
    return select_taps(padded, offsets, remap_weight, total_levels)


def solution(mesh):
    in_specs = (
        P(None, "lev", ("groups", "lat"), None),
        P("lev", ("groups", "lat"), None),
        P("lev", ("groups", "lat"), None),
        P(),
        P(None, ("groups", "lat"), "lev"),
        P(None, None, ("groups", "lat"), "lev"),
    )
    out_specs = P(None, None, ("groups", "lat"), "lev")
    return jax.shard_map(shards, mesh=mesh, in_specs=in_specs, out_specs=out_specs, check_vma=False)
```

profile of v0, /device:TPU:0, one launch (start us, length us, event | category | flops | bytes accessed | tf_op | source)
XLA Modules:
  0.0 115.9 jit_solution(12192553082553959515)
XLA Ops:
  0.0 1.5 %copy.84 = f32[8,2,18,1152]{3,0,2,1:T(8,128)S(1)} copy(f32[8,2,18,1152]{3,1,2,0:T(2,128)} %param.6) | data formatting | bytes 2654208 | tf_op args[0]
  1.5 4.9 %collective-permute-start.1 = (f32[8,2,3,1152]{3,0,2,1:T(8,128)S(1)}, f32[8,2,3,1152]{3,0,2,1:T(8,128)S(1)}, u32[]{:S(2)}, u32[]{:S(2)}) collective-permute-start(f32[8,2,3,1152]{3,0,2,1:T(8,128)S(1)} %get-tuple-element.22), channel_id=1, source_target_pairs={{0,4},{4,8},{8,12},{1,5},{5,9},{9,13},{2,6},{6,10},{10,14},{3,7},{... | collective-permute-start | bytes 663560 | tf_op jit(solution)/shard_map/ppermute | solution.py:24
  6.5 1.3 %collective-permute-start.2 = (f32[8,2,3,1152]{3,0,2,1:T(8,128)S(1)}, f32[8,2,3,1152]{3,0,2,1:T(8,128)S(1)}, u32[]{:S(2)}, u32[]{:S(2)}) collective-permute-start(f32[8,2,3,1152]{3,0,2,1:T(8,128)S(1)} %get-tuple-element.21), channel_id=1, source_target_pairs={{4,0},{8,4},{12,8},{5,1},{9,5},{13,9},{6,2},{10,6},{14,10},{7,3},{... | collective-permute-start | bytes 663560 | tf_op jit(solution)/shard_map/ppermute | solution.py:26
  7.9 1.3 %collective-permute-start = (f32[2,1,1152]{2,0,1:T(2,128)S(1)}, f32[2,1,1152]{2,0,1:T(2,128)S(1)}, u32[]{:S(2)}, u32[]{:S(2)}) collective-permute-start(f32[2,1,1152]{2,0,1:T(2,128)S(1)} %slice.325), channel_id=1, source_target_pairs={{4,0},{8,4},{12,8},{5,1},{9,5},{13,9},{6,2},{10,6},{14,10},{7,3},{... | collective-permute-start | bytes 27656 | tf_op jit(solution)/shard_map/ppermute | solution.py:13
  9.8 0.6 gather_fusion
  10.5 0.7 copy.85
  11.2 0.7 copy.87
  11.9 0.7 copy.88
  12.6 0.7 copy.89
  13.3 2.1 %collective-permute-done = f32[2,1,1152]{2,0,1:T(2,128)S(1)} collective-permute-done((f32[2,1,1152]{2,0,1:T(2,128)S(1)}, f32[2,1,1152]{2,0,1:T(2,128)S(1)}, u32[]{:S(2)}, u32[]{:S(2)}) %collective-permute-start) | collective-permute-done | bytes 9248 | tf_op jit(solution)/shard_map/ppermute | solution.py:13
  16.0 1.1 copy-done
  17.5 0.3 slice_subtract_fusion.7
  17.9 0.7 fusion.28
  18.7 0.8 fusion.75
  19.5 1.6 %concatenate.77 = f32[8,2,18,1158]{3,0,2,1:T(8,128)S(1)} concatenate(f32[8,2,18,3]{3,0,2,1:T(8,128)} %get-tuple-element.20, f32[8,2,18,1152]{3,0,2,1:T(8,128)S(1)} %fusion.62, f32[8,2,18,3]{3,0,2,1:T(8,128)} %get-tuple-element.19), dimensions={3} | concatenate | bytes 2668032 | tf_op jit(solution)/shard_map/concatenate | solution.py:66
  21.2 2.2 %fusion.12 = f32[8,2,18,1155]{3,0,2,1:T(8,128)S(1)} fusion(f32[8,2,18,1158]{3,0,2,1:T(8,128)S(1)} %concatenate.77, f32[8,2,18,1152]{3,0,2,1:T(8,128)S(1)} %fusion.62, f32[8,2,18,3]{3,0,2,1:T(8,128)} %get-tuple-element.20, f32[8,2,18,3]{3,0,2,1:T(8,128)} %get-tuple-element.19), kind=kLoop, calls=%fused_computation.32 | loop fusion | flops 2328480 | bytes 5325696 | tf_op jit(solution)/shard_map/sub | solution.py:40
  23.4 0.8 slice_subtract_fusion.6
  24.7 1.2 %fusion.58 = f32[8,2,18,1152]{3,0,2,1:T(8,128)S(1)} fusion(f32[8,2,18,1154]{3,0,2,1:T(8,128)S(1)} %get-tuple-element.12, f32[8,2,18,1154]{3,0,2,1:T(8,128)S(1)} %get-tuple-element.11, f32[8,2,18,1155]{3,0,2,1:T(8,128)S(1)} %fusion.12, f32[2,18,1152]{2,1,0:T(8,128)S(1)} %copy-done.9, f32[2,18,1152]{2,1,0:T(8,128)S(1)} %copy-done.7, ...), kind=kLoop, calls=%fused_computation.95 | loop fusion | flops 3317760 | bytes 8667648 | tf_op jit(solution)/shard_map/mul | solution.py:56
  25.9 0.4 slice.352
  26.3 0.3 fusion.63
  26.7 3.5 %collective-permute-start.3 = (f32[8,2,3,1152]{3,0,2,1:T(8,128)S(1)}, f32[8,2,3,1152]{3,0,2,1:T(8,128)S(1)}, u32[]{:S(2)}, u32[]{:S(2)}) collective-permute-start(f32[8,2,3,1152]{3,0,2,1:T(8,128)S(1)} %get-tuple-element.17), channel_id=1, source_target_pairs={{0,4},{4,8},{8,12},{1,5},{5,9},{9,13},{2,6},{6,10},{10,14},{3,7},{... | collective-permute-start | bytes 663560 | tf_op jit(solution)/shard_map/ppermute | solution.py:24
  30.2 1.5 %collective-permute-start.4 = (f32[8,2,3,1152]{3,0,2,1:T(8,128)S(1)}, f32[8,2,3,1152]{3,0,2,1:T(8,128)S(1)}, u32[]{:S(2)}, u32[]{:S(2)}) collective-permute-start(f32[8,2,3,1152]{3,0,2,1:T(8,128)S(1)} %get-tuple-element.18), channel_id=1, source_target_pairs={{4,0},{8,4},{12,8},{5,1},{9,5},{13,9},{6,2},{10,6},{14,10},{7,3},{... | collective-permute-start | bytes 663560 | tf_op jit(solution)/shard_map/ppermute | solution.py:26
  31.7 2.2 %collective-permute-done.3 = f32[8,2,3,1152]{3,0,2,1:T(8,128)S(1)} collective-permute-done((f32[8,2,3,1152]{3,0,2,1:T(8,128)S(1)}, f32[8,2,3,1152]{3,0,2,1:T(8,128)S(1)}, u32[]{:S(2)}, u32[]{:S(2)}) %collective-permute-start.3) | collective-permute-done | bytes 221216 | tf_op jit(solution)/shard_map/ppermute | solution.py:24
  33.9 4.1 %collective-permute-done.4 = f32[8,2,3,1152]{3,0,2,1:T(8,128)S(1)} collective-permute-done((f32[8,2,3,1152]{3,0,2,1:T(8,128)S(1)}, f32[8,2,3,1152]{3,0,2,1:T(8,128)S(1)}, u32[]{:S(2)}, u32[]{:S(2)}) %collective-permute-start.4) | collective-permute-done | bytes 221216 | tf_op jit(solution)/shard_map/ppermute | solution.py:26
  38.1 0.3 fusion.1
  38.8 0.7 copy-done.2
  39.4 0.7 fusion.20
  40.4 0.9 concatenate.84
  41.3 1.2 %fusion.8 = f32[8,2,18,1155]{3,0,2,1:T(8,128)S(1)} fusion(f32[8,2,18,1158]{3,0,2,1:T(8,128)S(1)} %concatenate.84, f32[8,2,18,1152]{3,0,2,1:T(8,128)S(1)} %fusion.53, f32[8,2,18,3]{3,0,2,1:T(8,128)S(1)} %get-tuple-element.16, f32[8,2,18,3]{3,0,2,1:T(8,128)S(1)} %get-tuple-element.15), kind=kLoop, calls=%fused_computation.25 | loop fusion | flops 2328480 | bytes 5325696 | tf_op jit(solution)/shard_map/sub | solution.py:40
  42.6 0.9 slice_subtract_fusion.4
  43.8 1.2 %fusion.49 = f32[8,2,18,1152]{3,0,2,1:T(8,128)S(1)} fusion(f32[8,2,18,1154]{3,0,2,1:T(8,128)S(1)} %get-tuple-element.10, f32[8,2,18,1154]{3,0,2,1:T(8,128)S(1)} %get-tuple-element.9, f32[8,2,18,1155]{3,0,2,1:T(8,128)S(1)} %fusion.8, f32[2,18,1152]{2,1,0:T(8,128)S(1)} %copy-done.10, f32[2,18,1152]{2,1,0:T(8,128)S(1)} %copy-done.8, ...), kind=kLoop, calls=%fused_computation.83 | loop fusion | flops 3317760 | bytes 8667648 | tf_op jit(solution)/shard_map/mul | solution.py:56
  45.1 0.4 slice.380
  45.5 0.3 fusion.64
  45.8 5.6 %copy.90 = f32[8,2,18,1152]{2,0,1,3:T(8,128)} copy(f32[8,2,18,1152]{3,0,2,1:T(8,128)S(1)} %fusion.64) | data formatting | bytes 2654208 | tf_op jit(solution)/shard_map/sub | solution.py:68
  51.4 11.5 %reshape.211 = f32[4,1,82944]{2,1,0:T(1,128)} reshape(f32[1152,2,8,18]{3,2,1,0:T(8,128)} %bitcast.49) | data formatting | bytes 2654208
  62.9 3.9 %all-to-all-start = ((f32[4,1,82944]{2,1,0:T(1,128)}), f32[4,1,82944]{2,1,0:T(1,128)S(1)}, u32[]{:S(2)}, u32[]{:S(2)}) async-start(f32[4,1,82944]{2,1,0:T(1,128)} %reshape.211), calls=%async_computation | async-start | bytes 2654208 | tf_op jit(solution)/shard_map/all_to_all | solution.py:98
  66.8 0.8 fusion.67
  67.6 0.5 fusion.77
  68.0 0.8 copy_bitcast_fusion
  68.8 0.8 copy_bitcast_fusion.2
  69.7 14.3 %all-to-all-done = f32[4,1,82944]{2,1,0:T(1,128)S(1)} async-done(((f32[4,1,82944]{2,1,0:T(1,128)}), f32[4,1,82944]{2,1,0:T(1,128)S(1)}, u32[]{:S(2)}, u32[]{:S(2)}) %all-to-all-start) | async-done | bytes 1327136 | tf_op jit(solution)/shard_map/all_to_all | solution.py:98
  84.0 0.5 broadcast.343
  84.5 4.5 %reduce = f32[4,82944]{1,0:T(4,128)S(1)} reduce(f32[4,1,82944]{2,1,0:T(1,128)S(1)} %all-to-all-done, f32[]{:T(128)} %broadcast.343), dimensions={1}, to_apply=%all_to_all.13.reduce_sub_computation | reduce | bytes 2654212 | tf_op jit(solution)/shard_map/all_to_all | solution.py:98
  89.0 14.7 %reshape.212 = f32[1152,2,8,18]{3,2,1,0:T(8,128)} reshape(f32[4,82944]{1,0:T(4,128)S(1)} %reduce) | data formatting | bytes 2654208
  103.7 7.5 %copy.96 = f32[8,2,18,4,288]{4,3,0,2,1:T(4,128)S(1)} copy(f32[8,2,18,4,288]{2,0,1,4,3:T(8,128)} %bitcast.50) | data formatting | bytes 2654208 | tf_op jit(solution)/shard_map/all_to_all | solution.py:98
  111.3 0.6 gather_fusion.1
  112.3 0.7 copy-done.12
  113.4 2.5 %fusion.38 = f32[8,6,18,288]{3,0,2,1:T(8,128)} fusion(f32[8,3,18,288]{3,0,2,1:T(8,128)S(1)} %reshape.194, f32[8,6,18,288]{3,0,2,1:T(8,128)S(1)} %select_bitcast_fusion, f32[8,3,18,288]{3,0,2,1:T(8,128)S(1)} %reshape.193, f32[6,18,288]{2,1,0:T(8,128)S(1)} %copy-done.12, f32[6,18,288]{2,1,0:T(8,128)S(1)} %copy-done.13, f32[6,18,288]{2,1,0:T(8,128)S(1)} %copy-done.14, ...), kind=kLoop, calls=%fused_computation.70 | loop fusion | flops 6220800 | bytes 3576960 | tf_op jit(solution)/shard_map/add | solution.py:78
  (88 shorter events, 4.0 us)
Async XLA Ops:
  0.0 7.8 %copy-start.23 = (f32[2,18,1152]{2,0,1:T(2,128)S(1)}, f32[2,18,1152]{2,0,1:T(2,128)}, u32[]{:S(2)}) copy-start(f32[2,18,1152]{2,0,1:T(2,128)} %param.8) | copy-start | bytes 497668
  0.0 9.2 %copy-start.11 = (f32[2,18,1152]{2,0,1:T(2,128)S(1)}, f32[2,18,1152]{2,0,1:T(2,128)}, u32[]{:S(2)}) copy-start(f32[2,18,1152]{2,0,1:T(2,128)} %param.7) | copy-start | bytes 497668
  1.5 8.1 %copy-start.24 = (s32[4]{0:T(128)S(1)}, s32[4]{0:T(128)}, u32[]{:S(2)}) copy-start(s32[4]{0:T(128)} %param.9) | copy-start | bytes 52
  1.5 14.5 %collective-permute-start.1 = (f32[8,2,3,1152]{3,0,2,1:T(8,128)S(1)}, f32[8,2,3,1152]{3,0,2,1:T(8,128)S(1)}, u32[]{:S(2)}, u32[]{:S(2)}) collective-permute-start(f32[8,2,3,1152]{3,0,2,1:T(8,128)S(1)} %get-tuple-element.22), channel_id=1, source_target_pairs={{0,4},{4,8},{8,12},{1,5},{5,9},{9,13},{2,6},{6,10},{10,14},{3,7},{... | collective-permute-start | bytes 663560 | tf_op jit(solution)/shard_map/ppermute | solution.py:24
  6.5 10.7 %collective-permute-start.2 = (f32[8,2,3,1152]{3,0,2,1:T(8,128)S(1)}, f32[8,2,3,1152]{3,0,2,1:T(8,128)S(1)}, u32[]{:S(2)}, u32[]{:S(2)}) collective-permute-start(f32[8,2,3,1152]{3,0,2,1:T(8,128)S(1)} %get-tuple-element.21), channel_id=1, source_target_pairs={{4,0},{8,4},{12,8},{5,1},{9,5},{13,9},{6,2},{10,6},{14,10},{7,3},{... | collective-permute-start | bytes 663560 | tf_op jit(solution)/shard_map/ppermute | solution.py:26
  7.9 7.5 %collective-permute-start = (f32[2,1,1152]{2,0,1:T(2,128)S(1)}, f32[2,1,1152]{2,0,1:T(2,128)S(1)}, u32[]{:S(2)}, u32[]{:S(2)}) collective-permute-start(f32[2,1,1152]{2,0,1:T(2,128)S(1)} %slice.325), channel_id=1, source_target_pairs={{4,0},{8,4},{12,8},{5,1},{9,5},{13,9},{6,2},{10,6},{14,10},{7,3},{... | collective-permute-start | bytes 27656 | tf_op jit(solution)/shard_map/ppermute | solution.py:13
  15.7 1.4 %copy-start = (f32[8,2,18,1152]{3,1,2,0:T(2,128)S(1)}, f32[8,2,18,1152]{3,1,2,0:T(2,128)}, u32[]{:S(2)}) copy-start(f32[8,2,18,1152]{3,1,2,0:T(2,128)} %param.6) | copy-start | bytes 3981316
  15.8 2.0 %copy-start.1 = (f32[2,19,1152]{2,1,0:T(8,128)}, f32[2,19,1152]{2,1,0:T(8,128)S(1)}, u32[]{:S(2)}) copy-start(f32[2,19,1152]{2,1,0:T(8,128)S(1)} %copy.83) | copy-start | bytes 525316
  16.0 1.8 %copy-start.17 = (pred[2,19,1152]{2,1,0:T(8,128)(4,1)}, pred[2,19,1152]{2,1,0:T(8,128)(4,1)S(1)}, u32[]{:S(2)}) copy-start(pred[2,19,1152]{2,1,0:T(8,128)(4,1)S(1)} %copy.75) | copy-start | bytes 131332
  23.4 0.9 copy-start.3
  23.4 1.0 copy-start.5
  23.4 1.1 copy-start.7
  23.4 1.2 %copy-start.9 = (f32[2,18,1152]{2,1,0:T(8,128)S(1)}, f32[2,18,1152]{2,1,0:T(8,128)}, u32[]{:S(2)}) copy-start(f32[2,18,1152]{2,1,0:T(8,128)} %copy.89) | copy-start | bytes 497668
  26.7 7.2 %collective-permute-start.3 = (f32[8,2,3,1152]{3,0,2,1:T(8,128)S(1)}, f32[8,2,3,1152]{3,0,2,1:T(8,128)S(1)}, u32[]{:S(2)}, u32[]{:S(2)}) collective-permute-start(f32[8,2,3,1152]{3,0,2,1:T(8,128)S(1)} %get-tuple-element.17), channel_id=1, source_target_pairs={{0,4},{4,8},{8,12},{1,5},{5,9},{9,13},{2,6},{6,10},{10,14},{3,7},{... | collective-permute-start | bytes 663560 | tf_op jit(solution)/shard_map/ppermute | solution.py:24
  30.2 7.8 %collective-permute-start.4 = (f32[8,2,3,1152]{3,0,2,1:T(8,128)S(1)}, f32[8,2,3,1152]{3,0,2,1:T(8,128)S(1)}, u32[]{:S(2)}, u32[]{:S(2)}) collective-permute-start(f32[8,2,3,1152]{3,0,2,1:T(8,128)S(1)} %get-tuple-element.18), channel_id=1, source_target_pairs={{4,0},{8,4},{12,8},{5,1},{9,5},{13,9},{6,2},{10,6},{14,10},{7,3},{... | collective-permute-start | bytes 663560 | tf_op jit(solution)/shard_map/ppermute | solution.py:26
  38.5 0.9 copy-start.2
  38.5 0.9 copy-start.18
  42.6 0.9 copy-start.4
  42.6 1.0 copy-start.6
  42.6 1.1 copy-start.8
  42.6 1.2 %copy-start.10 = (f32[2,18,1152]{2,1,0:T(8,128)S(1)}, f32[2,18,1152]{2,1,0:T(8,128)}, u32[]{:S(2)}) copy-start(f32[2,18,1152]{2,1,0:T(8,128)} %copy.89) | copy-start | bytes 497668
  62.9 3.9 %copy-start.22 = (s32[6,18,288]{2,1,0:T(8,128)S(1)}, s32[6,18,288]{2,1,0:T(8,128)}, u32[]{:S(2)}) copy-start(s32[6,18,288]{2,1,0:T(8,128)} %param.10) | copy-start | bytes 373252
  62.9 4.7 %copy-start.16 = (f32[4,6,18,288]{3,0,2,1:T(4,128)S(1)}, f32[4,6,18,288]{3,0,2,1:T(4,128)}, u32[]{:S(2)}) copy-start(f32[4,6,18,288]{3,0,2,1:T(4,128)} %param.11) | copy-start | bytes 1492996
  62.9 21.1 %all-to-all-start = ((f32[4,1,82944]{2,1,0:T(1,128)}), f32[4,1,82944]{2,1,0:T(1,128)S(1)}, u32[]{:S(2)}, u32[]{:S(2)}) async-start(f32[4,1,82944]{2,1,0:T(1,128)} %reshape.211), calls=%async_computation | async-start | bytes 2654208 | tf_op jit(solution)/shard_map/all_to_all | solution.py:98
  112.1 0.9 copy-start.12
  112.1 1.0 copy-start.13
  112.1 1.1 copy-start.14
  112.1 1.2 %copy-start.15 = (f32[6,18,288]{2,1,0:T(8,128)S(1)}, f32[6,18,288]{2,1,0:T(8,128)}, u32[]{:S(2)}) copy-start(f32[6,18,288]{2,1,0:T(8,128)} %get-tuple-element.40) | copy-start | bytes 373252
  112.1 1.2 %copy-start.19 = (pred[6,18,288]{2,1,0:T(8,128)(4,1)S(1)}, pred[6,18,288]{2,1,0:T(8,128)(4,1)}, u32[]{:S(2)}) copy-start(pred[6,18,288]{2,1,0:T(8,128)(4,1)} %get-tuple-element.27) | copy-start | bytes 93316
  112.2 1.2 %copy-start.20 = (pred[6,18,288]{2,1,0:T(8,128)(4,1)S(1)}, pred[6,18,288]{2,1,0:T(8,128)(4,1)}, u32[]{:S(2)}) copy-start(pred[6,18,288]{2,1,0:T(8,128)(4,1)} %get-tuple-element.28) | copy-start | bytes 93316
  112.2 1.2 %copy-start.21 = (pred[6,18,288]{2,1,0:T(8,128)(4,1)S(1)}, pred[6,18,288]{2,1,0:T(8,128)(4,1)}, u32[]{:S(2)}) copy-start(pred[6,18,288]{2,1,0:T(8,128)(4,1)} %get-tuple-element.29) | copy-start | bytes 93316
where the time goes:
time: 116 us
  local copies, waits for them, and re-layouts  55.8 us (48%)
  waiting for transfers between devices  22.8 us (20%)
  other arithmetic  20.3 us (18%)
  starting transfers between devices  16.4 us (14%)
    unnamed x56, local copies, waits for them, and re-layouts  32.1 us
    all_to_all x1, waiting for transfers between devices, shards(): lax.all_to_all(state, 'lev', split_axis=3, concat_axis=1, tiled=True)  14.3 us
    ppermute x2, starting transfers between devices, extended(): lax.ppermute(tail, axis, [(i, (i + 1) % count) for i in range(ends)])  8.43 us
    all_to_all x3, local copies, waits for them, and re-layouts, shards(): lax.all_to_all(state, 'lev', split_axis=3, concat_axis=1, tiled=True)  8.08 us
    sub x1, local copies, waits for them, and re-layouts, lon_step(): return field - (jnp.roll(flux, -1, axis=3) - flux)  5.55 us
    all_to_all x1, other arithmetic, shards(): lax.all_to_all(state, 'lev', split_axis=3, concat_axis=1, tiled=True)  4.48 us
    ppermute x2, waiting for transfers between devices, extended(): lax.ppermute(head, axis, [((i + 1) % count, i) for i in range(ends)])  4.13 us
    sub x4, other arithmetic, ppm_fluxes(): 7.0 / 12.0 * (cut(ext, 1, cells + 4, axis) + cut(ext, 2, cells + 5, axis))  4.03 us
  transfers between devices with their start and end apart: 6, of which 4 were waited for; matrix products, arithmetic and copies ran while one was open for 7% of the time, Pallas kernels for 0%

commit v1 on v0

v1 whole, which is shorter than its diff:
```python
import functools

import jax
import jax.numpy as jnp
from jax import lax
from jax.experimental import pallas as pl
from jax.experimental.pallas import tpu as pltpu
from jax.sharding import PartitionSpec as P

SUBSTEPS = 2
TAPS = 4
REACH = 3
HALO = REACH * SUBSTEPS
BLOCK = 6
LANES = 128
SUB = 8
FACES = 32


def spread(row):
    return jnp.broadcast_to(row, (SUB, LANES))


def lane_ids():
    return lax.broadcasted_iota(jnp.int32, (SUB, LANES), 1)


def from_west(tiles, steps, lane):
    turned = [pltpu.roll(t, steps, 1) for t in tiles]
    return [jnp.where(lane < steps, turned[j - 1], turned[j]) for j in range(len(tiles))]


def from_east(tiles, lane):
    turned = [pltpu.roll(t, LANES - 1, 1) for t in tiles]
    count = len(tiles)
    return [jnp.where(lane == LANES - 1, turned[(j + 1) % count], turned[j]) for j in range(count)]


def coefficients(wind):
    size = jnp.abs(wind)
    rest = 1.0 - size
    alpha = wind * rest * rest * (1.0 / 12.0)
    beta = wind * size * rest * (-1.0 / 12.0)
    gamma = wind * size * (3.0 - 2.0 * size)
    return alpha, beta, gamma


def packed_sizes(nlon, count):
    width = nlon // count
    mains, tail = width // LANES, width % LANES
    per = LANES // tail if tail else 1
    tails = -(-BLOCK // per) if tail else 0
    return width, mains, tail, per, BLOCK * mains + tails


def prep_kernel(rows, tracers, wx, wy, state, down, up):
    levels, nlon = state.shape[0], state.shape[3]
    nj = nlon // LANES
    row_stride = nj * levels
    tracer_stride = rows * row_stride

    def body(row, _):
        for level in range(levels):
            for j in range(nj):
                start = row * row_stride + j * levels + level
                state[level, row, :, j * LANES:(j + 1) * LANES] = tracers[pl.ds(start, SUB, stride=tracer_stride), :]
        return 0

    lax.fori_loop(0, rows, body, 0)
    for level in range(levels):
        for row in range(HALO):
            down[level, row] = state[level, row]
            up[level, row] = state[level, rows - HALO + row]
        for j in range(nj):
            lanes = slice(j * LANES, (j + 1) * LANES)
            at = lambda row: row * row_stride + j * levels + level
            down[level, HALO, 0:REACH, lanes] = wx[pl.ds(at(0), REACH, stride=row_stride), :]
            down[level, HALO, REACH:2 * REACH + 1, lanes] = wy[pl.ds(at(0), REACH + 1, stride=row_stride), :]
            up[level, HALO, 0:REACH, lanes] = wx[pl.ds(at(rows - REACH), REACH, stride=row_stride), :]
            up[level, HALO, REACH:2 * REACH + 1, lanes] = wy[pl.ds(at(rows - REACH - 1), REACH + 1, stride=row_stride), :]


def lat_pass(levels, nj, rows, cell, coef, store):
    def body(i, _):
        level = i // nj
        lanes = pl.ds(pl.multiple_of((i % nj) * LANES, LANES), LANES)
        for first, last in rows:
            a = {r: cell(level, r, lanes) for r in range(first - REACH, last + REACH)}
            inter = {f: 7.0 * (a[f - 1] + a[f]) - (a[f - 2] + a[f + 1]) for f in range(first - 1, last + 2)}
            flux = {}
            for f in range(first, last + 1):
                at = slice(f + REACH, f + REACH + 1)
                alpha, beta, gamma = [spread(coef[i, level, at, lanes]) for i in range(3)]
                north = gamma > 0
                behind = jnp.where(north, inter[f - 1], inter[f + 1])
                upwind = jnp.where(north, a[f - 1], a[f])
                flux[f] = alpha * inter[f] + beta * behind + gamma * upwind
                if f > first:
                    store(level, f - 1, lanes, a[f - 1] - (flux[f] - flux[f - 1]))
        return 0

    lax.fori_loop(0, levels * nj, body, 0)


def lon_row(b, alpha, beta, gamma, lane):
    count = len(b)
    each = range(count)
    west = from_west(b, 1, lane)
    west2 = from_west(b, 2, lane)
    east = from_east(b, lane)
    inter = [7.0 * (west[j] + b[j]) - (west2[j] + east[j]) for j in each]
    inter_w = from_west(inter, 1, lane)
    inter_e = from_east(inter, lane)
    flux = []
    for j in each:
        right = gamma[j] > 0
        behind = jnp.where(right, inter_w[j], inter_e[j])
        upwind = jnp.where(right, west[j], b[j])
        flux.append(alpha[j] * inter[j] + beta[j] * behind + gamma[j] * upwind)
    flux_e = from_east(flux, lane)
    return [b[j] - (flux_e[j] - flux[j]) for j in each]


def lon_block(level, row0, swept, coef, lane):
    nj = swept.shape[3] // LANES
    out = []
    for q in range(BLOCK):
        b = [swept[level, row0 + q, :, j * LANES:(j + 1) * LANES] for j in range(nj)]
        c = [[spread(coef[i, pl.ds((level * nj + j) * FACES + row0 + q, 1), :]) for j in range(nj)] for i in range(3)]
        out.append(lon_row(b, c[0], c[1], c[2], lane))
    return out


def pack_block(block, packed, level, number, count, lane):
    nlon = len(block[0]) * LANES
    width, mains, tail, per, size = packed_sizes(nlon, count)
    for d in range(count):
        j0, off = (d * width) // LANES, (d * width) % LANES
        for q, tiles in enumerate(block):
            turned = [pltpu.roll(tiles[j0 + m], LANES - off, 1) if off else tiles[j0 + m]
                      for m in range(mains + (1 if off else 0))]
            for m in range(mains):
                whole = jnp.where(lane < LANES - off, turned[m], turned[m + 1]) if off else turned[m]
                packed[d, level, number, q * mains + m] = whole
        if tail:
            for g in range(-(-BLOCK // per)):
                total = None
                for place in range(min(per, BLOCK - g * per)):
                    shift = (place * tail - off) % LANES
                    source = block[g * per + place][j0 + mains]
                    moved = pltpu.roll(source, shift, 1) if shift else source
                    total = moved if total is None else jnp.where(lane < place * tail, total, moved)
                packed[d, level, number, BLOCK * mains + g] = total


def transport_kernel(count, rows, state, low, high, wx, wy, packed, winds, cy, cx, swept, first):
    levels, nlon = state.shape[0], state.shape[3]
    nj = nlon // LANES
    row_stride = nj * levels
    lane = lane_ids()
    keep = (lax.axis_index("lat") != 0).astype(jnp.float32)

    for level in range(levels):
        winds[0, level, 0:REACH, :] = low[level, HALO, 0:REACH, :]
        winds[1, level, 0:REACH, :] = low[level, HALO, REACH + 1:2 * REACH + 1, :]
        winds[0, level, rows + REACH:rows + 2 * REACH, :] = high[level, HALO, 0:REACH, :]
        winds[1, level, rows + REACH:rows + 2 * REACH + 1, :] = high[level, HALO, REACH:2 * REACH + 1, :]
        for j in range(nj):
            lanes = slice(j * LANES, (j + 1) * LANES)
            own = pl.ds(j * levels + level, rows, stride=row_stride)
            winds[0, level, REACH:rows + REACH, lanes] = wx[own, :]
            winds[1, level, REACH:rows + REACH, lanes] = wy[own, :]
        winds[1, level, REACH:REACH + 1, :] = winds[1, level, REACH:REACH + 1, :] * keep

    def make(i, _):
        level = i // nj
        lanes = pl.ds(pl.multiple_of((i % nj) * LANES, LANES), LANES)
        parts = coefficients(winds[0, level, :, lanes])
        for p in range(3):
            cx[p, pl.ds(pl.multiple_of(i * FACES, FACES), FACES), :] = parts[p]
        parts = coefficients(winds[1, level, :, lanes])
        for p in range(3):
            cy[p, level, :, lanes] = parts[p]
        return 0

    lax.fori_loop(0, levels * nj, make, 0)

    def cell(level, row, lanes):
        if row < 0:
            return low[level, row + HALO, :, lanes]
        if row >= rows:
            return high[level, row - rows, :, lanes]
        return state[level, row, :, lanes]

    def put(level, row, lanes, value):
        swept[level, row + REACH, :, lanes] = value

    lat_pass(levels, nj, [(-REACH, rows + REACH)], cell, cy, put)
    blocks = (rows + 2 * REACH) // BLOCK

    def step(i, _):
        level, row0 = i // blocks, (i % blocks) * BLOCK
        done = lon_block(level, row0, swept, cx, lane)
        for q in range(BLOCK):
            for j in range(nj):
                first[level, row0 + q, :, j * LANES:(j + 1) * LANES] = done[q][j]
        return 0

    lax.fori_loop(0, levels * blocks, step, 0)

    def cell_first(level, row, lanes):
        return first[level, row + REACH, :, lanes]

    lat_pass(levels, nj, [(0, rows)], cell_first, cy, put)
    finals = rows // BLOCK

    def last(i, _):
        level, number = i // finals, i % finals
        done = lon_block(level, REACH + number * BLOCK, swept, cx, lane)
        pack_block(done, packed, level, number, count, lane)
        return 0

    lax.fori_loop(0, levels * finals, last, 0)


def weights_kernel(weights, source, out):
    targets, rows, taps, width = weights.shape

    for row in range(rows):
        for k in range(targets):
            lowest, highest = max(k - (TAPS - 1), 0), min(k, targets - TAPS)
            w = weights[k, row]
            w = jnp.concatenate([w, jnp.zeros((SUB - taps, width), jnp.float32)], axis=0)
            at = jnp.broadcast_to(source[k, row:row + 1, :], (SUB, width))
            total = w
            for g in range(lowest + 1, highest + 1):
                total = jnp.where(at == g, pltpu.roll(w, g - lowest, 0), total)
            out[k, row] = total


def remap_kernel(count, depth, counts, columns, weights, out):
    targets, rows, _, width = out.shape
    _, mains, tail, per, _ = packed_sizes(width * count, count)
    slots = []
    for level in range(targets):
        slot, start = jnp.int32(level), jnp.int32(0)
        for d in range(count):
            slot = jnp.where(level >= start, d * depth + level - start, slot)
            start = start + counts[d]
        slots.append(slot)

    def body(number, _):
        for q in range(BLOCK):
            row = number * BLOCK + q
            for m in range(mains + (1 if tail else 0)):
                wide = LANES if m < mains else tail
                lanes = slice(m * LANES, m * LANES + wide)
                values = []
                for level in range(targets):
                    if m < mains:
                        values.append(columns[slots[level], number, q * mains + m])
                    else:
                        tile = columns[slots[level], number, BLOCK * mains + q // per]
                        shift = (q % per) * tail
                        tile = pltpu.roll(tile, LANES - shift, 1) if shift else tile
                        values.append(tile[:, :wide])
                for k in range(targets):
                    lowest, highest = max(k - (TAPS - 1), 0), min(k, targets - TAPS) + TAPS - 1
                    total = None
                    for level in range(lowest, highest + 1):
                        j = level - lowest
                        w = jnp.broadcast_to(weights[k, row, j:j + 1, lanes], (SUB, wide))
                        term = w * values[level]
                        total = term if total is None else total + term
                    out[k, row, :, lanes] = total
        return 0

    lax.fori_loop(0, rows // BLOCK, body, 0)


def tiles_of(array):
    lead, levels, nlon = array.shape[:-2], array.shape[-2], array.shape[-1]
    split = array.reshape(lead + (levels, nlon // LANES, LANES))
    return jnp.swapaxes(split, -3, -2).reshape(-1, LANES)


VMEM = pl.BlockSpec(memory_space=pltpu.VMEM)
SMEM = pl.BlockSpec(memory_space=pltpu.SMEM)


def call(kernel, outs, args, specs=None, scratch=(), cost=None):
    return pl.pallas_call(
        kernel,
        out_shape=outs,
        in_specs=specs or [VMEM] * len(args),
        out_specs=jax.tree.map(lambda _: VMEM, outs),
        scratch_shapes=list(scratch),
        compiler_params=pltpu.CompilerParams(vmem_limit_bytes=40 << 20),
        cost_estimate=cost,
    )(*args)


def cost(flops, size):
    return pl.CostEstimate(flops=int(flops), bytes_accessed=int(size), transcendentals=0)


def f32(*shape):
    return jax.ShapeDtypeStruct(shape, jnp.float32)


def shards(tracers, wind_x, wind_y, level_counts, source_level, remap_weight):
    count = lax.axis_size("lev")
    bands = lax.axis_size("lat")
    number, depth, rows, nlon = tracers.shape
    targets, _, width = source_level.shape
    _, mains, tail, per, size = packed_sizes(nlon, count)
    finals = rows // BLOCK

    raw = tiles_of(jnp.transpose(tracers, (0, 2, 1, 3)))
    wx = tiles_of(jnp.transpose(wind_x, (1, 0, 2)))
    wy = tiles_of(jnp.transpose(wind_y, (1, 0, 2)))
    halo = f32(depth, HALO + 1, number, nlon)
    state, down, up = call(
        functools.partial(prep_kernel, rows),
        (f32(depth, rows, number, nlon), halo, halo), (raw, wx, wy),
        cost=cost(1, 8 * tracers.size))
    low = lax.ppermute(up, "lat", [(i, i + 1) for i in range(bands - 1)])
    high = lax.ppermute(down, "lat", [(i + 1, i) for i in range(bands - 1)])
    taps = call(
        weights_kernel, f32(targets, rows, SUB, width),
        (jnp.transpose(remap_weight, (1, 2, 0, 3)), source_level),
        cost=cost(20 * remap_weight.size, 16 * remap_weight.size))
    ext = rows + 2 * REACH
    packed = call(
        functools.partial(transport_kernel, count, rows),
        f32(count, depth, finals, size, SUB, LANES), (state, low, high, wx, wy),
        scratch=[
            pltpu.VMEM((2, depth, FACES, nlon), jnp.float32),
            pltpu.VMEM((3, depth, FACES, nlon), jnp.float32),
            pltpu.VMEM((3, depth * (nlon // LANES) * FACES, LANES), jnp.float32),
            pltpu.VMEM((depth, ext, number, nlon), jnp.float32),
            pltpu.VMEM((depth, ext, number, nlon), jnp.float32),
        ],
        cost=cost(120 * tracers.size, 8 * tracers.size))
    columns = lax.all_to_all(packed, "lev", split_axis=0, concat_axis=0, tiled=True)
    columns = columns.reshape(count * depth, finals, size, SUB, LANES)
    out = call(
        functools.partial(remap_kernel, count, depth),
        f32(targets, rows, number, width), (level_counts, columns, taps),
        specs=[SMEM, VMEM, VMEM],
        cost=cost(60 * remap_weight.size, 16 * remap_weight.size))
    return jnp.transpose(out, (2, 0, 1, 3))


def solution(mesh):
    in_specs = (
        P(None, "lev", ("groups", "lat"), None),
        P("lev", ("groups", "lat"), None),
        P("lev", ("groups", "lat"), None),
        P(),
        P(None, ("groups", "lat"), "lev"),
        P(None, None, ("groups", "lat"), "lev"),
    )
    out_specs = P(None, None, ("groups", "lat"), "lev")
    return jax.shard_map(shards, mesh=mesh, in_specs=in_specs, out_specs=out_specs, check_vma=False)
```

time: 116 us -> 66.4 us (0.57)
  local copies, waits for them, and re-layouts: 55.8 us -> 6.23 us
  other arithmetic: 20.3 us -> 0 us
  Pallas kernels: 0 us -> 19.2 us
  waiting for transfers between devices: 22.8 us -> 30.6 us
  starting transfers between devices: 16.4 us -> 9.93 us
    unnamed x56 -> x10, local copies, waits for them, and re-layouts: 32.1 us -> 0.95 us
    pallas_call x0 -> x4, Pallas kernels: none -> 19.2 us  [call(): pl.pallas_call(kernel, out_shape=outs, in_specs=specs or [VMEM] * len(arg...]
    all_to_all x3 -> x0, local copies, waits for them, and re-layouts: 8.08 us -> none  [shards(): lax.all_to_all(state, 'lev', split_axis=3, concat_axis=1, tiled=True)]
    sub x13 -> x0, other arithmetic: 7.23 us -> none  [the longest x4 4.03 us: ppm_fluxes(): 7.0 / 12.0 * (cut(ext, 1, cells + 4, axis) + cut(ext, 2, cells + 5, axis))]
    sub x3 -> x0, local copies, waits for them, and re-layouts: 6.27 us -> none  [the longest x1 5.55 us: lon_step(): return field - (jnp.roll(flux, -1, axis=3) - flux)]
    ppermute x5 -> x2, starting transfers between devices: 12.5 us -> 6.25 us  [the longest x1 4.96 us: shards(): low = lax.ppermute(up, 'lat', [(i, i + 1) for i in range(bands - 1)])]
    ppermute x5 -> x2, waiting for transfers between devices: 8.45 us -> 13.8 us  [the longest x1 9.66 us: shards(): low = lax.ppermute(up, 'lat', [(i, i + 1) for i in range(bands - 1)])]
    all_to_all x1 -> x0, other arithmetic: 4.48 us -> none  [shards(): lax.all_to_all(state, 'lev', split_axis=3, concat_axis=1, tiled=True)]
  transfers between devices with their start and end apart: 6 -> 3, of which waited for: 4 -> 3; matrix products, arithmetic and copies ran while one was open for 7% -> 0% of each run, Pallas kernels for 0% -> 0%
where the time goes in v1:
time: 66.4 us; the launch traced here: 66.1 us
  waiting for transfers between devices  30.6 us (46%)
  Pallas kernels  19.2 us (29%)
  starting transfers between devices  9.93 us (15%)
  local copies, waits for them, and re-layouts  6.23 us (9%)
    pallas_call x4, Pallas kernels, call(): pl.pallas_call(kernel, out_shape=outs, in_specs=specs or [VMEM] * len(arg...  19.2 us
    all_to_all x1, waiting for transfers between devices, shards(): lax.all_to_all(packed, 'lev', split_axis=0, concat_axis=0, tiled=True)  16.8 us
    ppermute x1, waiting for transfers between devices, shards(): low = lax.ppermute(up, 'lat', [(i, i + 1) for i in range(bands - 1)])  9.66 us
    ppermute x1, starting transfers between devices, shards(): low = lax.ppermute(up, 'lat', [(i, i + 1) for i in range(bands - 1)])  4.96 us
    ppermute x1, waiting for transfers between devices, shards(): high = lax.ppermute(down, 'lat', [(i + 1, i) for i in range(bands - 1)])  4.14 us
    all_to_all x1, starting transfers between devices, shards(): lax.all_to_all(packed, 'lev', split_axis=0, concat_axis=0, tiled=True)  3.68 us
    reshape x3, local copies, waits for them, and re-layouts, tiles_of(): split = array.reshape(lead + (levels, nlon // LANES, LANES))  2.7 us
  transfers between devices with their start and end apart: 3, of which 3 were waited for; matrix products, arithmetic and copies ran while one was open for 0% of the time, Pallas kernels for 0%

profile of v1, /device:TPU:0, one launch (start us, length us, event | category | flops | bytes accessed | tf_op | source)
XLA Modules:
  0.0 66.1 jit_solution(13090312547570231944)
XLA Ops:
  0.0 0.0 copy-start.4
  0.0 0.0 copy-start.3
  0.0 1.2 %reshape.23 = f32[18,2,9,128]{3,2,1,0:T(8,128)S(1)} reshape(f32[18,2,1152]{2,1,0:T(2,128)} %bitcast.21) | data formatting | bytes 331776 | tf_op jit(solution)/shard_map/reshape | solution.py:283
  1.2 0.1 copy.12
  1.3 0.1 reshape.24.wx
  1.4 0.0 copy-done.4
  1.4 0.1 reshape.25
  1.5 0.1 copy.13
  1.6 0.1 reshape.26.wy
  1.8 0.0 copy-done.3
  1.8 1.1 %copy.10 = f32[8,18,2,1152]{3,0,2,1:T(8,128)} copy(f32[8,18,2,1152]{3,2,1,0:T(2,128)S(1)} %bitcast.18) | data formatting | bytes 2654208 | tf_op jit(solution)/shard_map/transpose | solution.py:319
  2.9 1.4 %reshape.21 = f32[8,18,2,9,128]{4,3,0,2,1:T(8,128)S(1)} reshape(f32[8,18,2,1152]{3,0,2,1:T(8,128)} %copy.10) | data formatting | bytes 2654208 | tf_op jit(solution)/shard_map/reshape | solution.py:283
  4.3 1.0 %copy.11 = f32[8,18,9,2,128]{4,3,2,1,0:T(2,128)S(1)} copy(f32[8,18,9,2,128]{4,2,0,3,1:T(8,128)S(1)} %bitcast.17) | data formatting | bytes 2654208 | tf_op jit(solution)/shard_map/transpose | solution.py:284
  5.4 0.3 shard_map.64
  5.6 5.0 %collective-permute-start = (f32[2,7,8,1152]{3,2,1,0:T(8,128)S(1)}, f32[2,7,8,1152]{3,2,1,0:T(8,128)S(1)}, u32[]{:S(2)}, u32[]{:S(2)}) collective-permute-start(f32[2,7,8,1152]{3,2,1,0:T(8,128)S(1)} %get-tuple-element.9), channel_id=1, source_target_pairs={{0,4},{4,8},{8,12},{1,5},{5,9},{9,13},{2,6},{6,10},{10,14},{3,7},{... | collective-permute-start | bytes 1548296 | tf_op jit(solution)/shard_map/ppermute | solution.py:327
  10.6 1.3 %collective-permute-start.1 = (f32[2,7,8,1152]{3,2,1,0:T(8,128)S(1)}, f32[2,7,8,1152]{3,2,1,0:T(8,128)S(1)}, u32[]{:S(2)}, u32[]{:S(2)}) collective-permute-start(f32[2,7,8,1152]{3,2,1,0:T(8,128)S(1)} %get-tuple-element.10), channel_id=1, source_target_pairs={{4,0},{8,4},{12,8},{5,1},{9,5},{13,9},{6,2},{10,6},{14,10},{7,3},{... | collective-permute-start | bytes 1548296 | tf_op jit(solution)/shard_map/ppermute | solution.py:328
  11.9 9.7 %collective-permute-done.low = f32[2,7,8,1152]{3,2,1,0:T(8,128)S(1)} collective-permute-done((f32[2,7,8,1152]{3,2,1,0:T(8,128)S(1)}, f32[2,7,8,1152]{3,2,1,0:T(8,128)S(1)}, u32[]{:S(2)}, u32[]{:S(2)}) %collective-permute-start) | collective-permute-done | bytes 516128 | tf_op jit(solution)/shard_map/ppermute | solution.py:327
  21.6 4.1 %collective-permute-done.1.high = f32[2,7,8,1152]{3,2,1,0:T(8,128)S(1)} collective-permute-done((f32[2,7,8,1152]{3,2,1,0:T(8,128)S(1)}, f32[2,7,8,1152]{3,2,1,0:T(8,128)S(1)}, u32[]{:S(2)}, u32[]{:S(2)}) %collective-permute-start.1) | collective-permute-done | bytes 516128 | tf_op jit(solution)/shard_map/ppermute | solution.py:328
  25.7 16.4 %shard_map.65 = f32[4,2,3,14,8,128]{5,4,3,2,1,0:T(8,128)} custom-call(f32[2,18,8,1152]{3,2,1,0:T(8,128)S(1)} %get-tuple-element.8.state, f32[2,7,8,1152]{3,2,1,0:T(8,128)S(1)} %collective-permute-done.low, f32[2,7,8,1152]{3,2,1,0:T(8,128)S(1)} %collective-permute-done.1.high, f32[324,128]{1,0:T(8,128)S(1)} %reshape.24.wx, f32[324,128]{1,0:T(8,128)S(1)} %reshape.26.wy), custom_call_target="tpu_custom_call" | custom-call | flops 39813120 | bytes 2654208 | tf_op jit(solution)/shard_map/pallas_call | solution.py:292
  42.1 0.0 copy-start
  42.2 3.7 %all-to-all-start = ((f32[4,2,3,14,8,128]{5,4,3,2,1,0:T(8,128)}), f32[4,2,3,14,8,128]{5,4,3,2,1,0:T(8,128)S(1)}, u32[]{:S(2)}, u32[]{:S(2)}) async-start(f32[4,2,3,14,8,128]{5,4,3,2,1,0:T(8,128)} %shard_map.65), calls=%async_computation | async-start | bytes 2752512 | tf_op jit(solution)/shard_map/all_to_all | solution.py:345
  45.8 0.0 copy-start.2
  45.8 0.0 copy-done
  45.9 0.0 copy-start.1
  45.9 0.9 %copy-done.1 = s32[6,18,288]{2,1,0:T(8,128)S(1)} copy-done((s32[6,18,288]{2,1,0:T(8,128)S(1)}, s32[6,18,288]{2,1,0:T(8,128)}, u32[]{:S(2)}) %copy-start.1) | copy-done | bytes 124440
  46.8 0.2 shard_map.66.weights
  47.0 16.8 %all-to-all-done = f32[4,2,3,14,8,128]{5,4,3,2,1,0:T(8,128)S(1)} async-done(((f32[4,2,3,14,8,128]{5,4,3,2,1,0:T(8,128)}), f32[4,2,3,14,8,128]{5,4,3,2,1,0:T(8,128)S(1)}, u32[]{:S(2)}, u32[]{:S(2)}) %all-to-all-start) | async-done | bytes 1376288 | tf_op jit(solution)/shard_map/all_to_all | solution.py:345
  63.8 0.0 copy-done.2
  63.8 2.3 %shard_map.67 = f32[6,18,8,288]{3,2,1,0:T(8,128)} custom-call(s32[4]{0:T(128)S(1)} %copy-done.2, f32[8,3,14,8,128]{4,3,2,1,0:T(8,128)S(1)} %bitcast.14, f32[6,18,8,288]{3,2,1,0:T(8,128)S(1)} %shard_map.66.weights), custom_call_target="tpu_custom_call" | custom-call | flops 7464960 | bytes 1990656 | tf_op jit(solution)/shard_map/pallas_call | solution.py:292
Async XLA Ops:
  0.0 1.4 %copy-start.4 = (f32[2,18,1152]{2,0,1:T(2,128)S(1)}, f32[2,18,1152]{2,0,1:T(2,128)}, u32[]{:S(2)}) copy-start(f32[2,18,1152]{2,0,1:T(2,128)} %param.8) | copy-start | bytes 497668
  0.0 1.8 %copy-start.3 = (f32[8,2,18,1152]{3,1,2,0:T(2,128)S(1)}, f32[8,2,18,1152]{3,1,2,0:T(2,128)}, u32[]{:S(2)}) copy-start(f32[8,2,18,1152]{3,1,2,0:T(2,128)} %param.6) | copy-start | bytes 3981316
  5.6 15.9 %collective-permute-start = (f32[2,7,8,1152]{3,2,1,0:T(8,128)S(1)}, f32[2,7,8,1152]{3,2,1,0:T(8,128)S(1)}, u32[]{:S(2)}, u32[]{:S(2)}) collective-permute-start(f32[2,7,8,1152]{3,2,1,0:T(8,128)S(1)} %get-tuple-element.9), channel_id=1, source_target_pairs={{0,4},{4,8},{8,12},{1,5},{5,9},{9,13},{2,6},{6,10},{10,14},{3,7},{... | collective-permute-start | bytes 1548296 | tf_op jit(solution)/shard_map/ppermute | solution.py:327
  10.6 15.1 %collective-permute-start.1 = (f32[2,7,8,1152]{3,2,1,0:T(8,128)S(1)}, f32[2,7,8,1152]{3,2,1,0:T(8,128)S(1)}, u32[]{:S(2)}, u32[]{:S(2)}) collective-permute-start(f32[2,7,8,1152]{3,2,1,0:T(8,128)S(1)} %get-tuple-element.10), channel_id=1, source_target_pairs={{4,0},{8,4},{12,8},{5,1},{9,5},{13,9},{6,2},{10,6},{14,10},{7,3},{... | collective-permute-start | bytes 1548296 | tf_op jit(solution)/shard_map/ppermute | solution.py:328
  42.1 3.7 %copy-start = (f32[4,6,18,288]{3,0,2,1:T(4,128)S(1)}, f32[4,6,18,288]{3,0,2,1:T(4,128)}, u32[]{:S(2)}) copy-start(f32[4,6,18,288]{3,0,2,1:T(4,128)} %param.11) | copy-start | bytes 1492996
  42.2 21.6 %all-to-all-start = ((f32[4,2,3,14,8,128]{5,4,3,2,1,0:T(8,128)}), f32[4,2,3,14,8,128]{5,4,3,2,1,0:T(8,128)S(1)}, u32[]{:S(2)}, u32[]{:S(2)}) async-start(f32[4,2,3,14,8,128]{5,4,3,2,1,0:T(8,128)} %shard_map.65), calls=%async_computation | async-start | bytes 2752512 | tf_op jit(solution)/shard_map/all_to_all | solution.py:345
  45.8 17.9 %copy-start.2 = (s32[4]{0:T(128)S(1)}, s32[4]{0:T(128)}, u32[]{:S(2)}) copy-start(s32[4]{0:T(128)} %counts.1) | copy-start | bytes 52
  45.9 0.9 %copy-start.1 = (s32[6,18,288]{2,1,0:T(8,128)S(1)}, s32[6,18,288]{2,1,0:T(8,128)}, u32[]{:S(2)}) copy-start(s32[6,18,288]{2,1,0:T(8,128)} %source.1) | copy-start | bytes 373252

commit v2 on v1

--- a/solution.py
+++ b/solution.py
@@ -4,6 +4,7 @@
 import jax.numpy as jnp
 from jax import lax
 from jax.experimental import pallas as pl
+from jax.experimental.layout import Layout, with_layout_constraint
 from jax.experimental.pallas import tpu as pltpu
 from jax.sharding import PartitionSpec as P
 
@@ -14,7 +15,6 @@
 BLOCK = 6
 LANES = 128
 SUB = 8
-FACES = 32
 
 
 def spread(row):
@@ -80,17 +80,16 @@
             up[level, HALO, REACH:2 * REACH + 1, lanes] = wy[pl.ds(at(rows - REACH - 1), REACH + 1, stride=row_stride), :]
 
 
-def lat_pass(levels, nj, rows, cell, coef, store):
+def lat_pass(levels, nj, ranges, cell, coef, store):
     def body(i, _):
         level = i // nj
         lanes = pl.ds(pl.multiple_of((i % nj) * LANES, LANES), LANES)
-        for first, last in rows:
+        for first, last in ranges:
             a = {r: cell(level, r, lanes) for r in range(first - REACH, last + REACH)}
             inter = {f: 7.0 * (a[f - 1] + a[f]) - (a[f - 2] + a[f + 1]) for f in range(first - 1, last + 2)}
             flux = {}
             for f in range(first, last + 1):
-                at = slice(f + REACH, f + REACH + 1)
-                alpha, beta, gamma = [spread(coef[i, level, at, lanes]) for i in range(3)]
+                alpha, beta, gamma = [spread(coef(i, level, f, lanes)) for i in range(3)]
                 north = gamma > 0
                 behind = jnp.where(north, inter[f - 1], inter[f + 1])
                 upwind = jnp.where(north, a[f - 1], a[f])
@@ -102,32 +101,33 @@
     lax.fori_loop(0, levels * nj, body, 0)
 
 
-def lon_row(b, alpha, beta, gamma, lane):
-    count = len(b)
-    each = range(count)
-    west = from_west(b, 1, lane)
-    west2 = from_west(b, 2, lane)
-    east = from_east(b, lane)
-    inter = [7.0 * (west[j] + b[j]) - (west2[j] + east[j]) for j in each]
-    inter_w = from_west(inter, 1, lane)
-    inter_e = from_east(inter, lane)
-    flux = []
-    for j in each:
-        right = gamma[j] > 0
-        behind = jnp.where(right, inter_w[j], inter_e[j])
-        upwind = jnp.where(right, west[j], b[j])
-        flux.append(alpha[j] * inter[j] + beta[j] * behind + gamma[j] * upwind)
-    flux_e = from_east(flux, lane)
-    return [b[j] - (flux_e[j] - flux[j]) for j in each]
-
-
-def lon_block(level, row0, swept, coef, lane):
+def tile(j):
+    return slice(j * LANES, (j + 1) * LANES)
+
+
+def lon_block(level, row0, swept, at, coef, inter, west, flux, lane):
     nj = swept.shape[3] // LANES
+    each = range(nj)
     out = []
     for q in range(BLOCK):
-        b = [swept[level, row0 + q, :, j * LANES:(j + 1) * LANES] for j in range(nj)]
-        c = [[spread(coef[i, pl.ds((level * nj + j) * FACES + row0 + q, 1), :]) for j in range(nj)] for i in range(3)]
-        out.append(lon_row(b, c[0], c[1], c[2], lane))
+        b = [swept[level, at + q, :, tile(j)] for j in each]
+        w1, w2, e1 = from_west(b, 1, lane), from_west(b, 2, lane), from_east(b, lane)
+        for j in each:
+            inter[q, :, tile(j)] = 7.0 * (w1[j] + b[j]) - (w2[j] + e1[j])
+            west[q, :, tile(j)] = w1[j]
+    for q in range(BLOCK):
+        mid = [inter[q, :, tile(j)] for j in each]
+        w1, e1 = from_west(mid, 1, lane), from_east(mid, lane)
+        for j in each:
+            alpha, beta, gamma = [spread(coef(i, level, row0 + q, tile(j))) for i in range(3)]
+            right = gamma > 0
+            behind = jnp.where(right, w1[j], e1[j])
+            upwind = jnp.where(right, west[q, :, tile(j)], swept[level, at + q, :, tile(j)])
+            flux[q, :, tile(j)] = alpha * mid[j] + beta * behind + gamma * upwind
+    for q in range(BLOCK):
+        here = [flux[q, :, tile(j)] for j in each]
+        e1 = from_east(here, lane)
+        out.append([swept[level, at + q, :, tile(j)] - (e1[j] - here[j]) for j in each])
     return out
 
 
@@ -153,74 +153,125 @@
                 packed[d, level, number, BLOCK * mains + g] = total
 
 
-def transport_kernel(count, rows, state, low, high, wx, wy, packed, winds, cy, cx, swept, first):
+def own_coefficients(rows, wx, wy, cx, cy):
+    levels, nlon = cx.shape[1], cx.shape[3]
+    nj = nlon // LANES
+    keep = jnp.where(lax.axis_index("lat") == 0, 0.0, 1.0)
+    south = lax.broadcasted_iota(jnp.int32, (rows, LANES), 0) == 0
+    for level in range(levels):
+        for j in range(nj):
+            own = pl.ds(j * levels + level, rows, stride=nj * levels)
+            parts = coefficients(wx[own, :])
+            for p in range(3):
+                cx[p, level, 0:rows, tile(j)] = parts[p]
+            wind = wy[own, :]
+            parts = coefficients(jnp.where(south, wind * keep, wind))
+            for p in range(3):
+                cy[p, level, 0:rows, tile(j)] = parts[p]
+
+
+def interior_kernel(count, rows, state, wx, wy, packed, first, cx, cy, swept, inter, west, flux):
     levels, nlon = state.shape[0], state.shape[3]
     nj = nlon // LANES
-    row_stride = nj * levels
     lane = lane_ids()
-    keep = (lax.axis_index("lat") != 0).astype(jnp.float32)
-
+    own_coefficients(rows, wx, wy, cx, cy)
+    coef_x = lambda i, level, r, lanes: cx[i, level, r:r + 1, lanes]
+    coef_y = lambda i, level, f, lanes: cy[i, level, f:f + 1, lanes]
+
+    def put(level, row, lanes, value):
+        swept[level, row - REACH, :, lanes] = value
+
+    lat_pass(levels, nj, [(REACH, rows - REACH)], lambda level, r, lanes: state[level, r, :, lanes], coef_y, put)
+
+    def step(level, _):
+        for at in range(0, rows - 2 * REACH, BLOCK):
+            done = lon_block(level, REACH + at, swept, at, coef_x, inter, west, flux, lane)
+            for q in range(BLOCK):
+                for j in range(nj):
+                    first[level, at + q, :, tile(j)] = done[q][j]
+        return 0
+
+    lax.fori_loop(0, levels, step, 0)
+    lat_pass(levels, nj, [(HALO, rows - HALO)], lambda level, r, lanes: first[level, r - REACH, :, lanes], coef_y, put)
+
+    def last(level, _):
+        for number in range((rows - 2 * HALO) // BLOCK):
+            row0 = HALO + number * BLOCK
+            done = lon_block(level, row0, swept, row0 - REACH, coef_x, inter, west, flux, lane)
+            pack_block(done, packed, level, number, count, lane)
+        return 0
+
+    lax.fori_loop(0, levels, last, 0)
+
+
+def edge_kernel(count, rows, state, low, high, first, cx, cy, packed, near, far, swept, edge, inter, west, flux):
+    levels, nlon = state.shape[0], state.shape[3]
+    nj = nlon // LANES
+    lane = lane_ids()
     for level in range(levels):
-        winds[0, level, 0:REACH, :] = low[level, HALO, 0:REACH, :]
-        winds[1, level, 0:REACH, :] = low[level, HALO, REACH + 1:2 * REACH + 1, :]
-        winds[0, level, rows + REACH:rows + 2 * REACH, :] = high[level, HALO, 0:REACH, :]
-        winds[1, level, rows + REACH:rows + 2 * REACH + 1, :] = high[level, HALO, REACH:2 * REACH + 1, :]
-        for j in range(nj):
-            lanes = slice(j * LANES, (j + 1) * LANES)
-            own = pl.ds(j * levels + level, rows, stride=row_stride)
-            winds[0, level, REACH:rows + REACH, lanes] = wx[own, :]
-            winds[1, level, REACH:rows + REACH, lanes] = wy[own, :]
-        winds[1, level, REACH:REACH + 1, :] = winds[1, level, REACH:REACH + 1, :] * keep
-
-    def make(i, _):
-        level = i // nj
-        lanes = pl.ds(pl.multiple_of((i % nj) * LANES, LANES), LANES)
-        parts = coefficients(winds[0, level, :, lanes])
-        for p in range(3):
-            cx[p, pl.ds(pl.multiple_of(i * FACES, FACES), FACES), :] = parts[p]
-        parts = coefficients(winds[1, level, :, lanes])
-        for p in range(3):
-            cy[p, level, :, lanes] = parts[p]
-        return 0
-
-    lax.fori_loop(0, levels * nj, make, 0)
-
-    def cell(level, row, lanes):
-        if row < 0:
-            return low[level, row + HALO, :, lanes]
-        if row >= rows:
-            return high[level, row - rows, :, lanes]
-        return state[level, row, :, lanes]
+        for source, target in ((low, near), (high, far)):
+            parts = coefficients(source[level, HALO])
+            for p in range(3):
+                target[p, level] = parts[p]
+
+    def coef_x(i, level, r, lanes):
+        if r < 0:
+            return near[i, level, r + REACH:r + REACH + 1, lanes]
+        if r >= rows:
+            return far[i, level, r - rows:r - rows + 1, lanes]
+        return cx[i, level, r:r + 1, lanes]
+
+    def coef_y(i, level, f, lanes):
+        if f < 0:
+            return near[i, level, f + 2 * REACH + 1:f + 2 * REACH + 2, lanes]
+        if f >= rows:
+            return far[i, level, f - rows + REACH:f - rows + REACH + 1, lanes]
+        return cy[i, level, f:f + 1, lanes]
+
+    def cell(level, r, lanes):
+        if r < 0:
+            return low[level, r + HALO, :, lanes]
+        if r >= rows:
+            return high[level, r - rows, :, lanes]
+        return state[level, r, :, lanes]
+
+    def cell_first(level, r, lanes):
+        if r < REACH:
+            return edge[level, r + REACH, :, lanes]
+        if r >= rows - REACH:
+            return edge[level, r - (rows - REACH) + BLOCK, :, lanes]
+        return first[level, r - REACH, :, lanes]
+
+    ends = [(-REACH, REACH), (rows - REACH, rows + REACH)]
 
     def put(level, row, lanes, value):
-        swept[level, row + REACH, :, lanes] = value
-
-    lat_pass(levels, nj, [(-REACH, rows + REACH)], cell, cy, put)
-    blocks = (rows + 2 * REACH) // BLOCK
-
-    def step(i, _):
-        level, row0 = i // blocks, (i % blocks) * BLOCK
-        done = lon_block(level, row0, swept, cx, lane)
-        for q in range(BLOCK):
-            for j in range(nj):
-                first[level, row0 + q, :, j * LANES:(j + 1) * LANES] = done[q][j]
-        return 0
-
-    lax.fori_loop(0, levels * blocks, step, 0)
-
-    def cell_first(level, row, lanes):
-        return first[level, row + REACH, :, lanes]
-
-    lat_pass(levels, nj, [(0, rows)], cell_first, cy, put)
-    finals = rows // BLOCK
-
-    def last(i, _):
-        level, number = i // finals, i % finals
-        done = lon_block(level, REACH + number * BLOCK, swept, cx, lane)
-        pack_block(done, packed, level, number, count, lane)
-        return 0
-
-    lax.fori_loop(0, levels * finals, last, 0)
+        swept[level, row + REACH if row < REACH else row - (rows - REACH) + BLOCK, :, lanes] = value
+
+    lat_pass(levels, nj, ends, cell, coef_y, put)
+
+    def step(level, _):
+        for at, (row0, _) in zip((0, BLOCK), ends):
+            done = lon_block(level, row0, swept, at, coef_x, inter, west, flux, lane)
+            for q in range(BLOCK):
+                for j in range(nj):
+                    edge[level, at + q, :, tile(j)] = done[q][j]
+        return 0
+
+    lax.fori_loop(0, levels, step, 0)
+    ends_last = [(0, HALO), (rows - HALO, rows)]
+
+    def put_last(level, row, lanes, value):
+        swept[level, row if row < HALO else row - (rows - HALO) + BLOCK, :, lanes] = value
+
+    lat_pass(levels, nj, ends_last, cell_first, coef_y, put_last)
+
+    def last(level, _):
+        for number, (row0, _) in enumerate(ends_last):
+            done = lon_block(level, row0, swept, number * BLOCK, coef_x, inter, west, flux, lane)
+            pack_block(done, packed, level, number, count, lane)
+        return 0
+
+    lax.fori_loop(0, levels, last, 0)
 
 
 def weights_kernel(weights, source, out):
@@ -238,7 +289,8 @@
             out[k, row] = total
 
 
-def remap_kernel(count, depth, counts, columns, weights, out):
+def remap_kernel(count, depth, parts, counts, *refs):
+    columns, weights, out = refs[:len(parts)], refs[-2], refs[-1]
     targets, rows, _, width = out.shape
     _, mains, tail, per, _ = packed_sizes(width * count, count)
     slots = []
@@ -249,21 +301,21 @@
             start = start + counts[d]
         slots.append(slot)
 
-    def body(number, _):
+    def block(source, number, row0):
         for q in range(BLOCK):
-            row = number * BLOCK + q
+            row = row0 + q
             for m in range(mains + (1 if tail else 0)):
                 wide = LANES if m < mains else tail
                 lanes = slice(m * LANES, m * LANES + wide)
                 values = []
                 for level in range(targets):
                     if m < mains:
-                        values.append(columns[slots[level], number, q * mains + m])
+                        values.append(source[slots[level], number, q * mains + m])
                     else:
-                        tile = columns[slots[level], number, BLOCK * mains + q // per]
+                        last = source[slots[level], number, BLOCK * mains + q // per]
                         shift = (q % per) * tail
-                        tile = pltpu.roll(tile, LANES - shift, 1) if shift else tile
-                        values.append(tile[:, :wide])
+                        last = pltpu.roll(last, LANES - shift, 1) if shift else last
+                        values.append(last[:, :wide])
                 for k in range(targets):
                     lowest, highest = max(k - (TAPS - 1), 0), min(k, targets - TAPS) + TAPS - 1
                     total = None
@@ -273,14 +325,17 @@
                         term = w * values[level]
                         total = term if total is None else total + term
                     out[k, row, :, lanes] = total
-        return 0
-
-    lax.fori_loop(0, rows // BLOCK, body, 0)
+
+    for source, row0s in zip(columns, parts):
+        for number, row0 in enumerate(row0s):
+            block(source, number, row0)
 
 
 def tiles_of(array):
     lead, levels, nlon = array.shape[:-2], array.shape[-2], array.shape[-1]
     split = array.reshape(lead + (levels, nlon // LANES, LANES))
+    order = tuple(range(len(lead))) + (len(lead) + 1, len(lead), len(lead) + 2)
+    split = with_layout_constraint(split, Layout(major_to_minor=order))
     return jnp.swapaxes(split, -3, -2).reshape(-1, LANES)
 
 
@@ -308,13 +363,17 @@
     return jax.ShapeDtypeStruct(shape, jnp.float32)
 
 
+def exchanged(packed, slots):
+    columns = lax.all_to_all(packed, "lev", split_axis=0, concat_axis=0, tiled=True)
+    return columns.reshape((slots,) + packed.shape[2:])
+
+
 def shards(tracers, wind_x, wind_y, level_counts, source_level, remap_weight):
     count = lax.axis_size("lev")
     bands = lax.axis_size("lat")
     number, depth, rows, nlon = tracers.shape
     targets, _, width = source_level.shape
     _, mains, tail, per, size = packed_sizes(nlon, count)
-    finals = rows // BLOCK
 
     raw = tiles_of(jnp.transpose(tracers, (0, 2, 1, 3)))
     wx = tiles_of(jnp.transpose(wind_x, (1, 0, 2)))
@@ -330,24 +389,29 @@
         weights_kernel, f32(targets, rows, SUB, width),
         (jnp.transpose(remap_weight, (1, 2, 0, 3)), source_level),
         cost=cost(20 * remap_weight.size, 16 * remap_weight.size))
-    ext = rows + 2 * REACH
-    packed = call(
-        functools.partial(transport_kernel, count, rows),
-        f32(count, depth, finals, size, SUB, LANES), (state, low, high, wx, wy),
-        scratch=[
-            pltpu.VMEM((2, depth, FACES, nlon), jnp.float32),
-            pltpu.VMEM((3, depth, FACES, nlon), jnp.float32),
-            pltpu.VMEM((3, depth * (nlon // LANES) * FACES, LANES), jnp.float32),
-            pltpu.VMEM((depth, ext, number, nlon), jnp.float32),
-            pltpu.VMEM((depth, ext, number, nlon), jnp.float32),
-        ],
-        cost=cost(120 * tracers.size, 8 * tracers.size))
-    columns = lax.all_to_all(packed, "lev", split_axis=0, concat_axis=0, tiled=True)
-    columns = columns.reshape(count * depth, finals, size, SUB, LANES)
+    swept = pltpu.VMEM((depth, 2 * BLOCK, number, nlon), jnp.float32)
+    block = pltpu.VMEM((BLOCK, number, nlon), jnp.float32)
+    halo_coef = pltpu.VMEM((3, depth, SUB, nlon), jnp.float32)
+    held = -(-rows // SUB) * SUB
+    coef = f32(3, depth, held, nlon)
+    inner = rows - 2 * HALO
+    inner_packed, first, cx, cy = call(
+        functools.partial(interior_kernel, count, rows),
+        (f32(count, depth, inner // BLOCK, size, SUB, LANES), f32(depth, rows - 2 * REACH, number, nlon), coef, coef),
+        (state, wx, wy), scratch=[swept, block, block, block],
+        cost=cost(50 * tracers.size, 8 * tracers.size))
+    inner_columns = exchanged(inner_packed, count * depth)
+    edge_packed = call(
+        functools.partial(edge_kernel, count, rows),
+        f32(count, depth, 2 * HALO // BLOCK, size, SUB, LANES), (state, low, high, first, cx, cy),
+        scratch=[halo_coef, halo_coef, swept, swept, block, block, block],
+        cost=cost(60 * tracers.size, 8 * tracers.size))
+    edge_columns = exchanged(edge_packed, count * depth)
+    parts = (tuple(range(HALO, rows - HALO, BLOCK)), (0, rows - HALO))
     out = call(
-        functools.partial(remap_kernel, count, depth),
-        f32(targets, rows, number, width), (level_counts, columns, taps),
-        specs=[SMEM, VMEM, VMEM],
+        functools.partial(remap_kernel, count, depth, parts),
+        f32(targets, rows, number, width), (level_counts, inner_columns, edge_columns, taps),
+        specs=[SMEM, VMEM, VMEM, VMEM],
         cost=cost(60 * remap_weight.size, 16 * remap_weight.size))
     return jnp.transpose(out, (2, 0, 1, 3))
 

time: 66.4 us -> 53.6 us (0.81)
  waiting for transfers between devices: 30.6 us -> 15.5 us
  starting transfers between devices: 9.93 us -> 14.2 us
  Pallas kernels: 19.2 us -> 15.4 us
  local copies, waits for them, and re-layouts: 6.23 us -> 7.94 us
    ppermute x1, waiting for transfers between devices: 9.66 us -> 0.01 us  [shards(): low = lax.ppermute(up, 'lat', [(i, i + 1) for i in range(bands - 1)])]
    unnamed x10 -> x18, local copies, waits for them, and re-layouts: 0.95 us -> 5.88 us
    all_to_all x1 -> x2, waiting for transfers between devices: 16.8 us -> 11.9 us  [exchanged(): lax.all_to_all(packed, 'lev', split_axis=0, concat_axis=0, tiled=True)]
    pallas_call x4 -> x5, Pallas kernels: 19.2 us -> 15.4 us  [call(): pl.pallas_call(kernel, out_shape=outs, in_specs=specs or [VMEM] * len(arg...]
    all_to_all x1 -> x2, starting transfers between devices: 3.68 us -> 7.23 us  [exchanged(): lax.all_to_all(packed, 'lev', split_axis=0, concat_axis=0, tiled=True)]
    reshape x3 -> x0, local copies, waits for them, and re-layouts: 2.7 us -> none  [tiles_of(): split = array.reshape(lead + (levels, nlon // LANES, LANES))]
    transpose x4 -> x0, local copies, waits for them, and re-layouts: 2.35 us -> none  [the longest x3 1.2 us: tiles_of(): return jnp.swapaxes(split, -3, -2).reshape(-1, LANES)]
    reshape x2, local copies, waits for them, and re-layouts: 0.23 us -> 2.06 us  [tiles_of(): return jnp.swapaxes(split, -3, -2).reshape(-1, LANES)]
  transfers between devices with their start and end apart: 3 -> 4, of which waited for: 3 -> 2; matrix products, arithmetic and copies ran while one was open for 0% -> 0% of each run, Pallas kernels for 0% -> 23%
where the time goes in v2:
time: 53.6 us; the launch traced here: 53.2 us
  waiting for transfers between devices  15.5 us (29%)
  Pallas kernels  15.4 us (29%)
  starting transfers between devices  14.2 us (26%)
  local copies, waits for them, and re-layouts  7.94 us (15%)
    pallas_call x5, Pallas kernels, call(): pl.pallas_call(kernel, out_shape=outs, in_specs=specs or [VMEM] * len(arg...  15.4 us
    all_to_all x2, waiting for transfers between devices, exchanged(): lax.all_to_all(packed, 'lev', split_axis=0, concat_axis=0, tiled=True)  11.9 us
    all_to_all x2, starting transfers between devices, exchanged(): lax.all_to_all(packed, 'lev', split_axis=0, concat_axis=0, tiled=True)  7.23 us
    unnamed x18, local copies, waits for them, and re-layouts  5.88 us
    ppermute x1, starting transfers between devices, shards(): low = lax.ppermute(up, 'lat', [(i, i + 1) for i in range(bands - 1)])  5.71 us
    ppermute x1, waiting for transfers between devices, shards(): high = lax.ppermute(down, 'lat', [(i + 1, i) for i in range(bands - 1)])  3.66 us
    reshape x2, local copies, waits for them, and re-layouts, tiles_of(): return jnp.swapaxes(split, -3, -2).reshape(-1, LANES)  2.06 us
    ppermute x1, starting transfers between devices, shards(): high = lax.ppermute(down, 'lat', [(i + 1, i) for i in range(bands - 1)])  1.28 us
  transfers between devices with their start and end apart: 4, of which 2 were waited for; matrix products, arithmetic and copies ran while one was open for 0% of the time, Pallas kernels for 23%

profile of v2, /device:TPU:0, one launch (start us, length us, event | category | flops | bytes accessed | tf_op | source)
XLA Modules:
  0.0 53.2 jit_solution(2956519586448765390)
XLA Ops:
  0.0 1.0 %reshape.27.wx = f32[324,128]{1,0:T(8,128)S(1)} reshape(f32[18,9,2,128]{3,2,1,0:T(2,128)} %bitcast.25) | data formatting | bytes 331776 | tf_op jit(solution)/shard_map/reshape | solution.py:339
  1.0 1.0 %reshape.29.wy = f32[324,128]{1,0:T(8,128)S(1)} reshape(f32[18,9,2,128]{3,2,1,0:T(2,128)} %bitcast.26) | data formatting | bytes 331776 | tf_op jit(solution)/shard_map/reshape | solution.py:339
  2.1 0.0 copy-start
  2.1 1.3 %copy-done = f32[8,2,18,1152]{3,1,2,0:T(2,128)S(1)} copy-done((f32[8,2,18,1152]{3,1,2,0:T(2,128)S(1)}, f32[8,2,18,1152]{3,1,2,0:T(2,128)}, u32[]{:S(2)}) %copy-start) | copy-done | bytes 1327128
  3.4 1.2 %shard_map.64 = (f32[2,18,8,1152]{3,2,1,0:T(8,128)S(1)}, f32[2,7,8,1152]{3,2,1,0:T(8,128)}, f32[2,7,8,1152]{3,2,1,0:T(8,128)}) custom-call(f32[2592,128]{1,0:T(8,128)S(1)} %bitcast.23, f32[324,128]{1,0:T(8,128)S(1)} %reshape.27.wx, f32[324,128]{1,0:T(8,128)S(1)} %reshape.29.wy), custom_call_target="tpu_custom_call" | custom-call | flops 1 | bytes 2654208 | tf_op jit(solution)/shard_map/pallas_call | solution.py:347
  4.6 5.7 %collective-permute-start = (f32[2,7,8,1152]{3,2,1,0:T(8,128)}, f32[2,7,8,1152]{3,2,1,0:T(8,128)}, u32[]{:S(2)}, u32[]{:S(2)}) collective-permute-start(f32[2,7,8,1152]{3,2,1,0:T(8,128)} %get-tuple-element.14), channel_id=1, source_target_pairs={{0,4},{4,8},{8,12},{1,5},{5,9},{9,13},{2,6},{6,10},{10,14},{3,7},{... | collective-permute-start | bytes 1548296 | tf_op jit(solution)/shard_map/ppermute | solution.py:386
  10.3 1.3 %collective-permute-start.1 = (f32[2,7,8,1152]{3,2,1,0:T(8,128)}, f32[2,7,8,1152]{3,2,1,0:T(8,128)}, u32[]{:S(2)}, u32[]{:S(2)}) collective-permute-start(f32[2,7,8,1152]{3,2,1,0:T(8,128)} %get-tuple-element.15), channel_id=1, source_target_pairs={{4,0},{8,4},{12,8},{5,1},{9,5},{13,9},{6,2},{10,6},{14,10},{7,3},{... | collective-permute-start | bytes 1548296 | tf_op jit(solution)/shard_map/ppermute | solution.py:387
  11.6 4.3 %shard_map.65 = (f32[4,2,1,14,8,128]{5,4,3,2,1,0:T(8,128)S(1)}, f32[2,12,8,1152]{3,2,1,0:T(8,128)S(1)}, f32[3,2,24,1152]{3,2,1,0:T(8,128)S(1)}, f32[3,2,24,1152]{3,2,1,0:T(8,128)S(1)}) custom-call(f32[2,18,8,1152]{3,2,1,0:T(8,128)S(1)} %get-tuple-element.12.state, f32[324,128]{1,0:T(8,128)S(1)} %reshape.27.wx, f32[324,128]{1,0:T(8,128)S(1)} %reshape.29.wy), custom_call_target="tpu_custom_call" | custom-call | flops 16588800 | bytes 2654208 | tf_op jit(solution)/shard_map/pallas_call | solution.py:347
  15.9 0.0 copy-start.1
  15.9 0.9 %copy-done.1 = f32[2,12,8,1152]{3,2,1,0:T(8,128)} copy-done((f32[2,12,8,1152]{3,2,1,0:T(8,128)}, f32[2,12,8,1152]{3,2,1,0:T(8,128)S(1)}, u32[]{:S(2)}) %copy-start.1) | copy-done | bytes 884760
  16.8 0.0 copy-start.4
  16.9 0.8 %copy-done.4 = f32[3,2,24,1152]{3,2,1,0:T(8,128)} copy-done((f32[3,2,24,1152]{3,2,1,0:T(8,128)}, f32[3,2,24,1152]{3,2,1,0:T(8,128)S(1)}, u32[]{:S(2)}) %copy-start.4) | copy-done | bytes 663576
  17.7 0.0 copy-start.6
  17.7 0.8 %copy-done.6 = f32[4,2,1,14,8,128]{5,4,3,2,1,0:T(8,128)} copy-done((f32[4,2,1,14,8,128]{5,4,3,2,1,0:T(8,128)}, f32[4,2,1,14,8,128]{5,4,3,2,1,0:T(8,128)S(1)}, u32[]{:S(2)}) %copy-start.6) | copy-done | bytes 458776
  18.5 0.0 copy-start.2
  18.5 3.6 %all-to-all-start = ((f32[4,2,1,14,8,128]{5,4,3,2,1,0:T(8,128)}), f32[4,2,1,14,8,128]{5,4,3,2,1,0:T(8,128)S(1)}, u32[]{:S(2)}, u32[]{:S(2)}) async-start(f32[4,2,1,14,8,128]{5,4,3,2,1,0:T(8,128)} %copy-done.6), calls=%async_computation | async-start | bytes 917504 | tf_op jit(solution)/shard_map/all_to_all | solution.py:367
  22.1 0.0 collective-permute-done.low
  22.1 3.7 %collective-permute-done.1.high = f32[2,7,8,1152]{3,2,1,0:T(8,128)} collective-permute-done((f32[2,7,8,1152]{3,2,1,0:T(8,128)}, f32[2,7,8,1152]{3,2,1,0:T(8,128)}, u32[]{:S(2)}, u32[]{:S(2)}) %collective-permute-start.1) | collective-permute-done | bytes 516128 | tf_op jit(solution)/shard_map/ppermute | solution.py:387
  25.7 0.0 copy-done.2
  25.8 0.0 copy-start.5
  25.8 1.1 %copy-done.5 = f32[3,2,24,1152]{3,2,1,0:T(8,128)S(1)} copy-done((f32[3,2,24,1152]{3,2,1,0:T(8,128)S(1)}, f32[3,2,24,1152]{3,2,1,0:T(8,128)}, u32[]{:S(2)}) %copy-start.5) | copy-done | bytes 663576
  26.8 7.6 %shard_map.66 = f32[4,2,2,14,8,128]{5,4,3,2,1,0:T(8,128)} custom-call(f32[2,18,8,1152]{3,2,1,0:T(8,128)S(1)} %get-tuple-element.12.state, f32[2,7,8,1152]{3,2,1,0:T(8,128)} %collective-permute-done.low, f32[2,7,8,1152]{3,2,1,0:T(8,128)} %collective-permute-done.1.high, f32[2,12,8,1152]{3,2,1,0:T(8,128)S(1)} %copy-done.2, ...), custom_call_target="tpu_custom_call" | custom-call | flops 19906560 | bytes 2654208 | tf_op jit(solution)/shard_map/pallas_call | solution.py:347
  34.4 0.0 copy-start.3
  34.4 0.0 all-to-all-done
  34.4 3.6 %all-to-all-start.1 = ((f32[4,2,2,14,8,128]{5,4,3,2,1,0:T(8,128)}), f32[4,2,2,14,8,128]{5,4,3,2,1,0:T(8,128)S(1)}, u32[]{:S(2)}, u32[]{:S(2)}) async-start(f32[4,2,2,14,8,128]{5,4,3,2,1,0:T(8,128)} %shard_map.66), calls=%async_computation.1 | async-start | bytes 1835008 | tf_op jit(solution)/shard_map/all_to_all | solution.py:367
  38.1 0.0 copy-start.8
  38.1 0.0 copy-done.3
  38.1 0.0 copy-start.7
  38.1 0.9 %copy-done.7 = s32[6,18,288]{2,1,0:T(8,128)S(1)} copy-done((s32[6,18,288]{2,1,0:T(8,128)S(1)}, s32[6,18,288]{2,1,0:T(8,128)}, u32[]{:S(2)}) %copy-start.7) | copy-done | bytes 124440
  39.0 0.2 shard_map.67.refs_2_
  39.2 11.9 %all-to-all-done.1 = f32[4,2,2,14,8,128]{5,4,3,2,1,0:T(8,128)S(1)} async-done(((f32[4,2,2,14,8,128]{5,4,3,2,1,0:T(8,128)}), f32[4,2,2,14,8,128]{5,4,3,2,1,0:T(8,128)S(1)}, u32[]{:S(2)}, u32[]{:S(2)}) %all-to-all-start.1) | async-done | bytes 917536 | tf_op jit(solution)/shard_map/all_to_all | solution.py:367
  51.1 0.0 copy-done.8
  51.1 2.1 %shard_map.68 = f32[6,18,8,288]{3,2,1,0:T(8,128)} custom-call(s32[4]{0:T(128)S(1)} %copy-done.8, f32[8,1,14,8,128]{4,3,2,1,0:T(8,128)S(1)} %bitcast.22, f32[8,2,14,8,128]{4,3,2,1,0:T(8,128)S(1)} %bitcast.21, f32[6,18,8,288]{3,2,1,0:T(8,128)S(1)} %shard_map.67.refs_2_), custom_call_target="tpu_custom_call" | custom-call | flops 7464960 | bytes 1990656 | tf_op jit(solution)/shard_map/pallas_call | solution.py:347
Async XLA Ops:
  2.1 1.3 %copy-start = (f32[8,2,18,1152]{3,1,2,0:T(2,128)S(1)}, f32[8,2,18,1152]{3,1,2,0:T(2,128)}, u32[]{:S(2)}) copy-start(f32[8,2,18,1152]{3,1,2,0:T(2,128)} %param.6) | copy-start | bytes 3981316
  4.6 17.4 %collective-permute-start = (f32[2,7,8,1152]{3,2,1,0:T(8,128)}, f32[2,7,8,1152]{3,2,1,0:T(8,128)}, u32[]{:S(2)}, u32[]{:S(2)}) collective-permute-start(f32[2,7,8,1152]{3,2,1,0:T(8,128)} %get-tuple-element.14), channel_id=1, source_target_pairs={{0,4},{4,8},{8,12},{1,5},{5,9},{9,13},{2,6},{6,10},{10,14},{3,7},{... | collective-permute-start | bytes 1548296 | tf_op jit(solution)/shard_map/ppermute | solution.py:386
  10.3 15.4 %collective-permute-start.1 = (f32[2,7,8,1152]{3,2,1,0:T(8,128)}, f32[2,7,8,1152]{3,2,1,0:T(8,128)}, u32[]{:S(2)}, u32[]{:S(2)}) collective-permute-start(f32[2,7,8,1152]{3,2,1,0:T(8,128)} %get-tuple-element.15), channel_id=1, source_target_pairs={{4,0},{8,4},{12,8},{5,1},{9,5},{13,9},{6,2},{10,6},{14,10},{7,3},{... | collective-permute-start | bytes 1548296 | tf_op jit(solution)/shard_map/ppermute | solution.py:387
  15.9 0.9 %copy-start.1 = (f32[2,12,8,1152]{3,2,1,0:T(8,128)}, f32[2,12,8,1152]{3,2,1,0:T(8,128)S(1)}, u32[]{:S(2)}) copy-start(f32[2,12,8,1152]{3,2,1,0:T(8,128)S(1)} %get-tuple-element.16.first) | copy-start | bytes 2654212
  16.8 0.8 %copy-start.4 = (f32[3,2,24,1152]{3,2,1,0:T(8,128)}, f32[3,2,24,1152]{3,2,1,0:T(8,128)S(1)}, u32[]{:S(2)}) copy-start(f32[3,2,24,1152]{3,2,1,0:T(8,128)S(1)} %get-tuple-element.18.cy) | copy-start | bytes 1990660
  17.7 0.8 %copy-start.6 = (f32[4,2,1,14,8,128]{5,4,3,2,1,0:T(8,128)}, f32[4,2,1,14,8,128]{5,4,3,2,1,0:T(8,128)S(1)}, u32[]{:S(2)}) copy-start(f32[4,2,1,14,8,128]{5,4,3,2,1,0:T(8,128)S(1)} %get-tuple-element.13) | copy-start | bytes 1376260
  18.5 7.3 %copy-start.2 = (f32[2,12,8,1152]{3,2,1,0:T(8,128)S(1)}, f32[2,12,8,1152]{3,2,1,0:T(8,128)}, u32[]{:S(2)}) copy-start(f32[2,12,8,1152]{3,2,1,0:T(8,128)} %copy-done.1) | copy-start | bytes 2654212
  18.5 16.0 %all-to-all-start = ((f32[4,2,1,14,8,128]{5,4,3,2,1,0:T(8,128)}), f32[4,2,1,14,8,128]{5,4,3,2,1,0:T(8,128)S(1)}, u32[]{:S(2)}, u32[]{:S(2)}) async-start(f32[4,2,1,14,8,128]{5,4,3,2,1,0:T(8,128)} %copy-done.6), calls=%async_computation | async-start | bytes 917504 | tf_op jit(solution)/shard_map/all_to_all | solution.py:367
  25.8 1.1 %copy-start.5 = (f32[3,2,24,1152]{3,2,1,0:T(8,128)S(1)}, f32[3,2,24,1152]{3,2,1,0:T(8,128)}, u32[]{:S(2)}) copy-start(f32[3,2,24,1152]{3,2,1,0:T(8,128)} %copy-done.4) | copy-start | bytes 1990660
  34.4 3.7 %copy-start.3 = (f32[4,6,18,288]{3,0,2,1:T(4,128)S(1)}, f32[4,6,18,288]{3,0,2,1:T(4,128)}, u32[]{:S(2)}) copy-start(f32[4,6,18,288]{3,0,2,1:T(4,128)} %param.11) | copy-start | bytes 1492996
  34.4 16.7 %all-to-all-start.1 = ((f32[4,2,2,14,8,128]{5,4,3,2,1,0:T(8,128)}), f32[4,2,2,14,8,128]{5,4,3,2,1,0:T(8,128)S(1)}, u32[]{:S(2)}, u32[]{:S(2)}) async-start(f32[4,2,2,14,8,128]{5,4,3,2,1,0:T(8,128)} %shard_map.66), calls=%async_computation.1 | async-start | bytes 1835008 | tf_op jit(solution)/shard_map/all_to_all | solution.py:367
  38.1 13.0 %copy-start.8 = (s32[4]{0:T(128)S(1)}, s32[4]{0:T(128)}, u32[]{:S(2)}) copy-start(s32[4]{0:T(128)} %counts.1) | copy-start | bytes 52
  38.1 0.9 %copy-start.7 = (s32[6,18,288]{2,1,0:T(8,128)S(1)}, s32[6,18,288]{2,1,0:T(8,128)}, u32[]{:S(2)}) copy-start(s32[6,18,288]{2,1,0:T(8,128)} %source.1) | copy-start | bytes 373252

commit v3 on v2

--- a/solution.py
+++ b/solution.py
@@ -53,17 +53,30 @@
     return width, mains, tail, per, BLOCK * mains + tails
 
 
-def prep_kernel(rows, tracers, wx, wy, state, down, up):
+def prep_kernel(rows, tracers, wind_x, wind_y, state, down, up, wx, wy, raw, sems):
     levels, nlon = state.shape[0], state.shape[3]
     nj = nlon // LANES
     row_stride = nj * levels
     tracer_stride = rows * row_stride
+    copies = [pltpu.make_async_copy(source, target, sems.at[i])
+              for i, (source, target) in enumerate(((tracers, raw), (wind_x, wx), (wind_y, wy)))]
+    for copy in copies:
+        copy.start()
+    for copy in copies[1:]:
+        copy.wait()
+    for level in range(levels):
+        for target, row_x, row_y in ((down, 0, 0), (up, rows - REACH, rows - REACH - 1)):
+            for q in range(REACH):
+                target[level, HALO, q:q + 1, :] = wx[row_x + q, level:level + 1, :]
+            for q in range(REACH + 1):
+                target[level, HALO, REACH + q:REACH + q + 1, :] = wy[row_y + q, level:level + 1, :]
+    copies[0].wait()
 
     def body(row, _):
         for level in range(levels):
             for j in range(nj):
                 start = row * row_stride + j * levels + level
-                state[level, row, :, j * LANES:(j + 1) * LANES] = tracers[pl.ds(start, SUB, stride=tracer_stride), :]
+                state[level, row, :, tile(j)] = raw[pl.ds(start, SUB, stride=tracer_stride), :]
         return 0
 
     lax.fori_loop(0, rows, body, 0)
@@ -71,19 +84,18 @@
         for row in range(HALO):
             down[level, row] = state[level, row]
             up[level, row] = state[level, rows - HALO + row]
-        for j in range(nj):
-            lanes = slice(j * LANES, (j + 1) * LANES)
-            at = lambda row: row * row_stride + j * levels + level
-            down[level, HALO, 0:REACH, lanes] = wx[pl.ds(at(0), REACH, stride=row_stride), :]
-            down[level, HALO, REACH:2 * REACH + 1, lanes] = wy[pl.ds(at(0), REACH + 1, stride=row_stride), :]
-            up[level, HALO, 0:REACH, lanes] = wx[pl.ds(at(rows - REACH), REACH, stride=row_stride), :]
-            up[level, HALO, REACH:2 * REACH + 1, lanes] = wy[pl.ds(at(rows - REACH - 1), REACH + 1, stride=row_stride), :]
 
 
 def lat_pass(levels, nj, ranges, cell, coef, store):
+    group = 3 if nj % 3 == 0 else 1
+
     def body(i, _):
-        level = i // nj
-        lanes = pl.ds(pl.multiple_of((i % nj) * LANES, LANES), LANES)
+        level = i // (nj // group)
+        for u in range(group):
+            one(level, pl.ds(pl.multiple_of(((i % (nj // group)) * group + u) * LANES, LANES), LANES))
+        return 0
+
+    def one(level, lanes):
         for first, last in ranges:
             a = {r: cell(level, r, lanes) for r in range(first - REACH, last + REACH)}
             inter = {f: 7.0 * (a[f - 1] + a[f]) - (a[f - 2] + a[f + 1]) for f in range(first - 1, last + 2)}
@@ -96,39 +108,53 @@
                 flux[f] = alpha * inter[f] + beta * behind + gamma * upwind
                 if f > first:
                     store(level, f - 1, lanes, a[f - 1] - (flux[f] - flux[f - 1]))
-        return 0
-
-    lax.fori_loop(0, levels * nj, body, 0)
+
+    lax.fori_loop(0, levels * nj // group, body, 0)
 
 
 def tile(j):
     return slice(j * LANES, (j + 1) * LANES)
 
 
-def lon_block(level, row0, swept, at, coef, inter, west, flux, lane):
+def lon_pass(work, swept, coef, inter, west, flux, lane, finish):
     nj = swept.shape[3] // LANES
     each = range(nj)
-    out = []
-    for q in range(BLOCK):
-        b = [swept[level, at + q, :, tile(j)] for j in each]
+
+    def interfaces(n):
+        level, _, at = work[n]
+        b = [swept[level, at, :, tile(j)] for j in each]
         w1, w2, e1 = from_west(b, 1, lane), from_west(b, 2, lane), from_east(b, lane)
         for j in each:
-            inter[q, :, tile(j)] = 7.0 * (w1[j] + b[j]) - (w2[j] + e1[j])
-            west[q, :, tile(j)] = w1[j]
-    for q in range(BLOCK):
-        mid = [inter[q, :, tile(j)] for j in each]
+            inter[n, :, tile(j)] = 7.0 * (w1[j] + b[j]) - (w2[j] + e1[j])
+            west[n, :, tile(j)] = w1[j]
+
+    def fluxes(n):
+        level, row, at = work[n]
+        mid = [inter[n, :, tile(j)] for j in each]
         w1, e1 = from_west(mid, 1, lane), from_east(mid, lane)
         for j in each:
-            alpha, beta, gamma = [spread(coef(i, level, row0 + q, tile(j))) for i in range(3)]
+            alpha, beta, gamma = [spread(coef(i, level, row, tile(j))) for i in range(3)]
             right = gamma > 0
             behind = jnp.where(right, w1[j], e1[j])
-            upwind = jnp.where(right, west[q, :, tile(j)], swept[level, at + q, :, tile(j)])
-            flux[q, :, tile(j)] = alpha * mid[j] + beta * behind + gamma * upwind
-    for q in range(BLOCK):
-        here = [flux[q, :, tile(j)] for j in each]
+            upwind = jnp.where(right, west[n, :, tile(j)], swept[level, at, :, tile(j)])
+            flux[n, :, tile(j)] = alpha * mid[j] + beta * behind + gamma * upwind
+
+    def update(n):
+        level, _, at = work[n]
+        here = [flux[n, :, tile(j)] for j in each]
         e1 = from_east(here, lane)
-        out.append([swept[level, at + q, :, tile(j)] - (e1[j] - here[j]) for j in each])
-    return out
+        return [swept[level, at, :, tile(j)] - (e1[j] - here[j]) for j in each]
+
+    groups = len(work) // BLOCK
+    for g in range(groups + 2):
+        if g < groups:
+            for q in range(BLOCK):
+                interfaces(g * BLOCK + q)
+        if 1 <= g <= groups:
+            for q in range(BLOCK):
+                fluxes((g - 1) * BLOCK + q)
+        if g >= 2:
+            finish(g - 2, [update((g - 2) * BLOCK + q) for q in range(BLOCK)])
 
 
 def pack_block(block, packed, level, number, count, lane):
@@ -153,28 +179,32 @@
                 packed[d, level, number, BLOCK * mains + g] = total
 
 
-def own_coefficients(rows, wx, wy, cx, cy):
-    levels, nlon = cx.shape[1], cx.shape[3]
-    nj = nlon // LANES
+def own_coefficients(rows, wx, wy, winds, cx, cy):
+    levels, held, nlon = cx.shape[1:]
     keep = jnp.where(lax.axis_index("lat") == 0, 0.0, 1.0)
-    south = lax.broadcasted_iota(jnp.int32, (rows, LANES), 0) == 0
     for level in range(levels):
-        for j in range(nj):
-            own = pl.ds(j * levels + level, rows, stride=nj * levels)
-            parts = coefficients(wx[own, :])
-            for p in range(3):
-                cx[p, level, 0:rows, tile(j)] = parts[p]
-            wind = wy[own, :]
-            parts = coefficients(jnp.where(south, wind * keep, wind))
-            for p in range(3):
-                cy[p, level, 0:rows, tile(j)] = parts[p]
-
-
-def interior_kernel(count, rows, state, wx, wy, packed, first, cx, cy, swept, inter, west, flux):
+        for way, source in enumerate((wx, wy)):
+            for row in range(rows):
+                winds[way, level, row:row + 1, :] = source[row, level:level + 1, :]
+        winds[1, level, 0:1, :] = winds[1, level, 0:1, :] * keep
+        for way, target in enumerate((cx, cy)):
+            for j in range(nlon // LANES):
+                parts = coefficients(winds[way, level, :, tile(j)])
+                for p in range(3):
+                    target[p, level, :, tile(j)] = parts[p]
+
+
+def put_rows(target, level, at, rows):
+    for q, row in enumerate(rows):
+        for j, part in enumerate(row):
+            target[level, at + q, :, tile(j)] = part
+
+
+def interior_kernel(count, rows, state, wx, wy, packed, first, cx, cy, winds, swept, inter, west, flux):
     levels, nlon = state.shape[0], state.shape[3]
     nj = nlon // LANES
     lane = lane_ids()
-    own_coefficients(rows, wx, wy, cx, cy)
+    own_coefficients(rows, wx, wy, winds, cx, cy)
     coef_x = lambda i, level, r, lanes: cx[i, level, r:r + 1, lanes]
     coef_y = lambda i, level, f, lanes: cy[i, level, f:f + 1, lanes]
 
@@ -182,26 +212,21 @@
         swept[level, row - REACH, :, lanes] = value
 
     lat_pass(levels, nj, [(REACH, rows - REACH)], lambda level, r, lanes: state[level, r, :, lanes], coef_y, put)
-
-    def step(level, _):
-        for at in range(0, rows - 2 * REACH, BLOCK):
-            done = lon_block(level, REACH + at, swept, at, coef_x, inter, west, flux, lane)
-            for q in range(BLOCK):
-                for j in range(nj):
-                    first[level, at + q, :, tile(j)] = done[q][j]
-        return 0
-
-    lax.fori_loop(0, levels, step, 0)
+    work = [(level, row, row - REACH) for level in range(levels) for row in range(REACH, rows - REACH)]
+
+    def keep_first(group, done):
+        level, _, at = work[group * BLOCK]
+        put_rows(first, level, at, done)
+
+    lon_pass(work, swept, coef_x, inter, west, flux, lane, keep_first)
     lat_pass(levels, nj, [(HALO, rows - HALO)], lambda level, r, lanes: first[level, r - REACH, :, lanes], coef_y, put)
-
-    def last(level, _):
-        for number in range((rows - 2 * HALO) // BLOCK):
-            row0 = HALO + number * BLOCK
-            done = lon_block(level, row0, swept, row0 - REACH, coef_x, inter, west, flux, lane)
-            pack_block(done, packed, level, number, count, lane)
-        return 0
-
-    lax.fori_loop(0, levels, last, 0)
+    work_last = [(level, row, row - REACH) for level in range(levels) for row in range(HALO, rows - HALO)]
+
+    def send(group, done):
+        level, row, _ = work_last[group * BLOCK]
+        pack_block(done, packed, level, (row - HALO) // BLOCK, count, lane)
+
+    lon_pass(work_last, swept, coef_x, inter, west, flux, lane, send)
 
 
 def edge_kernel(count, rows, state, low, high, first, cx, cy, packed, near, far, swept, edge, inter, west, flux):
@@ -210,9 +235,10 @@
     lane = lane_ids()
     for level in range(levels):
         for source, target in ((low, near), (high, far)):
-            parts = coefficients(source[level, HALO])
-            for p in range(3):
-                target[p, level] = parts[p]
+            for j in range(nj):
+                parts = coefficients(source[level, HALO, :, tile(j)])
+                for p in range(3):
+                    target[p, level, :, tile(j)] = parts[p]
 
     def coef_x(i, level, r, lanes):
         if r < 0:
@@ -243,35 +269,35 @@
         return first[level, r - REACH, :, lanes]
 
     ends = [(-REACH, REACH), (rows - REACH, rows + REACH)]
+    ends_last = [(0, HALO), (rows - HALO, rows)]
+
+    def place(row, ranges):
+        (a, b), (c, _) = ranges
+        return row - a if row < b else row - c + BLOCK
 
     def put(level, row, lanes, value):
-        swept[level, row + REACH if row < REACH else row - (rows - REACH) + BLOCK, :, lanes] = value
+        swept[level, place(row, ends), :, lanes] = value
+
+    def put_last(level, row, lanes, value):
+        swept[level, place(row, ends_last), :, lanes] = value
+
+    def listed(ranges):
+        return [(level, row, place(row, ranges)) for level in range(levels) for a, b in ranges for row in range(a, b)]
 
     lat_pass(levels, nj, ends, cell, coef_y, put)
-
-    def step(level, _):
-        for at, (row0, _) in zip((0, BLOCK), ends):
-            done = lon_block(level, row0, swept, at, coef_x, inter, west, flux, lane)
-            for q in range(BLOCK):
-                for j in range(nj):
-                    edge[level, at + q, :, tile(j)] = done[q][j]
-        return 0
-
-    lax.fori_loop(0, levels, step, 0)
-    ends_last = [(0, HALO), (rows - HALO, rows)]
-
-    def put_last(level, row, lanes, value):
-        swept[level, row if row < HALO else row - (rows - HALO) + BLOCK, :, lanes] = value
-
+    work, work_last = listed(ends), listed(ends_last)
+
+    def keep_edge(group, done):
+        level, _, at = work[group * BLOCK]
+        put_rows(edge, level, at, done)
+
+    def send(group, done):
+        level, _, at = work_last[group * BLOCK]
+        pack_block(done, packed, level, at // BLOCK, count, lane)
+
+    lon_pass(work, swept, coef_x, inter, west, flux, lane, keep_edge)
     lat_pass(levels, nj, ends_last, cell_first, coef_y, put_last)
-
-    def last(level, _):
-        for number, (row0, _) in enumerate(ends_last):
-            done = lon_block(level, row0, swept, number * BLOCK, coef_x, inter, west, flux, lane)
-            pack_block(done, packed, level, number, count, lane)
-        return 0
-
-    lax.fori_loop(0, levels, last, 0)
+    lon_pass(work_last, swept, coef_x, inter, west, flux, lane, send)
 
 
 def weights_kernel(weights, source, out):
@@ -340,6 +366,7 @@
 
 
 VMEM = pl.BlockSpec(memory_space=pltpu.VMEM)
+HBM = pl.BlockSpec(memory_space=pltpu.HBM)
 SMEM = pl.BlockSpec(memory_space=pltpu.SMEM)
 
 
@@ -350,7 +377,7 @@
         in_specs=specs or [VMEM] * len(args),
         out_specs=jax.tree.map(lambda _: VMEM, outs),
         scratch_shapes=list(scratch),
-        compiler_params=pltpu.CompilerParams(vmem_limit_bytes=40 << 20),
+        compiler_params=pltpu.CompilerParams(vmem_limit_bytes=16 << 20),
         cost_estimate=cost,
     )(*args)
 
@@ -376,12 +403,14 @@
     _, mains, tail, per, size = packed_sizes(nlon, count)
 
     raw = tiles_of(jnp.transpose(tracers, (0, 2, 1, 3)))
-    wx = tiles_of(jnp.transpose(wind_x, (1, 0, 2)))
-    wy = tiles_of(jnp.transpose(wind_y, (1, 0, 2)))
+    wind = f32(rows, depth, nlon)
     halo = f32(depth, HALO + 1, number, nlon)
-    state, down, up = call(
+    state, down, up, wx, wy = call(
         functools.partial(prep_kernel, rows),
-        (f32(depth, rows, number, nlon), halo, halo), (raw, wx, wy),
+        (f32(depth, rows, number, nlon), halo, halo, wind, wind),
+        (raw, jnp.transpose(wind_x, (1, 0, 2)), jnp.transpose(wind_y, (1, 0, 2))),
+        specs=[HBM, HBM, HBM],
+        scratch=[pltpu.VMEM(raw.shape, jnp.float32), pltpu.SemaphoreType.DMA((3,))],
         cost=cost(1, 8 * tracers.size))
     low = lax.ppermute(up, "lat", [(i, i + 1) for i in range(bands - 1)])
     high = lax.ppermute(down, "lat", [(i + 1, i) for i in range(bands - 1)])
@@ -390,7 +419,7 @@
         (jnp.transpose(remap_weight, (1, 2, 0, 3)), source_level),
         cost=cost(20 * remap_weight.size, 16 * remap_weight.size))
     swept = pltpu.VMEM((depth, 2 * BLOCK, number, nlon), jnp.float32)
-    block = pltpu.VMEM((BLOCK, number, nlon), jnp.float32)
+    stage = pltpu.VMEM((2 * BLOCK * depth, number, nlon), jnp.float32)
     halo_coef = pltpu.VMEM((3, depth, SUB, nlon), jnp.float32)
     held = -(-rows // SUB) * SUB
     coef = f32(3, depth, held, nlon)
@@ -398,13 +427,13 @@
     inner_packed, first, cx, cy = call(
         functools.partial(interior_kernel, count, rows),
         (f32(count, depth, inner // BLOCK, size, SUB, LANES), f32(depth, rows - 2 * REACH, number, nlon), coef, coef),
-        (state, wx, wy), scratch=[swept, block, block, block],
+        (state, wx, wy), scratch=[pltpu.VMEM((2, depth, held, nlon), jnp.float32), swept, stage, stage, stage],
         cost=cost(50 * tracers.size, 8 * tracers.size))
     inner_columns = exchanged(inner_packed, count * depth)
     edge_packed = call(
         functools.partial(edge_kernel, count, rows),
         f32(count, depth, 2 * HALO // BLOCK, size, SUB, LANES), (state, low, high, first, cx, cy),
-        scratch=[halo_coef, halo_coef, swept, swept, block, block, block],
+        scratch=[halo_coef, halo_coef, swept, swept, stage, stage, stage],
         cost=cost(60 * tracers.size, 8 * tracers.size))
     edge_columns = exchanged(edge_packed, count * depth)
     parts = (tuple(range(HALO, rows - HALO, BLOCK)), (0, rows - HALO))

time: 53.6 us -> 53.2 us (level)
  waiting for transfers between devices: 15.5 us -> 17.3 us
  local copies, waits for them, and re-layouts: 7.94 us -> 6.8 us
  Pallas kernels: 15.4 us -> 14.5 us
    reshape x2 -> x0, local copies, waits for them, and re-layouts: 2.06 us -> none  [tiles_of(): return jnp.swapaxes(split, -3, -2).reshape(-1, LANES)]
    ppermute x1, waiting for transfers between devices: 3.66 us -> 4.93 us  [shards(): high = lax.ppermute(down, 'lat', [(i + 1, i) for i in range(bands - 1)])]
    pallas_call x5, Pallas kernels: 15.4 us -> 14.5 us  [call(): pl.pallas_call(kernel, out_shape=outs, in_specs=specs or [VMEM] * len(arg...]
    unnamed x18, local copies, waits for them, and re-layouts: 5.88 us -> 6.8 us
  transfers between devices with their start and end apart: 4 -> 4, of which waited for: 2 -> 3; matrix products, arithmetic and copies ran while one was open for 0% -> 0% of each run, Pallas kernels for 23% -> 20%
where the time goes in v3:
time: 53.2 us; the launch traced here: 52.8 us
  waiting for transfers between devices  17.3 us (33%)
  Pallas kernels  14.5 us (27%)
  starting transfers between devices  14.1 us (27%)
  local copies, waits for them, and re-layouts  6.8 us (13%)
    pallas_call x5, Pallas kernels, call(): pl.pallas_call(kernel, out_shape=outs, in_specs=specs or [VMEM] * len(arg...  14.5 us
    all_to_all x2, waiting for transfers between devices, exchanged(): lax.all_to_all(packed, 'lev', split_axis=0, concat_axis=0, tiled=True)  11.9 us
    all_to_all x2, starting transfers between devices, exchanged(): lax.all_to_all(packed, 'lev', split_axis=0, concat_axis=0, tiled=True)  7.1 us
    unnamed x18, local copies, waits for them, and re-layouts  6.8 us
    ppermute x1, starting transfers between devices, shards(): low = lax.ppermute(up, 'lat', [(i, i + 1) for i in range(bands - 1)])  5.76 us
    ppermute x1, waiting for transfers between devices, shards(): high = lax.ppermute(down, 'lat', [(i + 1, i) for i in range(bands - 1)])  4.93 us
    ppermute x1, starting transfers between devices, shards(): high = lax.ppermute(down, 'lat', [(i + 1, i) for i in range(bands - 1)])  1.28 us
  transfers between devices with their start and end apart: 4, of which 3 were waited for; matrix products, arithmetic and copies ran while one was open for 0% of the time, Pallas kernels for 20%

profile of v3, /device:TPU:0, one launch (start us, length us, event | category | flops | bytes accessed | tf_op | source)
XLA Modules:
  0.0 52.8 jit_solution(7187106766154864488)
XLA Ops:
  0.0 0.0 copy-start
  0.0 1.3 %copy-done = f32[8,2,18,1152]{3,1,2,0:T(2,128)S(1)} copy-done((f32[8,2,18,1152]{3,1,2,0:T(2,128)S(1)}, f32[8,2,18,1152]{3,1,2,0:T(2,128)}, u32[]{:S(2)}) %copy-start) | copy-done | bytes 1327128
  1.3 0.0 copy-start.6
  1.3 0.9 %copy-done.6 = f32[2,18,1152]{2,0,1:T(2,128)S(1)} copy-done((f32[2,18,1152]{2,0,1:T(2,128)S(1)}, f32[2,18,1152]{2,0,1:T(2,128)}, u32[]{:S(2)}) %copy-start.6) | copy-done | bytes 165912
  2.2 0.0 copy-start.7
  2.2 0.9 %copy-done.7 = f32[2,18,1152]{2,0,1:T(2,128)S(1)} copy-done((f32[2,18,1152]{2,0,1:T(2,128)S(1)}, f32[2,18,1152]{2,0,1:T(2,128)}, u32[]{:S(2)}) %copy-start.7) | copy-done | bytes 165912
  3.2 1.8 %shard_map.64 = (f32[2,18,8,1152]{3,2,1,0:T(8,128)S(1)}, f32[2,7,8,1152]{3,2,1,0:T(8,128)}, f32[2,7,8,1152]{3,2,1,0:T(8,128)}, f32[18,2,1152]{2,1,0:T(2,128)S(1)}, f32[18,2,1152]{2,1,0:T(2,128)S(1)}) custom-call(f32[2592,128]{1,0:T(8,128)S(1)} %bitcast.15, f32[18,2,1152]{2,1,0:T(2,128)S(1)} %bitcast.17, f32[18,2,1152]{2,1,0:T(2,128)S(1)} %bitcast.18), custom_call_target="tpu_custom_call" | custom-call | flops 1 | bytes 2654208 | tf_op jit(solution)/shard_map/pallas_call | solution.py:374
  5.0 5.8 %collective-permute-start = (f32[2,7,8,1152]{3,2,1,0:T(8,128)}, f32[2,7,8,1152]{3,2,1,0:T(8,128)}, u32[]{:S(2)}, u32[]{:S(2)}) collective-permute-start(f32[2,7,8,1152]{3,2,1,0:T(8,128)} %get-tuple-element.18), channel_id=1, source_target_pairs={{0,4},{4,8},{8,12},{1,5},{5,9},{9,13},{2,6},{6,10},{10,14},{3,7},{... | collective-permute-start | bytes 1548296 | tf_op jit(solution)/shard_map/ppermute | solution.py:415
  10.7 1.3 %collective-permute-start.1 = (f32[2,7,8,1152]{3,2,1,0:T(8,128)}, f32[2,7,8,1152]{3,2,1,0:T(8,128)}, u32[]{:S(2)}, u32[]{:S(2)}) collective-permute-start(f32[2,7,8,1152]{3,2,1,0:T(8,128)} %get-tuple-element.19), channel_id=1, source_target_pairs={{4,0},{8,4},{12,8},{5,1},{9,5},{13,9},{6,2},{10,6},{14,10},{7,3},{... | collective-permute-start | bytes 1548296 | tf_op jit(solution)/shard_map/ppermute | solution.py:416
  12.0 3.6 %shard_map.65 = (f32[4,2,1,14,8,128]{5,4,3,2,1,0:T(8,128)S(1)}, f32[2,12,8,1152]{3,2,1,0:T(8,128)S(1)}, f32[3,2,24,1152]{3,2,1,0:T(8,128)S(1)}, f32[3,2,24,1152]{3,2,1,0:T(8,128)S(1)}) custom-call(f32[2,18,8,1152]{3,2,1,0:T(8,128)S(1)} %get-tuple-element.14.state, f32[18,2,1152]{2,1,0:T(2,128)S(1)} %get-tuple-element.15.wx, ...), custom_call_target="tpu_custom_call" | custom-call | flops 16588800 | bytes 2654208 | tf_op jit(solution)/shard_map/pallas_call | solution.py:374
  15.6 0.0 copy-start.2
  15.6 0.8 %copy-done.2 = f32[3,2,24,1152]{3,2,1,0:T(8,128)} copy-done((f32[3,2,24,1152]{3,2,1,0:T(8,128)}, f32[3,2,24,1152]{3,2,1,0:T(8,128)S(1)}, u32[]{:S(2)}) %copy-start.2) | copy-done | bytes 663576
  16.5 0.0 copy-start.4
  16.5 0.8 %copy-done.4 = f32[4,2,1,14,8,128]{5,4,3,2,1,0:T(8,128)} copy-done((f32[4,2,1,14,8,128]{5,4,3,2,1,0:T(8,128)}, f32[4,2,1,14,8,128]{5,4,3,2,1,0:T(8,128)S(1)}, u32[]{:S(2)}) %copy-start.4) | copy-done | bytes 458776
  17.3 3.5 %all-to-all-start = ((f32[4,2,1,14,8,128]{5,4,3,2,1,0:T(8,128)}), f32[4,2,1,14,8,128]{5,4,3,2,1,0:T(8,128)S(1)}, u32[]{:S(2)}, u32[]{:S(2)}) async-start(f32[4,2,1,14,8,128]{5,4,3,2,1,0:T(8,128)} %copy-done.4), calls=%async_computation | async-start | bytes 917504 | tf_op jit(solution)/shard_map/all_to_all | solution.py:394
  20.7 0.5 collective-permute-done.low
  21.2 4.9 %collective-permute-done.1.high = f32[2,7,8,1152]{3,2,1,0:T(8,128)} collective-permute-done((f32[2,7,8,1152]{3,2,1,0:T(8,128)}, f32[2,7,8,1152]{3,2,1,0:T(8,128)}, u32[]{:S(2)}, u32[]{:S(2)}) %collective-permute-start.1) | collective-permute-done | bytes 516128 | tf_op jit(solution)/shard_map/ppermute | solution.py:416
  26.1 0.0 copy-start.3
  26.1 1.1 %copy-done.3 = f32[3,2,24,1152]{3,2,1,0:T(8,128)S(1)} copy-done((f32[3,2,24,1152]{3,2,1,0:T(8,128)S(1)}, f32[3,2,24,1152]{3,2,1,0:T(8,128)}, u32[]{:S(2)}) %copy-start.3) | copy-done | bytes 663576
  27.2 6.8 %shard_map.66 = f32[4,2,2,14,8,128]{5,4,3,2,1,0:T(8,128)} custom-call(f32[2,18,8,1152]{3,2,1,0:T(8,128)S(1)} %get-tuple-element.14.state, f32[2,7,8,1152]{3,2,1,0:T(8,128)} %collective-permute-done.low, f32[2,7,8,1152]{3,2,1,0:T(8,128)} %collective-permute-done.1.high, f32[2,12,8,1152]{3,2,1,0:T(8,128)S(1)} %get-tuple-element.20.first, ...), custom_call_target="tpu_custom_call" | custom-call | flops 19906560 | bytes 2654208 | tf_op jit(solution)/shard_map/pallas_call | solution.py:374
  34.0 0.0 copy-start.1
  34.0 0.0 all-to-all-done
  34.0 3.6 %all-to-all-start.1 = ((f32[4,2,2,14,8,128]{5,4,3,2,1,0:T(8,128)}), f32[4,2,2,14,8,128]{5,4,3,2,1,0:T(8,128)S(1)}, u32[]{:S(2)}, u32[]{:S(2)}) async-start(f32[4,2,2,14,8,128]{5,4,3,2,1,0:T(8,128)} %shard_map.66), calls=%async_computation.1 | async-start | bytes 1835008 | tf_op jit(solution)/shard_map/all_to_all | solution.py:394
  37.7 0.0 copy-start.8
  37.7 0.0 copy-done.1
  37.7 0.0 copy-start.5
  37.7 0.9 %copy-done.5 = s32[6,18,288]{2,1,0:T(8,128)S(1)} copy-done((s32[6,18,288]{2,1,0:T(8,128)S(1)}, s32[6,18,288]{2,1,0:T(8,128)}, u32[]{:S(2)}) %copy-start.5) | copy-done | bytes 124440
  38.6 0.2 shard_map.67.refs_2_
  38.8 11.9 %all-to-all-done.1 = f32[4,2,2,14,8,128]{5,4,3,2,1,0:T(8,128)S(1)} async-done(((f32[4,2,2,14,8,128]{5,4,3,2,1,0:T(8,128)}), f32[4,2,2,14,8,128]{5,4,3,2,1,0:T(8,128)S(1)}, u32[]{:S(2)}, u32[]{:S(2)}) %all-to-all-start.1) | async-done | bytes 917536 | tf_op jit(solution)/shard_map/all_to_all | solution.py:394
  50.7 0.0 copy-done.8
  50.7 2.1 %shard_map.68 = f32[6,18,8,288]{3,2,1,0:T(8,128)} custom-call(s32[4]{0:T(128)S(1)} %copy-done.8, f32[8,1,14,8,128]{4,3,2,1,0:T(8,128)S(1)} %bitcast.14, f32[8,2,14,8,128]{4,3,2,1,0:T(8,128)S(1)} %bitcast.13, f32[6,18,8,288]{3,2,1,0:T(8,128)S(1)} %shard_map.67.refs_2_), custom_call_target="tpu_custom_call" | custom-call | flops 7464960 | bytes 1990656 | tf_op jit(solution)/shard_map/pallas_call | solution.py:374
Async XLA Ops:
  0.0 1.3 %copy-start = (f32[8,2,18,1152]{3,1,2,0:T(2,128)S(1)}, f32[8,2,18,1152]{3,1,2,0:T(2,128)}, u32[]{:S(2)}) copy-start(f32[8,2,18,1152]{3,1,2,0:T(2,128)} %param.6) | copy-start | bytes 3981316
  1.3 0.9 %copy-start.6 = (f32[2,18,1152]{2,0,1:T(2,128)S(1)}, f32[2,18,1152]{2,0,1:T(2,128)}, u32[]{:S(2)}) copy-start(f32[2,18,1152]{2,0,1:T(2,128)} %param.7) | copy-start | bytes 497668
  2.2 0.9 %copy-start.7 = (f32[2,18,1152]{2,0,1:T(2,128)S(1)}, f32[2,18,1152]{2,0,1:T(2,128)}, u32[]{:S(2)}) copy-start(f32[2,18,1152]{2,0,1:T(2,128)} %param.8) | copy-start | bytes 497668
  5.0 16.2 %collective-permute-start = (f32[2,7,8,1152]{3,2,1,0:T(8,128)}, f32[2,7,8,1152]{3,2,1,0:T(8,128)}, u32[]{:S(2)}, u32[]{:S(2)}) collective-permute-start(f32[2,7,8,1152]{3,2,1,0:T(8,128)} %get-tuple-element.18), channel_id=1, source_target_pairs={{0,4},{4,8},{8,12},{1,5},{5,9},{9,13},{2,6},{6,10},{10,14},{3,7},{... | collective-permute-start | bytes 1548296 | tf_op jit(solution)/shard_map/ppermute | solution.py:415
  10.7 15.4 %collective-permute-start.1 = (f32[2,7,8,1152]{3,2,1,0:T(8,128)}, f32[2,7,8,1152]{3,2,1,0:T(8,128)}, u32[]{:S(2)}, u32[]{:S(2)}) collective-permute-start(f32[2,7,8,1152]{3,2,1,0:T(8,128)} %get-tuple-element.19), channel_id=1, source_target_pairs={{4,0},{8,4},{12,8},{5,1},{9,5},{13,9},{6,2},{10,6},{14,10},{7,3},{... | collective-permute-start | bytes 1548296 | tf_op jit(solution)/shard_map/ppermute | solution.py:416
  15.6 0.8 %copy-start.2 = (f32[3,2,24,1152]{3,2,1,0:T(8,128)}, f32[3,2,24,1152]{3,2,1,0:T(8,128)S(1)}, u32[]{:S(2)}) copy-start(f32[3,2,24,1152]{3,2,1,0:T(8,128)S(1)} %get-tuple-element.22.cy) | copy-start | bytes 1990660
  16.5 0.8 %copy-start.4 = (f32[4,2,1,14,8,128]{5,4,3,2,1,0:T(8,128)}, f32[4,2,1,14,8,128]{5,4,3,2,1,0:T(8,128)S(1)}, u32[]{:S(2)}) copy-start(f32[4,2,1,14,8,128]{5,4,3,2,1,0:T(8,128)S(1)} %get-tuple-element.17) | copy-start | bytes 1376260
  17.3 16.8 %all-to-all-start = ((f32[4,2,1,14,8,128]{5,4,3,2,1,0:T(8,128)}), f32[4,2,1,14,8,128]{5,4,3,2,1,0:T(8,128)S(1)}, u32[]{:S(2)}, u32[]{:S(2)}) async-start(f32[4,2,1,14,8,128]{5,4,3,2,1,0:T(8,128)} %copy-done.4), calls=%async_computation | async-start | bytes 917504 | tf_op jit(solution)/shard_map/all_to_all | solution.py:394
  26.1 1.1 %copy-start.3 = (f32[3,2,24,1152]{3,2,1,0:T(8,128)S(1)}, f32[3,2,24,1152]{3,2,1,0:T(8,128)}, u32[]{:S(2)}) copy-start(f32[3,2,24,1152]{3,2,1,0:T(8,128)} %copy-done.2) | copy-start | bytes 1990660
  34.0 3.7 %copy-start.1 = (f32[4,6,18,288]{3,0,2,1:T(4,128)S(1)}, f32[4,6,18,288]{3,0,2,1:T(4,128)}, u32[]{:S(2)}) copy-start(f32[4,6,18,288]{3,0,2,1:T(4,128)} %param.11) | copy-start | bytes 1492996
  34.0 16.7 %all-to-all-start.1 = ((f32[4,2,2,14,8,128]{5,4,3,2,1,0:T(8,128)}), f32[4,2,2,14,8,128]{5,4,3,2,1,0:T(8,128)S(1)}, u32[]{:S(2)}, u32[]{:S(2)}) async-start(f32[4,2,2,14,8,128]{5,4,3,2,1,0:T(8,128)} %shard_map.66), calls=%async_computation.1 | async-start | bytes 1835008 | tf_op jit(solution)/shard_map/all_to_all | solution.py:394
  37.7 13.0 %copy-start.8 = (s32[4]{0:T(128)S(1)}, s32[4]{0:T(128)}, u32[]{:S(2)}) copy-start(s32[4]{0:T(128)} %counts.1) | copy-start | bytes 52
  37.7 0.9 %copy-start.5 = (s32[6,18,288]{2,1,0:T(8,128)S(1)}, s32[6,18,288]{2,1,0:T(8,128)}, u32[]{:S(2)}) copy-start(s32[6,18,288]{2,1,0:T(8,128)} %source.1) | copy-start | bytes 373252

commit v4 on v3

--- a/solution.py
+++ b/solution.py
@@ -53,30 +53,17 @@
     return width, mains, tail, per, BLOCK * mains + tails
 
 
-def prep_kernel(rows, tracers, wind_x, wind_y, state, down, up, wx, wy, raw, sems):
+def prep_kernel(rows, tracers, winds, state, down, up):
     levels, nlon = state.shape[0], state.shape[3]
     nj = nlon // LANES
     row_stride = nj * levels
     tracer_stride = rows * row_stride
-    copies = [pltpu.make_async_copy(source, target, sems.at[i])
-              for i, (source, target) in enumerate(((tracers, raw), (wind_x, wx), (wind_y, wy)))]
-    for copy in copies:
-        copy.start()
-    for copy in copies[1:]:
-        copy.wait()
-    for level in range(levels):
-        for target, row_x, row_y in ((down, 0, 0), (up, rows - REACH, rows - REACH - 1)):
-            for q in range(REACH):
-                target[level, HALO, q:q + 1, :] = wx[row_x + q, level:level + 1, :]
-            for q in range(REACH + 1):
-                target[level, HALO, REACH + q:REACH + q + 1, :] = wy[row_y + q, level:level + 1, :]
-    copies[0].wait()
 
     def body(row, _):
         for level in range(levels):
             for j in range(nj):
                 start = row * row_stride + j * levels + level
-                state[level, row, :, tile(j)] = raw[pl.ds(start, SUB, stride=tracer_stride), :]
+                state[level, row, :, tile(j)] = tracers[pl.ds(start, SUB, stride=tracer_stride), :]
         return 0
 
     lax.fori_loop(0, rows, body, 0)
@@ -84,6 +71,11 @@
         for row in range(HALO):
             down[level, row] = state[level, row]
             up[level, row] = state[level, rows - HALO + row]
+        for target, row_x, row_y in ((down, 0, 0), (up, rows - REACH, rows - REACH - 1)):
+            for q in range(REACH):
+                target[level, HALO, q:q + 1, :] = winds[row_x + q, level:level + 1, :]
+            for q in range(REACH + 1):
+                target[level, HALO, REACH + q:REACH + q + 1, :] = winds[rows + row_y + q, level:level + 1, :]
 
 
 def lat_pass(levels, nj, ranges, cell, coef, store):
@@ -158,6 +150,7 @@
 
 
 def pack_block(block, packed, level, number, count, lane):
+    me = lax.axis_index("lev")
     nlon = len(block[0]) * LANES
     width, mains, tail, per, size = packed_sizes(nlon, count)
     for d in range(count):
@@ -167,7 +160,7 @@
                       for m in range(mains + (1 if off else 0))]
             for m in range(mains):
                 whole = jnp.where(lane < LANES - off, turned[m], turned[m + 1]) if off else turned[m]
-                packed[d, level, number, q * mains + m] = whole
+                packed[d ^ me, level, number, q * mains + m] = whole
         if tail:
             for g in range(-(-BLOCK // per)):
                 total = None
@@ -176,16 +169,24 @@
                     source = block[g * per + place][j0 + mains]
                     moved = pltpu.roll(source, shift, 1) if shift else source
                     total = moved if total is None else jnp.where(lane < place * tail, total, moved)
-                packed[d, level, number, BLOCK * mains + g] = total
-
-
-def own_coefficients(rows, wx, wy, winds, cx, cy):
+                packed[d ^ me, level, number, BLOCK * mains + g] = total
+
+
+def copy_blocks(source, target, start=0):
+    levels, blocks, size = source.shape[:3]
+    for level in range(levels):
+        for number in range(blocks):
+            for i in range(size):
+                target[level, start + number, i] = source[level, number, i]
+
+
+def own_coefficients(rows, joined, winds, cx, cy):
     levels, held, nlon = cx.shape[1:]
     keep = jnp.where(lax.axis_index("lat") == 0, 0.0, 1.0)
     for level in range(levels):
-        for way, source in enumerate((wx, wy)):
+        for way in range(2):
             for row in range(rows):
-                winds[way, level, row:row + 1, :] = source[row, level:level + 1, :]
+                winds[way, level, row:row + 1, :] = joined[way * rows + row, level:level + 1, :]
         winds[1, level, 0:1, :] = winds[1, level, 0:1, :] * keep
         for way, target in enumerate((cx, cy)):
             for j in range(nlon // LANES):
@@ -200,11 +201,12 @@
             target[level, at + q, :, tile(j)] = part
 
 
-def interior_kernel(count, rows, state, wx, wy, packed, first, cx, cy, winds, swept, inter, west, flux):
+def interior_kernel(count, rows, state, joined, *refs):
+    outs, (first, cx, cy, packed, winds, swept, inter, west, flux) = refs[:count], refs[count:]
     levels, nlon = state.shape[0], state.shape[3]
     nj = nlon // LANES
     lane = lane_ids()
-    own_coefficients(rows, wx, wy, winds, cx, cy)
+    own_coefficients(rows, joined, winds, cx, cy)
     coef_x = lambda i, level, r, lanes: cx[i, level, r:r + 1, lanes]
     coef_y = lambda i, level, f, lanes: cy[i, level, f:f + 1, lanes]
 
@@ -227,77 +229,72 @@
         pack_block(done, packed, level, (row - HALO) // BLOCK, count, lane)
 
     lon_pass(work_last, swept, coef_x, inter, west, flux, lane, send)
-
-
-def edge_kernel(count, rows, state, low, high, first, cx, cy, packed, near, far, swept, edge, inter, west, flux):
+    for k in range(count):
+        copy_blocks(packed.at[k], outs[k])
+
+
+def edge_kernel(count, rows, south, state, halo, first, cx, cy, *refs):
+    others = () if south else refs[:2]
+    outs, (packed, beyond, swept, edge, inter, west, flux) = refs[len(others):len(others) + count], refs[len(others) + count:]
     levels, nlon = state.shape[0], state.shape[3]
     nj = nlon // LANES
     lane = lane_ids()
     for level in range(levels):
-        for source, target in ((low, near), (high, far)):
-            for j in range(nj):
-                parts = coefficients(source[level, HALO, :, tile(j)])
-                for p in range(3):
-                    target[p, level, :, tile(j)] = parts[p]
+        for j in range(nj):
+            parts = coefficients(halo[level, HALO, :, tile(j)])
+            for p in range(3):
+                beyond[p, level, :, tile(j)] = parts[p]
 
     def coef_x(i, level, r, lanes):
-        if r < 0:
-            return near[i, level, r + REACH:r + REACH + 1, lanes]
-        if r >= rows:
-            return far[i, level, r - rows:r - rows + 1, lanes]
-        return cx[i, level, r:r + 1, lanes]
+        if 0 <= r < rows:
+            return cx[i, level, r:r + 1, lanes]
+        at = r + REACH if south else r - rows
+        return beyond[i, level, at:at + 1, lanes]
 
     def coef_y(i, level, f, lanes):
-        if f < 0:
-            return near[i, level, f + 2 * REACH + 1:f + 2 * REACH + 2, lanes]
-        if f >= rows:
-            return far[i, level, f - rows + REACH:f - rows + REACH + 1, lanes]
-        return cy[i, level, f:f + 1, lanes]
+        if 0 <= f < rows:
+            return cy[i, level, f:f + 1, lanes]
+        at = f + 2 * REACH + 1 if south else f - rows + REACH
+        return beyond[i, level, at:at + 1, lanes]
 
     def cell(level, r, lanes):
-        if r < 0:
-            return low[level, r + HALO, :, lanes]
-        if r >= rows:
-            return high[level, r - rows, :, lanes]
-        return state[level, r, :, lanes]
+        if 0 <= r < rows:
+            return state[level, r, :, lanes]
+        return halo[level, r + HALO if south else r - rows, :, lanes]
+
+    base = -REACH if south else rows - REACH
+    base_last = 0 if south else rows - HALO
 
     def cell_first(level, r, lanes):
-        if r < REACH:
-            return edge[level, r + REACH, :, lanes]
-        if r >= rows - REACH:
-            return edge[level, r - (rows - REACH) + BLOCK, :, lanes]
-        return first[level, r - REACH, :, lanes]
-
-    ends = [(-REACH, REACH), (rows - REACH, rows + REACH)]
-    ends_last = [(0, HALO), (rows - HALO, rows)]
-
-    def place(row, ranges):
-        (a, b), (c, _) = ranges
-        return row - a if row < b else row - c + BLOCK
+        if REACH <= r < rows - REACH:
+            return first[level, r - REACH, :, lanes]
+        return edge[level, r - base, :, lanes]
 
     def put(level, row, lanes, value):
-        swept[level, place(row, ends), :, lanes] = value
+        swept[level, row - base, :, lanes] = value
 
     def put_last(level, row, lanes, value):
-        swept[level, place(row, ends_last), :, lanes] = value
-
-    def listed(ranges):
-        return [(level, row, place(row, ranges)) for level in range(levels) for a, b in ranges for row in range(a, b)]
-
-    lat_pass(levels, nj, ends, cell, coef_y, put)
-    work, work_last = listed(ends), listed(ends_last)
+        swept[level, row - base_last, :, lanes] = value
+
+    def listed(start):
+        return [(level, start + q, q) for level in range(levels) for q in range(BLOCK)]
 
     def keep_edge(group, done):
-        level, _, at = work[group * BLOCK]
-        put_rows(edge, level, at, done)
+        put_rows(edge, group, 0, done)
 
     def send(group, done):
-        level, _, at = work_last[group * BLOCK]
-        pack_block(done, packed, level, at // BLOCK, count, lane)
-
-    lon_pass(work, swept, coef_x, inter, west, flux, lane, keep_edge)
-    lat_pass(levels, nj, ends_last, cell_first, coef_y, put_last)
-    lon_pass(work_last, swept, coef_x, inter, west, flux, lane, send)
+        pack_block(done, packed, group, 0, count, lane)
+
+    lat_pass(levels, nj, [(base, base + BLOCK)], cell, coef_y, put)
+    lon_pass(listed(base), swept, coef_x, inter, west, flux, lane, keep_edge)
+    lat_pass(levels, nj, [(base_last, base_last + BLOCK)], cell_first, coef_y, put_last)
+    lon_pass(listed(base_last), swept, coef_x, inter, west, flux, lane, send)
+    for k in range(count):
+        start = 0
+        for other in others if k == 1 else ():
+            copy_blocks(other, outs[k], start)
+            start += other.shape[1]
+        copy_blocks(packed.at[k], outs[k], start)
 
 
 def weights_kernel(weights, source, out):
@@ -315,8 +312,11 @@
             out[k, row] = total
 
 
-def remap_kernel(count, depth, parts, counts, *refs):
-    columns, weights, out = refs[:len(parts)], refs[-2], refs[-1]
+def remap_kernel(count, depth, plan, counts, *refs):
+    chunks, (weights, out, columns) = refs[:len(plan)], refs[len(plan):]
+    me = lax.axis_index("lev")
+    for (k, start), chunk in zip(plan, chunks):
+        copy_blocks(chunk, columns.at[pl.ds((me ^ k) * depth, depth)], start)
     targets, rows, _, width = out.shape
     _, mains, tail, per, _ = packed_sizes(width * count, count)
     slots = []
@@ -327,18 +327,18 @@
             start = start + counts[d]
         slots.append(slot)
 
-    def block(source, number, row0):
+    def block(number):
         for q in range(BLOCK):
-            row = row0 + q
+            row = number * BLOCK + q
             for m in range(mains + (1 if tail else 0)):
                 wide = LANES if m < mains else tail
                 lanes = slice(m * LANES, m * LANES + wide)
                 values = []
                 for level in range(targets):
                     if m < mains:
-                        values.append(source[slots[level], number, q * mains + m])
+                        values.append(columns[slots[level], number, q * mains + m])
                     else:
-                        last = source[slots[level], number, BLOCK * mains + q // per]
+                        last = columns[slots[level], number, BLOCK * mains + q // per]
                         shift = (q % per) * tail
                         last = pltpu.roll(last, LANES - shift, 1) if shift else last
                         values.append(last[:, :wide])
@@ -352,9 +352,8 @@
                         total = term if total is None else total + term
                     out[k, row, :, lanes] = total
 
-    for source, row0s in zip(columns, parts):
-        for number, row0 in enumerate(row0s):
-            block(source, number, row0)
+    for number in range(rows // BLOCK):
+        block(number)
 
 
 def tiles_of(array):
@@ -366,7 +365,6 @@
 
 
 VMEM = pl.BlockSpec(memory_space=pltpu.VMEM)
-HBM = pl.BlockSpec(memory_space=pltpu.HBM)
 SMEM = pl.BlockSpec(memory_space=pltpu.SMEM)
 
 
@@ -390,9 +388,9 @@
     return jax.ShapeDtypeStruct(shape, jnp.float32)
 
 
-def exchanged(packed, slots):
-    columns = lax.all_to_all(packed, "lev", split_axis=0, concat_axis=0, tiled=True)
-    return columns.reshape((slots,) + packed.shape[2:])
+def swapped(value, k):
+    count = lax.axis_size("lev")
+    return lax.ppermute(value, "lev", [(i, i ^ k) for i in range(count)])
 
 
 def shards(tracers, wind_x, wind_y, level_counts, source_level, remap_weight):
@@ -400,17 +398,17 @@
     bands = lax.axis_size("lat")
     number, depth, rows, nlon = tracers.shape
     targets, _, width = source_level.shape
-    _, mains, tail, per, size = packed_sizes(nlon, count)
+    size = packed_sizes(nlon, count)[-1]
+    blocks = rows // BLOCK
+    inner = (rows - 2 * HALO) // BLOCK
+    partners = range(count - 1, 1, -1)
 
     raw = tiles_of(jnp.transpose(tracers, (0, 2, 1, 3)))
-    wind = f32(rows, depth, nlon)
+    joined = jnp.concatenate([jnp.transpose(wind_x, (1, 0, 2)), jnp.transpose(wind_y, (1, 0, 2))], axis=0)
     halo = f32(depth, HALO + 1, number, nlon)
-    state, down, up, wx, wy = call(
+    state, down, up = call(
         functools.partial(prep_kernel, rows),
-        (f32(depth, rows, number, nlon), halo, halo, wind, wind),
-        (raw, jnp.transpose(wind_x, (1, 0, 2)), jnp.transpose(wind_y, (1, 0, 2))),
-        specs=[HBM, HBM, HBM],
-        scratch=[pltpu.VMEM(raw.shape, jnp.float32), pltpu.SemaphoreType.DMA((3,))],
+        (f32(depth, rows, number, nlon), halo, halo), (raw, joined),
         cost=cost(1, 8 * tracers.size))
     low = lax.ppermute(up, "lat", [(i, i + 1) for i in range(bands - 1)])
     high = lax.ppermute(down, "lat", [(i + 1, i) for i in range(bands - 1)])
@@ -418,29 +416,55 @@
         weights_kernel, f32(targets, rows, SUB, width),
         (jnp.transpose(remap_weight, (1, 2, 0, 3)), source_level),
         cost=cost(20 * remap_weight.size, 16 * remap_weight.size))
-    swept = pltpu.VMEM((depth, 2 * BLOCK, number, nlon), jnp.float32)
-    stage = pltpu.VMEM((2 * BLOCK * depth, number, nlon), jnp.float32)
-    halo_coef = pltpu.VMEM((3, depth, SUB, nlon), jnp.float32)
+
+    def box(n, *lead):
+        return lead + (depth, n, size, SUB, LANES)
+
+    def vmem(*shape):
+        return pltpu.VMEM(shape, jnp.float32)
+
     held = -(-rows // SUB) * SUB
     coef = f32(3, depth, held, nlon)
-    inner = rows - 2 * HALO
-    inner_packed, first, cx, cy = call(
+    swept = vmem(depth, rows - 2 * REACH, number, nlon)
+    stage = vmem(depth * (rows - 2 * REACH), number, nlon)
+    result = call(
         functools.partial(interior_kernel, count, rows),
-        (f32(count, depth, inner // BLOCK, size, SUB, LANES), f32(depth, rows - 2 * REACH, number, nlon), coef, coef),
-        (state, wx, wy), scratch=[pltpu.VMEM((2, depth, held, nlon), jnp.float32), swept, stage, stage, stage],
+        [f32(*box(inner))] * count + [f32(depth, rows - 2 * REACH, number, nlon), coef, coef],
+        (state, joined), scratch=[vmem(*box(inner, count)), vmem(2, depth, held, nlon), swept, stage, stage, stage],
         cost=cost(50 * tracers.size, 8 * tracers.size))
-    inner_columns = exchanged(inner_packed, count * depth)
-    edge_packed = call(
-        functools.partial(edge_kernel, count, rows),
-        f32(count, depth, 2 * HALO // BLOCK, size, SUB, LANES), (state, low, high, first, cx, cy),
-        scratch=[halo_coef, halo_coef, swept, swept, stage, stage, stage],
-        cost=cost(60 * tracers.size, 8 * tracers.size))
-    edge_columns = exchanged(edge_packed, count * depth)
-    parts = (tuple(range(HALO, rows - HALO, BLOCK)), (0, rows - HALO))
+    middle, (first, cx, cy) = result[:count], result[count:]
+    plan, chunks = [], []
+
+    def received(k, start, chunk):
+        plan.append((k, start))
+        chunks.append(chunk)
+
+    def send(sent, start):
+        received(0, start, sent[0])
+        for k in partners:
+            received(k, start, swapped(sent[k], k))
+
+    send(middle, 1)
+    swept = vmem(depth, BLOCK, number, nlon)
+    stage = vmem(depth * BLOCK, number, nlon)
+    scratch = [vmem(*box(1, count)), vmem(3, depth, SUB, nlon), swept, swept, stage, stage, stage]
+    south = call(
+        functools.partial(edge_kernel, count, rows, True),
+        [f32(*box(1))] * count, (state, low, first, cx, cy), scratch=scratch,
+        cost=cost(30 * tracers.size, 4 * tracers.size))
+    send(south, 0)
+    north = call(
+        functools.partial(edge_kernel, count, rows, False),
+        [f32(*box(blocks if k == 1 else 1)) for k in range(count)],
+        (state, high, first, cx, cy, south[1], middle[1]), scratch=scratch,
+        cost=cost(30 * tracers.size, 4 * tracers.size))
+    send(north, blocks - 1)
+    received(1, 0, swapped(north[1], 1))
     out = call(
-        functools.partial(remap_kernel, count, depth, parts),
-        f32(targets, rows, number, width), (level_counts, inner_columns, edge_columns, taps),
-        specs=[SMEM, VMEM, VMEM, VMEM],
+        functools.partial(remap_kernel, count, depth, tuple(plan)),
+        f32(targets, rows, number, width), (level_counts, *chunks, taps),
+        specs=[SMEM] + [VMEM] * (len(chunks) + 1),
+        scratch=[vmem(count * depth, blocks, size, SUB, LANES)],
         cost=cost(60 * remap_weight.size, 16 * remap_weight.size))
     return jnp.transpose(out, (2, 0, 1, 3))
 

time: 53.2 us -> 45.7 us (0.86)
  local copies, waits for them, and re-layouts: 6.8 us -> 1.33 us
  Pallas kernels: 14.5 us -> 11.7 us
  other arithmetic: 0 us -> 1.14 us
  starting transfers between devices: 14.1 us -> 13.4 us
  waiting for transfers between devices: 17.3 us -> 17.9 us
    all_to_all x2 -> x0, waiting for transfers between devices: 11.9 us -> none  [exchanged(): lax.all_to_all(packed, 'lev', split_axis=0, concat_axis=0, tiled=True)]
    ppermute x0 -> x7, waiting for transfers between devices: none -> 10.5 us  [swapped(): return lax.ppermute(value, 'lev', [(i, i ^ k) for i in range(count)])]
    ppermute x0 -> x7, starting transfers between devices: none -> 7.13 us  [swapped(): return lax.ppermute(value, 'lev', [(i, i ^ k) for i in range(count)])]
    all_to_all x2 -> x0, starting transfers between devices: 7.1 us -> none  [exchanged(): lax.all_to_all(packed, 'lev', split_axis=0, concat_axis=0, tiled=True)]
    unnamed x18 -> x8, local copies, waits for them, and re-layouts: 6.8 us -> 1.33 us
    ppermute x1, waiting for transfers between devices: 0.47 us -> 5.85 us  [shards(): low = lax.ppermute(up, 'lat', [(i, i + 1) for i in range(bands - 1)])]
    ppermute x1, waiting for transfers between devices: 4.93 us -> 1.53 us  [shards(): high = lax.ppermute(down, 'lat', [(i + 1, i) for i in range(bands - 1)])]
    pallas_call x5 -> x6, Pallas kernels: 14.5 us -> 11.7 us  [call(): pl.pallas_call(kernel, out_shape=outs, in_specs=specs or [VMEM] * len(arg...]
  transfers between devices with their start and end apart: 4 -> 9, of which waited for: 3 -> 7; matrix products, arithmetic and copies ran while one was open for 0% -> 0% of each run, Pallas kernels for 20% -> 15%
where the time goes in v4:
time: 45.7 us; the launch traced here: 45.5 us
  waiting for transfers between devices  17.9 us (39%)
  starting transfers between devices  13.4 us (29%)
  Pallas kernels  11.7 us (26%)
  local copies, waits for them, and re-layouts  1.33 us (3%)
  other arithmetic  1.14 us (2%)
    pallas_call x6, Pallas kernels, call(): pl.pallas_call(kernel, out_shape=outs, in_specs=specs or [VMEM] * len(arg...  11.7 us
    ppermute x7, waiting for transfers between devices, swapped(): return lax.ppermute(value, 'lev', [(i, i ^ k) for i in range(count)])  10.5 us
    ppermute x7, starting transfers between devices, swapped(): return lax.ppermute(value, 'lev', [(i, i ^ k) for i in range(count)])  7.13 us
    ppermute x1, waiting for transfers between devices, shards(): low = lax.ppermute(up, 'lat', [(i, i + 1) for i in range(bands - 1)])  5.85 us
    ppermute x1, starting transfers between devices, shards(): low = lax.ppermute(up, 'lat', [(i, i + 1) for i in range(bands - 1)])  4.96 us
    ppermute x1, waiting for transfers between devices, shards(): high = lax.ppermute(down, 'lat', [(i + 1, i) for i in range(bands - 1)])  1.53 us
    unnamed x8, local copies, waits for them, and re-layouts  1.33 us
    ppermute x1, starting transfers between devices, shards(): high = lax.ppermute(down, 'lat', [(i + 1, i) for i in range(bands - 1)])  1.29 us
  transfers between devices with their start and end apart: 9, of which 7 were waited for; matrix products, arithmetic and copies ran while one was open for 0% of the time, Pallas kernels for 15%

profile of v4, /device:TPU:0, one launch (start us, length us, event | category | flops | bytes accessed | tf_op | source)
XLA Modules:
  0.0 45.5 jit_solution(8032359263284503198)
XLA Ops:
  0.0 1.1 %pad_maximum_fusion.winds.joined = f32[36,2,1152]{2,1,0:T(2,128)S(1)} fusion(f32[18,2,1152]{2,1,0:T(2,128)} %bitcast.13, f32[18,2,1152]{2,1,0:T(2,128)} %bitcast.14), kind=kLoop, calls=%fused_computation | loop fusion | flops 82944 | bytes 663552 | tf_op jit(solution)/shard_map/concatenate | solution.py:407
  1.1 0.0 copy-start
  1.2 1.3 %copy-done = f32[8,2,18,1152]{3,1,2,0:T(2,128)S(1)} copy-done((f32[8,2,18,1152]{3,1,2,0:T(2,128)S(1)}, f32[8,2,18,1152]{3,1,2,0:T(2,128)}, u32[]{:S(2)}) %copy-start) | copy-done | bytes 1327128
  2.5 0.3 shard_map.64
  2.7 5.0 %collective-permute-start.2 = (f32[2,7,8,1152]{3,2,1,0:T(8,128)S(1)}, f32[2,7,8,1152]{3,2,1,0:T(8,128)S(1)}, u32[]{:S(2)}, u32[]{:S(2)}) collective-permute-start(f32[2,7,8,1152]{3,2,1,0:T(8,128)S(1)} %get-tuple-element.27), channel_id=1, source_target_pairs={{0,4},{4,8},{8,12},{1,5},{5,9},{9,13},{2,6},{6,10},{10,14},{3,7},{... | collective-permute-start | bytes 1548296 | tf_op jit(solution)/shard_map/ppermute | solution.py:413
  7.7 1.3 %collective-permute-start.5 = (f32[2,7,8,1152]{3,2,1,0:T(8,128)S(1)}, f32[2,7,8,1152]{3,2,1,0:T(8,128)S(1)}, u32[]{:S(2)}, u32[]{:S(2)}) collective-permute-start(f32[2,7,8,1152]{3,2,1,0:T(8,128)S(1)} %get-tuple-element.34), channel_id=1, source_target_pairs={{4,0},{8,4},{12,8},{5,1},{9,5},{13,9},{6,2},{10,6},{14,10},{7,3},{... | collective-permute-start | bytes 1548296 | tf_op jit(solution)/shard_map/ppermute | solution.py:414
  9.0 3.8 %shard_map.65 = (f32[2,1,14,8,128]{4,3,2,1,0:T(8,128)S(1)}, f32[2,1,14,8,128]{4,3,2,1,0:T(8,128)S(1)}, f32[2,1,14,8,128]{4,3,2,1,0:T(8,128)S(1)}, f32[2,1,14,8,1...) custom-call(f32[2,18,8,1152]{3,2,1,0:T(8,128)S(1)} %get-tuple-elemen, ...), custom_call_target="tpu_custom_call" | custom-call | flops 16588800 | bytes 2654208 | tf_op jit(solution)/shard_map/pallas_call | solution.py:372
  12.8 5.9 %collective-permute-done.2.halo = f32[2,7,8,1152]{3,2,1,0:T(8,128)S(1)} collective-permute-done((f32[2,7,8,1152]{3,2,1,0:T(8,128)S(1)}, f32[2,7,8,1152]{3,2,1,0:T(8,128)S(1)}, u32[]{:S(2)}, u32[]{:S(2)}) %collective-permute-start.2) | collective-permute-done | bytes 516128 | tf_op jit(solution)/shard_map/ppermute | solution.py:413
  18.7 2.6 %shard_map.66 = (f32[2,1,14,8,128]{4,3,2,1,0:T(8,128)S(1)}, f32[2,1,14,8,128]{4,3,2,1,0:T(8,128)S(1)}, f32[2,1,14,8,128]{4,3,2,1,0:T(8,128)S(1)}, f32[2,1,14,8,128]{4,3,2,1,0:T(8,128)S(1)}) custom-call(f32[2,18,8,1152]{3,2,1,0:T(8,128)S(1)} %get-tuple-element.23.state, f32[2,7,8,1152]{3,2,1,0:T(8,128)S(1)} %collective-permute-done.2.halo, ...), custom_call_target="tpu_custom_call" | custom-call | flops 9953280 | bytes 1327104 | tf_op jit(solution)/shard_map/pallas_call | solution.py:372
  21.3 1.5 %collective-permute-done.5.halo = f32[2,7,8,1152]{3,2,1,0:T(8,128)S(1)} collective-permute-done((f32[2,7,8,1152]{3,2,1,0:T(8,128)S(1)}, f32[2,7,8,1152]{3,2,1,0:T(8,128)S(1)}, u32[]{:S(2)}, u32[]{:S(2)}) %collective-permute-start.5) | collective-permute-done | bytes 516128 | tf_op jit(solution)/shard_map/ppermute | solution.py:414
  22.8 0.0 copy-start.1
  22.8 0.0 copy-start.2
  22.8 2.6 %shard_map.67 = (f32[2,1,14,8,128]{4,3,2,1,0:T(8,128)S(1)}, f32[2,3,14,8,128]{4,3,2,1,0:T(8,128)S(1)}, f32[2,1,14,8,128]{4,3,2,1,0:T(8,128)S(1)}, f32[2,1,14,8,128]{4,3,2,1,0:T(8,128)S(1)}) custom-call(f32[2,18,8,1152]{3,2,1,0:T(8,128)S(1)} %get-tuple-element.23.state, f32[2,7,8,1152]{3,2,1,0:T(8,128)S(1)} %collective-permute-done.5.halo, ...), custom_call_target="tpu_custom_call" | custom-call | flops 9953280 | bytes 1327104 | tf_op jit(solution)/shard_map/pallas_call | solution.py:372
  25.4 0.0 copy-start.3
  25.4 0.1 collective-permute-start.8
  25.5 1.6 %collective-permute-start = (f32[2,1,14,8,128]{4,3,2,1,0:T(8,128)S(1)}, f32[2,1,14,8,128]{4,3,2,1,0:T(8,128)S(1)}, u32[]{:S(2)}, u32[]{:S(2)}) collective-permute-start(f32[2,1,14,8,128]{4,3,2,1,0:T(8,128)S(1)} %get-tuple-element.25), channel_id=1, source_target_pairs={{0,3},{1,2},{2,1},{3,0},{4,7},{5,6},{6,5},{7,4},{8,11},{9,10},{10,... | collective-permute-start | bytes 344072 | tf_op jit(solution)/shard_map/ppermute | solution.py:393
  27.1 0.5 %collective-permute-start.1 = (f32[2,1,14,8,128]{4,3,2,1,0:T(8,128)S(1)}, f32[2,1,14,8,128]{4,3,2,1,0:T(8,128)S(1)}, u32[]{:S(2)}, u32[]{:S(2)}) collective-permute-start(f32[2,1,14,8,128]{4,3,2,1,0:T(8,128)S(1)} %get-tuple-element.26), channel_id=1, source_target_pairs={{0,2},{1,3},{2,0},{3,1},{4,6},{5,7},{6,4},{7,5},{8,10},{9,11},{10,... | collective-permute-start | bytes 344072 | tf_op jit(solution)/shard_map/ppermute | solution.py:393
  27.6 0.9 %collective-permute-start.3 = (f32[2,1,14,8,128]{4,3,2,1,0:T(8,128)S(1)}, f32[2,1,14,8,128]{4,3,2,1,0:T(8,128)S(1)}, u32[]{:S(2)}, u32[]{:S(2)}) collective-permute-start(f32[2,1,14,8,128]{4,3,2,1,0:T(8,128)S(1)} %get-tuple-element.32), channel_id=1, source_target_pairs={{0,3},{1,2},{2,1},{3,0},{4,7},{5,6},{6,5},{7,4},{8,11},{9,10},{10,... | collective-permute-start | bytes 344072 | tf_op jit(solution)/shard_map/ppermute | solution.py:393
  28.5 0.6 %collective-permute-start.4 = (f32[2,1,14,8,128]{4,3,2,1,0:T(8,128)S(1)}, f32[2,1,14,8,128]{4,3,2,1,0:T(8,128)S(1)}, u32[]{:S(2)}, u32[]{:S(2)}) collective-permute-start(f32[2,1,14,8,128]{4,3,2,1,0:T(8,128)S(1)} %get-tuple-element.33), channel_id=1, source_target_pairs={{0,2},{1,3},{2,0},{3,1},{4,6},{5,7},{6,4},{7,5},{8,10},{9,11},{10,... | collective-permute-start | bytes 344072 | tf_op jit(solution)/shard_map/ppermute | solution.py:393
  29.2 1.4 %collective-permute-done.refs_1_ = f32[2,1,14,8,128]{4,3,2,1,0:T(8,128)S(1)} collective-permute-done((f32[2,1,14,8,128]{4,3,2,1,0:T(8,128)S(1)}, f32[2,1,14,8,128]{4,3,2,1,0:T(8,128)S(1)}, u32[]{:S(2)}, u32[]{:S(2)}) %collective-permute-start) | collective-permute-done | bytes 114720 | tf_op jit(solution)/shard_map/ppermute | solution.py:393
  30.6 1.9 %collective-permute-start.6 = (f32[2,1,14,8,128]{4,3,2,1,0:T(8,128)S(1)}, f32[2,1,14,8,128]{4,3,2,1,0:T(8,128)S(1)}, u32[]{:S(2)}, u32[]{:S(2)}) collective-permute-start(f32[2,1,14,8,128]{4,3,2,1,0:T(8,128)S(1)} %get-tuple-element.38), channel_id=1, source_target_pairs={{0,3},{1,2},{2,1},{3,0},{4,7},{5,6},{6,5},{7,4},{8,11},{9,10},{10,... | collective-permute-start | bytes 344072 | tf_op jit(solution)/shard_map/ppermute | solution.py:393
  32.5 1.5 %collective-permute-done.1.refs_2_ = f32[2,1,14,8,128]{4,3,2,1,0:T(8,128)S(1)} collective-permute-done((f32[2,1,14,8,128]{4,3,2,1,0:T(8,128)S(1)}, f32[2,1,14,8,128]{4,3,2,1,0:T(8,128)S(1)}, u32[]{:S(2)}, u32[]{:S(2)}) %collective-permute-start.1) | collective-permute-done | bytes 114720 | tf_op jit(solution)/shard_map/ppermute | solution.py:393
  34.0 1.5 %collective-permute-start.7 = (f32[2,1,14,8,128]{4,3,2,1,0:T(8,128)S(1)}, f32[2,1,14,8,128]{4,3,2,1,0:T(8,128)S(1)}, u32[]{:S(2)}, u32[]{:S(2)}) collective-permute-start(f32[2,1,14,8,128]{4,3,2,1,0:T(8,128)S(1)} %get-tuple-element.39), channel_id=1, source_target_pairs={{0,2},{1,3},{2,0},{3,1},{4,6},{5,7},{6,4},{7,5},{8,10},{9,11},{10,... | collective-permute-start | bytes 344072 | tf_op jit(solution)/shard_map/ppermute | solution.py:393
  35.5 0.0 copy-done.1
  35.5 0.0 copy-done.2
  35.5 0.2 shard_map.68.refs_10_
  35.7 0.0 collective-permute-done.3.refs_4_
  35.7 3.2 %collective-permute-done.4.refs_5_ = f32[2,1,14,8,128]{4,3,2,1,0:T(8,128)S(1)} collective-permute-done((f32[2,1,14,8,128]{4,3,2,1,0:T(8,128)S(1)}, f32[2,1,14,8,128]{4,3,2,1,0:T(8,128)S(1)}, u32[]{:S(2)}, u32[]{:S(2)}) %collective-permute-start.4) | collective-permute-done | bytes 114720 | tf_op jit(solution)/shard_map/ppermute | solution.py:393
  38.9 1.5 %collective-permute-done.6.refs_7_ = f32[2,1,14,8,128]{4,3,2,1,0:T(8,128)S(1)} collective-permute-done((f32[2,1,14,8,128]{4,3,2,1,0:T(8,128)S(1)}, f32[2,1,14,8,128]{4,3,2,1,0:T(8,128)S(1)}, u32[]{:S(2)}, u32[]{:S(2)}) %collective-permute-start.6) | collective-permute-done | bytes 114720 | tf_op jit(solution)/shard_map/ppermute | solution.py:393
  40.4 2.9 %collective-permute-done.7.refs_8_ = f32[2,1,14,8,128]{4,3,2,1,0:T(8,128)S(1)} collective-permute-done((f32[2,1,14,8,128]{4,3,2,1,0:T(8,128)S(1)}, f32[2,1,14,8,128]{4,3,2,1,0:T(8,128)S(1)}, u32[]{:S(2)}, u32[]{:S(2)}) %collective-permute-start.7) | collective-permute-done | bytes 114720 | tf_op jit(solution)/shard_map/ppermute | solution.py:393
  43.3 0.0 collective-permute-done.8.refs_9_
  43.3 0.0 copy-done.3
  43.3 2.2 %shard_map.69 = f32[6,18,8,288]{3,2,1,0:T(8,128)} custom-call(s32[4]{0:T(128)S(1)} %copy-done.3, f32[2,1,14,8,128]{4,3,2,1,0:T(8,128)S(1)} %get-tuple-element.24.refs_0_, f32[2,1,14,8,128]{4,3,2,1,0:T(8,128)S(1)} %collective-permute-done.refs_1_, f32[2,1,14,8,128]{4,3,2,1,0:T(8,128)S(1)} %collective-permute-done.1.refs_2_, ...), custom_call_target="tpu_custom_call" | custom-call | flops 7464960 | bytes 1990656 | tf_op jit(solution)/shard_map/pallas_call | solution.py:372
Async XLA Ops:
  1.1 1.3 %copy-start = (f32[8,2,18,1152]{3,1,2,0:T(2,128)S(1)}, f32[8,2,18,1152]{3,1,2,0:T(2,128)}, u32[]{:S(2)}) copy-start(f32[8,2,18,1152]{3,1,2,0:T(2,128)} %param.6) | copy-start | bytes 3981316
  2.7 15.9 %collective-permute-start.2 = (f32[2,7,8,1152]{3,2,1,0:T(8,128)S(1)}, f32[2,7,8,1152]{3,2,1,0:T(8,128)S(1)}, u32[]{:S(2)}, u32[]{:S(2)}) collective-permute-start(f32[2,7,8,1152]{3,2,1,0:T(8,128)S(1)} %get-tuple-element.27), channel_id=1, source_target_pairs={{0,4},{4,8},{8,12},{1,5},{5,9},{9,13},{2,6},{6,10},{10,14},{3,7},{... | collective-permute-start | bytes 1548296 | tf_op jit(solution)/shard_map/ppermute | solution.py:413
  7.7 15.1 %collective-permute-start.5 = (f32[2,7,8,1152]{3,2,1,0:T(8,128)S(1)}, f32[2,7,8,1152]{3,2,1,0:T(8,128)S(1)}, u32[]{:S(2)}, u32[]{:S(2)}) collective-permute-start(f32[2,7,8,1152]{3,2,1,0:T(8,128)S(1)} %get-tuple-element.34), channel_id=1, source_target_pairs={{4,0},{8,4},{12,8},{5,1},{9,5},{13,9},{6,2},{10,6},{14,10},{7,3},{... | collective-permute-start | bytes 1548296 | tf_op jit(solution)/shard_map/ppermute | solution.py:414
  22.8 12.7 %copy-start.1 = (f32[4,6,18,288]{3,0,2,1:T(4,128)S(1)}, f32[4,6,18,288]{3,0,2,1:T(4,128)}, u32[]{:S(2)}) copy-start(f32[4,6,18,288]{3,0,2,1:T(4,128)} %param.11) | copy-start | bytes 1492996
  22.8 12.7 %copy-start.2 = (s32[6,18,288]{2,1,0:T(8,128)S(1)}, s32[6,18,288]{2,1,0:T(8,128)}, u32[]{:S(2)}) copy-start(s32[6,18,288]{2,1,0:T(8,128)} %source.1) | copy-start | bytes 373252
  25.4 17.9 %copy-start.3 = (s32[4]{0:T(128)S(1)}, s32[4]{0:T(128)}, u32[]{:S(2)}) copy-start(s32[4]{0:T(128)} %counts.1) | copy-start | bytes 52
  25.4 17.9 %collective-permute-start.8 = (f32[2,3,14,8,128]{4,3,2,1,0:T(8,128)S(1)}, f32[2,3,14,8,128]{4,3,2,1,0:T(8,128)S(1)}, u32[]{:S(2)}, u32[]{:S(2)}) collective-permute-start(f32[2,3,14,8,128]{4,3,2,1,0:T(8,128)S(1)} %get-tuple-element.40), channel_id=1, source_target_pairs={{0,1},{1,0},{2,3},{3,2},{4,5},{5,4},{6,7},{7,6},{8,9},{9,8},{10,11... | collective-permute-start | bytes 1032200 | tf_op jit(solution)/shard_map/ppermute | solution.py:393
  25.5 5.1 %collective-permute-start = (f32[2,1,14,8,128]{4,3,2,1,0:T(8,128)S(1)}, f32[2,1,14,8,128]{4,3,2,1,0:T(8,128)S(1)}, u32[]{:S(2)}, u32[]{:S(2)}) collective-permute-start(f32[2,1,14,8,128]{4,3,2,1,0:T(8,128)S(1)} %get-tuple-element.25), channel_id=1, source_target_pairs={{0,3},{1,2},{2,1},{3,0},{4,7},{5,6},{6,5},{7,4},{8,11},{9,10},{10,... | collective-permute-start | bytes 344072 | tf_op jit(solution)/shard_map/ppermute | solution.py:393
  27.1 6.9 %collective-permute-start.1 = (f32[2,1,14,8,128]{4,3,2,1,0:T(8,128)S(1)}, f32[2,1,14,8,128]{4,3,2,1,0:T(8,128)S(1)}, u32[]{:S(2)}, u32[]{:S(2)}) collective-permute-start(f32[2,1,14,8,128]{4,3,2,1,0:T(8,128)S(1)} %get-tuple-element.26), channel_id=1, source_target_pairs={{0,2},{1,3},{2,0},{3,1},{4,6},{5,7},{6,4},{7,5},{8,10},{9,11},{10,... | collective-permute-start | bytes 344072 | tf_op jit(solution)/shard_map/ppermute | solution.py:393
  27.6 8.1 %collective-permute-start.3 = (f32[2,1,14,8,128]{4,3,2,1,0:T(8,128)S(1)}, f32[2,1,14,8,128]{4,3,2,1,0:T(8,128)S(1)}, u32[]{:S(2)}, u32[]{:S(2)}) collective-permute-start(f32[2,1,14,8,128]{4,3,2,1,0:T(8,128)S(1)} %get-tuple-element.32), channel_id=1, source_target_pairs={{0,3},{1,2},{2,1},{3,0},{4,7},{5,6},{6,5},{7,4},{8,11},{9,10},{10,... | collective-permute-start | bytes 344072 | tf_op jit(solution)/shard_map/ppermute | solution.py:393
  28.5 10.4 %collective-permute-start.4 = (f32[2,1,14,8,128]{4,3,2,1,0:T(8,128)S(1)}, f32[2,1,14,8,128]{4,3,2,1,0:T(8,128)S(1)}, u32[]{:S(2)}, u32[]{:S(2)}) collective-permute-start(f32[2,1,14,8,128]{4,3,2,1,0:T(8,128)S(1)} %get-tuple-element.33), channel_id=1, source_target_pairs={{0,2},{1,3},{2,0},{3,1},{4,6},{5,7},{6,4},{7,5},{8,10},{9,11},{10,... | collective-permute-start | bytes 344072 | tf_op jit(solution)/shard_map/ppermute | solution.py:393
  30.6 9.8 %collective-permute-start.6 = (f32[2,1,14,8,128]{4,3,2,1,0:T(8,128)S(1)}, f32[2,1,14,8,128]{4,3,2,1,0:T(8,128)S(1)}, u32[]{:S(2)}, u32[]{:S(2)}) collective-permute-start(f32[2,1,14,8,128]{4,3,2,1,0:T(8,128)S(1)} %get-tuple-element.38), channel_id=1, source_target_pairs={{0,3},{1,2},{2,1},{3,0},{4,7},{5,6},{6,5},{7,4},{8,11},{9,10},{10,... | collective-permute-start | bytes 344072 | tf_op jit(solution)/shard_map/ppermute | solution.py:393
  34.0 9.3 %collective-permute-start.7 = (f32[2,1,14,8,128]{4,3,2,1,0:T(8,128)S(1)}, f32[2,1,14,8,128]{4,3,2,1,0:T(8,128)S(1)}, u32[]{:S(2)}, u32[]{:S(2)}) collective-permute-start(f32[2,1,14,8,128]{4,3,2,1,0:T(8,128)S(1)} %get-tuple-element.39), channel_id=1, source_target_pairs={{0,2},{1,3},{2,0},{3,1},{4,6},{5,7},{6,4},{7,5},{8,10},{9,11},{10,... | collective-permute-start | bytes 344072 | tf_op jit(solution)/shard_map/ppermute | solution.py:393

commit v5 on v4

--- a/solution.py
+++ b/solution.py
@@ -53,11 +53,15 @@
     return width, mains, tail, per, BLOCK * mains + tails
 
 
-def prep_kernel(rows, tracers, winds, state, down, up):
+def prep_kernel(rows, tracers, winds, state, first_round, second_round):
     levels, nlon = state.shape[0], state.shape[3]
     nj = nlon // LANES
     row_stride = nj * levels
     tracer_stride = rows * row_stride
+    band, bands = lax.axis_index("lat"), lax.axis_size("lat")
+    even = band % 2 == 0
+    alone = (band == 0) | (band == bands - 1)
+    keep = jnp.where(alone, 0.0, 1.0)
 
     def body(row, _):
         for level in range(levels):
@@ -67,15 +71,18 @@
         return 0
 
     lax.fori_loop(0, rows, body, 0)
-    for level in range(levels):
-        for row in range(HALO):
-            down[level, row] = state[level, row]
-            up[level, row] = state[level, rows - HALO + row]
-        for target, row_x, row_y in ((down, 0, 0), (up, rows - REACH, rows - REACH - 1)):
+    for target, north, scale in ((first_round, even, None), (second_round, jnp.logical_not(even), keep)):
+        scaled = (lambda v: v) if scale is None else (lambda v: v * scale)
+        row_t = jnp.where(north, rows - HALO, 0)
+        row_x = jnp.where(north, rows - REACH, 0)
+        row_y = jnp.where(north, rows - REACH - 1, 0)
+        for level in range(levels):
+            for row in range(HALO):
+                target[level, row] = scaled(state[level, row_t + row])
             for q in range(REACH):
-                target[level, HALO, q:q + 1, :] = winds[row_x + q, level:level + 1, :]
+                target[level, HALO, q:q + 1, :] = scaled(winds[row_x + q, level:level + 1, :])
             for q in range(REACH + 1):
-                target[level, HALO, REACH + q:REACH + q + 1, :] = winds[rows + row_y + q, level:level + 1, :]
+                target[level, HALO, REACH + q:REACH + q + 1, :] = scaled(winds[rows + row_y + q, level:level + 1, :])
 
 
 def lat_pass(levels, nj, ranges, cell, coef, store):
@@ -233,15 +240,21 @@
         copy_blocks(packed.at[k], outs[k])
 
 
-def edge_kernel(count, rows, south, state, halo, first, cx, cy, *refs):
-    others = () if south else refs[:2]
-    outs, (packed, beyond, swept, edge, inter, west, flux) = refs[len(others):len(others) + count], refs[len(others) + count:]
+def edge_kernel(count, rows, south, joint, state, first_round, second_round, first, cx, cy, *refs):
+    others = refs[:joint]
+    outs, (packed, beyond, swept, edge, inter, west, flux) = refs[-7 - count:-7], refs[-7:]
+    odd = lax.axis_index("lat") % 2 == 1
+    from_first = odd if south else jnp.logical_not(odd)
+
+    def halo(*at):
+        return jnp.where(from_first, first_round[at], second_round[at])
+
     levels, nlon = state.shape[0], state.shape[3]
     nj = nlon // LANES
     lane = lane_ids()
     for level in range(levels):
         for j in range(nj):
-            parts = coefficients(halo[level, HALO, :, tile(j)])
+            parts = coefficients(halo(level, HALO, slice(None), tile(j)))
             for p in range(3):
                 beyond[p, level, :, tile(j)] = parts[p]
 
@@ -260,7 +273,7 @@
     def cell(level, r, lanes):
         if 0 <= r < rows:
             return state[level, r, :, lanes]
-        return halo[level, r + HALO if south else r - rows, :, lanes]
+        return halo(level, r + HALO if south else r - rows, slice(None), lanes)
 
     base = -REACH if south else rows - REACH
     base_last = 0 if south else rows - HALO
@@ -290,11 +303,11 @@
     lat_pass(levels, nj, [(base_last, base_last + BLOCK)], cell_first, coef_y, put_last)
     lon_pass(listed(base_last), swept, coef_x, inter, west, flux, lane, send)
     for k in range(count):
-        start = 0
-        for other in others if k == 1 else ():
-            copy_blocks(other, outs[k], start)
-            start += other.shape[1]
-        copy_blocks(packed.at[k], outs[k], start)
+        copy_blocks(packed.at[k], outs[k])
+    start = 1
+    for other in others:
+        copy_blocks(other, outs[1], start)
+        start += other.shape[1]
 
 
 def weights_kernel(weights, source, out):
@@ -365,6 +378,7 @@
 
 
 VMEM = pl.BlockSpec(memory_space=pltpu.VMEM)
+ANY = pl.BlockSpec(memory_space=pl.ANY)
 SMEM = pl.BlockSpec(memory_space=pltpu.SMEM)
 
 
@@ -406,12 +420,13 @@
     raw = tiles_of(jnp.transpose(tracers, (0, 2, 1, 3)))
     joined = jnp.concatenate([jnp.transpose(wind_x, (1, 0, 2)), jnp.transpose(wind_y, (1, 0, 2))], axis=0)
     halo = f32(depth, HALO + 1, number, nlon)
-    state, down, up = call(
+    state, *rounds = call(
         functools.partial(prep_kernel, rows),
         (f32(depth, rows, number, nlon), halo, halo), (raw, joined),
         cost=cost(1, 8 * tracers.size))
-    low = lax.ppermute(up, "lat", [(i, i + 1) for i in range(bands - 1)])
-    high = lax.ppermute(down, "lat", [(i + 1, i) for i in range(bands - 1)])
+    swaps = [[(i, i ^ 1) for i in range(bands)],
+             [(i, i if i in (0, bands - 1) else ((i - 1) ^ 1) + 1) for i in range(bands)]]
+    rounds = [lax.ppermute(sent, "lat", pairs) for sent, pairs in zip(rounds, swaps)]
     taps = call(
         weights_kernel, f32(targets, rows, SUB, width),
         (jnp.transpose(remap_weight, (1, 2, 0, 3)), source_level),
@@ -438,28 +453,31 @@
     def received(k, start, chunk):
         plan.append((k, start))
         chunks.append(chunk)
+        return chunk
 
     def send(sent, start):
         received(0, start, sent[0])
-        for k in partners:
-            received(k, start, swapped(sent[k], k))
-
-    send(middle, 1)
+        return [received(k, start, swapped(sent[k], k)) for k in partners]
+
     swept = vmem(depth, BLOCK, number, nlon)
     stage = vmem(depth * BLOCK, number, nlon)
-    scratch = [vmem(*box(1, count)), vmem(3, depth, SUB, nlon), swept, swept, stage, stage, stage]
-    south = call(
-        functools.partial(edge_kernel, count, rows, True),
-        [f32(*box(1))] * count, (state, low, first, cx, cy), scratch=scratch,
-        cost=cost(30 * tracers.size, 4 * tracers.size))
+
+    def edge(south, joint, after):
+        args = (state, *rounds, first, cx, cy, *joint, *after)
+        return call(
+            functools.partial(edge_kernel, count, rows, south, len(joint)),
+            [f32(*box(1 + sum(c.shape[1] for c in joint) if k == 1 else 1)) for k in range(count)], args,
+            specs=[VMEM] * (len(args) - len(after)) + [ANY] * len(after),
+            scratch=[vmem(*box(1, count)), vmem(3, depth, SUB, nlon), swept, swept, stage, stage, stage],
+            cost=cost(30 * tracers.size, 4 * tracers.size))
+
+    arrived = send(middle, 1)
+    south = edge(True, (middle[1],), (taps,))
     send(south, 0)
-    north = call(
-        functools.partial(edge_kernel, count, rows, False),
-        [f32(*box(blocks if k == 1 else 1)) for k in range(count)],
-        (state, high, first, cx, cy, south[1], middle[1]), scratch=scratch,
-        cost=cost(30 * tracers.size, 4 * tracers.size))
+    received(1, 0, swapped(south[1], 1))
+    north = edge(False, (), arrived)
     send(north, blocks - 1)
-    received(1, 0, swapped(north[1], 1))
+    received(1, blocks - 1, swapped(north[1], 1))
     out = call(
         functools.partial(remap_kernel, count, depth, tuple(plan)),
         f32(targets, rows, number, width), (level_counts, *chunks, taps),

time: 45.7 us -> 37.5 us (0.82)
  the two profiles are of different devices: /device:TPU:0 before, /device:TPU:17 now
where the time goes in v5:
time: 37.5 us; the launch traced here: 37.3 us
  waiting for transfers between devices  12.1 us (32%)
  Pallas kernels  11.4 us (30%)
  starting transfers between devices  11.3 us (30%)
  local copies, waits for them, and re-layouts  1.33 us (4%)
  other arithmetic  1.14 us (3%)
    pallas_call x6, Pallas kernels, call(): pl.pallas_call(kernel, out_shape=outs, in_specs=specs or [VMEM] * len(arg...  11.4 us
    ppermute x8, starting transfers between devices, swapped(): return lax.ppermute(value, 'lev', [(i, i ^ k) for i in range(count)])  8.08 us
    ppermute x2, waiting for transfers between devices, shards(): lax.ppermute(sent, 'lat', pairs)  6.04 us
    ppermute x8, waiting for transfers between devices, swapped(): return lax.ppermute(value, 'lev', [(i, i ^ k) for i in range(count)])  6.03 us
    ppermute x2, starting transfers between devices, shards(): lax.ppermute(sent, 'lat', pairs)  3.27 us
    unnamed x8, local copies, waits for them, and re-layouts  1.33 us
    concatenate x1, other arithmetic, shards(): jnp.concatenate([jnp.transpose(wind_x, (1, 0, 2)), jnp.transpose(wind_y,...  1.14 us
  transfers between devices with their start and end apart: 10, of which 5 were waited for; matrix products, arithmetic and copies ran while one was open for 0% of the time, Pallas kernels for 24%

profile of v5, /device:TPU:17, one launch (start us, length us, event | category | flops | bytes accessed | tf_op | source)
XLA Modules:
  0.0 37.3 jit_solution(584251652309084040)
XLA Ops:
  0.0 1.1 %pad_maximum_fusion.winds.joined = f32[36,2,1152]{2,1,0:T(2,128)S(1)} fusion(f32[18,2,1152]{2,1,0:T(2,128)} %bitcast.13, f32[18,2,1152]{2,1,0:T(2,128)} %bitcast.14), kind=kLoop, calls=%fused_computation | loop fusion | flops 82944 | bytes 663552 | tf_op jit(solution)/shard_map/concatenate | solution.py:421
  1.1 0.0 copy-start
  1.2 1.3 %copy-done = f32[8,2,18,1152]{3,1,2,0:T(2,128)S(1)} copy-done((f32[8,2,18,1152]{3,1,2,0:T(2,128)S(1)}, f32[8,2,18,1152]{3,1,2,0:T(2,128)}, u32[]{:S(2)}) %copy-start) | copy-done | bytes 1327128
  2.5 0.0 copy-start.1
  2.5 0.0 copy-start.2
  2.5 0.3 shard_map.64
  2.7 1.4 %collective-permute-start.2 = (f32[2,7,8,1152]{3,2,1,0:T(8,128)S(1)}, f32[2,7,8,1152]{3,2,1,0:T(8,128)S(1)}, u32[]{:S(2)}, u32[]{:S(2)}) collective-permute-start(f32[2,7,8,1152]{3,2,1,0:T(8,128)S(1)} %get-tuple-element.27), channel_id=1, source_target_pairs={{0,4},{4,0},{8,12},{12,8},{1,5},{5,1},{9,13},{13,9},{2,6},{6,2},{1... | collective-permute-start | bytes 1548296 | tf_op jit(solution)/shard_map/ppermute | solution.py:429
  4.1 1.9 %collective-permute-start.3 = (f32[2,7,8,1152]{3,2,1,0:T(8,128)S(1)}, f32[2,7,8,1152]{3,2,1,0:T(8,128)S(1)}, u32[]{:S(2)}, u32[]{:S(2)}) collective-permute-start(f32[2,7,8,1152]{3,2,1,0:T(8,128)S(1)} %get-tuple-element.28), channel_id=1, source_target_pairs={{0,0},{4,8},{8,4},{12,12},{1,1},{5,9},{9,5},{13,13},{2,2},{6,10},{... | collective-permute-start | bytes 1548296 | tf_op jit(solution)/shard_map/ppermute | solution.py:429
  6.0 3.6 %shard_map.65 = (f32[2,1,14,8,128]{4,3,2,1,0:T(8,128)S(1)}, f32[2,1,14,8,128]{4,3,2,1,0:T(8,128)S(1)}, f32[2,1,14,8,128]{4,3,2,1,0:T(8,128)S(1)}, f32[2,1,14,8,1...) custom-call(f32[2,18,8,1152]{3,2,1,0:T(8,128)S(1)} %get-tuple-elemen, ...), custom_call_target="tpu_custom_call" | custom-call | flops 16588800 | bytes 2654208 | tf_op jit(solution)/shard_map/pallas_call | solution.py:386
  9.7 2.1 %collective-permute-start = (f32[2,1,14,8,128]{4,3,2,1,0:T(8,128)S(1)}, f32[2,1,14,8,128]{4,3,2,1,0:T(8,128)S(1)}, u32[]{:S(2)}, u32[]{:S(2)}) collective-permute-start(f32[2,1,14,8,128]{4,3,2,1,0:T(8,128)S(1)} %get-tuple-element.25), channel_id=1, source_target_pairs={{0,3},{1,2},{2,1},{3,0},{4,7},{5,6},{6,5},{7,4},{8,11},{9,10},{10,... | collective-permute-start | bytes 344072 | tf_op jit(solution)/shard_map/ppermute | solution.py:407
  11.8 0.3 collective-permute-start.1
  12.0 0.0 copy-done.1
  12.0 0.0 copy-done.2
  12.0 0.2 shard_map.66.refs_1_.refs_11_
  12.2 3.2 %collective-permute-done.2.first_round = f32[2,7,8,1152]{3,2,1,0:T(8,128)S(1)} collective-permute-done((f32[2,7,8,1152]{3,2,1,0:T(8,128)S(1)}, f32[2,7,8,1152]{3,2,1,0:T(8,128)S(1)}, u32[]{:S(2)}, u32[]{:S(2)}) %collective-permute-start.2) | collective-permute-done | bytes 516128 | tf_op jit(solution)/shard_map/ppermute | solution.py:429
  15.4 2.9 %collective-permute-done.3.second_round = f32[2,7,8,1152]{3,2,1,0:T(8,128)S(1)} collective-permute-done((f32[2,7,8,1152]{3,2,1,0:T(8,128)S(1)}, f32[2,7,8,1152]{3,2,1,0:T(8,128)S(1)}, u32[]{:S(2)}, u32[]{:S(2)}) %collective-permute-start.3) | collective-permute-done | bytes 516128 | tf_op jit(solution)/shard_map/ppermute | solution.py:429
  18.3 2.5 %shard_map.67 = (f32[2,1,14,8,128]{4,3,2,1,0:T(8,128)S(1)}, f32[2,2,14,8,128]{4,3,2,1,0:T(8,128)S(1)}, f32[2,1,14,8,128]{4,3,2,1,0:T(8,128)S(1)}, f32[2,1,14,8,128]{4,3,2,1,0:T(8,128)S(1)}) custom-call(f32[2,18,8,1152]{3,2,1,0:T(8,128)S(1)} %get-tuple-element.23.state, f32[2,7,8,1152]{3,2,1,0:T(8,128)S(1)} %collective-permute-done.2.first_round, ...), custom_call_target="tpu_custom_call" | custom-call | flops 9953280 | bytes 1327104 | tf_op jit(solution)/shard_map/pallas_call | solution.py:386
  20.8 3.0 %collective-permute-start.4 = (f32[2,1,14,8,128]{4,3,2,1,0:T(8,128)S(1)}, f32[2,1,14,8,128]{4,3,2,1,0:T(8,128)S(1)}, u32[]{:S(2)}, u32[]{:S(2)}) collective-permute-start(f32[2,1,14,8,128]{4,3,2,1,0:T(8,128)S(1)} %get-tuple-element.34), channel_id=1, source_target_pairs={{0,3},{1,2},{2,1},{3,0},{4,7},{5,6},{6,5},{7,4},{8,11},{9,10},{10,... | collective-permute-start | bytes 344072 | tf_op jit(solution)/shard_map/ppermute | solution.py:407
  23.9 0.0 collective-permute-start.6
  23.9 0.0 copy-start.3
  23.9 0.3 collective-permute-start.5
  24.1 0.0 collective-permute-done.refs_0_.refs_1_
  24.1 0.0 collective-permute-done.1.refs_1_.refs_2_
  24.1 2.6 %shard_map.68 = (f32[2,1,14,8,128]{4,3,2,1,0:T(8,128)S(1)}, f32[2,1,14,8,128]{4,3,2,1,0:T(8,128)S(1)}, f32[2,1,14,8,128]{4,3,2,1,0:T(8,128)S(1)}, f32[2,1,14,8,128]{4,3,2,1,0:T(8,128)S(1)}) custom-call(f32[2,18,8,1152]{3,2,1,0:T(8,128)S(1)} %get-tuple-element.23.state, f32[2,7,8,1152]{3,2,1,0:T(8,128)S(1)} %collective-permute-done.2.first_round, ...), custom_call_target="tpu_custom_call" | custom-call | flops 9953280 | bytes 1327104 | tf_op jit(solution)/shard_map/pallas_call | solution.py:386
  26.7 1.9 %collective-permute-start.7 = (f32[2,1,14,8,128]{4,3,2,1,0:T(8,128)S(1)}, f32[2,1,14,8,128]{4,3,2,1,0:T(8,128)S(1)}, u32[]{:S(2)}, u32[]{:S(2)}) collective-permute-start(f32[2,1,14,8,128]{4,3,2,1,0:T(8,128)S(1)} %get-tuple-element.38), channel_id=1, source_target_pairs={{0,3},{1,2},{2,1},{3,0},{4,7},{5,6},{6,5},{7,4},{8,11},{9,10},{10,... | collective-permute-start | bytes 344072 | tf_op jit(solution)/shard_map/ppermute | solution.py:407
  28.6 0.3 collective-permute-start.8
  28.9 0.0 collective-permute-done.4.refs_4_
  28.9 0.2 collective-permute-start.9
  29.1 1.1 %collective-permute-done.5.refs_5_ = f32[2,1,14,8,128]{4,3,2,1,0:T(8,128)S(1)} collective-permute-done((f32[2,1,14,8,128]{4,3,2,1,0:T(8,128)S(1)}, f32[2,1,14,8,128]{4,3,2,1,0:T(8,128)S(1)}, u32[]{:S(2)}, u32[]{:S(2)}) %collective-permute-start.5) | collective-permute-done | bytes 114720 | tf_op jit(solution)/shard_map/ppermute | solution.py:407
  30.2 2.5 %collective-permute-done.7.refs_8_ = f32[2,1,14,8,128]{4,3,2,1,0:T(8,128)S(1)} collective-permute-done((f32[2,1,14,8,128]{4,3,2,1,0:T(8,128)S(1)}, f32[2,1,14,8,128]{4,3,2,1,0:T(8,128)S(1)}, u32[]{:S(2)}, u32[]{:S(2)}) %collective-permute-start.7) | collective-permute-done | bytes 114720 | tf_op jit(solution)/shard_map/ppermute | solution.py:407
  32.7 2.5 %collective-permute-done.8.refs_9_ = f32[2,1,14,8,128]{4,3,2,1,0:T(8,128)S(1)} collective-permute-done((f32[2,1,14,8,128]{4,3,2,1,0:T(8,128)S(1)}, f32[2,1,14,8,128]{4,3,2,1,0:T(8,128)S(1)}, u32[]{:S(2)}, u32[]{:S(2)}) %collective-permute-start.8) | collective-permute-done | bytes 114720 | tf_op jit(solution)/shard_map/ppermute | solution.py:407
  35.1 0.0 collective-permute-done.9.refs_10_
  35.1 0.0 collective-permute-done.6.refs_6_
  35.1 0.0 copy-done.3
  35.1 2.2 %shard_map.69 = f32[6,18,8,288]{3,2,1,0:T(8,128)} custom-call(s32[4]{0:T(128)S(1)} %copy-done.3, f32[2,1,14,8,128]{4,3,2,1,0:T(8,128)S(1)} %get-tuple-element.24.refs_0_, f32[2,1,14,8,128]{4,3,2,1,0:T(8,128)S(1)} %collective-permute-done.refs_0_.refs_1_, f32[2,1,14,8,128]{4,3,2,1,0:T(8,128)S(1)} %collective-permute-done.1.refs_1_.refs_2_, ...), custom_call_target="tpu_custom_call" | custom-call | flops 7464960 | bytes 1990656 | tf_op jit(solution)/shard_map/pallas_call | solution.py:386
Async XLA Ops:
  1.1 1.3 %copy-start = (f32[8,2,18,1152]{3,1,2,0:T(2,128)S(1)}, f32[8,2,18,1152]{3,1,2,0:T(2,128)}, u32[]{:S(2)}) copy-start(f32[8,2,18,1152]{3,1,2,0:T(2,128)} %param.6) | copy-start | bytes 3981316
  2.5 9.6 %copy-start.1 = (f32[4,6,18,288]{3,0,2,1:T(4,128)S(1)}, f32[4,6,18,288]{3,0,2,1:T(4,128)}, u32[]{:S(2)}) copy-start(f32[4,6,18,288]{3,0,2,1:T(4,128)} %param.11) | copy-start | bytes 1492996
  2.5 9.6 %copy-start.2 = (s32[6,18,288]{2,1,0:T(8,128)S(1)}, s32[6,18,288]{2,1,0:T(8,128)}, u32[]{:S(2)}) copy-start(s32[6,18,288]{2,1,0:T(8,128)} %source.1) | copy-start | bytes 373252
  2.7 12.7 %collective-permute-start.2 = (f32[2,7,8,1152]{3,2,1,0:T(8,128)S(1)}, f32[2,7,8,1152]{3,2,1,0:T(8,128)S(1)}, u32[]{:S(2)}, u32[]{:S(2)}) collective-permute-start(f32[2,7,8,1152]{3,2,1,0:T(8,128)S(1)} %get-tuple-element.27), channel_id=1, source_target_pairs={{0,4},{4,0},{8,12},{12,8},{1,5},{5,1},{9,13},{13,9},{2,6},{6,2},{1... | collective-permute-start | bytes 1548296 | tf_op jit(solution)/shard_map/ppermute | solution.py:429
  4.1 14.2 %collective-permute-start.3 = (f32[2,7,8,1152]{3,2,1,0:T(8,128)S(1)}, f32[2,7,8,1152]{3,2,1,0:T(8,128)S(1)}, u32[]{:S(2)}, u32[]{:S(2)}) collective-permute-start(f32[2,7,8,1152]{3,2,1,0:T(8,128)S(1)} %get-tuple-element.28), channel_id=1, source_target_pairs={{0,0},{4,8},{8,4},{12,12},{1,1},{5,9},{9,5},{13,13},{2,2},{6,10},{... | collective-permute-start | bytes 1548296 | tf_op jit(solution)/shard_map/ppermute | solution.py:429
  9.7 14.5 %collective-permute-start = (f32[2,1,14,8,128]{4,3,2,1,0:T(8,128)S(1)}, f32[2,1,14,8,128]{4,3,2,1,0:T(8,128)S(1)}, u32[]{:S(2)}, u32[]{:S(2)}) collective-permute-start(f32[2,1,14,8,128]{4,3,2,1,0:T(8,128)S(1)} %get-tuple-element.25), channel_id=1, source_target_pairs={{0,3},{1,2},{2,1},{3,0},{4,7},{5,6},{6,5},{7,4},{8,11},{9,10},{10,... | collective-permute-start | bytes 344072 | tf_op jit(solution)/shard_map/ppermute | solution.py:407
  11.8 12.3 %collective-permute-start.1 = (f32[2,1,14,8,128]{4,3,2,1,0:T(8,128)S(1)}, f32[2,1,14,8,128]{4,3,2,1,0:T(8,128)S(1)}, u32[]{:S(2)}, u32[]{:S(2)}) collective-permute-start(f32[2,1,14,8,128]{4,3,2,1,0:T(8,128)S(1)} %get-tuple-element.26), channel_id=1, source_target_pairs={{0,2},{1,3},{2,0},{3,1},{4,6},{5,7},{6,4},{7,5},{8,10},{9,11},{10,... | collective-permute-start | bytes 344072 | tf_op jit(solution)/shard_map/ppermute | solution.py:407
  20.8 8.1 %collective-permute-start.4 = (f32[2,1,14,8,128]{4,3,2,1,0:T(8,128)S(1)}, f32[2,1,14,8,128]{4,3,2,1,0:T(8,128)S(1)}, u32[]{:S(2)}, u32[]{:S(2)}) collective-permute-start(f32[2,1,14,8,128]{4,3,2,1,0:T(8,128)S(1)} %get-tuple-element.34), channel_id=1, source_target_pairs={{0,3},{1,2},{2,1},{3,0},{4,7},{5,6},{6,5},{7,4},{8,11},{9,10},{10,... | collective-permute-start | bytes 344072 | tf_op jit(solution)/shard_map/ppermute | solution.py:407
  23.9 11.3 %collective-permute-start.6 = (f32[2,2,14,8,128]{4,3,2,1,0:T(8,128)S(1)}, f32[2,2,14,8,128]{4,3,2,1,0:T(8,128)S(1)}, u32[]{:S(2)}, u32[]{:S(2)}) collective-permute-start(f32[2,2,14,8,128]{4,3,2,1,0:T(8,128)S(1)} %get-tuple-element.36), channel_id=1, source_target_pairs={{0,1},{1,0},{2,3},{3,2},{4,5},{5,4},{6,7},{7,6},{8,9},{9,8},{10,11... | collective-permute-start | bytes 688136 | tf_op jit(solution)/shard_map/ppermute | solution.py:407
  23.9 11.3 %copy-start.3 = (s32[4]{0:T(128)S(1)}, s32[4]{0:T(128)}, u32[]{:S(2)}) copy-start(s32[4]{0:T(128)} %counts.1) | copy-start | bytes 52
  23.9 6.4 %collective-permute-start.5 = (f32[2,1,14,8,128]{4,3,2,1,0:T(8,128)S(1)}, f32[2,1,14,8,128]{4,3,2,1,0:T(8,128)S(1)}, u32[]{:S(2)}, u32[]{:S(2)}) collective-permute-start(f32[2,1,14,8,128]{4,3,2,1,0:T(8,128)S(1)} %get-tuple-element.35), channel_id=1, source_target_pairs={{0,2},{1,3},{2,0},{3,1},{4,6},{5,7},{6,4},{7,5},{8,10},{9,11},{10,... | collective-permute-start | bytes 344072 | tf_op jit(solution)/shard_map/ppermute | solution.py:407
  26.7 6.0 %collective-permute-start.7 = (f32[2,1,14,8,128]{4,3,2,1,0:T(8,128)S(1)}, f32[2,1,14,8,128]{4,3,2,1,0:T(8,128)S(1)}, u32[]{:S(2)}, u32[]{:S(2)}) collective-permute-start(f32[2,1,14,8,128]{4,3,2,1,0:T(8,128)S(1)} %get-tuple-element.38), channel_id=1, source_target_pairs={{0,3},{1,2},{2,1},{3,0},{4,7},{5,6},{6,5},{7,4},{8,11},{9,10},{10,... | collective-permute-start | bytes 344072 | tf_op jit(solution)/shard_map/ppermute | solution.py:407
  28.6 6.5 %collective-permute-start.8 = (f32[2,1,14,8,128]{4,3,2,1,0:T(8,128)S(1)}, f32[2,1,14,8,128]{4,3,2,1,0:T(8,128)S(1)}, u32[]{:S(2)}, u32[]{:S(2)}) collective-permute-start(f32[2,1,14,8,128]{4,3,2,1,0:T(8,128)S(1)} %get-tuple-element.39), channel_id=1, source_target_pairs={{0,2},{1,3},{2,0},{3,1},{4,6},{5,7},{6,4},{7,5},{8,10},{9,11},{10,... | collective-permute-start | bytes 344072 | tf_op jit(solution)/shard_map/ppermute | solution.py:407
  28.9 6.2 %collective-permute-start.9 = (f32[2,1,14,8,128]{4,3,2,1,0:T(8,128)S(1)}, f32[2,1,14,8,128]{4,3,2,1,0:T(8,128)S(1)}, u32[]{:S(2)}, u32[]{:S(2)}) collective-permute-start(f32[2,1,14,8,128]{4,3,2,1,0:T(8,128)S(1)} %get-tuple-element.40), channel_id=1, source_target_pairs={{0,1},{1,0},{2,3},{3,2},{4,5},{5,4},{6,7},{7,6},{8,9},{9,8},{10,11... | collective-permute-start | bytes 344072 | tf_op jit(solution)/shard_map/ppermute | solution.py:407

commit v6 on v5

--- a/solution.py
+++ b/solution.py
@@ -53,7 +53,7 @@
     return width, mains, tail, per, BLOCK * mains + tails
 
 
-def prep_kernel(rows, tracers, winds, state, first_round, second_round):
+def prep_kernel(rows, tracers, winds, state, *sent):
     levels, nlon = state.shape[0], state.shape[3]
     nj = nlon // LANES
     row_stride = nj * levels
@@ -71,18 +71,18 @@
         return 0
 
     lax.fori_loop(0, rows, body, 0)
-    for target, north, scale in ((first_round, even, None), (second_round, jnp.logical_not(even), keep)):
-        scaled = (lambda v: v) if scale is None else (lambda v: v * scale)
-        row_t = jnp.where(north, rows - HALO, 0)
-        row_x = jnp.where(north, rows - REACH, 0)
-        row_y = jnp.where(north, rows - REACH - 1, 0)
-        for level in range(levels):
+    for level in range(levels):
+        for target, north, scale in ((sent[2 * level], even, None), (sent[2 * level + 1], jnp.logical_not(even), keep)):
+            scaled = (lambda v: v) if scale is None else (lambda v: v * scale)
+            row_t = jnp.where(north, rows - HALO, 0)
+            row_x = jnp.where(north, rows - REACH, 0)
+            row_y = jnp.where(north, rows - REACH - 1, 0)
             for row in range(HALO):
-                target[level, row] = scaled(state[level, row_t + row])
+                target[row] = scaled(state[level, row_t + row])
             for q in range(REACH):
-                target[level, HALO, q:q + 1, :] = scaled(winds[row_x + q, level:level + 1, :])
+                target[HALO, q:q + 1, :] = scaled(winds[row_x + q, level:level + 1, :])
             for q in range(REACH + 1):
-                target[level, HALO, REACH + q:REACH + q + 1, :] = scaled(winds[rows + row_y + q, level:level + 1, :])
+                target[HALO, REACH + q:REACH + q + 1, :] = scaled(winds[rows + row_y + q, level:level + 1, :])
 
 
 def lat_pass(levels, nj, ranges, cell, coef, store):
@@ -156,7 +156,7 @@
             finish(g - 2, [update((g - 2) * BLOCK + q) for q in range(BLOCK)])
 
 
-def pack_block(block, packed, level, number, count, lane):
+def pack_block(block, packed, unit, count, lane):
     me = lax.axis_index("lev")
     nlon = len(block[0]) * LANES
     width, mains, tail, per, size = packed_sizes(nlon, count)
@@ -167,7 +167,7 @@
                       for m in range(mains + (1 if off else 0))]
             for m in range(mains):
                 whole = jnp.where(lane < LANES - off, turned[m], turned[m + 1]) if off else turned[m]
-                packed[d ^ me, level, number, q * mains + m] = whole
+                packed[d ^ me, unit, q * mains + m] = whole
         if tail:
             for g in range(-(-BLOCK // per)):
                 total = None
@@ -176,15 +176,13 @@
                     source = block[g * per + place][j0 + mains]
                     moved = pltpu.roll(source, shift, 1) if shift else source
                     total = moved if total is None else jnp.where(lane < place * tail, total, moved)
-                packed[d ^ me, level, number, BLOCK * mains + g] = total
-
-
-def copy_blocks(source, target, start=0):
-    levels, blocks, size = source.shape[:3]
-    for level in range(levels):
-        for number in range(blocks):
-            for i in range(size):
-                target[level, start + number, i] = source[level, number, i]
+                packed[d ^ me, unit, BLOCK * mains + g] = total
+
+
+def copy_units(source, target, start=0):
+    for unit in range(source.shape[0]):
+        for i in range(source.shape[1]):
+            target[start + unit, i] = source[unit, i]
 
 
 def own_coefficients(rows, joined, winds, cx, cy):
@@ -232,82 +230,83 @@
     work_last = [(level, row, row - REACH) for level in range(levels) for row in range(HALO, rows - HALO)]
 
     def send(group, done):
-        level, row, _ = work_last[group * BLOCK]
-        pack_block(done, packed, level, (row - HALO) // BLOCK, count, lane)
+        pack_block(done, packed, group, count, lane)
 
     lon_pass(work_last, swept, coef_x, inter, west, flux, lane, send)
     for k in range(count):
-        copy_blocks(packed.at[k], outs[k])
-
-
-def edge_kernel(count, rows, south, joint, state, first_round, second_round, first, cx, cy, *refs):
+        copy_units(packed.at[k], outs[k])
+
+
+def edge_kernel(count, rows, slot, joint, state, first_round, second_round, first, cx, cy, *refs):
     others = refs[:joint]
     outs, (packed, beyond, swept, edge, inter, west, flux) = refs[-7 - count:-7], refs[-7:]
-    odd = lax.axis_index("lat") % 2 == 1
-    from_first = odd if south else jnp.logical_not(odd)
-
-    def halo(*at):
-        return jnp.where(from_first, first_round[at], second_round[at])
-
-    levels, nlon = state.shape[0], state.shape[3]
+    nlon = state.shape[3]
     nj = nlon // LANES
     lane = lane_ids()
-    for level in range(levels):
+    odd = lax.axis_index("lat") % 2 == 1
+
+    def halo(south, *at):
+        one, two = first_round[at], second_round[at]
+        return jnp.where(odd, one, two) if south else jnp.where(odd, two, one)
+
+    for end, south in enumerate((True, False)):
         for j in range(nj):
-            parts = coefficients(halo(level, HALO, slice(None), tile(j)))
+            parts = coefficients(halo(south, HALO, slice(None), tile(j)))
             for p in range(3):
-                beyond[p, level, :, tile(j)] = parts[p]
-
-    def coef_x(i, level, r, lanes):
+                beyond[p, end, :, tile(j)] = parts[p]
+
+    def coef_x(i, _, r, lanes):
         if 0 <= r < rows:
-            return cx[i, level, r:r + 1, lanes]
-        at = r + REACH if south else r - rows
-        return beyond[i, level, at:at + 1, lanes]
-
-    def coef_y(i, level, f, lanes):
+            return cx[i, slot, r:r + 1, lanes]
+        end, at = (0, r + REACH) if r < 0 else (1, r - rows)
+        return beyond[i, end, at:at + 1, lanes]
+
+    def coef_y(i, _, f, lanes):
         if 0 <= f < rows:
-            return cy[i, level, f:f + 1, lanes]
-        at = f + 2 * REACH + 1 if south else f - rows + REACH
-        return beyond[i, level, at:at + 1, lanes]
-
-    def cell(level, r, lanes):
+            return cy[i, slot, f:f + 1, lanes]
+        end, at = (0, f + 2 * REACH + 1) if f < 0 else (1, f - rows + REACH)
+        return beyond[i, end, at:at + 1, lanes]
+
+    def cell(_, r, lanes):
         if 0 <= r < rows:
-            return state[level, r, :, lanes]
-        return halo(level, r + HALO if south else r - rows, slice(None), lanes)
-
-    base = -REACH if south else rows - REACH
-    base_last = 0 if south else rows - HALO
-
-    def cell_first(level, r, lanes):
+            return state[slot, r, :, lanes]
+        return halo(r < 0, r + HALO if r < 0 else r - rows, slice(None), lanes)
+
+    ends = [(-REACH, REACH), (rows - REACH, rows + REACH)]
+    ends_last = [(0, HALO), (rows - HALO, rows)]
+
+    def place(row, ranges):
+        (a, b), (c, _) = ranges
+        return row - a if row < b else row - c + BLOCK
+
+    def cell_first(_, r, lanes):
         if REACH <= r < rows - REACH:
-            return first[level, r - REACH, :, lanes]
-        return edge[level, r - base, :, lanes]
-
-    def put(level, row, lanes, value):
-        swept[level, row - base, :, lanes] = value
-
-    def put_last(level, row, lanes, value):
-        swept[level, row - base_last, :, lanes] = value
-
-    def listed(start):
-        return [(level, start + q, q) for level in range(levels) for q in range(BLOCK)]
+            return first[slot, r - REACH, :, lanes]
+        return edge[0, place(r, ends), :, lanes]
+
+    def put(_, row, lanes, value):
+        swept[0, place(row, ends), :, lanes] = value
+
+    def put_last(_, row, lanes, value):
+        swept[0, place(row, ends_last), :, lanes] = value
+
+    def listed(ranges):
+        return [(0, row, place(row, ranges)) for a, b in ranges for row in range(a, b)]
 
     def keep_edge(group, done):
-        put_rows(edge, group, 0, done)
+        put_rows(edge, 0, group * BLOCK, done)
 
     def send(group, done):
-        pack_block(done, packed, group, 0, count, lane)
-
-    lat_pass(levels, nj, [(base, base + BLOCK)], cell, coef_y, put)
-    lon_pass(listed(base), swept, coef_x, inter, west, flux, lane, keep_edge)
-    lat_pass(levels, nj, [(base_last, base_last + BLOCK)], cell_first, coef_y, put_last)
-    lon_pass(listed(base_last), swept, coef_x, inter, west, flux, lane, send)
+        pack_block(done, packed, group, count, lane)
+
+    lat_pass(1, nj, ends, cell, coef_y, put)
+    lon_pass(listed(ends), swept, coef_x, inter, west, flux, lane, keep_edge)
+    lat_pass(1, nj, ends_last, cell_first, coef_y, put_last)
+    lon_pass(listed(ends_last), swept, coef_x, inter, west, flux, lane, send)
     for k in range(count):
-        copy_blocks(packed.at[k], outs[k])
-    start = 1
-    for other in others:
-        copy_blocks(other, outs[1], start)
-        start += other.shape[1]
+        copy_units(packed.at[k], outs[k])
+    for other, out in zip(others, outs):
+        copy_units(other, out, packed.shape[1])
 
 
 def weights_kernel(weights, source, out):
@@ -325,12 +324,21 @@
             out[k, row] = total
 
 
-def remap_kernel(count, depth, plan, counts, *refs):
-    chunks, (weights, out, columns) = refs[:len(plan)], refs[len(plan):]
+def remap_kernel(count, depth, plan, numbers, counts, *refs):
+    chunks, (weights, *ready, out, columns) = refs[:len(plan)], refs[len(plan):]
     me = lax.axis_index("lev")
-    for (k, start), chunk in zip(plan, chunks):
-        copy_blocks(chunk, columns.at[pl.ds((me ^ k) * depth, depth)], start)
-    targets, rows, _, width = out.shape
+    for (k, units), chunk in zip(plan, chunks):
+        for unit, (slot, number) in enumerate(units):
+            if number in numbers:
+                for i in range(chunk.shape[1]):
+                    columns[(me ^ k) * depth + slot, number, i] = chunk[unit, i]
+    first_out = 0 if ready else numbers[0]
+    if ready:
+        copied = [n for n in range(out.shape[1] // BLOCK) if n not in numbers]
+        for k in range(out.shape[0]):
+            for row in range(len(copied) * BLOCK):
+                out[k, copied[0] * BLOCK + row] = ready[0][k, row]
+    targets, _, _, width = out.shape
     _, mains, tail, per, _ = packed_sizes(width * count, count)
     slots = []
     for level in range(targets):
@@ -363,9 +371,9 @@
                         w = jnp.broadcast_to(weights[k, row, j:j + 1, lanes], (SUB, wide))
                         term = w * values[level]
                         total = term if total is None else total + term
-                    out[k, row, :, lanes] = total
-
-    for number in range(rows // BLOCK):
+                    out[k, row - first_out * BLOCK, :, lanes] = total
+
+    for number in numbers:
         block(number)
 
 
@@ -402,11 +410,6 @@
     return jax.ShapeDtypeStruct(shape, jnp.float32)
 
 
-def swapped(value, k):
-    count = lax.axis_size("lev")
-    return lax.ppermute(value, "lev", [(i, i ^ k) for i in range(count)])
-
-
 def shards(tracers, wind_x, wind_y, level_counts, source_level, remap_weight):
     count = lax.axis_size("lev")
     bands = lax.axis_size("lat")
@@ -415,25 +418,24 @@
     size = packed_sizes(nlon, count)[-1]
     blocks = rows // BLOCK
     inner = (rows - 2 * HALO) // BLOCK
-    partners = range(count - 1, 1, -1)
 
     raw = tiles_of(jnp.transpose(tracers, (0, 2, 1, 3)))
     joined = jnp.concatenate([jnp.transpose(wind_x, (1, 0, 2)), jnp.transpose(wind_y, (1, 0, 2))], axis=0)
-    halo = f32(depth, HALO + 1, number, nlon)
-    state, *rounds = call(
+    halo = f32(HALO + 1, number, nlon)
+    state, *sent = call(
         functools.partial(prep_kernel, rows),
-        (f32(depth, rows, number, nlon), halo, halo), (raw, joined),
-        cost=cost(1, 8 * tracers.size))
+        [f32(depth, rows, number, nlon)] + [halo] * (2 * depth), (raw, joined),
+        cost=cost(1, 1))
     swaps = [[(i, i ^ 1) for i in range(bands)],
              [(i, i if i in (0, bands - 1) else ((i - 1) ^ 1) + 1) for i in range(bands)]]
-    rounds = [lax.ppermute(sent, "lat", pairs) for sent, pairs in zip(rounds, swaps)]
+    rounds = [lax.ppermute(buffer, "lat", swaps[i % 2]) for i, buffer in enumerate(sent)]
     taps = call(
         weights_kernel, f32(targets, rows, SUB, width),
         (jnp.transpose(remap_weight, (1, 2, 0, 3)), source_level),
-        cost=cost(20 * remap_weight.size, 16 * remap_weight.size))
-
-    def box(n, *lead):
-        return lead + (depth, n, size, SUB, LANES)
+        cost=cost(1, 1))
+
+    def box(units, *lead):
+        return lead + (units, size, SUB, LANES)
 
     def vmem(*shape):
         return pltpu.VMEM(shape, jnp.float32)
@@ -444,46 +446,43 @@
     stage = vmem(depth * (rows - 2 * REACH), number, nlon)
     result = call(
         functools.partial(interior_kernel, count, rows),
-        [f32(*box(inner))] * count + [f32(depth, rows - 2 * REACH, number, nlon), coef, coef],
-        (state, joined), scratch=[vmem(*box(inner, count)), vmem(2, depth, held, nlon), swept, stage, stage, stage],
-        cost=cost(50 * tracers.size, 8 * tracers.size))
+        [f32(*box(depth * inner))] * count + [f32(depth, rows - 2 * REACH, number, nlon), coef, coef],
+        (state, joined), scratch=[vmem(*box(depth * inner, count)), vmem(2, depth, held, nlon), swept, stage, stage, stage],
+        cost=cost(1, 1))
     middle, (first, cx, cy) = result[:count], result[count:]
     plan, chunks = [], []
-
-    def received(k, start, chunk):
-        plan.append((k, start))
-        chunks.append(chunk)
-        return chunk
-
-    def send(sent, start):
-        received(0, start, sent[0])
-        return [received(k, start, swapped(sent[k], k)) for k in partners]
-
-    swept = vmem(depth, BLOCK, number, nlon)
-    stage = vmem(depth * BLOCK, number, nlon)
-
-    def edge(south, joint, after):
-        args = (state, *rounds, first, cx, cy, *joint, *after)
+    swept = vmem(1, 2 * HALO, number, nlon)
+    stage = vmem(2 * HALO, number, nlon)
+
+    def edge(slot, joint, after):
+        args = (state, *rounds[2 * slot:2 * slot + 2], first, cx, cy, *joint, after)
+        units = 2 + (joint[0].shape[0] if joint else 0)
         return call(
-            functools.partial(edge_kernel, count, rows, south, len(joint)),
-            [f32(*box(1 + sum(c.shape[1] for c in joint) if k == 1 else 1)) for k in range(count)], args,
-            specs=[VMEM] * (len(args) - len(after)) + [ANY] * len(after),
-            scratch=[vmem(*box(1, count)), vmem(3, depth, SUB, nlon), swept, swept, stage, stage, stage],
-            cost=cost(30 * tracers.size, 4 * tracers.size))
-
-    arrived = send(middle, 1)
-    south = edge(True, (middle[1],), (taps,))
-    send(south, 0)
-    received(1, 0, swapped(south[1], 1))
-    north = edge(False, (), arrived)
-    send(north, blocks - 1)
-    received(1, blocks - 1, swapped(north[1], 1))
-    out = call(
-        functools.partial(remap_kernel, count, depth, tuple(plan)),
-        f32(targets, rows, number, width), (level_counts, *chunks, taps),
-        specs=[SMEM] + [VMEM] * (len(chunks) + 1),
-        scratch=[vmem(count * depth, blocks, size, SUB, LANES)],
-        cost=cost(60 * remap_weight.size, 16 * remap_weight.size))
+            functools.partial(edge_kernel, count, rows, slot, len(joint)),
+            [f32(*box(units))] * count, args,
+            specs=[VMEM] * (len(args) - 1) + [ANY],
+            scratch=[vmem(*box(2, count)), vmem(3, 2, SUB, nlon), swept, swept, stage, stage, stage],
+            cost=cost(60 * tracers.size, 8 * tracers.size))
+
+    after, joint, joint_units = taps, middle, tuple((slot, 1 + b) for slot in range(depth) for b in range(inner))
+    for slot in range(depth):
+        done = edge(slot, joint, after)
+        plan += [(k, ((slot, 0), (slot, blocks - 1)) + joint_units) for k in range(count)]
+        chunks += [done[0]] + [None] * (count - 1)
+        for k in range(count - 1, 0, -1):
+            chunks[k - count] = lax.ppermute(done[k], "lev", [(i, i ^ k) for i in range(count)])
+        after, joint, joint_units = done[0], (), ()
+    def remap(part, numbers, height, ready):
+        args = (level_counts, *chunks[:part], taps, *ready)
+        return call(
+            functools.partial(remap_kernel, count, depth, tuple(plan[:part]), numbers),
+            f32(targets, height, number, width), args,
+            specs=[SMEM] + [VMEM] * (len(args) - 1),
+            scratch=[vmem(count * depth, blocks, size, SUB, LANES)],
+            cost=cost(1, 1))
+
+    middle_rows = remap(count, tuple(range(1, blocks - 1)), inner * BLOCK, ())
+    out = remap(len(chunks), (0, blocks - 1), rows, (middle_rows,))
     return jnp.transpose(out, (2, 0, 1, 3))
 
 

time: 37.5 us -> 38.1 us (1.016)
  the two profiles are of different devices: /device:TPU:17 before, /device:TPU:0 now
where the time goes in v6:
time: 38.1 us; the launch traced here: 37.8 us
  starting transfers between devices  12.7 us (33%)
  Pallas kernels  12.1 us (32%)
  waiting for transfers between devices  10.3 us (27%)
  local copies, waits for them, and re-layouts  1.33 us (3%)
  other arithmetic  1.14 us (3%)
    pallas_call x7, Pallas kernels, call(): pl.pallas_call(kernel, out_shape=outs, in_specs=specs or [VMEM] * len(arg...  12.1 us
    ppermute x6, waiting for transfers between devices, shards(): lax.ppermute(done[k], 'lev', [(i, i ^ k) for i in range(count)])  10.3 us
    ppermute x4, starting transfers between devices, shards(): lax.ppermute(buffer, 'lat', swaps[i % 2])  8.87 us
    ppermute x6, starting transfers between devices, shards(): lax.ppermute(done[k], 'lev', [(i, i ^ k) for i in range(count)])  3.87 us
    unnamed x8, local copies, waits for them, and re-layouts  1.33 us
    concatenate x1, other arithmetic, shards(): jnp.concatenate([jnp.transpose(wind_x, (1, 0, 2)), jnp.transpose(wind_y,...  1.14 us
  transfers between devices with their start and end apart: 10, of which 4 were waited for; matrix products, arithmetic and copies ran while one was open for 0% of the time, Pallas kernels for 26%

profile of v6, /device:TPU:0, one launch (start us, length us, event | category | flops | bytes accessed | tf_op | source)
XLA Modules:
  0.0 37.8 jit_solution(9269985505454109032)
XLA Ops:
  0.0 1.1 %pad_maximum_fusion.winds.joined = f32[36,2,1152]{2,1,0:T(2,128)S(1)} fusion(f32[18,2,1152]{2,1,0:T(2,128)} %bitcast.13, f32[18,2,1152]{2,1,0:T(2,128)} %bitcast.14), kind=kLoop, calls=%fused_computation | loop fusion | flops 82944 | bytes 663552 | tf_op jit(solution)/shard_map/concatenate | solution.py:423
  1.1 0.0 copy-start
  1.2 1.3 %copy-done = f32[8,2,18,1152]{3,1,2,0:T(2,128)S(1)} copy-done((f32[8,2,18,1152]{3,1,2,0:T(2,128)S(1)}, f32[8,2,18,1152]{3,1,2,0:T(2,128)}, u32[]{:S(2)}) %copy-start) | copy-done | bytes 1327128
  2.5 0.0 copy-start.1
  2.5 0.0 copy-start.2
  2.5 0.3 shard_map.64
  2.7 3.1 %collective-permute-start = (f32[7,8,1152]{2,1,0:T(8,128)S(1)}, f32[7,8,1152]{2,1,0:T(8,128)S(1)}, u32[]{:S(2)}, u32[]{:S(2)}) collective-permute-start(f32[7,8,1152]{2,1,0:T(8,128)S(1)} %get-tuple-element.26), channel_id=1, source_target_pairs={{0,4},{4,0},{8,12},{12,8},{1,5},{5,1},{9,13},{13,9},{2,6},{6,2},{1... | collective-permute-start | bytes 774152 | tf_op jit(solution)/shard_map/ppermute | solution.py:431
  5.8 0.7 %collective-permute-start.1 = (f32[7,8,1152]{2,1,0:T(8,128)S(1)}, f32[7,8,1152]{2,1,0:T(8,128)S(1)}, u32[]{:S(2)}, u32[]{:S(2)}) collective-permute-start(f32[7,8,1152]{2,1,0:T(8,128)S(1)} %get-tuple-element.27), channel_id=1, source_target_pairs={{0,0},{4,8},{8,4},{12,12},{1,1},{5,9},{9,5},{13,13},{2,2},{6,10},{... | collective-permute-start | bytes 774152 | tf_op jit(solution)/shard_map/ppermute | solution.py:431
  6.5 4.4 %collective-permute-start.5 = (f32[7,8,1152]{2,1,0:T(8,128)S(1)}, f32[7,8,1152]{2,1,0:T(8,128)S(1)}, u32[]{:S(2)}, u32[]{:S(2)}) collective-permute-start(f32[7,8,1152]{2,1,0:T(8,128)S(1)} %get-tuple-element.39), channel_id=1, source_target_pairs={{0,4},{4,0},{8,12},{12,8},{1,5},{5,1},{9,13},{13,9},{2,6},{6,2},{1... | collective-permute-start | bytes 774152 | tf_op jit(solution)/shard_map/ppermute | solution.py:431
  10.9 0.7 %collective-permute-start.6 = (f32[7,8,1152]{2,1,0:T(8,128)S(1)}, f32[7,8,1152]{2,1,0:T(8,128)S(1)}, u32[]{:S(2)}, u32[]{:S(2)}) collective-permute-start(f32[7,8,1152]{2,1,0:T(8,128)S(1)} %get-tuple-element.40), channel_id=1, source_target_pairs={{0,0},{4,8},{8,4},{12,12},{1,1},{5,9},{9,5},{13,13},{2,2},{6,10},{... | collective-permute-start | bytes 774152 | tf_op jit(solution)/shard_map/ppermute | solution.py:431
  11.6 3.8 %shard_map.65 = (f32[2,14,8,128]{3,2,1,0:T(8,128)S(1)}, f32[2,14,8,128]{3,2,1,0:T(8,128)S(1)}, f32[2,14,8,128]{3,2,1,0:T(8,128)S(1)}, f32[2,14,8,128]{3,2,1,0:T(...) custom-call(f32[2,18,8,1152]{3,2,1,0:T(8,128)S(1)} %get-tuple-element.25., ...), custom_call_target="tpu_custom_call" | custom-call | flops 1 | bytes 1 | tf_op jit(solution)/shard_map/pallas_call | solution.py:394
  15.4 0.0 copy-done.1
  15.4 0.0 copy-done.2
  15.4 0.2 shard_map.66.refs_4_.refs_8_
  15.6 0.0 collective-permute-done.first_round
  15.7 0.0 collective-permute-done.1.second_round
  15.7 2.6 %shard_map.67 = (f32[4,14,8,128]{3,2,1,0:T(8,128)S(1)}, f32[4,14,8,128]{3,2,1,0:T(8,128)S(1)}, f32[4,14,8,128]{3,2,1,0:T(8,128)S(1)}, f32[4,14,8,128]{3,2,1,0:T(8,128)S(1)}) custom-call(f32[2,18,8,1152]{3,2,1,0:T(8,128)S(1)} %get-tuple-element.25.state, f32[7,8,1152]{2,1,0:T(8,128)S(1)} %collective-permute-done.first_round, ...), custom_call_target="tpu_custom_call" | custom-call | flops 19906560 | bytes 2654208 | tf_op jit(solution)/shard_map/pallas_call | solution.py:394
  18.2 0.1 collective-permute-start.2
  18.3 1.6 %collective-permute-start.3 = (f32[4,14,8,128]{3,2,1,0:T(8,128)S(1)}, f32[4,14,8,128]{3,2,1,0:T(8,128)S(1)}, u32[]{:S(2)}, u32[]{:S(2)}) collective-permute-start(f32[4,14,8,128]{3,2,1,0:T(8,128)S(1)} %get-tuple-element.37), channel_id=1, source_target_pairs={{0,2},{1,3},{2,0},{3,1},{4,6},{5,7},{6,4},{7,5},{8,10},{9,11},{10,... | collective-permute-start | bytes 688136 | tf_op jit(solution)/shard_map/ppermute | solution.py:473
  19.9 0.3 collective-permute-start.4
  20.2 0.0 collective-permute-done.5.first_round
  20.2 0.0 collective-permute-done.6.second_round
  20.2 0.0 copy-start.3
  20.2 2.5 %shard_map.68 = (f32[2,14,8,128]{3,2,1,0:T(8,128)S(1)}, f32[2,14,8,128]{3,2,1,0:T(8,128)S(1)}, f32[2,14,8,128]{3,2,1,0:T(8,128)S(1)}, f32[2,14,8,128]{3,2,1,0:T(8,128)S(1)}) custom-call(f32[2,18,8,1152]{3,2,1,0:T(8,128)S(1)} %get-tuple-element.25.state, f32[7,8,1152]{2,1,0:T(8,128)S(1)} %collective-permute-done.5.first_round, ...), custom_call_target="tpu_custom_call" | custom-call | flops 19906560 | bytes 2654208 | tf_op jit(solution)/shard_map/pallas_call | solution.py:394
  22.7 0.4 %collective-permute-start.7 = (f32[2,14,8,128]{3,2,1,0:T(8,128)S(1)}, f32[2,14,8,128]{3,2,1,0:T(8,128)S(1)}, u32[]{:S(2)}, u32[]{:S(2)}) collective-permute-start(f32[2,14,8,128]{3,2,1,0:T(8,128)S(1)} %get-tuple-element.42), channel_id=1, source_target_pairs={{0,1},{1,0},{2,3},{3,2},{4,5},{5,4},{6,7},{7,6},{8,9},{9,8},{10,11... | collective-permute-start | bytes 344072 | tf_op jit(solution)/shard_map/ppermute | solution.py:473
  23.2 1.5 %collective-permute-start.8 = (f32[2,14,8,128]{3,2,1,0:T(8,128)S(1)}, f32[2,14,8,128]{3,2,1,0:T(8,128)S(1)}, u32[]{:S(2)}, u32[]{:S(2)}) collective-permute-start(f32[2,14,8,128]{3,2,1,0:T(8,128)S(1)} %get-tuple-element.43), channel_id=1, source_target_pairs={{0,2},{1,3},{2,0},{3,1},{4,6},{5,7},{6,4},{7,5},{8,10},{9,11},{10,... | collective-permute-start | bytes 344072 | tf_op jit(solution)/shard_map/ppermute | solution.py:473
  24.6 0.0 collective-permute-done.2.refs_1_
  24.6 0.0 collective-permute-start.9
  24.7 2.1 %collective-permute-done.3.refs_2_ = f32[4,14,8,128]{3,2,1,0:T(8,128)S(1)} collective-permute-done((f32[4,14,8,128]{3,2,1,0:T(8,128)S(1)}, f32[4,14,8,128]{3,2,1,0:T(8,128)S(1)}, u32[]{:S(2)}, u32[]{:S(2)}) %collective-permute-start.3) | collective-permute-done | bytes 229408 | tf_op jit(solution)/shard_map/ppermute | solution.py:473
  26.8 4.0 %collective-permute-done.4.refs_3_ = f32[4,14,8,128]{3,2,1,0:T(8,128)S(1)} collective-permute-done((f32[4,14,8,128]{3,2,1,0:T(8,128)S(1)}, f32[4,14,8,128]{3,2,1,0:T(8,128)S(1)}, u32[]{:S(2)}, u32[]{:S(2)}) %collective-permute-start.4) | collective-permute-done | bytes 229408 | tf_op jit(solution)/shard_map/ppermute | solution.py:473
  30.8 0.0 copy-done.3
  30.8 0.7 %shard_map.69.refs_9_ = f32[6,6,8,288]{3,2,1,0:T(8,128)S(1)} custom-call(s32[4]{0:T(128)S(1)} %copy-done.3, f32[4,14,8,128]{3,2,1,0:T(8,128)S(1)} %get-tuple-element.35.refs_0_, f32[4,14,8,128]{3,2,1,0:T(8,128)S(1)} %collective-permute-done.2.refs_1_, f32[4,14,8,128]{3,2,1,0:T(8,128)S(1)} %collective-permute-done.3.refs_2_, ...), custom_call_target="tpu_custom_call" | custom-call | flops 1 | bytes 1 | tf_op jit(solution)/shard_map/pallas_call | solution.py:394
  31.5 0.0 collective-permute-done.7.refs_5_
  31.6 2.6 %collective-permute-done.8.refs_6_ = f32[2,14,8,128]{3,2,1,0:T(8,128)S(1)} collective-permute-done((f32[2,14,8,128]{3,2,1,0:T(8,128)S(1)}, f32[2,14,8,128]{3,2,1,0:T(8,128)S(1)}, u32[]{:S(2)}, u32[]{:S(2)}) %collective-permute-start.8) | collective-permute-done | bytes 114720 | tf_op jit(solution)/shard_map/ppermute | solution.py:473
  34.2 1.6 %collective-permute-done.9.refs_7_ = f32[2,14,8,128]{3,2,1,0:T(8,128)S(1)} collective-permute-done((f32[2,14,8,128]{3,2,1,0:T(8,128)S(1)}, f32[2,14,8,128]{3,2,1,0:T(8,128)S(1)}, u32[]{:S(2)}, u32[]{:S(2)}) %collective-permute-start.9) | collective-permute-done | bytes 114720 | tf_op jit(solution)/shard_map/ppermute | solution.py:473
  35.7 2.0 %shard_map.70 = f32[6,18,8,288]{3,2,1,0:T(8,128)} custom-call(s32[4]{0:T(128)S(1)} %copy-done.3, f32[4,14,8,128]{3,2,1,0:T(8,128)S(1)} %get-tuple-element.35.refs_0_, f32[4,14,8,128]{3,2,1,0:T(8,128)S(1)} %collective-permute-done.2.refs_1_, f32[4,14,8,128]{3,2,1,0:T(8,128)S(1)} %collective-permute-done.3.refs_2_, ...), custom_call_target="tpu_custom_call" | custom-call | flops 1 | bytes 1 | tf_op jit(solution)/shard_map/pallas_call | solution.py:394
Async XLA Ops:
  1.1 1.3 %copy-start = (f32[8,2,18,1152]{3,1,2,0:T(2,128)S(1)}, f32[8,2,18,1152]{3,1,2,0:T(2,128)}, u32[]{:S(2)}) copy-start(f32[8,2,18,1152]{3,1,2,0:T(2,128)} %param.6) | copy-start | bytes 3981316
  2.5 13.0 %copy-start.1 = (f32[4,6,18,288]{3,0,2,1:T(4,128)S(1)}, f32[4,6,18,288]{3,0,2,1:T(4,128)}, u32[]{:S(2)}) copy-start(f32[4,6,18,288]{3,0,2,1:T(4,128)} %param.11) | copy-start | bytes 1492996
  2.5 13.0 %copy-start.2 = (s32[6,18,288]{2,1,0:T(8,128)S(1)}, s32[6,18,288]{2,1,0:T(8,128)}, u32[]{:S(2)}) copy-start(s32[6,18,288]{2,1,0:T(8,128)} %source.1) | copy-start | bytes 373252
  2.7 12.9 %collective-permute-start = (f32[7,8,1152]{2,1,0:T(8,128)S(1)}, f32[7,8,1152]{2,1,0:T(8,128)S(1)}, u32[]{:S(2)}, u32[]{:S(2)}) collective-permute-start(f32[7,8,1152]{2,1,0:T(8,128)S(1)} %get-tuple-element.26), channel_id=1, source_target_pairs={{0,4},{4,0},{8,12},{12,8},{1,5},{5,1},{9,13},{13,9},{2,6},{6,2},{1... | collective-permute-start | bytes 774152 | tf_op jit(solution)/shard_map/ppermute | solution.py:431
  5.8 9.8 %collective-permute-start.1 = (f32[7,8,1152]{2,1,0:T(8,128)S(1)}, f32[7,8,1152]{2,1,0:T(8,128)S(1)}, u32[]{:S(2)}, u32[]{:S(2)}) collective-permute-start(f32[7,8,1152]{2,1,0:T(8,128)S(1)} %get-tuple-element.27), channel_id=1, source_target_pairs={{0,0},{4,8},{8,4},{12,12},{1,1},{5,9},{9,5},{13,13},{2,2},{6,10},{... | collective-permute-start | bytes 774152 | tf_op jit(solution)/shard_map/ppermute | solution.py:431
  6.5 13.7 %collective-permute-start.5 = (f32[7,8,1152]{2,1,0:T(8,128)S(1)}, f32[7,8,1152]{2,1,0:T(8,128)S(1)}, u32[]{:S(2)}, u32[]{:S(2)}) collective-permute-start(f32[7,8,1152]{2,1,0:T(8,128)S(1)} %get-tuple-element.39), channel_id=1, source_target_pairs={{0,4},{4,0},{8,12},{12,8},{1,5},{5,1},{9,13},{13,9},{2,6},{6,2},{1... | collective-permute-start | bytes 774152 | tf_op jit(solution)/shard_map/ppermute | solution.py:431
  10.9 9.2 %collective-permute-start.6 = (f32[7,8,1152]{2,1,0:T(8,128)S(1)}, f32[7,8,1152]{2,1,0:T(8,128)S(1)}, u32[]{:S(2)}, u32[]{:S(2)}) collective-permute-start(f32[7,8,1152]{2,1,0:T(8,128)S(1)} %get-tuple-element.40), channel_id=1, source_target_pairs={{0,0},{4,8},{8,4},{12,12},{1,1},{5,9},{9,5},{13,13},{2,2},{6,10},{... | collective-permute-start | bytes 774152 | tf_op jit(solution)/shard_map/ppermute | solution.py:431
  18.2 6.4 %collective-permute-start.2 = (f32[4,14,8,128]{3,2,1,0:T(8,128)S(1)}, f32[4,14,8,128]{3,2,1,0:T(8,128)S(1)}, u32[]{:S(2)}, u32[]{:S(2)}) collective-permute-start(f32[4,14,8,128]{3,2,1,0:T(8,128)S(1)} %get-tuple-element.36), channel_id=1, source_target_pairs={{0,1},{1,0},{2,3},{3,2},{4,5},{5,4},{6,7},{7,6},{8,9},{9,8},{10,11... | collective-permute-start | bytes 688136 | tf_op jit(solution)/shard_map/ppermute | solution.py:473
  18.3 8.5 %collective-permute-start.3 = (f32[4,14,8,128]{3,2,1,0:T(8,128)S(1)}, f32[4,14,8,128]{3,2,1,0:T(8,128)S(1)}, u32[]{:S(2)}, u32[]{:S(2)}) collective-permute-start(f32[4,14,8,128]{3,2,1,0:T(8,128)S(1)} %get-tuple-element.37), channel_id=1, source_target_pairs={{0,2},{1,3},{2,0},{3,1},{4,6},{5,7},{6,4},{7,5},{8,10},{9,11},{10,... | collective-permute-start | bytes 688136 | tf_op jit(solution)/shard_map/ppermute | solution.py:473
  19.9 10.9 %collective-permute-start.4 = (f32[4,14,8,128]{3,2,1,0:T(8,128)S(1)}, f32[4,14,8,128]{3,2,1,0:T(8,128)S(1)}, u32[]{:S(2)}, u32[]{:S(2)}) collective-permute-start(f32[4,14,8,128]{3,2,1,0:T(8,128)S(1)} %get-tuple-element.38), channel_id=1, source_target_pairs={{0,3},{1,2},{2,1},{3,0},{4,7},{5,6},{6,5},{7,4},{8,11},{9,10},{10,... | collective-permute-start | bytes 688136 | tf_op jit(solution)/shard_map/ppermute | solution.py:473
  20.2 10.6 %copy-start.3 = (s32[4]{0:T(128)S(1)}, s32[4]{0:T(128)}, u32[]{:S(2)}) copy-start(s32[4]{0:T(128)} %counts.3) | copy-start | bytes 52
  22.7 8.8 %collective-permute-start.7 = (f32[2,14,8,128]{3,2,1,0:T(8,128)S(1)}, f32[2,14,8,128]{3,2,1,0:T(8,128)S(1)}, u32[]{:S(2)}, u32[]{:S(2)}) collective-permute-start(f32[2,14,8,128]{3,2,1,0:T(8,128)S(1)} %get-tuple-element.42), channel_id=1, source_target_pairs={{0,1},{1,0},{2,3},{3,2},{4,5},{5,4},{6,7},{7,6},{8,9},{9,8},{10,11... | collective-permute-start | bytes 344072 | tf_op jit(solution)/shard_map/ppermute | solution.py:473
  23.2 11.0 %collective-permute-start.8 = (f32[2,14,8,128]{3,2,1,0:T(8,128)S(1)}, f32[2,14,8,128]{3,2,1,0:T(8,128)S(1)}, u32[]{:S(2)}, u32[]{:S(2)}) collective-permute-start(f32[2,14,8,128]{3,2,1,0:T(8,128)S(1)} %get-tuple-element.43), channel_id=1, source_target_pairs={{0,2},{1,3},{2,0},{3,1},{4,6},{5,7},{6,4},{7,5},{8,10},{9,11},{10,... | collective-permute-start | bytes 344072 | tf_op jit(solution)/shard_map/ppermute | solution.py:473
  24.6 11.1 %collective-permute-start.9 = (f32[2,14,8,128]{3,2,1,0:T(8,128)S(1)}, f32[2,14,8,128]{3,2,1,0:T(8,128)S(1)}, u32[]{:S(2)}, u32[]{:S(2)}) collective-permute-start(f32[2,14,8,128]{3,2,1,0:T(8,128)S(1)} %get-tuple-element.44), channel_id=1, source_target_pairs={{0,3},{1,2},{2,1},{3,0},{4,7},{5,6},{6,5},{7,4},{8,11},{9,10},{10,... | collective-permute-start | bytes 344072 | tf_op jit(solution)/shard_map/ppermute | solution.py:473

commit v7 on v6

--- a/solution.py
+++ b/solution.py
@@ -53,7 +53,7 @@
     return width, mains, tail, per, BLOCK * mains + tails
 
 
-def prep_kernel(rows, tracers, winds, state, *sent):
+def prep_kernel(rows, tracers, winds, state, first_round, *second_rounds):
     levels, nlon = state.shape[0], state.shape[3]
     nj = nlon // LANES
     row_stride = nj * levels
@@ -72,7 +72,7 @@
 
     lax.fori_loop(0, rows, body, 0)
     for level in range(levels):
-        for target, north, scale in ((sent[2 * level], even, None), (sent[2 * level + 1], jnp.logical_not(even), keep)):
+        for target, north, scale in ((first_round.at[level], even, None), (second_rounds[level], jnp.logical_not(even), keep)):
             scaled = (lambda v: v) if scale is None else (lambda v: v * scale)
             row_t = jnp.where(north, rows - HALO, 0)
             row_x = jnp.where(north, rows - REACH, 0)
@@ -246,7 +246,7 @@
     odd = lax.axis_index("lat") % 2 == 1
 
     def halo(south, *at):
-        one, two = first_round[at], second_round[at]
+        one, two = first_round[(slot,) + at], second_round[at]
         return jnp.where(odd, one, two) if south else jnp.where(odd, two, one)
 
     for end, south in enumerate((True, False)):
@@ -305,8 +305,8 @@
     lon_pass(listed(ends_last), swept, coef_x, inter, west, flux, lane, send)
     for k in range(count):
         copy_units(packed.at[k], outs[k])
-    for other, out in zip(others, outs):
-        copy_units(other, out, packed.shape[1])
+    for other in others:
+        copy_units(other, outs[1], packed.shape[1])
 
 
 def weights_kernel(weights, source, out):
@@ -421,14 +421,15 @@
 
     raw = tiles_of(jnp.transpose(tracers, (0, 2, 1, 3)))
     joined = jnp.concatenate([jnp.transpose(wind_x, (1, 0, 2)), jnp.transpose(wind_y, (1, 0, 2))], axis=0)
-    halo = f32(HALO + 1, number, nlon)
+    halo = (HALO + 1, number, nlon)
     state, *sent = call(
         functools.partial(prep_kernel, rows),
-        [f32(depth, rows, number, nlon)] + [halo] * (2 * depth), (raw, joined),
+        [f32(depth, rows, number, nlon), f32(depth, *halo)] + [f32(*halo)] * depth, (raw, joined),
         cost=cost(1, 1))
-    swaps = [[(i, i ^ 1) for i in range(bands)],
-             [(i, i if i in (0, bands - 1) else ((i - 1) ^ 1) + 1) for i in range(bands)]]
-    rounds = [lax.ppermute(buffer, "lat", swaps[i % 2]) for i, buffer in enumerate(sent)]
+    first_swap = [(i, i ^ 1) for i in range(bands)]
+    second_swap = [(i, i if i in (0, bands - 1) else ((i - 1) ^ 1) + 1) for i in range(bands)]
+    first_round = lax.ppermute(sent[0], "lat", first_swap)
+    second_rounds = [lax.ppermute(buffer, "lat", second_swap) for buffer in sent[1:]]
     taps = call(
         weights_kernel, f32(targets, rows, SUB, width),
         (jnp.transpose(remap_weight, (1, 2, 0, 3)), source_level),
@@ -455,23 +456,31 @@
     stage = vmem(2 * HALO, number, nlon)
 
     def edge(slot, joint, after):
-        args = (state, *rounds[2 * slot:2 * slot + 2], first, cx, cy, *joint, after)
+        args = (state, first_round, second_rounds[slot], first, cx, cy, *joint, *after)
         units = 2 + (joint[0].shape[0] if joint else 0)
         return call(
             functools.partial(edge_kernel, count, rows, slot, len(joint)),
-            [f32(*box(units))] * count, args,
-            specs=[VMEM] * (len(args) - 1) + [ANY],
+            [f32(*box(units if k == 1 else 2)) for k in range(count)], args,
+            specs=[VMEM] * (len(args) - len(after)) + [ANY] * len(after),
             scratch=[vmem(*box(2, count)), vmem(3, 2, SUB, nlon), swept, swept, stage, stage, stage],
             cost=cost(60 * tracers.size, 8 * tracers.size))
 
-    after, joint, joint_units = taps, middle, tuple((slot, 1 + b) for slot in range(depth) for b in range(inner))
+    def swapped(sent, k):
+        return lax.ppermute(sent, "lev", [(i, i ^ k) for i in range(count)])
+
+    partners = range(count - 1, 1, -1)
+    units = tuple((slot, 1 + b) for slot in range(depth) for b in range(inner))
+    plan += [(k, units) for k in partners] + [(0, units)]
+    chunks += [swapped(middle[k], k) for k in partners] + [middle[0]]
+    after, joint = (taps,), (middle[1],)
     for slot in range(depth):
+        own = ((slot, 0), (slot, blocks - 1))
         done = edge(slot, joint, after)
-        plan += [(k, ((slot, 0), (slot, blocks - 1)) + joint_units) for k in range(count)]
-        chunks += [done[0]] + [None] * (count - 1)
-        for k in range(count - 1, 0, -1):
-            chunks[k - count] = lax.ppermute(done[k], "lev", [(i, i ^ k) for i in range(count)])
-        after, joint, joint_units = done[0], (), ()
+        plan += [(k, own) for k in partners] + [(0, own), (1, own + units if joint else own)]
+        chunks += [swapped(done[k], k) for k in partners] + [done[0], swapped(done[1], 1)]
+        if slot == 0:
+            after, joint, early = (done[0], *chunks[:len(partners)]), (), len(chunks)
+
     def remap(part, numbers, height, ready):
         args = (level_counts, *chunks[:part], taps, *ready)
         return call(
@@ -481,7 +490,7 @@
             scratch=[vmem(count * depth, blocks, size, SUB, LANES)],
             cost=cost(1, 1))
 
-    middle_rows = remap(count, tuple(range(1, blocks - 1)), inner * BLOCK, ())
+    middle_rows = remap(early, tuple(range(1, blocks - 1)), inner * BLOCK, ())
     out = remap(len(chunks), (0, blocks - 1), rows, (middle_rows,))
     return jnp.transpose(out, (2, 0, 1, 3))
 

time: 38.1 us -> 35.3 us (0.927)
  starting transfers between devices: 12.7 us -> 10.2 us
    ppermute x10 -> x11, starting transfers between devices: 12.7 us -> 10.2 us  [the longest x8 5.8 us: swapped(): return lax.ppermute(sent, 'lev', [(i, i ^ k) for i in range(count)])]
    ppermute x10 -> x11, waiting for transfers between devices: 10.3 us -> 10.3 us  [the longest x8 5.5 us: swapped(): return lax.ppermute(sent, 'lev', [(i, i ^ k) for i in range(count)])]
  transfers between devices with their start and end apart: 10 -> 11, of which waited for: 4 -> 4; matrix products, arithmetic and copies ran while one was open for 0% -> 0% of each run, Pallas kernels for 26% -> 28%
where the time goes in v7:
time: 35.3 us; the launch traced here: 35.1 us
  Pallas kernels  12.1 us (34%)
  waiting for transfers between devices  10.3 us (29%)
  starting transfers between devices  10.2 us (29%)
  local copies, waits for them, and re-layouts  1.33 us (4%)
  other arithmetic  1.14 us (3%)
    pallas_call x7, Pallas kernels, call(): pl.pallas_call(kernel, out_shape=outs, in_specs=specs or [VMEM] * len(arg...  12.1 us
    ppermute x8, starting transfers between devices, swapped(): return lax.ppermute(sent, 'lev', [(i, i ^ k) for i in range(count)])  5.8 us
    ppermute x8, waiting for transfers between devices, swapped(): return lax.ppermute(sent, 'lev', [(i, i ^ k) for i in range(count)])  5.5 us
    ppermute x1, waiting for transfers between devices, shards(): first_round = lax.ppermute(sent[0], 'lat', first_swap)  4.75 us
    ppermute x1, starting transfers between devices, shards(): first_round = lax.ppermute(sent[0], 'lat', first_swap)  3.09 us
    ppermute x2, starting transfers between devices, shards(): lax.ppermute(buffer, 'lat', second_swap)  1.34 us
    unnamed x8, local copies, waits for them, and re-layouts  1.33 us
    concatenate x1, other arithmetic, shards(): jnp.concatenate([jnp.transpose(wind_x, (1, 0, 2)), jnp.transpose(wind_y,...  1.14 us
  transfers between devices with their start and end apart: 11, of which 4 were waited for; matrix products, arithmetic and copies ran while one was open for 0% of the time, Pallas kernels for 28%

profile of v7, /device:TPU:0, one launch (start us, length us, event | category | flops | bytes accessed | tf_op | source)
XLA Modules:
  0.0 35.1 jit_solution(6710194141805558092)
XLA Ops:
  0.0 1.1 %pad_maximum_fusion.winds.joined = f32[36,2,1152]{2,1,0:T(2,128)S(1)} fusion(f32[18,2,1152]{2,1,0:T(2,128)} %bitcast.13, f32[18,2,1152]{2,1,0:T(2,128)} %bitcast.14), kind=kLoop, calls=%fused_computation | loop fusion | flops 82944 | bytes 663552 | tf_op jit(solution)/shard_map/concatenate | solution.py:423
  1.1 0.0 copy-start
  1.2 1.3 %copy-done = f32[8,2,18,1152]{3,1,2,0:T(2,128)S(1)} copy-done((f32[8,2,18,1152]{3,1,2,0:T(2,128)S(1)}, f32[8,2,18,1152]{3,1,2,0:T(2,128)}, u32[]{:S(2)}) %copy-start) | copy-done | bytes 1327128
  2.5 0.0 copy-start.1
  2.5 0.0 copy-start.2
  2.5 0.3 shard_map.64
  2.7 3.1 %collective-permute-start.2 = (f32[2,7,8,1152]{3,2,1,0:T(8,128)S(1)}, f32[2,7,8,1152]{3,2,1,0:T(8,128)S(1)}, u32[]{:S(2)}, u32[]{:S(2)}) collective-permute-start(f32[2,7,8,1152]{3,2,1,0:T(8,128)S(1)} %get-tuple-element.28), channel_id=1, source_target_pairs={{0,4},{4,0},{8,12},{12,8},{1,5},{5,1},{9,13},{13,9},{2,6},{6,2},{1... | collective-permute-start | bytes 1548296 | tf_op jit(solution)/shard_map/ppermute | solution.py:431
  5.8 0.7 %collective-permute-start.3 = (f32[7,8,1152]{2,1,0:T(8,128)S(1)}, f32[7,8,1152]{2,1,0:T(8,128)S(1)}, u32[]{:S(2)}, u32[]{:S(2)}) collective-permute-start(f32[7,8,1152]{2,1,0:T(8,128)S(1)} %get-tuple-element.29), channel_id=1, source_target_pairs={{0,0},{4,8},{8,4},{12,12},{1,1},{5,9},{9,5},{13,13},{2,2},{6,10},{... | collective-permute-start | bytes 774152 | tf_op jit(solution)/shard_map/ppermute | solution.py:432
  6.5 0.7 %collective-permute-start.7 = (f32[7,8,1152]{2,1,0:T(8,128)S(1)}, f32[7,8,1152]{2,1,0:T(8,128)S(1)}, u32[]{:S(2)}, u32[]{:S(2)}) collective-permute-start(f32[7,8,1152]{2,1,0:T(8,128)S(1)} %get-tuple-element.38), channel_id=1, source_target_pairs={{0,0},{4,8},{8,4},{12,12},{1,1},{5,9},{9,5},{13,13},{2,2},{6,10},{... | collective-permute-start | bytes 774152 | tf_op jit(solution)/shard_map/ppermute | solution.py:432
  7.2 3.8 %shard_map.65 = (f32[2,14,8,128]{3,2,1,0:T(8,128)S(1)}, f32[2,14,8,128]{3,2,1,0:T(8,128)S(1)}, f32[2,14,8,128]{3,2,1,0:T(8,128)S(1)}, f32[2,14,8,128]{3,2,1,0:T(...) custom-call(f32[2,18,8,1152]{3,2,1,0:T(8,128)S(1)} %get-tuple-element.24., ...), custom_call_target="tpu_custom_call" | custom-call | flops 1 | bytes 1 | tf_op jit(solution)/shard_map/pallas_call | solution.py:394
  11.0 0.7 %collective-permute-start = (f32[2,14,8,128]{3,2,1,0:T(8,128)S(1)}, f32[2,14,8,128]{3,2,1,0:T(8,128)S(1)}, u32[]{:S(2)}, u32[]{:S(2)}) collective-permute-start(f32[2,14,8,128]{3,2,1,0:T(8,128)S(1)} %get-tuple-element.25), channel_id=1, source_target_pairs={{0,3},{1,2},{2,1},{3,0},{4,7},{5,6},{6,5},{7,4},{8,11},{9,10},{10,... | collective-permute-start | bytes 344072 | tf_op jit(solution)/shard_map/ppermute | solution.py:469
  11.7 0.9 %collective-permute-start.1 = (f32[2,14,8,128]{3,2,1,0:T(8,128)S(1)}, f32[2,14,8,128]{3,2,1,0:T(8,128)S(1)}, u32[]{:S(2)}, u32[]{:S(2)}) collective-permute-start(f32[2,14,8,128]{3,2,1,0:T(8,128)S(1)} %get-tuple-element.26), channel_id=1, source_target_pairs={{0,2},{1,3},{2,0},{3,1},{4,6},{5,7},{6,4},{7,5},{8,10},{9,11},{10,... | collective-permute-start | bytes 344072 | tf_op jit(solution)/shard_map/ppermute | solution.py:469
  12.6 0.0 copy-done.1
  12.6 0.0 copy-done.2
  12.6 0.2 shard_map.66.refs_1_.refs_7_.refs_11_
  12.8 0.0 collective-permute-done.3.second_round
  12.8 4.8 %collective-permute-done.2.first_round = f32[2,7,8,1152]{3,2,1,0:T(8,128)S(1)} collective-permute-done((f32[2,7,8,1152]{3,2,1,0:T(8,128)S(1)}, f32[2,7,8,1152]{3,2,1,0:T(8,128)S(1)}, u32[]{:S(2)}, u32[]{:S(2)}) %collective-permute-start.2) | collective-permute-done | bytes 516128 | tf_op jit(solution)/shard_map/ppermute | solution.py:431
  17.6 2.5 %shard_map.67 = (f32[2,14,8,128]{3,2,1,0:T(8,128)S(1)}, f32[4,14,8,128]{3,2,1,0:T(8,128)S(1)}, f32[2,14,8,128]{3,2,1,0:T(8,128)S(1)}, f32[2,14,8,128]{3,2,1,0:T(8,128)S(1)}) custom-call(f32[2,18,8,1152]{3,2,1,0:T(8,128)S(1)} %get-tuple-element.24.state, f32[2,7,8,1152]{3,2,1,0:T(8,128)S(1)} %collective-permute-done.2.first_round, ...), custom_call_target="tpu_custom_call" | custom-call | flops 19906560 | bytes 2654208 | tf_op jit(solution)/shard_map/pallas_call | solution.py:394
  20.1 0.1 collective-permute-start.6
  20.2 1.8 %collective-permute-start.4 = (f32[2,14,8,128]{3,2,1,0:T(8,128)S(1)}, f32[2,14,8,128]{3,2,1,0:T(8,128)S(1)}, u32[]{:S(2)}, u32[]{:S(2)}) collective-permute-start(f32[2,14,8,128]{3,2,1,0:T(8,128)S(1)} %get-tuple-element.34), channel_id=1, source_target_pairs={{0,3},{1,2},{2,1},{3,0},{4,7},{5,6},{6,5},{7,4},{8,11},{9,10},{10,... | collective-permute-start | bytes 344072 | tf_op jit(solution)/shard_map/ppermute | solution.py:469
  22.0 0.0 collective-permute-done.refs_1_.refs_0_
  22.0 0.4 %collective-permute-start.5 = (f32[2,14,8,128]{3,2,1,0:T(8,128)S(1)}, f32[2,14,8,128]{3,2,1,0:T(8,128)S(1)}, u32[]{:S(2)}, u32[]{:S(2)}) collective-permute-start(f32[2,14,8,128]{3,2,1,0:T(8,128)S(1)} %get-tuple-element.35), channel_id=1, source_target_pairs={{0,2},{1,3},{2,0},{3,1},{4,6},{5,7},{6,4},{7,5},{8,10},{9,11},{10,... | collective-permute-start | bytes 344072 | tf_op jit(solution)/shard_map/ppermute | solution.py:469
  22.3 0.0 collective-permute-done.1.refs_2_.refs_1_
  22.3 0.0 collective-permute-done.7.second_round
  22.3 0.0 copy-start.3
  22.3 2.5 %shard_map.68 = (f32[2,14,8,128]{3,2,1,0:T(8,128)S(1)}, f32[2,14,8,128]{3,2,1,0:T(8,128)S(1)}, f32[2,14,8,128]{3,2,1,0:T(8,128)S(1)}, f32[2,14,8,128]{3,2,1,0:T(8,128)S(1)}) custom-call(f32[2,18,8,1152]{3,2,1,0:T(8,128)S(1)} %get-tuple-element.24.state, f32[2,7,8,1152]{3,2,1,0:T(8,128)S(1)} %collective-permute-done.2.first_round, ...), custom_call_target="tpu_custom_call" | custom-call | flops 19906560 | bytes 2654208 | tf_op jit(solution)/shard_map/pallas_call | solution.py:394
  24.9 1.1 %collective-permute-start.8 = (f32[2,14,8,128]{3,2,1,0:T(8,128)S(1)}, f32[2,14,8,128]{3,2,1,0:T(8,128)S(1)}, u32[]{:S(2)}, u32[]{:S(2)}) collective-permute-start(f32[2,14,8,128]{3,2,1,0:T(8,128)S(1)} %get-tuple-element.39), channel_id=1, source_target_pairs={{0,3},{1,2},{2,1},{3,0},{4,7},{5,6},{6,5},{7,4},{8,11},{9,10},{10,... | collective-permute-start | bytes 344072 | tf_op jit(solution)/shard_map/ppermute | solution.py:469
  26.0 0.7 %collective-permute-start.9 = (f32[2,14,8,128]{3,2,1,0:T(8,128)S(1)}, f32[2,14,8,128]{3,2,1,0:T(8,128)S(1)}, u32[]{:S(2)}, u32[]{:S(2)}) collective-permute-start(f32[2,14,8,128]{3,2,1,0:T(8,128)S(1)} %get-tuple-element.40), channel_id=1, source_target_pairs={{0,2},{1,3},{2,0},{3,1},{4,6},{5,7},{6,4},{7,5},{8,10},{9,11},{10,... | collective-permute-start | bytes 344072 | tf_op jit(solution)/shard_map/ppermute | solution.py:469
  26.7 0.0 collective-permute-done.4.refs_3_
  26.7 0.1 collective-permute-start.10
  26.8 1.5 %collective-permute-done.5.refs_4_ = f32[2,14,8,128]{3,2,1,0:T(8,128)S(1)} collective-permute-done((f32[2,14,8,128]{3,2,1,0:T(8,128)S(1)}, f32[2,14,8,128]{3,2,1,0:T(8,128)S(1)}, u32[]{:S(2)}, u32[]{:S(2)}) %collective-permute-start.5) | collective-permute-done | bytes 114720 | tf_op jit(solution)/shard_map/ppermute | solution.py:469
  28.3 0.0 collective-permute-done.6.refs_6_
  28.3 0.0 copy-done.3
  28.3 0.7 %shard_map.69.refs_12_ = f32[6,6,8,288]{3,2,1,0:T(8,128)S(1)} custom-call(s32[4]{0:T(128)S(1)} %copy-done.3, f32[2,14,8,128]{3,2,1,0:T(8,128)S(1)} %collective-permute-done.refs_1_.refs_0_, f32[2,14,8,128]{3,2,1,0:T(8,128)S(1)} %collective-permute-done.1.refs_2_.refs_1_, f32[2,14,8,128]{3,2,1,0:T(8,128)S(1)} %get-tuple-element.27.refs_2_, ...), custom_call_target="tpu_custom_call" | custom-call | flops 1 | bytes 1 | tf_op jit(solution)/shard_map/pallas_call | solution.py:394
  29.1 1.4 %collective-permute-done.8.refs_7_ = f32[2,14,8,128]{3,2,1,0:T(8,128)S(1)} collective-permute-done((f32[2,14,8,128]{3,2,1,0:T(8,128)S(1)}, f32[2,14,8,128]{3,2,1,0:T(8,128)S(1)}, u32[]{:S(2)}, u32[]{:S(2)}) %collective-permute-start.8) | collective-permute-done | bytes 114720 | tf_op jit(solution)/shard_map/ppermute | solution.py:469
  30.5 2.6 %collective-permute-done.9.refs_8_ = f32[2,14,8,128]{3,2,1,0:T(8,128)S(1)} collective-permute-done((f32[2,14,8,128]{3,2,1,0:T(8,128)S(1)}, f32[2,14,8,128]{3,2,1,0:T(8,128)S(1)}, u32[]{:S(2)}, u32[]{:S(2)}) %collective-permute-start.9) | collective-permute-done | bytes 114720 | tf_op jit(solution)/shard_map/ppermute | solution.py:469
  33.1 0.0 collective-permute-done.10.refs_10_
  33.1 2.1 %shard_map.70 = f32[6,18,8,288]{3,2,1,0:T(8,128)} custom-call(s32[4]{0:T(128)S(1)} %copy-done.3, f32[2,14,8,128]{3,2,1,0:T(8,128)S(1)} %collective-permute-done.refs_1_.refs_0_, f32[2,14,8,128]{3,2,1,0:T(8,128)S(1)} %collective-permute-done.1.refs_2_.refs_1_, f32[2,14,8,128]{3,2,1,0:T(8,128)S(1)} %get-tuple-element.27.refs_2_, ...), custom_call_target="tpu_custom_call" | custom-call | flops 1 | bytes 1 | tf_op jit(solution)/shard_map/pallas_call | solution.py:394
Async XLA Ops:
  1.1 1.3 %copy-start = (f32[8,2,18,1152]{3,1,2,0:T(2,128)S(1)}, f32[8,2,18,1152]{3,1,2,0:T(2,128)}, u32[]{:S(2)}) copy-start(f32[8,2,18,1152]{3,1,2,0:T(2,128)} %param.6) | copy-start | bytes 3981316
  2.5 10.1 %copy-start.1 = (f32[4,6,18,288]{3,0,2,1:T(4,128)S(1)}, f32[4,6,18,288]{3,0,2,1:T(4,128)}, u32[]{:S(2)}) copy-start(f32[4,6,18,288]{3,0,2,1:T(4,128)} %param.11) | copy-start | bytes 1492996
  2.5 10.1 %copy-start.2 = (s32[6,18,288]{2,1,0:T(8,128)S(1)}, s32[6,18,288]{2,1,0:T(8,128)}, u32[]{:S(2)}) copy-start(s32[6,18,288]{2,1,0:T(8,128)} %source.1) | copy-start | bytes 373252
  2.7 14.8 %collective-permute-start.2 = (f32[2,7,8,1152]{3,2,1,0:T(8,128)S(1)}, f32[2,7,8,1152]{3,2,1,0:T(8,128)S(1)}, u32[]{:S(2)}, u32[]{:S(2)}) collective-permute-start(f32[2,7,8,1152]{3,2,1,0:T(8,128)S(1)} %get-tuple-element.28), channel_id=1, source_target_pairs={{0,4},{4,0},{8,12},{12,8},{1,5},{5,1},{9,13},{13,9},{2,6},{6,2},{1... | collective-permute-start | bytes 1548296 | tf_op jit(solution)/shard_map/ppermute | solution.py:431
  5.8 7.0 %collective-permute-start.3 = (f32[7,8,1152]{2,1,0:T(8,128)S(1)}, f32[7,8,1152]{2,1,0:T(8,128)S(1)}, u32[]{:S(2)}, u32[]{:S(2)}) collective-permute-start(f32[7,8,1152]{2,1,0:T(8,128)S(1)} %get-tuple-element.29), channel_id=1, source_target_pairs={{0,0},{4,8},{8,4},{12,12},{1,1},{5,9},{9,5},{13,13},{2,2},{6,10},{... | collective-permute-start | bytes 774152 | tf_op jit(solution)/shard_map/ppermute | solution.py:432
  6.5 15.8 %collective-permute-start.7 = (f32[7,8,1152]{2,1,0:T(8,128)S(1)}, f32[7,8,1152]{2,1,0:T(8,128)S(1)}, u32[]{:S(2)}, u32[]{:S(2)}) collective-permute-start(f32[7,8,1152]{2,1,0:T(8,128)S(1)} %get-tuple-element.38), channel_id=1, source_target_pairs={{0,0},{4,8},{8,4},{12,12},{1,1},{5,9},{9,5},{13,13},{2,2},{6,10},{... | collective-permute-start | bytes 774152 | tf_op jit(solution)/shard_map/ppermute | solution.py:432
  11.0 11.0 %collective-permute-start = (f32[2,14,8,128]{3,2,1,0:T(8,128)S(1)}, f32[2,14,8,128]{3,2,1,0:T(8,128)S(1)}, u32[]{:S(2)}, u32[]{:S(2)}) collective-permute-start(f32[2,14,8,128]{3,2,1,0:T(8,128)S(1)} %get-tuple-element.25), channel_id=1, source_target_pairs={{0,3},{1,2},{2,1},{3,0},{4,7},{5,6},{6,5},{7,4},{8,11},{9,10},{10,... | collective-permute-start | bytes 344072 | tf_op jit(solution)/shard_map/ppermute | solution.py:469
  11.7 10.6 %collective-permute-start.1 = (f32[2,14,8,128]{3,2,1,0:T(8,128)S(1)}, f32[2,14,8,128]{3,2,1,0:T(8,128)S(1)}, u32[]{:S(2)}, u32[]{:S(2)}) collective-permute-start(f32[2,14,8,128]{3,2,1,0:T(8,128)S(1)} %get-tuple-element.26), channel_id=1, source_target_pairs={{0,2},{1,3},{2,0},{3,1},{4,6},{5,7},{6,4},{7,5},{8,10},{9,11},{10,... | collective-permute-start | bytes 344072 | tf_op jit(solution)/shard_map/ppermute | solution.py:469
  20.1 8.2 %collective-permute-start.6 = (f32[4,14,8,128]{3,2,1,0:T(8,128)S(1)}, f32[4,14,8,128]{3,2,1,0:T(8,128)S(1)}, u32[]{:S(2)}, u32[]{:S(2)}) collective-permute-start(f32[4,14,8,128]{3,2,1,0:T(8,128)S(1)} %get-tuple-element.37), channel_id=1, source_target_pairs={{0,1},{1,0},{2,3},{3,2},{4,5},{5,4},{6,7},{7,6},{8,9},{9,8},{10,11... | collective-permute-start | bytes 688136 | tf_op jit(solution)/shard_map/ppermute | solution.py:469
  20.2 6.5 %collective-permute-start.4 = (f32[2,14,8,128]{3,2,1,0:T(8,128)S(1)}, f32[2,14,8,128]{3,2,1,0:T(8,128)S(1)}, u32[]{:S(2)}, u32[]{:S(2)}) collective-permute-start(f32[2,14,8,128]{3,2,1,0:T(8,128)S(1)} %get-tuple-element.34), channel_id=1, source_target_pairs={{0,3},{1,2},{2,1},{3,0},{4,7},{5,6},{6,5},{7,4},{8,11},{9,10},{10,... | collective-permute-start | bytes 344072 | tf_op jit(solution)/shard_map/ppermute | solution.py:469
  22.0 6.3 %collective-permute-start.5 = (f32[2,14,8,128]{3,2,1,0:T(8,128)S(1)}, f32[2,14,8,128]{3,2,1,0:T(8,128)S(1)}, u32[]{:S(2)}, u32[]{:S(2)}) collective-permute-start(f32[2,14,8,128]{3,2,1,0:T(8,128)S(1)} %get-tuple-element.35), channel_id=1, source_target_pairs={{0,2},{1,3},{2,0},{3,1},{4,6},{5,7},{6,4},{7,5},{8,10},{9,11},{10,... | collective-permute-start | bytes 344072 | tf_op jit(solution)/shard_map/ppermute | solution.py:469
  22.3 6.0 %copy-start.3 = (s32[4]{0:T(128)S(1)}, s32[4]{0:T(128)}, u32[]{:S(2)}) copy-start(s32[4]{0:T(128)} %counts.3) | copy-start | bytes 52
  24.9 5.6 %collective-permute-start.8 = (f32[2,14,8,128]{3,2,1,0:T(8,128)S(1)}, f32[2,14,8,128]{3,2,1,0:T(8,128)S(1)}, u32[]{:S(2)}, u32[]{:S(2)}) collective-permute-start(f32[2,14,8,128]{3,2,1,0:T(8,128)S(1)} %get-tuple-element.39), channel_id=1, source_target_pairs={{0,3},{1,2},{2,1},{3,0},{4,7},{5,6},{6,5},{7,4},{8,11},{9,10},{10,... | collective-permute-start | bytes 344072 | tf_op jit(solution)/shard_map/ppermute | solution.py:469
  26.0 7.1 %collective-permute-start.9 = (f32[2,14,8,128]{3,2,1,0:T(8,128)S(1)}, f32[2,14,8,128]{3,2,1,0:T(8,128)S(1)}, u32[]{:S(2)}, u32[]{:S(2)}) collective-permute-start(f32[2,14,8,128]{3,2,1,0:T(8,128)S(1)} %get-tuple-element.40), channel_id=1, source_target_pairs={{0,2},{1,3},{2,0},{3,1},{4,6},{5,7},{6,4},{7,5},{8,10},{9,11},{10,... | collective-permute-start | bytes 344072 | tf_op jit(solution)/shard_map/ppermute | solution.py:469
  26.7 6.4 %collective-permute-start.10 = (f32[2,14,8,128]{3,2,1,0:T(8,128)S(1)}, f32[2,14,8,128]{3,2,1,0:T(8,128)S(1)}, u32[]{:S(2)}, u32[]{:S(2)}) collective-permute-start(f32[2,14,8,128]{3,2,1,0:T(8,128)S(1)} %get-tuple-element.42), channel_id=1, source_target_pairs={{0,1},{1,0},{2,3},{3,2},{4,5},{5,4},{6,7},{7,6},{8,9},{9,8},{10,11... | collective-permute-start | bytes 344072 | tf_op jit(solution)/shard_map/ppermute | solution.py:469

commit v8 on v7

--- a/solution.py
+++ b/solution.py
@@ -90,11 +90,16 @@
 
     def body(i, _):
         level = i // (nj // group)
+        results = []
         for u in range(group):
-            one(level, pl.ds(pl.multiple_of(((i % (nj // group)) * group + u) * LANES, LANES), LANES))
+            lanes = pl.ds(pl.multiple_of(((i % (nj // group)) * group + u) * LANES, LANES), LANES)
+            results += [(level, row, lanes, value) for row, value in one(level, lanes)]
+        for result in results:
+            store(*result)
         return 0
 
     def one(level, lanes):
+        results = []
         for first, last in ranges:
             a = {r: cell(level, r, lanes) for r in range(first - REACH, last + REACH)}
             inter = {f: 7.0 * (a[f - 1] + a[f]) - (a[f - 2] + a[f + 1]) for f in range(first - 1, last + 2)}
@@ -106,7 +111,8 @@
                 upwind = jnp.where(north, a[f - 1], a[f])
                 flux[f] = alpha * inter[f] + beta * behind + gamma * upwind
                 if f > first:
-                    store(level, f - 1, lanes, a[f - 1] - (flux[f] - flux[f - 1]))
+                    results.append((f - 1, a[f - 1] - (flux[f] - flux[f - 1])))
+        return results
 
     lax.fori_loop(0, levels * nj // group, body, 0)
 
@@ -157,7 +163,6 @@
 
 
 def pack_block(block, packed, unit, count, lane):
-    me = lax.axis_index("lev")
     nlon = len(block[0]) * LANES
     width, mains, tail, per, size = packed_sizes(nlon, count)
     for d in range(count):
@@ -167,7 +172,7 @@
                       for m in range(mains + (1 if off else 0))]
             for m in range(mains):
                 whole = jnp.where(lane < LANES - off, turned[m], turned[m + 1]) if off else turned[m]
-                packed[d ^ me, unit, q * mains + m] = whole
+                packed[d, unit, q * mains + m] = whole
         if tail:
             for g in range(-(-BLOCK // per)):
                 total = None
@@ -176,13 +181,24 @@
                     source = block[g * per + place][j0 + mains]
                     moved = pltpu.roll(source, shift, 1) if shift else source
                     total = moved if total is None else jnp.where(lane < place * tail, total, moved)
-                packed[d ^ me, unit, BLOCK * mains + g] = total
+                packed[d, unit, BLOCK * mains + g] = total
+
+
+def copy_tiles(pairs):
+    values = [source[at] for (source, at), _ in pairs]
+    for value, (_, (target, at)) in zip(values, pairs):
+        target[at] = value
 
 
 def copy_units(source, target, start=0):
     for unit in range(source.shape[0]):
-        for i in range(source.shape[1]):
-            target[start + unit, i] = source[unit, i]
+        copy_tiles([((source, (unit, i)), (target, (start + unit, i))) for i in range(source.shape[1])])
+
+
+def hand_out(packed, outs):
+    me = lax.axis_index("lev")
+    for k, out in enumerate(outs):
+        copy_units(packed.at[me ^ k], out)
 
 
 def own_coefficients(rows, joined, winds, cx, cy):
@@ -233,8 +249,7 @@
         pack_block(done, packed, group, count, lane)
 
     lon_pass(work_last, swept, coef_x, inter, west, flux, lane, send)
-    for k in range(count):
-        copy_units(packed.at[k], outs[k])
+    hand_out(packed, outs)
 
 
 def edge_kernel(count, rows, slot, joint, state, first_round, second_round, first, cx, cy, *refs):
@@ -303,8 +318,7 @@
     lon_pass(listed(ends), swept, coef_x, inter, west, flux, lane, keep_edge)
     lat_pass(1, nj, ends_last, cell_first, coef_y, put_last)
     lon_pass(listed(ends_last), swept, coef_x, inter, west, flux, lane, send)
-    for k in range(count):
-        copy_units(packed.at[k], outs[k])
+    hand_out(packed, outs)
     for other in others:
         copy_units(other, outs[1], packed.shape[1])
 
@@ -324,31 +338,36 @@
             out[k, row] = total
 
 
-def remap_kernel(count, depth, plan, numbers, counts, *refs):
-    chunks, (weights, *ready, out, columns) = refs[:len(plan)], refs[len(plan):]
+def remap_kernel(count, plan, numbers, counts, *refs):
+    chunks, (weights, *ready, out, levels, result, sems) = refs[:len(plan)], refs[len(plan):]
     me = lax.axis_index("lev")
+    targets, _, _, width = result.shape
+    _, mains, tail, per, _ = packed_sizes(width * count, count)
+    copies = []
+
+    def leave(source, target):
+        copy = pltpu.make_async_copy(source, target, sems.at[len(copies)])
+        copy.start()
+        copies.append(copy)
+
+    if ready:
+        others = [n for n in range(out.shape[1] // BLOCK) if n not in numbers]
+        leave(ready[0], out.at[:, pl.ds(others[0] * BLOCK, len(others) * BLOCK)])
+
+    def level_of(k, slot):
+        d = me ^ k
+        start = jnp.int32(0)
+        for e in range(count):
+            start = start + jnp.where(e < d, counts[e], 0)
+        return jnp.where(slot < counts[d], start + slot, targets)
+
     for (k, units), chunk in zip(plan, chunks):
         for unit, (slot, number) in enumerate(units):
             if number in numbers:
-                for i in range(chunk.shape[1]):
-                    columns[(me ^ k) * depth + slot, number, i] = chunk[unit, i]
-    first_out = 0 if ready else numbers[0]
-    if ready:
-        copied = [n for n in range(out.shape[1] // BLOCK) if n not in numbers]
-        for k in range(out.shape[0]):
-            for row in range(len(copied) * BLOCK):
-                out[k, copied[0] * BLOCK + row] = ready[0][k, row]
-    targets, _, _, width = out.shape
-    _, mains, tail, per, _ = packed_sizes(width * count, count)
-    slots = []
-    for level in range(targets):
-        slot, start = jnp.int32(level), jnp.int32(0)
-        for d in range(count):
-            slot = jnp.where(level >= start, d * depth + level - start, slot)
-            start = start + counts[d]
-        slots.append(slot)
-
-    def block(number):
+                at = numbers.index(number)
+                copy_tiles([((chunk, (unit, i)), (levels, (level_of(k, slot), at, i))) for i in range(chunk.shape[1])])
+
+    for at, number in enumerate(numbers):
         for q in range(BLOCK):
             row = number * BLOCK + q
             for m in range(mains + (1 if tail else 0)):
@@ -357,24 +376,25 @@
                 values = []
                 for level in range(targets):
                     if m < mains:
-                        values.append(columns[slots[level], number, q * mains + m])
+                        values.append(levels[level, at, q * mains + m])
                     else:
-                        last = columns[slots[level], number, BLOCK * mains + q // per]
+                        last = levels[level, at, BLOCK * mains + q // per]
                         shift = (q % per) * tail
-                        last = pltpu.roll(last, LANES - shift, 1) if shift else last
-                        values.append(last[:, :wide])
+                        values.append(pltpu.roll(last, LANES - shift, 1) if shift else last)
                 for k in range(targets):
                     lowest, highest = max(k - (TAPS - 1), 0), min(k, targets - TAPS) + TAPS - 1
                     total = None
                     for level in range(lowest, highest + 1):
                         j = level - lowest
-                        w = jnp.broadcast_to(weights[k, row, j:j + 1, lanes], (SUB, wide))
-                        term = w * values[level]
+                        term = jnp.broadcast_to(weights[k, row, j:j + 1, lanes], (SUB, wide)) * values[level][:, :wide]
                         total = term if total is None else total + term
-                    out[k, row - first_out * BLOCK, :, lanes] = total
-
-    for number in numbers:
-        block(number)
+                    result[k, at * BLOCK + q, :, lanes] = total
+        if ready:
+            leave(result.at[:, pl.ds(at * BLOCK, BLOCK)], out.at[:, pl.ds(number * BLOCK, BLOCK)])
+    if not ready:
+        leave(result, out)
+    for copy in copies:
+        copy.wait()
 
 
 def tiles_of(array):
@@ -483,12 +503,19 @@
 
     def remap(part, numbers, height, ready):
         args = (level_counts, *chunks[:part], taps, *ready)
-        return call(
-            functools.partial(remap_kernel, count, depth, tuple(plan[:part]), numbers),
-            f32(targets, height, number, width), args,
-            specs=[SMEM] + [VMEM] * (len(args) - 1),
-            scratch=[vmem(count * depth, blocks, size, SUB, LANES)],
-            cost=cost(1, 1))
+        return pl.pallas_call(
+            functools.partial(remap_kernel, count, tuple(plan[:part]), numbers),
+            out_shape=f32(targets, height, number, width),
+            in_specs=[SMEM] + [VMEM] * (len(args) - 1),
+            out_specs=ANY,
+            scratch_shapes=[
+                vmem(targets + 1, len(numbers), size, SUB, LANES),
+                vmem(targets, len(numbers) * BLOCK, number, width),
+                pltpu.SemaphoreType.DMA((len(numbers) + 1,)),
+            ],
+            compiler_params=pltpu.CompilerParams(vmem_limit_bytes=16 << 20),
+            cost_estimate=cost(1, 1),
+        )(*args)
 
     middle_rows = remap(early, tuple(range(1, blocks - 1)), inner * BLOCK, ())
     out = remap(len(chunks), (0, blocks - 1), rows, (middle_rows,))

time: 35.3 us -> 35 us (level)
    pallas_call x7 -> x5, Pallas kernels: 12.1 us -> 9.31 us  [call(): pl.pallas_call(kernel, out_shape=outs, in_specs=specs or [VMEM] * len(arg...]
    pallas_call x0 -> x2, Pallas kernels: none -> 2.78 us  [remap(): pl.pallas_call(functools.partial(remap_kernel, count, tuple(plan[:part]),...]
  transfers between devices with their start and end apart: 11 -> 11, of which waited for: 4 -> 4; matrix products, arithmetic and copies ran while one was open for 0% -> 0% of each run, Pallas kernels for 28% -> 29%
where the time goes in v8:
time: 35 us; the launch traced here: 34.8 us
  Pallas kernels  12.1 us (35%)
  starting transfers between devices  10.2 us (29%)
  waiting for transfers between devices  9.97 us (28%)
  local copies, waits for them, and re-layouts  1.33 us (4%)
  other arithmetic  1.14 us (3%)
    pallas_call x5, Pallas kernels, call(): pl.pallas_call(kernel, out_shape=outs, in_specs=specs or [VMEM] * len(arg...  9.31 us
    ppermute x8, starting transfers between devices, swapped(): return lax.ppermute(sent, 'lev', [(i, i ^ k) for i in range(count)])  5.8 us
    ppermute x8, waiting for transfers between devices, swapped(): return lax.ppermute(sent, 'lev', [(i, i ^ k) for i in range(count)])  5.21 us
    ppermute x1, waiting for transfers between devices, shards(): first_round = lax.ppermute(sent[0], 'lat', first_swap)  4.75 us
    ppermute x1, starting transfers between devices, shards(): first_round = lax.ppermute(sent[0], 'lat', first_swap)  3.09 us
    pallas_call x2, Pallas kernels, remap(): pl.pallas_call(functools.partial(remap_kernel, count, tuple(plan[:part]),...  2.78 us
    ppermute x2, starting transfers between devices, shards(): lax.ppermute(buffer, 'lat', second_swap)  1.34 us
    unnamed x8, local copies, waits for them, and re-layouts  1.33 us
  transfers between devices with their start and end apart: 11, of which 4 were waited for; matrix products, arithmetic and copies ran while one was open for 0% of the time, Pallas kernels for 29%

profile of v8, /device:TPU:0, one launch (start us, length us, event | category | flops | bytes accessed | tf_op | source)
XLA Modules:
  0.0 34.8 jit_solution(2743707170470600511)
XLA Ops:
  0.0 1.1 %pad_maximum_fusion.winds.joined = f32[36,2,1152]{2,1,0:T(2,128)S(1)} fusion(f32[18,2,1152]{2,1,0:T(2,128)} %bitcast.13, f32[18,2,1152]{2,1,0:T(2,128)} %bitcast.14), kind=kLoop, calls=%fused_computation | loop fusion | flops 82944 | bytes 663552 | tf_op jit(solution)/shard_map/concatenate | solution.py:443
  1.1 0.0 copy-start
  1.2 1.3 %copy-done = f32[8,2,18,1152]{3,1,2,0:T(2,128)S(1)} copy-done((f32[8,2,18,1152]{3,1,2,0:T(2,128)S(1)}, f32[8,2,18,1152]{3,1,2,0:T(2,128)}, u32[]{:S(2)}) %copy-start) | copy-done | bytes 1327128
  2.5 0.0 copy-start.1
  2.5 0.0 copy-start.2
  2.5 0.3 shard_map.64
  2.7 3.1 %collective-permute-start.2 = (f32[2,7,8,1152]{3,2,1,0:T(8,128)S(1)}, f32[2,7,8,1152]{3,2,1,0:T(8,128)S(1)}, u32[]{:S(2)}, u32[]{:S(2)}) collective-permute-start(f32[2,7,8,1152]{3,2,1,0:T(8,128)S(1)} %get-tuple-element.28), channel_id=1, source_target_pairs={{0,4},{4,0},{8,12},{12,8},{1,5},{5,1},{9,13},{13,9},{2,6},{6,2},{1... | collective-permute-start | bytes 1548296 | tf_op jit(solution)/shard_map/ppermute | solution.py:451
  5.8 0.7 %collective-permute-start.3 = (f32[7,8,1152]{2,1,0:T(8,128)S(1)}, f32[7,8,1152]{2,1,0:T(8,128)S(1)}, u32[]{:S(2)}, u32[]{:S(2)}) collective-permute-start(f32[7,8,1152]{2,1,0:T(8,128)S(1)} %get-tuple-element.29), channel_id=1, source_target_pairs={{0,0},{4,8},{8,4},{12,12},{1,1},{5,9},{9,5},{13,13},{2,2},{6,10},{... | collective-permute-start | bytes 774152 | tf_op jit(solution)/shard_map/ppermute | solution.py:452
  6.5 0.7 %collective-permute-start.7 = (f32[7,8,1152]{2,1,0:T(8,128)S(1)}, f32[7,8,1152]{2,1,0:T(8,128)S(1)}, u32[]{:S(2)}, u32[]{:S(2)}) collective-permute-start(f32[7,8,1152]{2,1,0:T(8,128)S(1)} %get-tuple-element.38), channel_id=1, source_target_pairs={{0,0},{4,8},{8,4},{12,12},{1,1},{5,9},{9,5},{13,13},{2,2},{6,10},{... | collective-permute-start | bytes 774152 | tf_op jit(solution)/shard_map/ppermute | solution.py:452
  7.2 3.8 %shard_map.65 = (f32[2,14,8,128]{3,2,1,0:T(8,128)S(1)}, f32[2,14,8,128]{3,2,1,0:T(8,128)S(1)}, f32[2,14,8,128]{3,2,1,0:T(8,128)S(1)}, f32[2,14,8,128]{3,2,1,0:T(...) custom-call(f32[2,18,8,1152]{3,2,1,0:T(8,128)S(1)} %get-tuple-element.24., ...), custom_call_target="tpu_custom_call" | custom-call | flops 1 | bytes 1 | tf_op jit(solution)/shard_map/pallas_call | solution.py:414
  11.0 0.7 %collective-permute-start = (f32[2,14,8,128]{3,2,1,0:T(8,128)S(1)}, f32[2,14,8,128]{3,2,1,0:T(8,128)S(1)}, u32[]{:S(2)}, u32[]{:S(2)}) collective-permute-start(f32[2,14,8,128]{3,2,1,0:T(8,128)S(1)} %get-tuple-element.25), channel_id=1, source_target_pairs={{0,3},{1,2},{2,1},{3,0},{4,7},{5,6},{6,5},{7,4},{8,11},{9,10},{10,... | collective-permute-start | bytes 344072 | tf_op jit(solution)/shard_map/ppermute | solution.py:489
  11.7 0.9 %collective-permute-start.1 = (f32[2,14,8,128]{3,2,1,0:T(8,128)S(1)}, f32[2,14,8,128]{3,2,1,0:T(8,128)S(1)}, u32[]{:S(2)}, u32[]{:S(2)}) collective-permute-start(f32[2,14,8,128]{3,2,1,0:T(8,128)S(1)} %get-tuple-element.26), channel_id=1, source_target_pairs={{0,2},{1,3},{2,0},{3,1},{4,6},{5,7},{6,4},{7,5},{8,10},{9,11},{10,... | collective-permute-start | bytes 344072 | tf_op jit(solution)/shard_map/ppermute | solution.py:489
  12.6 0.0 copy-done.1
  12.6 0.0 copy-done.2
  12.6 0.2 shard_map.66.refs_1_.refs_7_.refs_11_
  12.8 0.0 collective-permute-done.3.second_round
  12.8 4.7 %collective-permute-done.2.first_round = f32[2,7,8,1152]{3,2,1,0:T(8,128)S(1)} collective-permute-done((f32[2,7,8,1152]{3,2,1,0:T(8,128)S(1)}, f32[2,7,8,1152]{3,2,1,0:T(8,128)S(1)}, u32[]{:S(2)}, u32[]{:S(2)}) %collective-permute-start.2) | collective-permute-done | bytes 516128 | tf_op jit(solution)/shard_map/ppermute | solution.py:451
  17.6 2.5 %shard_map.67 = (f32[2,14,8,128]{3,2,1,0:T(8,128)S(1)}, f32[4,14,8,128]{3,2,1,0:T(8,128)S(1)}, f32[2,14,8,128]{3,2,1,0:T(8,128)S(1)}, f32[2,14,8,128]{3,2,1,0:T(8,128)S(1)}) custom-call(f32[2,18,8,1152]{3,2,1,0:T(8,128)S(1)} %get-tuple-element.24.state, f32[2,7,8,1152]{3,2,1,0:T(8,128)S(1)} %collective-permute-done.2.first_round, ...), custom_call_target="tpu_custom_call" | custom-call | flops 19906560 | bytes 2654208 | tf_op jit(solution)/shard_map/pallas_call | solution.py:414
  20.1 0.1 collective-permute-start.6
  20.2 1.8 %collective-permute-start.4 = (f32[2,14,8,128]{3,2,1,0:T(8,128)S(1)}, f32[2,14,8,128]{3,2,1,0:T(8,128)S(1)}, u32[]{:S(2)}, u32[]{:S(2)}) collective-permute-start(f32[2,14,8,128]{3,2,1,0:T(8,128)S(1)} %get-tuple-element.34), channel_id=1, source_target_pairs={{0,3},{1,2},{2,1},{3,0},{4,7},{5,6},{6,5},{7,4},{8,11},{9,10},{10,... | collective-permute-start | bytes 344072 | tf_op jit(solution)/shard_map/ppermute | solution.py:489
  22.0 0.0 collective-permute-done.refs_1_.refs_0_
  22.0 0.4 %collective-permute-start.5 = (f32[2,14,8,128]{3,2,1,0:T(8,128)S(1)}, f32[2,14,8,128]{3,2,1,0:T(8,128)S(1)}, u32[]{:S(2)}, u32[]{:S(2)}) collective-permute-start(f32[2,14,8,128]{3,2,1,0:T(8,128)S(1)} %get-tuple-element.35), channel_id=1, source_target_pairs={{0,2},{1,3},{2,0},{3,1},{4,6},{5,7},{6,4},{7,5},{8,10},{9,11},{10,... | collective-permute-start | bytes 344072 | tf_op jit(solution)/shard_map/ppermute | solution.py:489
  22.3 0.0 collective-permute-done.1.refs_2_.refs_1_
  22.3 0.0 collective-permute-done.7.second_round
  22.3 0.0 copy-start.3
  22.3 2.5 %shard_map.68 = (f32[2,14,8,128]{3,2,1,0:T(8,128)S(1)}, f32[2,14,8,128]{3,2,1,0:T(8,128)S(1)}, f32[2,14,8,128]{3,2,1,0:T(8,128)S(1)}, f32[2,14,8,128]{3,2,1,0:T(8,128)S(1)}) custom-call(f32[2,18,8,1152]{3,2,1,0:T(8,128)S(1)} %get-tuple-element.24.state, f32[2,7,8,1152]{3,2,1,0:T(8,128)S(1)} %collective-permute-done.2.first_round, ...), custom_call_target="tpu_custom_call" | custom-call | flops 19906560 | bytes 2654208 | tf_op jit(solution)/shard_map/pallas_call | solution.py:414
  24.9 1.1 %collective-permute-start.8 = (f32[2,14,8,128]{3,2,1,0:T(8,128)S(1)}, f32[2,14,8,128]{3,2,1,0:T(8,128)S(1)}, u32[]{:S(2)}, u32[]{:S(2)}) collective-permute-start(f32[2,14,8,128]{3,2,1,0:T(8,128)S(1)} %get-tuple-element.39), channel_id=1, source_target_pairs={{0,3},{1,2},{2,1},{3,0},{4,7},{5,6},{6,5},{7,4},{8,11},{9,10},{10,... | collective-permute-start | bytes 344072 | tf_op jit(solution)/shard_map/ppermute | solution.py:489
  26.0 0.7 %collective-permute-start.9 = (f32[2,14,8,128]{3,2,1,0:T(8,128)S(1)}, f32[2,14,8,128]{3,2,1,0:T(8,128)S(1)}, u32[]{:S(2)}, u32[]{:S(2)}) collective-permute-start(f32[2,14,8,128]{3,2,1,0:T(8,128)S(1)} %get-tuple-element.40), channel_id=1, source_target_pairs={{0,2},{1,3},{2,0},{3,1},{4,6},{5,7},{6,4},{7,5},{8,10},{9,11},{10,... | collective-permute-start | bytes 344072 | tf_op jit(solution)/shard_map/ppermute | solution.py:489
  26.7 0.0 collective-permute-done.4.refs_3_
  26.7 0.1 collective-permute-start.10
  26.9 1.5 %collective-permute-done.5.refs_4_ = f32[2,14,8,128]{3,2,1,0:T(8,128)S(1)} collective-permute-done((f32[2,14,8,128]{3,2,1,0:T(8,128)S(1)}, f32[2,14,8,128]{3,2,1,0:T(8,128)S(1)}, u32[]{:S(2)}, u32[]{:S(2)}) %collective-permute-start.5) | collective-permute-done | bytes 114720 | tf_op jit(solution)/shard_map/ppermute | solution.py:489
  28.3 0.0 collective-permute-done.6.refs_6_
  28.3 0.0 copy-done.3
  28.3 1.0 %shard_map.69.refs_12_ = f32[6,6,8,288]{3,2,1,0:T(8,128)S(1)} custom-call(s32[4]{0:T(128)S(1)} %copy-done.3, f32[2,14,8,128]{3,2,1,0:T(8,128)S(1)} %collective-permute-done.refs_1_.refs_0_, f32[2,14,8,128]{3,2,1,0:T(8,128)S(1)} %collective-permute-done.1.refs_2_.refs_1_, f32[2,14,8,128]{3,2,1,0:T(8,128)S(1)} %get-tuple-element.27.refs_2_, ...), custom_call_target="tpu_custom_call" | custom-call | flops 1 | bytes 1 | tf_op jit(solution)/shard_map/pallas_call | solution.py:506
  29.3 1.1 %collective-permute-done.8.refs_7_ = f32[2,14,8,128]{3,2,1,0:T(8,128)S(1)} collective-permute-done((f32[2,14,8,128]{3,2,1,0:T(8,128)S(1)}, f32[2,14,8,128]{3,2,1,0:T(8,128)S(1)}, u32[]{:S(2)}, u32[]{:S(2)}) %collective-permute-start.8) | collective-permute-done | bytes 114720 | tf_op jit(solution)/shard_map/ppermute | solution.py:489
  30.5 2.6 %collective-permute-done.9.refs_8_ = f32[2,14,8,128]{3,2,1,0:T(8,128)S(1)} collective-permute-done((f32[2,14,8,128]{3,2,1,0:T(8,128)S(1)}, f32[2,14,8,128]{3,2,1,0:T(8,128)S(1)}, u32[]{:S(2)}, u32[]{:S(2)}) %collective-permute-start.9) | collective-permute-done | bytes 114720 | tf_op jit(solution)/shard_map/ppermute | solution.py:489
  33.1 0.0 collective-permute-done.10.refs_10_
  33.1 1.8 %shard_map.70 = f32[6,18,8,288]{3,2,1,0:T(8,128)} custom-call(s32[4]{0:T(128)S(1)} %copy-done.3, f32[2,14,8,128]{3,2,1,0:T(8,128)S(1)} %collective-permute-done.refs_1_.refs_0_, f32[2,14,8,128]{3,2,1,0:T(8,128)S(1)} %collective-permute-done.1.refs_2_.refs_1_, f32[2,14,8,128]{3,2,1,0:T(8,128)S(1)} %get-tuple-element.27.refs_2_, ...), custom_call_target="tpu_custom_call" | custom-call | flops 1 | bytes 1 | tf_op jit(solution)/shard_map/pallas_call | solution.py:506
Async XLA Ops:
  1.1 1.3 %copy-start = (f32[8,2,18,1152]{3,1,2,0:T(2,128)S(1)}, f32[8,2,18,1152]{3,1,2,0:T(2,128)}, u32[]{:S(2)}) copy-start(f32[8,2,18,1152]{3,1,2,0:T(2,128)} %param.6) | copy-start | bytes 3981316
  2.5 10.1 %copy-start.1 = (f32[4,6,18,288]{3,0,2,1:T(4,128)S(1)}, f32[4,6,18,288]{3,0,2,1:T(4,128)}, u32[]{:S(2)}) copy-start(f32[4,6,18,288]{3,0,2,1:T(4,128)} %param.11) | copy-start | bytes 1492996
  2.5 10.1 %copy-start.2 = (s32[6,18,288]{2,1,0:T(8,128)S(1)}, s32[6,18,288]{2,1,0:T(8,128)}, u32[]{:S(2)}) copy-start(s32[6,18,288]{2,1,0:T(8,128)} %source.1) | copy-start | bytes 373252
  2.7 14.8 %collective-permute-start.2 = (f32[2,7,8,1152]{3,2,1,0:T(8,128)S(1)}, f32[2,7,8,1152]{3,2,1,0:T(8,128)S(1)}, u32[]{:S(2)}, u32[]{:S(2)}) collective-permute-start(f32[2,7,8,1152]{3,2,1,0:T(8,128)S(1)} %get-tuple-element.28), channel_id=1, source_target_pairs={{0,4},{4,0},{8,12},{12,8},{1,5},{5,1},{9,13},{13,9},{2,6},{6,2},{1... | collective-permute-start | bytes 1548296 | tf_op jit(solution)/shard_map/ppermute | solution.py:451
  5.8 7.0 %collective-permute-start.3 = (f32[7,8,1152]{2,1,0:T(8,128)S(1)}, f32[7,8,1152]{2,1,0:T(8,128)S(1)}, u32[]{:S(2)}, u32[]{:S(2)}) collective-permute-start(f32[7,8,1152]{2,1,0:T(8,128)S(1)} %get-tuple-element.29), channel_id=1, source_target_pairs={{0,0},{4,8},{8,4},{12,12},{1,1},{5,9},{9,5},{13,13},{2,2},{6,10},{... | collective-permute-start | bytes 774152 | tf_op jit(solution)/shard_map/ppermute | solution.py:452
  6.5 15.8 %collective-permute-start.7 = (f32[7,8,1152]{2,1,0:T(8,128)S(1)}, f32[7,8,1152]{2,1,0:T(8,128)S(1)}, u32[]{:S(2)}, u32[]{:S(2)}) collective-permute-start(f32[7,8,1152]{2,1,0:T(8,128)S(1)} %get-tuple-element.38), channel_id=1, source_target_pairs={{0,0},{4,8},{8,4},{12,12},{1,1},{5,9},{9,5},{13,13},{2,2},{6,10},{... | collective-permute-start | bytes 774152 | tf_op jit(solution)/shard_map/ppermute | solution.py:452
  11.0 11.0 %collective-permute-start = (f32[2,14,8,128]{3,2,1,0:T(8,128)S(1)}, f32[2,14,8,128]{3,2,1,0:T(8,128)S(1)}, u32[]{:S(2)}, u32[]{:S(2)}) collective-permute-start(f32[2,14,8,128]{3,2,1,0:T(8,128)S(1)} %get-tuple-element.25), channel_id=1, source_target_pairs={{0,3},{1,2},{2,1},{3,0},{4,7},{5,6},{6,5},{7,4},{8,11},{9,10},{10,... | collective-permute-start | bytes 344072 | tf_op jit(solution)/shard_map/ppermute | solution.py:489
  11.7 10.6 %collective-permute-start.1 = (f32[2,14,8,128]{3,2,1,0:T(8,128)S(1)}, f32[2,14,8,128]{3,2,1,0:T(8,128)S(1)}, u32[]{:S(2)}, u32[]{:S(2)}) collective-permute-start(f32[2,14,8,128]{3,2,1,0:T(8,128)S(1)} %get-tuple-element.26), channel_id=1, source_target_pairs={{0,2},{1,3},{2,0},{3,1},{4,6},{5,7},{6,4},{7,5},{8,10},{9,11},{10,... | collective-permute-start | bytes 344072 | tf_op jit(solution)/shard_map/ppermute | solution.py:489
  20.1 8.2 %collective-permute-start.6 = (f32[4,14,8,128]{3,2,1,0:T(8,128)S(1)}, f32[4,14,8,128]{3,2,1,0:T(8,128)S(1)}, u32[]{:S(2)}, u32[]{:S(2)}) collective-permute-start(f32[4,14,8,128]{3,2,1,0:T(8,128)S(1)} %get-tuple-element.37), channel_id=1, source_target_pairs={{0,1},{1,0},{2,3},{3,2},{4,5},{5,4},{6,7},{7,6},{8,9},{9,8},{10,11... | collective-permute-start | bytes 688136 | tf_op jit(solution)/shard_map/ppermute | solution.py:489
  20.2 6.5 %collective-permute-start.4 = (f32[2,14,8,128]{3,2,1,0:T(8,128)S(1)}, f32[2,14,8,128]{3,2,1,0:T(8,128)S(1)}, u32[]{:S(2)}, u32[]{:S(2)}) collective-permute-start(f32[2,14,8,128]{3,2,1,0:T(8,128)S(1)} %get-tuple-element.34), channel_id=1, source_target_pairs={{0,3},{1,2},{2,1},{3,0},{4,7},{5,6},{6,5},{7,4},{8,11},{9,10},{10,... | collective-permute-start | bytes 344072 | tf_op jit(solution)/shard_map/ppermute | solution.py:489
  22.0 6.3 %collective-permute-start.5 = (f32[2,14,8,128]{3,2,1,0:T(8,128)S(1)}, f32[2,14,8,128]{3,2,1,0:T(8,128)S(1)}, u32[]{:S(2)}, u32[]{:S(2)}) collective-permute-start(f32[2,14,8,128]{3,2,1,0:T(8,128)S(1)} %get-tuple-element.35), channel_id=1, source_target_pairs={{0,2},{1,3},{2,0},{3,1},{4,6},{5,7},{6,4},{7,5},{8,10},{9,11},{10,... | collective-permute-start | bytes 344072 | tf_op jit(solution)/shard_map/ppermute | solution.py:489
  22.3 6.0 %copy-start.3 = (s32[4]{0:T(128)S(1)}, s32[4]{0:T(128)}, u32[]{:S(2)}) copy-start(s32[4]{0:T(128)} %counts.3) | copy-start | bytes 52
  24.9 5.6 %collective-permute-start.8 = (f32[2,14,8,128]{3,2,1,0:T(8,128)S(1)}, f32[2,14,8,128]{3,2,1,0:T(8,128)S(1)}, u32[]{:S(2)}, u32[]{:S(2)}) collective-permute-start(f32[2,14,8,128]{3,2,1,0:T(8,128)S(1)} %get-tuple-element.39), channel_id=1, source_target_pairs={{0,3},{1,2},{2,1},{3,0},{4,7},{5,6},{6,5},{7,4},{8,11},{9,10},{10,... | collective-permute-start | bytes 344072 | tf_op jit(solution)/shard_map/ppermute | solution.py:489
  26.0 7.1 %collective-permute-start.9 = (f32[2,14,8,128]{3,2,1,0:T(8,128)S(1)}, f32[2,14,8,128]{3,2,1,0:T(8,128)S(1)}, u32[]{:S(2)}, u32[]{:S(2)}) collective-permute-start(f32[2,14,8,128]{3,2,1,0:T(8,128)S(1)} %get-tuple-element.40), channel_id=1, source_target_pairs={{0,2},{1,3},{2,0},{3,1},{4,6},{5,7},{6,4},{7,5},{8,10},{9,11},{10,... | collective-permute-start | bytes 344072 | tf_op jit(solution)/shard_map/ppermute | solution.py:489
  26.7 6.4 %collective-permute-start.10 = (f32[2,14,8,128]{3,2,1,0:T(8,128)S(1)}, f32[2,14,8,128]{3,2,1,0:T(8,128)S(1)}, u32[]{:S(2)}, u32[]{:S(2)}) collective-permute-start(f32[2,14,8,128]{3,2,1,0:T(8,128)S(1)} %get-tuple-element.42), channel_id=1, source_target_pairs={{0,1},{1,0},{2,3},{3,2},{4,5},{5,4},{6,7},{7,6},{8,9},{9,8},{10,11... | collective-permute-start | bytes 344072 | tf_op jit(solution)/shard_map/ppermute | solution.py:489

commit v9 on v8

--- a/solution.py
+++ b/solution.py
@@ -53,15 +53,28 @@
     return width, mains, tail, per, BLOCK * mains + tails
 
 
-def prep_kernel(rows, tracers, winds, state, first_round, *second_rounds):
+def fill_halos(rows, slot, state, winds, first_round, second_round):
+    band, bands = lax.axis_index("lat"), lax.axis_size("lat")
+    even = band % 2 == 0
+    keep = jnp.where((band == 0) | (band == bands - 1), 0.0, 1.0)
+    for target, north, scale in ((first_round, even, None), (second_round, jnp.logical_not(even), keep)):
+        scaled = (lambda v: v) if scale is None else (lambda v: v * scale)
+        row_t = jnp.where(north, rows - HALO, 0)
+        row_x = jnp.where(north, rows - REACH, 0)
+        row_y = jnp.where(north, rows - REACH - 1, 0)
+        for row in range(HALO):
+            target[row] = scaled(state[slot, row_t + row])
+        for q in range(REACH):
+            target[HALO, q:q + 1, :] = scaled(winds[row_x + q, slot:slot + 1, :])
+        for q in range(REACH + 1):
+            target[HALO, REACH + q:REACH + q + 1, :] = scaled(winds[rows + row_y + q, slot:slot + 1, :])
+
+
+def prep_kernel(rows, tracers, winds, state, first_round, second_round):
     levels, nlon = state.shape[0], state.shape[3]
     nj = nlon // LANES
     row_stride = nj * levels
     tracer_stride = rows * row_stride
-    band, bands = lax.axis_index("lat"), lax.axis_size("lat")
-    even = band % 2 == 0
-    alone = (band == 0) | (band == bands - 1)
-    keep = jnp.where(alone, 0.0, 1.0)
 
     def body(row, _):
         for level in range(levels):
@@ -71,18 +84,7 @@
         return 0
 
     lax.fori_loop(0, rows, body, 0)
-    for level in range(levels):
-        for target, north, scale in ((first_round.at[level], even, None), (second_rounds[level], jnp.logical_not(even), keep)):
-            scaled = (lambda v: v) if scale is None else (lambda v: v * scale)
-            row_t = jnp.where(north, rows - HALO, 0)
-            row_x = jnp.where(north, rows - REACH, 0)
-            row_y = jnp.where(north, rows - REACH - 1, 0)
-            for row in range(HALO):
-                target[row] = scaled(state[level, row_t + row])
-            for q in range(REACH):
-                target[HALO, q:q + 1, :] = scaled(winds[row_x + q, level:level + 1, :])
-            for q in range(REACH + 1):
-                target[HALO, REACH + q:REACH + q + 1, :] = scaled(winds[rows + row_y + q, level:level + 1, :])
+    fill_halos(rows, 0, state, winds, first_round, second_round)
 
 
 def lat_pass(levels, nj, ranges, cell, coef, store):
@@ -223,10 +225,13 @@
 
 
 def interior_kernel(count, rows, state, joined, *refs):
-    outs, (first, cx, cy, packed, winds, swept, inter, west, flux) = refs[:count], refs[count:]
+    outs, (first, cx, cy), refs = refs[:count], refs[count:count + 3], refs[count + 3:]
+    halos, (packed, winds, swept, inter, west, flux) = refs[:-6], refs[-6:]
     levels, nlon = state.shape[0], state.shape[3]
     nj = nlon // LANES
     lane = lane_ids()
+    for slot in range(1, levels):
+        fill_halos(rows, slot, state, joined, *halos[2 * slot - 2:2 * slot])
     own_coefficients(rows, joined, winds, cx, cy)
     coef_x = lambda i, level, r, lanes: cx[i, level, r:r + 1, lanes]
     coef_y = lambda i, level, f, lanes: cy[i, level, f:f + 1, lanes]
@@ -261,7 +266,7 @@
     odd = lax.axis_index("lat") % 2 == 1
 
     def halo(south, *at):
-        one, two = first_round[(slot,) + at], second_round[at]
+        one, two = first_round[at], second_round[at]
         return jnp.where(odd, one, two) if south else jnp.where(odd, two, one)
 
     for end, south in enumerate((True, False)):
@@ -441,15 +446,18 @@
 
     raw = tiles_of(jnp.transpose(tracers, (0, 2, 1, 3)))
     joined = jnp.concatenate([jnp.transpose(wind_x, (1, 0, 2)), jnp.transpose(wind_y, (1, 0, 2))], axis=0)
-    halo = (HALO + 1, number, nlon)
+    halo = f32(HALO + 1, number, nlon)
     state, *sent = call(
         functools.partial(prep_kernel, rows),
-        [f32(depth, rows, number, nlon), f32(depth, *halo)] + [f32(*halo)] * depth, (raw, joined),
+        [f32(depth, rows, number, nlon), halo, halo], (raw, joined),
         cost=cost(1, 1))
-    first_swap = [(i, i ^ 1) for i in range(bands)]
-    second_swap = [(i, i if i in (0, bands - 1) else ((i - 1) ^ 1) + 1) for i in range(bands)]
-    first_round = lax.ppermute(sent[0], "lat", first_swap)
-    second_rounds = [lax.ppermute(buffer, "lat", second_swap) for buffer in sent[1:]]
+    swaps = ([(i, i ^ 1) for i in range(bands)],
+             [(i, i if i in (0, bands - 1) else ((i - 1) ^ 1) + 1) for i in range(bands)])
+
+    def beside(sent):
+        return [lax.ppermute(buffer, "lat", pairs) for buffer, pairs in zip(sent, swaps)]
+
+    rounds = [beside(sent)]
     taps = call(
         weights_kernel, f32(targets, rows, SUB, width),
         (jnp.transpose(remap_weight, (1, 2, 0, 3)), source_level),
@@ -467,16 +475,17 @@
     stage = vmem(depth * (rows - 2 * REACH), number, nlon)
     result = call(
         functools.partial(interior_kernel, count, rows),
-        [f32(*box(depth * inner))] * count + [f32(depth, rows - 2 * REACH, number, nlon), coef, coef],
+        [f32(*box(depth * inner))] * count + [f32(depth, rows - 2 * REACH, number, nlon), coef, coef] + [halo] * (2 * depth - 2),
         (state, joined), scratch=[vmem(*box(depth * inner, count)), vmem(2, depth, held, nlon), swept, stage, stage, stage],
         cost=cost(1, 1))
-    middle, (first, cx, cy) = result[:count], result[count:]
+    middle, (first, cx, cy), sent = result[:count], result[count:count + 3], result[count + 3:]
+    rounds += [beside(sent[2 * i:2 * i + 2]) for i in range(depth - 1)]
     plan, chunks = [], []
     swept = vmem(1, 2 * HALO, number, nlon)
     stage = vmem(2 * HALO, number, nlon)
 
     def edge(slot, joint, after):
-        args = (state, first_round, second_rounds[slot], first, cx, cy, *joint, *after)
+        args = (state, *rounds[slot], first, cx, cy, *joint, *after)
         units = 2 + (joint[0].shape[0] if joint else 0)
         return call(
             functools.partial(edge_kernel, count, rows, slot, len(joint)),

time: 35 us -> 35.9 us (1.026)
  starting transfers between devices: 10.2 us -> 13.7 us
  waiting for transfers between devices: 9.97 us -> 7.34 us
    ppermute x3 -> x4, waiting for transfers between devices: 4.75 us -> 0.01 us  [beside(): lax.ppermute(buffer, 'lat', pairs)]
    ppermute x3 -> x4, starting transfers between devices: 4.43 us -> 8.87 us  [beside(): lax.ppermute(buffer, 'lat', pairs)]
    ppermute x8, waiting for transfers between devices: 5.21 us -> 7.33 us  [swapped(): return lax.ppermute(sent, 'lev', [(i, i ^ k) for i in range(count)])]
    ppermute x8, starting transfers between devices: 5.8 us -> 4.82 us  [swapped(): return lax.ppermute(sent, 'lev', [(i, i ^ k) for i in range(count)])]
  transfers between devices with their start and end apart: 11 -> 12, of which waited for: 4 -> 5; matrix products, arithmetic and copies ran while one was open for 0% -> 0% of each run, Pallas kernels for 29% -> 28%
where the time goes in v9:
time: 35.9 us; the launch traced here: 35.7 us
  starting transfers between devices  13.7 us (38%)
  Pallas kernels  12.1 us (34%)
  waiting for transfers between devices  7.34 us (20%)
  local copies, waits for them, and re-layouts  1.33 us (4%)
  other arithmetic  1.14 us (3%)
    pallas_call x5, Pallas kernels, call(): pl.pallas_call(kernel, out_shape=outs, in_specs=specs or [VMEM] * len(arg...  9.35 us
    ppermute x4, starting transfers between devices, beside(): lax.ppermute(buffer, 'lat', pairs)  8.87 us
    ppermute x8, waiting for transfers between devices, swapped(): return lax.ppermute(sent, 'lev', [(i, i ^ k) for i in range(count)])  7.33 us
    ppermute x8, starting transfers between devices, swapped(): return lax.ppermute(sent, 'lev', [(i, i ^ k) for i in range(count)])  4.82 us
    pallas_call x2, Pallas kernels, remap(): pl.pallas_call(functools.partial(remap_kernel, count, tuple(plan[:part]),...  2.78 us
    unnamed x8, local copies, waits for them, and re-layouts  1.33 us
    concatenate x1, other arithmetic, shards(): jnp.concatenate([jnp.transpose(wind_x, (1, 0, 2)), jnp.transpose(wind_y,...  1.14 us
  transfers between devices with their start and end apart: 12, of which 5 were waited for; matrix products, arithmetic and copies ran while one was open for 0% of the time, Pallas kernels for 28%

profile of v9, /device:TPU:0, one launch (start us, length us, event | category | flops | bytes accessed | tf_op | source)
XLA Modules:
  0.0 35.7 jit_solution(11288989460935131514)
XLA Ops:
  0.0 1.1 %pad_maximum_fusion.winds.joined = f32[36,2,1152]{2,1,0:T(2,128)S(1)} fusion(f32[18,2,1152]{2,1,0:T(2,128)} %bitcast.13, f32[18,2,1152]{2,1,0:T(2,128)} %bitcast.14), kind=kLoop, calls=%fused_computation | loop fusion | flops 82944 | bytes 663552 | tf_op jit(solution)/shard_map/concatenate | solution.py:448
  1.1 0.0 copy-start
  1.2 1.3 %copy-done = f32[8,2,18,1152]{3,1,2,0:T(2,128)S(1)} copy-done((f32[8,2,18,1152]{3,1,2,0:T(2,128)S(1)}, f32[8,2,18,1152]{3,1,2,0:T(2,128)}, u32[]{:S(2)}) %copy-start) | copy-done | bytes 1327128
  2.5 0.0 copy-start.1
  2.5 0.0 copy-start.2
  2.5 0.2 shard_map.64
  2.7 3.1 %collective-permute-start.2 = (f32[7,8,1152]{2,1,0:T(8,128)S(1)}, f32[7,8,1152]{2,1,0:T(8,128)S(1)}, u32[]{:S(2)}, u32[]{:S(2)}) collective-permute-start(f32[7,8,1152]{2,1,0:T(8,128)S(1)} %get-tuple-element.29), channel_id=1, source_target_pairs={{0,4},{4,0},{8,12},{12,8},{1,5},{5,1},{9,13},{13,9},{2,6},{6,2},{1... | collective-permute-start | bytes 774152 | tf_op jit(solution)/shard_map/ppermute | solution.py:458
  5.8 0.7 %collective-permute-start.3 = (f32[7,8,1152]{2,1,0:T(8,128)S(1)}, f32[7,8,1152]{2,1,0:T(8,128)S(1)}, u32[]{:S(2)}, u32[]{:S(2)}) collective-permute-start(f32[7,8,1152]{2,1,0:T(8,128)S(1)} %get-tuple-element.30), channel_id=1, source_target_pairs={{0,0},{4,8},{8,4},{12,12},{1,1},{5,9},{9,5},{13,13},{2,2},{6,10},{... | collective-permute-start | bytes 774152 | tf_op jit(solution)/shard_map/ppermute | solution.py:458
  6.5 3.8 %shard_map.65 = (f32[2,14,8,128]{3,2,1,0:T(8,128)S(1)}, f32[2,14,8,128]{3,2,1,0:T(8,128)S(1)}, f32[2,14,8,128]{3,2,1,0:T(8,128)S(1)}, f32[2,14,8,128]{3,2,1,0:T(...) custom-call(f32[2,18,8,1152]{3,2,1,0:T(8,128)S(1)} %get-tuple-elemen, ...), custom_call_target="tpu_custom_call" | custom-call | flops 1 | bytes 1 | tf_op jit(solution)/shard_map/pallas_call | solution.py:419
  10.3 4.5 %collective-permute-start.7 = (f32[7,8,1152]{2,1,0:T(8,128)S(1)}, f32[7,8,1152]{2,1,0:T(8,128)S(1)}, u32[]{:S(2)}, u32[]{:S(2)}) collective-permute-start(f32[7,8,1152]{2,1,0:T(8,128)S(1)} %get-tuple-element.39), channel_id=1, source_target_pairs={{0,4},{4,0},{8,12},{12,8},{1,5},{5,1},{9,13},{13,9},{2,6},{6,2},{1... | collective-permute-start | bytes 774152 | tf_op jit(solution)/shard_map/ppermute | solution.py:458
  14.8 0.7 %collective-permute-start.8 = (f32[7,8,1152]{2,1,0:T(8,128)S(1)}, f32[7,8,1152]{2,1,0:T(8,128)S(1)}, u32[]{:S(2)}, u32[]{:S(2)}) collective-permute-start(f32[7,8,1152]{2,1,0:T(8,128)S(1)} %get-tuple-element.40), channel_id=1, source_target_pairs={{0,0},{4,8},{8,4},{12,12},{1,1},{5,9},{9,5},{13,13},{2,2},{6,10},{... | collective-permute-start | bytes 774152 | tf_op jit(solution)/shard_map/ppermute | solution.py:458
  15.4 0.2 collective-permute-start
  15.6 0.0 copy-done.1
  15.6 0.0 copy-done.2
  15.6 0.2 shard_map.66.refs_1_.refs_7_.refs_11_
  15.8 0.0 collective-permute-done.2.first_round
  15.8 1.5 %collective-permute-start.1 = (f32[2,14,8,128]{3,2,1,0:T(8,128)S(1)}, f32[2,14,8,128]{3,2,1,0:T(8,128)S(1)}, u32[]{:S(2)}, u32[]{:S(2)}) collective-permute-start(f32[2,14,8,128]{3,2,1,0:T(8,128)S(1)} %get-tuple-element.27), channel_id=1, source_target_pairs={{0,2},{1,3},{2,0},{3,1},{4,6},{5,7},{6,4},{7,5},{8,10},{9,11},{10,... | collective-permute-start | bytes 344072 | tf_op jit(solution)/shard_map/ppermute | solution.py:498
  17.3 0.0 collective-permute-done.3.second_round
  17.3 2.5 %shard_map.67 = (f32[2,14,8,128]{3,2,1,0:T(8,128)S(1)}, f32[4,14,8,128]{3,2,1,0:T(8,128)S(1)}, f32[2,14,8,128]{3,2,1,0:T(8,128)S(1)}, f32[2,14,8,128]{3,2,1,0:T(8,128)S(1)}) custom-call(f32[2,18,8,1152]{3,2,1,0:T(8,128)S(1)} %get-tuple-element.25.state, f32[7,8,1152]{2,1,0:T(8,128)S(1)} %collective-permute-done.2.first_round, ...), custom_call_target="tpu_custom_call" | custom-call | flops 19906560 | bytes 2654208 | tf_op jit(solution)/shard_map/pallas_call | solution.py:419
  19.9 0.4 %collective-permute-start.6 = (f32[4,14,8,128]{3,2,1,0:T(8,128)S(1)}, f32[4,14,8,128]{3,2,1,0:T(8,128)S(1)}, u32[]{:S(2)}, u32[]{:S(2)}) collective-permute-start(f32[4,14,8,128]{3,2,1,0:T(8,128)S(1)} %get-tuple-element.38), channel_id=1, source_target_pairs={{0,1},{1,0},{2,3},{3,2},{4,5},{5,4},{6,7},{7,6},{8,9},{9,8},{10,11... | collective-permute-start | bytes 688136 | tf_op jit(solution)/shard_map/ppermute | solution.py:498
  20.3 0.6 %collective-permute-done.refs_1_.refs_0_ = f32[2,14,8,128]{3,2,1,0:T(8,128)S(1)} collective-permute-done((f32[2,14,8,128]{3,2,1,0:T(8,128)S(1)}, f32[2,14,8,128]{3,2,1,0:T(8,128)S(1)}, u32[]{:S(2)}, u32[]{:S(2)}) %collective-permute-start) | collective-permute-done | bytes 114720 | tf_op jit(solution)/shard_map/ppermute | solution.py:498
  20.9 0.6 %collective-permute-start.4 = (f32[2,14,8,128]{3,2,1,0:T(8,128)S(1)}, f32[2,14,8,128]{3,2,1,0:T(8,128)S(1)}, u32[]{:S(2)}, u32[]{:S(2)}) collective-permute-start(f32[2,14,8,128]{3,2,1,0:T(8,128)S(1)} %get-tuple-element.35), channel_id=1, source_target_pairs={{0,3},{1,2},{2,1},{3,0},{4,7},{5,6},{6,5},{7,4},{8,11},{9,10},{10,... | collective-permute-start | bytes 344072 | tf_op jit(solution)/shard_map/ppermute | solution.py:498
  21.5 1.9 %collective-permute-done.1.refs_2_.refs_1_ = f32[2,14,8,128]{3,2,1,0:T(8,128)S(1)} collective-permute-done((f32[2,14,8,128]{3,2,1,0:T(8,128)S(1)}, f32[2,14,8,128]{3,2,1,0:T(8,128)S(1)}, u32[]{:S(2)}, u32[]{:S(2)}) %collective-permute-start.1) | collective-permute-done | bytes 114720 | tf_op jit(solution)/shard_map/ppermute | solution.py:498
  23.4 0.0 collective-permute-start.5
  23.4 0.0 collective-permute-done.7.first_round
  23.4 0.0 collective-permute-done.8.second_round
  23.4 0.0 copy-start.3
  23.4 2.5 %shard_map.68 = (f32[2,14,8,128]{3,2,1,0:T(8,128)S(1)}, f32[2,14,8,128]{3,2,1,0:T(8,128)S(1)}, f32[2,14,8,128]{3,2,1,0:T(8,128)S(1)}, f32[2,14,8,128]{3,2,1,0:T(8,128)S(1)}) custom-call(f32[2,18,8,1152]{3,2,1,0:T(8,128)S(1)} %get-tuple-element.25.state, f32[7,8,1152]{2,1,0:T(8,128)S(1)} %collective-permute-done.7.first_round, ...), custom_call_target="tpu_custom_call" | custom-call | flops 19906560 | bytes 2654208 | tf_op jit(solution)/shard_map/pallas_call | solution.py:419
  26.0 1.5 %collective-permute-start.9 = (f32[2,14,8,128]{3,2,1,0:T(8,128)S(1)}, f32[2,14,8,128]{3,2,1,0:T(8,128)S(1)}, u32[]{:S(2)}, u32[]{:S(2)}) collective-permute-start(f32[2,14,8,128]{3,2,1,0:T(8,128)S(1)} %get-tuple-element.41), channel_id=1, source_target_pairs={{0,3},{1,2},{2,1},{3,0},{4,7},{5,6},{6,5},{7,4},{8,11},{9,10},{10,... | collective-permute-start | bytes 344072 | tf_op jit(solution)/shard_map/ppermute | solution.py:498
  27.5 0.7 %collective-permute-start.10 = (f32[2,14,8,128]{3,2,1,0:T(8,128)S(1)}, f32[2,14,8,128]{3,2,1,0:T(8,128)S(1)}, u32[]{:S(2)}, u32[]{:S(2)}) collective-permute-start(f32[2,14,8,128]{3,2,1,0:T(8,128)S(1)} %get-tuple-element.42), channel_id=1, source_target_pairs={{0,2},{1,3},{2,0},{3,1},{4,6},{5,7},{6,4},{7,5},{8,10},{9,11},{10,... | collective-permute-start | bytes 344072 | tf_op jit(solution)/shard_map/ppermute | solution.py:498
  28.1 0.0 collective-permute-done.4.refs_3_
  28.1 0.0 collective-permute-start.11
  28.2 0.6 %collective-permute-done.5.refs_4_ = f32[2,14,8,128]{3,2,1,0:T(8,128)S(1)} collective-permute-done((f32[2,14,8,128]{3,2,1,0:T(8,128)S(1)}, f32[2,14,8,128]{3,2,1,0:T(8,128)S(1)}, u32[]{:S(2)}, u32[]{:S(2)}) %collective-permute-start.5) | collective-permute-done | bytes 114720 | tf_op jit(solution)/shard_map/ppermute | solution.py:498
  28.8 0.0 collective-permute-done.6.refs_6_
  28.8 0.0 copy-done.3
  28.8 1.0 %shard_map.69.refs_12_ = f32[6,6,8,288]{3,2,1,0:T(8,128)S(1)} custom-call(s32[4]{0:T(128)S(1)} %copy-done.3, f32[2,14,8,128]{3,2,1,0:T(8,128)S(1)} %collective-permute-done.refs_1_.refs_0_, f32[2,14,8,128]{3,2,1,0:T(8,128)S(1)} %collective-permute-done.1.refs_2_.refs_1_, f32[2,14,8,128]{3,2,1,0:T(8,128)S(1)} %get-tuple-element.28.refs_2_, ...), custom_call_target="tpu_custom_call" | custom-call | flops 1 | bytes 1 | tf_op jit(solution)/shard_map/pallas_call | solution.py:515
  29.8 1.2 %collective-permute-done.9.refs_7_ = f32[2,14,8,128]{3,2,1,0:T(8,128)S(1)} collective-permute-done((f32[2,14,8,128]{3,2,1,0:T(8,128)S(1)}, f32[2,14,8,128]{3,2,1,0:T(8,128)S(1)}, u32[]{:S(2)}, u32[]{:S(2)}) %collective-permute-start.9) | collective-permute-done | bytes 114720 | tf_op jit(solution)/shard_map/ppermute | solution.py:498
  31.0 3.0 %collective-permute-done.10.refs_8_ = f32[2,14,8,128]{3,2,1,0:T(8,128)S(1)} collective-permute-done((f32[2,14,8,128]{3,2,1,0:T(8,128)S(1)}, f32[2,14,8,128]{3,2,1,0:T(8,128)S(1)}, u32[]{:S(2)}, u32[]{:S(2)}) %collective-permute-start.10) | collective-permute-done | bytes 114720 | tf_op jit(solution)/shard_map/ppermute | solution.py:498
  34.0 0.0 collective-permute-done.11.refs_10_
  34.0 1.8 %shard_map.70 = f32[6,18,8,288]{3,2,1,0:T(8,128)} custom-call(s32[4]{0:T(128)S(1)} %copy-done.3, f32[2,14,8,128]{3,2,1,0:T(8,128)S(1)} %collective-permute-done.refs_1_.refs_0_, f32[2,14,8,128]{3,2,1,0:T(8,128)S(1)} %collective-permute-done.1.refs_2_.refs_1_, f32[2,14,8,128]{3,2,1,0:T(8,128)S(1)} %get-tuple-element.28.refs_2_, ...), custom_call_target="tpu_custom_call" | custom-call | flops 1 | bytes 1 | tf_op jit(solution)/shard_map/pallas_call | solution.py:515
Async XLA Ops:
  1.1 1.3 %copy-start = (f32[8,2,18,1152]{3,1,2,0:T(2,128)S(1)}, f32[8,2,18,1152]{3,1,2,0:T(2,128)}, u32[]{:S(2)}) copy-start(f32[8,2,18,1152]{3,1,2,0:T(2,128)} %param.6) | copy-start | bytes 3981316
  2.5 13.1 %copy-start.1 = (f32[4,6,18,288]{3,0,2,1:T(4,128)S(1)}, f32[4,6,18,288]{3,0,2,1:T(4,128)}, u32[]{:S(2)}) copy-start(f32[4,6,18,288]{3,0,2,1:T(4,128)} %param.11) | copy-start | bytes 1492996
  2.5 13.1 %copy-start.2 = (s32[6,18,288]{2,1,0:T(8,128)S(1)}, s32[6,18,288]{2,1,0:T(8,128)}, u32[]{:S(2)}) copy-start(s32[6,18,288]{2,1,0:T(8,128)} %source.1) | copy-start | bytes 373252
  2.7 13.1 %collective-permute-start.2 = (f32[7,8,1152]{2,1,0:T(8,128)S(1)}, f32[7,8,1152]{2,1,0:T(8,128)S(1)}, u32[]{:S(2)}, u32[]{:S(2)}) collective-permute-start(f32[7,8,1152]{2,1,0:T(8,128)S(1)} %get-tuple-element.29), channel_id=1, source_target_pairs={{0,4},{4,0},{8,12},{12,8},{1,5},{5,1},{9,13},{13,9},{2,6},{6,2},{1... | collective-permute-start | bytes 774152 | tf_op jit(solution)/shard_map/ppermute | solution.py:458
  5.8 11.5 %collective-permute-start.3 = (f32[7,8,1152]{2,1,0:T(8,128)S(1)}, f32[7,8,1152]{2,1,0:T(8,128)S(1)}, u32[]{:S(2)}, u32[]{:S(2)}) collective-permute-start(f32[7,8,1152]{2,1,0:T(8,128)S(1)} %get-tuple-element.30), channel_id=1, source_target_pairs={{0,0},{4,8},{8,4},{12,12},{1,1},{5,9},{9,5},{13,13},{2,2},{6,10},{... | collective-permute-start | bytes 774152 | tf_op jit(solution)/shard_map/ppermute | solution.py:458
  10.3 13.1 %collective-permute-start.7 = (f32[7,8,1152]{2,1,0:T(8,128)S(1)}, f32[7,8,1152]{2,1,0:T(8,128)S(1)}, u32[]{:S(2)}, u32[]{:S(2)}) collective-permute-start(f32[7,8,1152]{2,1,0:T(8,128)S(1)} %get-tuple-element.39), channel_id=1, source_target_pairs={{0,4},{4,0},{8,12},{12,8},{1,5},{5,1},{9,13},{13,9},{2,6},{6,2},{1... | collective-permute-start | bytes 774152 | tf_op jit(solution)/shard_map/ppermute | solution.py:458
  14.8 8.7 %collective-permute-start.8 = (f32[7,8,1152]{2,1,0:T(8,128)S(1)}, f32[7,8,1152]{2,1,0:T(8,128)S(1)}, u32[]{:S(2)}, u32[]{:S(2)}) collective-permute-start(f32[7,8,1152]{2,1,0:T(8,128)S(1)} %get-tuple-element.40), channel_id=1, source_target_pairs={{0,0},{4,8},{8,4},{12,12},{1,1},{5,9},{9,5},{13,13},{2,2},{6,10},{... | collective-permute-start | bytes 774152 | tf_op jit(solution)/shard_map/ppermute | solution.py:458
  15.4 5.5 %collective-permute-start = (f32[2,14,8,128]{3,2,1,0:T(8,128)S(1)}, f32[2,14,8,128]{3,2,1,0:T(8,128)S(1)}, u32[]{:S(2)}, u32[]{:S(2)}) collective-permute-start(f32[2,14,8,128]{3,2,1,0:T(8,128)S(1)} %get-tuple-element.26), channel_id=1, source_target_pairs={{0,3},{1,2},{2,1},{3,0},{4,7},{5,6},{6,5},{7,4},{8,11},{9,10},{10,... | collective-permute-start | bytes 344072 | tf_op jit(solution)/shard_map/ppermute | solution.py:498
  15.8 7.6 %collective-permute-start.1 = (f32[2,14,8,128]{3,2,1,0:T(8,128)S(1)}, f32[2,14,8,128]{3,2,1,0:T(8,128)S(1)}, u32[]{:S(2)}, u32[]{:S(2)}) collective-permute-start(f32[2,14,8,128]{3,2,1,0:T(8,128)S(1)} %get-tuple-element.27), channel_id=1, source_target_pairs={{0,2},{1,3},{2,0},{3,1},{4,6},{5,7},{6,4},{7,5},{8,10},{9,11},{10,... | collective-permute-start | bytes 344072 | tf_op jit(solution)/shard_map/ppermute | solution.py:498
  19.9 9.0 %collective-permute-start.6 = (f32[4,14,8,128]{3,2,1,0:T(8,128)S(1)}, f32[4,14,8,128]{3,2,1,0:T(8,128)S(1)}, u32[]{:S(2)}, u32[]{:S(2)}) collective-permute-start(f32[4,14,8,128]{3,2,1,0:T(8,128)S(1)} %get-tuple-element.38), channel_id=1, source_target_pairs={{0,1},{1,0},{2,3},{3,2},{4,5},{5,4},{6,7},{7,6},{8,9},{9,8},{10,11... | collective-permute-start | bytes 688136 | tf_op jit(solution)/shard_map/ppermute | solution.py:498
  20.9 7.2 %collective-permute-start.4 = (f32[2,14,8,128]{3,2,1,0:T(8,128)S(1)}, f32[2,14,8,128]{3,2,1,0:T(8,128)S(1)}, u32[]{:S(2)}, u32[]{:S(2)}) collective-permute-start(f32[2,14,8,128]{3,2,1,0:T(8,128)S(1)} %get-tuple-element.35), channel_id=1, source_target_pairs={{0,3},{1,2},{2,1},{3,0},{4,7},{5,6},{6,5},{7,4},{8,11},{9,10},{10,... | collective-permute-start | bytes 344072 | tf_op jit(solution)/shard_map/ppermute | solution.py:498
  23.4 5.4 %collective-permute-start.5 = (f32[2,14,8,128]{3,2,1,0:T(8,128)S(1)}, f32[2,14,8,128]{3,2,1,0:T(8,128)S(1)}, u32[]{:S(2)}, u32[]{:S(2)}) collective-permute-start(f32[2,14,8,128]{3,2,1,0:T(8,128)S(1)} %get-tuple-element.36), channel_id=1, source_target_pairs={{0,2},{1,3},{2,0},{3,1},{4,6},{5,7},{6,4},{7,5},{8,10},{9,11},{10,... | collective-permute-start | bytes 344072 | tf_op jit(solution)/shard_map/ppermute | solution.py:498
  23.4 5.4 %copy-start.3 = (s32[4]{0:T(128)S(1)}, s32[4]{0:T(128)}, u32[]{:S(2)}) copy-start(s32[4]{0:T(128)} %counts.3) | copy-start | bytes 52
  26.0 5.0 %collective-permute-start.9 = (f32[2,14,8,128]{3,2,1,0:T(8,128)S(1)}, f32[2,14,8,128]{3,2,1,0:T(8,128)S(1)}, u32[]{:S(2)}, u32[]{:S(2)}) collective-permute-start(f32[2,14,8,128]{3,2,1,0:T(8,128)S(1)} %get-tuple-element.41), channel_id=1, source_target_pairs={{0,3},{1,2},{2,1},{3,0},{4,7},{5,6},{6,5},{7,4},{8,11},{9,10},{10,... | collective-permute-start | bytes 344072 | tf_op jit(solution)/shard_map/ppermute | solution.py:498
  27.5 6.5 %collective-permute-start.10 = (f32[2,14,8,128]{3,2,1,0:T(8,128)S(1)}, f32[2,14,8,128]{3,2,1,0:T(8,128)S(1)}, u32[]{:S(2)}, u32[]{:S(2)}) collective-permute-start(f32[2,14,8,128]{3,2,1,0:T(8,128)S(1)} %get-tuple-element.42), channel_id=1, source_target_pairs={{0,2},{1,3},{2,0},{3,1},{4,6},{5,7},{6,4},{7,5},{8,10},{9,11},{10,... | collective-permute-start | bytes 344072 | tf_op jit(solution)/shard_map/ppermute | solution.py:498
  28.1 5.8 %collective-permute-start.11 = (f32[2,14,8,128]{3,2,1,0:T(8,128)S(1)}, f32[2,14,8,128]{3,2,1,0:T(8,128)S(1)}, u32[]{:S(2)}, u32[]{:S(2)}) collective-permute-start(f32[2,14,8,128]{3,2,1,0:T(8,128)S(1)} %get-tuple-element.44), channel_id=1, source_target_pairs={{0,1},{1,0},{2,3},{3,2},{4,5},{5,4},{6,7},{7,6},{8,9},{9,8},{10,11... | collective-permute-start | bytes 344072 | tf_op jit(solution)/shard_map/ppermute | solution.py:498

commit v10 on v9

--- a/solution.py
+++ b/solution.py
@@ -451,11 +451,13 @@
         functools.partial(prep_kernel, rows),
         [f32(depth, rows, number, nlon), halo, halo], (raw, joined),
         cost=cost(1, 1))
-    swaps = ([(i, i ^ 1) for i in range(bands)],
-             [(i, i if i in (0, bands - 1) else ((i - 1) ^ 1) + 1) for i in range(bands)])
+    second = {i: ((i - 1) ^ 1) + 1 for i in range(1, bands - 1)}
+    second_pairs = [(i * count + d, second[i] * count + d if i in second else i * count + (d ^ 1))
+                    for i in range(bands) for d in range(count)]
 
     def beside(sent):
-        return [lax.ppermute(buffer, "lat", pairs) for buffer, pairs in zip(sent, swaps)]
+        return [lax.ppermute(sent[0], "lat", [(i, i ^ 1) for i in range(bands)]),
+                lax.ppermute(sent[1], ("lat", "lev"), second_pairs)]
 
     rounds = [beside(sent)]
     taps = call(

time: 35.9 us -> 33.5 us (0.933)
  waiting for transfers between devices: 7.34 us -> 4.76 us
    ppermute x8, starting transfers between devices: 4.82 us -> 7.59 us  [swapped(): return lax.ppermute(sent, 'lev', [(i, i ^ k) for i in range(count)])]
    ppermute x8, waiting for transfers between devices: 7.33 us -> 4.75 us  [swapped(): return lax.ppermute(sent, 'lev', [(i, i ^ k) for i in range(count)])]
    ppermute x4, starting transfers between devices: 8.87 us -> 6.31 us  [the longest x2 6.31 us: beside(): lax.ppermute(sent[0], 'lat', [(i, i ^ 1) for i in range(bands)])]
  transfers between devices with their start and end apart: 12 -> 12, of which waited for: 5 -> 3; matrix products, arithmetic and copies ran while one was open for 0% -> 0% of each run, Pallas kernels for 28% -> 30%
where the time goes in v10:
time: 33.5 us; the launch traced here: 33.4 us
  starting transfers between devices  13.9 us (41%)
  Pallas kernels  12.1 us (36%)
  waiting for transfers between devices  4.76 us (14%)
  local copies, waits for them, and re-layouts  1.33 us (4%)
  other arithmetic  1.14 us (3%)
    pallas_call x5, Pallas kernels, call(): pl.pallas_call(kernel, out_shape=outs, in_specs=specs or [VMEM] * len(arg...  9.34 us
    ppermute x8, starting transfers between devices, swapped(): return lax.ppermute(sent, 'lev', [(i, i ^ k) for i in range(count)])  7.59 us
    ppermute x2, starting transfers between devices, beside(): lax.ppermute(sent[0], 'lat', [(i, i ^ 1) for i in range(bands)])  6.31 us
    ppermute x8, waiting for transfers between devices, swapped(): return lax.ppermute(sent, 'lev', [(i, i ^ k) for i in range(count)])  4.75 us
    pallas_call x2, Pallas kernels, remap(): pl.pallas_call(functools.partial(remap_kernel, count, tuple(plan[:part]),...  2.78 us
    unnamed x8, local copies, waits for them, and re-layouts  1.33 us
    concatenate x1, other arithmetic, shards(): jnp.concatenate([jnp.transpose(wind_x, (1, 0, 2)), jnp.transpose(wind_y,...  1.14 us
  transfers between devices with their start and end apart: 12, of which 3 were waited for; matrix products, arithmetic and copies ran while one was open for 0% of the time, Pallas kernels for 30%

profile of v10, /device:TPU:0, one launch (start us, length us, event | category | flops | bytes accessed | tf_op | source)
XLA Modules:
  0.0 33.4 jit_solution(1880231550581211416)
XLA Ops:
  0.0 1.1 %pad_maximum_fusion.winds.joined = f32[36,2,1152]{2,1,0:T(2,128)S(1)} fusion(f32[18,2,1152]{2,1,0:T(2,128)} %bitcast.13, f32[18,2,1152]{2,1,0:T(2,128)} %bitcast.14), kind=kLoop, calls=%fused_computation | loop fusion | flops 82944 | bytes 663552 | tf_op jit(solution)/shard_map/concatenate | solution.py:448
  1.1 0.0 copy-start
  1.2 1.3 %copy-done = f32[8,2,18,1152]{3,1,2,0:T(2,128)S(1)} copy-done((f32[8,2,18,1152]{3,1,2,0:T(2,128)S(1)}, f32[8,2,18,1152]{3,1,2,0:T(2,128)}, u32[]{:S(2)}) %copy-start) | copy-done | bytes 1327128
  2.5 0.0 copy-start.1
  2.5 0.0 copy-start.2
  2.5 0.2 shard_map.64
  2.7 3.1 %collective-permute-start.2 = (f32[7,8,1152]{2,1,0:T(8,128)S(1)}, f32[7,8,1152]{2,1,0:T(8,128)S(1)}, u32[]{:S(2)}, u32[]{:S(2)}) collective-permute-start(f32[7,8,1152]{2,1,0:T(8,128)S(1)} %get-tuple-element.29), channel_id=1, source_target_pairs={{0,4},{4,0},{8,12},{12,8},{1,5},{5,1},{9,13},{13,9},{2,6},{6,2},{1... | collective-permute-start | bytes 774152 | tf_op jit(solution)/shard_map/ppermute | solution.py:459
  5.8 0.0 collective-permute-start.3
  5.8 3.8 %shard_map.65 = (f32[2,14,8,128]{3,2,1,0:T(8,128)S(1)}, f32[2,14,8,128]{3,2,1,0:T(8,128)S(1)}, f32[2,14,8,128]{3,2,1,0:T(8,128)S(1)}, f32[2,14,8,128]{3,2,1,0:T(...) custom-call(f32[2,18,8,1152]{3,2,1,0:T(8,128)S(1)} %get-tuple-elemen, ...), custom_call_target="tpu_custom_call" | custom-call | flops 1 | bytes 1 | tf_op jit(solution)/shard_map/pallas_call | solution.py:419
  9.6 3.2 %collective-permute-start.7 = (f32[7,8,1152]{2,1,0:T(8,128)S(1)}, f32[7,8,1152]{2,1,0:T(8,128)S(1)}, u32[]{:S(2)}, u32[]{:S(2)}) collective-permute-start(f32[7,8,1152]{2,1,0:T(8,128)S(1)} %get-tuple-element.39), channel_id=1, source_target_pairs={{0,4},{4,0},{8,12},{12,8},{1,5},{5,1},{9,13},{13,9},{2,6},{6,2},{1... | collective-permute-start | bytes 774152 | tf_op jit(solution)/shard_map/ppermute | solution.py:459
  12.9 0.0 collective-permute-start.8
  12.9 1.6 %collective-permute-start = (f32[2,14,8,128]{3,2,1,0:T(8,128)S(1)}, f32[2,14,8,128]{3,2,1,0:T(8,128)S(1)}, u32[]{:S(2)}, u32[]{:S(2)}) collective-permute-start(f32[2,14,8,128]{3,2,1,0:T(8,128)S(1)} %get-tuple-element.26), channel_id=1, source_target_pairs={{0,3},{1,2},{2,1},{3,0},{4,7},{5,6},{6,5},{7,4},{8,11},{9,10},{10,... | collective-permute-start | bytes 344072 | tf_op jit(solution)/shard_map/ppermute | solution.py:500
  14.5 0.0 copy-done.1
  14.5 0.0 copy-done.2
  14.5 0.2 shard_map.66.refs_1_.refs_7_.refs_11_
  14.7 0.0 collective-permute-done.2.first_round
  14.7 0.6 %collective-permute-start.1 = (f32[2,14,8,128]{3,2,1,0:T(8,128)S(1)}, f32[2,14,8,128]{3,2,1,0:T(8,128)S(1)}, u32[]{:S(2)}, u32[]{:S(2)}) collective-permute-start(f32[2,14,8,128]{3,2,1,0:T(8,128)S(1)} %get-tuple-element.27), channel_id=1, source_target_pairs={{0,2},{1,3},{2,0},{3,1},{4,6},{5,7},{6,4},{7,5},{8,10},{9,11},{10,... | collective-permute-start | bytes 344072 | tf_op jit(solution)/shard_map/ppermute | solution.py:500
  15.3 0.0 collective-permute-done.3.second_round
  15.3 2.5 %shard_map.67 = (f32[2,14,8,128]{3,2,1,0:T(8,128)S(1)}, f32[4,14,8,128]{3,2,1,0:T(8,128)S(1)}, f32[2,14,8,128]{3,2,1,0:T(8,128)S(1)}, f32[2,14,8,128]{3,2,1,0:T(8,128)S(1)}) custom-call(f32[2,18,8,1152]{3,2,1,0:T(8,128)S(1)} %get-tuple-element.25.state, f32[7,8,1152]{2,1,0:T(8,128)S(1)} %collective-permute-done.2.first_round, ...), custom_call_target="tpu_custom_call" | custom-call | flops 19906560 | bytes 2654208 | tf_op jit(solution)/shard_map/pallas_call | solution.py:419
  17.8 0.1 collective-permute-start.6
  17.9 0.0 collective-permute-done.refs_1_.refs_0_
  18.0 1.9 %collective-permute-start.4 = (f32[2,14,8,128]{3,2,1,0:T(8,128)S(1)}, f32[2,14,8,128]{3,2,1,0:T(8,128)S(1)}, u32[]{:S(2)}, u32[]{:S(2)}) collective-permute-start(f32[2,14,8,128]{3,2,1,0:T(8,128)S(1)} %get-tuple-element.35), channel_id=1, source_target_pairs={{0,3},{1,2},{2,1},{3,0},{4,7},{5,6},{6,5},{7,4},{8,11},{9,10},{10,... | collective-permute-start | bytes 344072 | tf_op jit(solution)/shard_map/ppermute | solution.py:500
  19.9 0.9 %collective-permute-done.1.refs_2_.refs_1_ = f32[2,14,8,128]{3,2,1,0:T(8,128)S(1)} collective-permute-done((f32[2,14,8,128]{3,2,1,0:T(8,128)S(1)}, f32[2,14,8,128]{3,2,1,0:T(8,128)S(1)}, u32[]{:S(2)}, u32[]{:S(2)}) %collective-permute-start.1) | collective-permute-done | bytes 114720 | tf_op jit(solution)/shard_map/ppermute | solution.py:500
  20.8 1.5 %collective-permute-start.5 = (f32[2,14,8,128]{3,2,1,0:T(8,128)S(1)}, f32[2,14,8,128]{3,2,1,0:T(8,128)S(1)}, u32[]{:S(2)}, u32[]{:S(2)}) collective-permute-start(f32[2,14,8,128]{3,2,1,0:T(8,128)S(1)} %get-tuple-element.36), channel_id=1, source_target_pairs={{0,2},{1,3},{2,0},{3,1},{4,6},{5,7},{6,4},{7,5},{8,10},{9,11},{10,... | collective-permute-start | bytes 344072 | tf_op jit(solution)/shard_map/ppermute | solution.py:500
  22.3 0.0 collective-permute-done.7.first_round
  22.3 0.0 collective-permute-done.8.second_round
  22.3 0.0 copy-start.3
  22.3 2.5 %shard_map.68 = (f32[2,14,8,128]{3,2,1,0:T(8,128)S(1)}, f32[2,14,8,128]{3,2,1,0:T(8,128)S(1)}, f32[2,14,8,128]{3,2,1,0:T(8,128)S(1)}, f32[2,14,8,128]{3,2,1,0:T(8,128)S(1)}) custom-call(f32[2,18,8,1152]{3,2,1,0:T(8,128)S(1)} %get-tuple-element.25.state, f32[7,8,1152]{2,1,0:T(8,128)S(1)} %collective-permute-done.7.first_round, ...), custom_call_target="tpu_custom_call" | custom-call | flops 19906560 | bytes 2654208 | tf_op jit(solution)/shard_map/pallas_call | solution.py:419
  24.8 0.1 collective-permute-start.9
  24.9 0.8 %collective-permute-start.10 = (f32[2,14,8,128]{3,2,1,0:T(8,128)S(1)}, f32[2,14,8,128]{3,2,1,0:T(8,128)S(1)}, u32[]{:S(2)}, u32[]{:S(2)}) collective-permute-start(f32[2,14,8,128]{3,2,1,0:T(8,128)S(1)} %get-tuple-element.42), channel_id=1, source_target_pairs={{0,2},{1,3},{2,0},{3,1},{4,6},{5,7},{6,4},{7,5},{8,10},{9,11},{10,... | collective-permute-start | bytes 344072 | tf_op jit(solution)/shard_map/ppermute | solution.py:500
  25.7 0.0 collective-permute-done.4.refs_3_
  25.7 1.0 %collective-permute-start.11 = (f32[2,14,8,128]{3,2,1,0:T(8,128)S(1)}, f32[2,14,8,128]{3,2,1,0:T(8,128)S(1)}, u32[]{:S(2)}, u32[]{:S(2)}) collective-permute-start(f32[2,14,8,128]{3,2,1,0:T(8,128)S(1)} %get-tuple-element.44), channel_id=1, source_target_pairs={{0,1},{1,0},{2,3},{3,2},{4,5},{5,4},{6,7},{7,6},{8,9},{9,8},{10,11... | collective-permute-start | bytes 344072 | tf_op jit(solution)/shard_map/ppermute | solution.py:500
  26.8 0.0 collective-permute-done.5.refs_4_
  26.8 0.0 collective-permute-done.6.refs_6_
  26.8 0.0 copy-done.3
  26.8 1.0 %shard_map.69.refs_12_ = f32[6,6,8,288]{3,2,1,0:T(8,128)S(1)} custom-call(s32[4]{0:T(128)S(1)} %copy-done.3, f32[2,14,8,128]{3,2,1,0:T(8,128)S(1)} %collective-permute-done.refs_1_.refs_0_, f32[2,14,8,128]{3,2,1,0:T(8,128)S(1)} %collective-permute-done.1.refs_2_.refs_1_, f32[2,14,8,128]{3,2,1,0:T(8,128)S(1)} %get-tuple-element.28.refs_2_, ...), custom_call_target="tpu_custom_call" | custom-call | flops 1 | bytes 1 | tf_op jit(solution)/shard_map/pallas_call | solution.py:517
  27.8 2.5 %collective-permute-done.9.refs_7_ = f32[2,14,8,128]{3,2,1,0:T(8,128)S(1)} collective-permute-done((f32[2,14,8,128]{3,2,1,0:T(8,128)S(1)}, f32[2,14,8,128]{3,2,1,0:T(8,128)S(1)}, u32[]{:S(2)}, u32[]{:S(2)}) %collective-permute-start.9) | collective-permute-done | bytes 114720 | tf_op jit(solution)/shard_map/ppermute | solution.py:500
  30.3 1.3 %collective-permute-done.10.refs_8_ = f32[2,14,8,128]{3,2,1,0:T(8,128)S(1)} collective-permute-done((f32[2,14,8,128]{3,2,1,0:T(8,128)S(1)}, f32[2,14,8,128]{3,2,1,0:T(8,128)S(1)}, u32[]{:S(2)}, u32[]{:S(2)}) %collective-permute-start.10) | collective-permute-done | bytes 114720 | tf_op jit(solution)/shard_map/ppermute | solution.py:500
  31.6 0.0 collective-permute-done.11.refs_10_
  31.6 1.8 %shard_map.70 = f32[6,18,8,288]{3,2,1,0:T(8,128)} custom-call(s32[4]{0:T(128)S(1)} %copy-done.3, f32[2,14,8,128]{3,2,1,0:T(8,128)S(1)} %collective-permute-done.refs_1_.refs_0_, f32[2,14,8,128]{3,2,1,0:T(8,128)S(1)} %collective-permute-done.1.refs_2_.refs_1_, f32[2,14,8,128]{3,2,1,0:T(8,128)S(1)} %get-tuple-element.28.refs_2_, ...), custom_call_target="tpu_custom_call" | custom-call | flops 1 | bytes 1 | tf_op jit(solution)/shard_map/pallas_call | solution.py:517
Async XLA Ops:
  1.1 1.3 %copy-start = (f32[8,2,18,1152]{3,1,2,0:T(2,128)S(1)}, f32[8,2,18,1152]{3,1,2,0:T(2,128)}, u32[]{:S(2)}) copy-start(f32[8,2,18,1152]{3,1,2,0:T(2,128)} %param.6) | copy-start | bytes 3981316
  2.5 12.0 %copy-start.1 = (f32[4,6,18,288]{3,0,2,1:T(4,128)S(1)}, f32[4,6,18,288]{3,0,2,1:T(4,128)}, u32[]{:S(2)}) copy-start(f32[4,6,18,288]{3,0,2,1:T(4,128)} %param.11) | copy-start | bytes 1492996
  2.5 12.0 %copy-start.2 = (s32[6,18,288]{2,1,0:T(8,128)S(1)}, s32[6,18,288]{2,1,0:T(8,128)}, u32[]{:S(2)}) copy-start(s32[6,18,288]{2,1,0:T(8,128)} %source.1) | copy-start | bytes 373252
  2.7 12.0 %collective-permute-start.2 = (f32[7,8,1152]{2,1,0:T(8,128)S(1)}, f32[7,8,1152]{2,1,0:T(8,128)S(1)}, u32[]{:S(2)}, u32[]{:S(2)}) collective-permute-start(f32[7,8,1152]{2,1,0:T(8,128)S(1)} %get-tuple-element.29), channel_id=1, source_target_pairs={{0,4},{4,0},{8,12},{12,8},{1,5},{5,1},{9,13},{13,9},{2,6},{6,2},{1... | collective-permute-start | bytes 774152 | tf_op jit(solution)/shard_map/ppermute | solution.py:459
  5.8 9.5 %collective-permute-start.3 = (f32[7,8,1152]{2,1,0:T(8,128)S(1)}, f32[7,8,1152]{2,1,0:T(8,128)S(1)}, u32[]{:S(2)}, u32[]{:S(2)}) collective-permute-start(f32[7,8,1152]{2,1,0:T(8,128)S(1)} %get-tuple-element.30), channel_id=1, source_target_pairs={{0,1},{1,0},{2,3},{3,2},{4,8},{5,9},{6,10},{7,11},{8,4},{9,5},{10,... | collective-permute-start | bytes 774152 | tf_op jit(solution)/shard_map/ppermute | solution.py:460
  9.6 12.6 %collective-permute-start.7 = (f32[7,8,1152]{2,1,0:T(8,128)S(1)}, f32[7,8,1152]{2,1,0:T(8,128)S(1)}, u32[]{:S(2)}, u32[]{:S(2)}) collective-permute-start(f32[7,8,1152]{2,1,0:T(8,128)S(1)} %get-tuple-element.39), channel_id=1, source_target_pairs={{0,4},{4,0},{8,12},{12,8},{1,5},{5,1},{9,13},{13,9},{2,6},{6,2},{1... | collective-permute-start | bytes 774152 | tf_op jit(solution)/shard_map/ppermute | solution.py:459
  12.9 9.4 %collective-permute-start.8 = (f32[7,8,1152]{2,1,0:T(8,128)S(1)}, f32[7,8,1152]{2,1,0:T(8,128)S(1)}, u32[]{:S(2)}, u32[]{:S(2)}) collective-permute-start(f32[7,8,1152]{2,1,0:T(8,128)S(1)} %get-tuple-element.40), channel_id=1, source_target_pairs={{0,1},{1,0},{2,3},{3,2},{4,8},{5,9},{6,10},{7,11},{8,4},{9,5},{10,... | collective-permute-start | bytes 774152 | tf_op jit(solution)/shard_map/ppermute | solution.py:460
  12.9 5.1 %collective-permute-start = (f32[2,14,8,128]{3,2,1,0:T(8,128)S(1)}, f32[2,14,8,128]{3,2,1,0:T(8,128)S(1)}, u32[]{:S(2)}, u32[]{:S(2)}) collective-permute-start(f32[2,14,8,128]{3,2,1,0:T(8,128)S(1)} %get-tuple-element.26), channel_id=1, source_target_pairs={{0,3},{1,2},{2,1},{3,0},{4,7},{5,6},{6,5},{7,4},{8,11},{9,10},{10,... | collective-permute-start | bytes 344072 | tf_op jit(solution)/shard_map/ppermute | solution.py:500
  14.7 6.1 %collective-permute-start.1 = (f32[2,14,8,128]{3,2,1,0:T(8,128)S(1)}, f32[2,14,8,128]{3,2,1,0:T(8,128)S(1)}, u32[]{:S(2)}, u32[]{:S(2)}) collective-permute-start(f32[2,14,8,128]{3,2,1,0:T(8,128)S(1)} %get-tuple-element.27), channel_id=1, source_target_pairs={{0,2},{1,3},{2,0},{3,1},{4,6},{5,7},{6,4},{7,5},{8,10},{9,11},{10,... | collective-permute-start | bytes 344072 | tf_op jit(solution)/shard_map/ppermute | solution.py:500
  17.8 8.9 %collective-permute-start.6 = (f32[4,14,8,128]{3,2,1,0:T(8,128)S(1)}, f32[4,14,8,128]{3,2,1,0:T(8,128)S(1)}, u32[]{:S(2)}, u32[]{:S(2)}) collective-permute-start(f32[4,14,8,128]{3,2,1,0:T(8,128)S(1)} %get-tuple-element.38), channel_id=1, source_target_pairs={{0,1},{1,0},{2,3},{3,2},{4,5},{5,4},{6,7},{7,6},{8,9},{9,8},{10,11... | collective-permute-start | bytes 688136 | tf_op jit(solution)/shard_map/ppermute | solution.py:500
  18.0 7.8 %collective-permute-start.4 = (f32[2,14,8,128]{3,2,1,0:T(8,128)S(1)}, f32[2,14,8,128]{3,2,1,0:T(8,128)S(1)}, u32[]{:S(2)}, u32[]{:S(2)}) collective-permute-start(f32[2,14,8,128]{3,2,1,0:T(8,128)S(1)} %get-tuple-element.35), channel_id=1, source_target_pairs={{0,3},{1,2},{2,1},{3,0},{4,7},{5,6},{6,5},{7,4},{8,11},{9,10},{10,... | collective-permute-start | bytes 344072 | tf_op jit(solution)/shard_map/ppermute | solution.py:500
  20.8 6.0 %collective-permute-start.5 = (f32[2,14,8,128]{3,2,1,0:T(8,128)S(1)}, f32[2,14,8,128]{3,2,1,0:T(8,128)S(1)}, u32[]{:S(2)}, u32[]{:S(2)}) collective-permute-start(f32[2,14,8,128]{3,2,1,0:T(8,128)S(1)} %get-tuple-element.36), channel_id=1, source_target_pairs={{0,2},{1,3},{2,0},{3,1},{4,6},{5,7},{6,4},{7,5},{8,10},{9,11},{10,... | collective-permute-start | bytes 344072 | tf_op jit(solution)/shard_map/ppermute | solution.py:500
  22.3 4.5 %copy-start.3 = (s32[4]{0:T(128)S(1)}, s32[4]{0:T(128)}, u32[]{:S(2)}) copy-start(s32[4]{0:T(128)} %counts.3) | copy-start | bytes 52
  24.8 5.5 %collective-permute-start.9 = (f32[2,14,8,128]{3,2,1,0:T(8,128)S(1)}, f32[2,14,8,128]{3,2,1,0:T(8,128)S(1)}, u32[]{:S(2)}, u32[]{:S(2)}) collective-permute-start(f32[2,14,8,128]{3,2,1,0:T(8,128)S(1)} %get-tuple-element.41), channel_id=1, source_target_pairs={{0,3},{1,2},{2,1},{3,0},{4,7},{5,6},{6,5},{7,4},{8,11},{9,10},{10,... | collective-permute-start | bytes 344072 | tf_op jit(solution)/shard_map/ppermute | solution.py:500
  24.9 6.7 %collective-permute-start.10 = (f32[2,14,8,128]{3,2,1,0:T(8,128)S(1)}, f32[2,14,8,128]{3,2,1,0:T(8,128)S(1)}, u32[]{:S(2)}, u32[]{:S(2)}) collective-permute-start(f32[2,14,8,128]{3,2,1,0:T(8,128)S(1)} %get-tuple-element.42), channel_id=1, source_target_pairs={{0,2},{1,3},{2,0},{3,1},{4,6},{5,7},{6,4},{7,5},{8,10},{9,11},{10,... | collective-permute-start | bytes 344072 | tf_op jit(solution)/shard_map/ppermute | solution.py:500
  25.7 5.9 %collective-permute-start.11 = (f32[2,14,8,128]{3,2,1,0:T(8,128)S(1)}, f32[2,14,8,128]{3,2,1,0:T(8,128)S(1)}, u32[]{:S(2)}, u32[]{:S(2)}) collective-permute-start(f32[2,14,8,128]{3,2,1,0:T(8,128)S(1)} %get-tuple-element.44), channel_id=1, source_target_pairs={{0,1},{1,0},{2,3},{3,2},{4,5},{5,4},{6,7},{7,6},{8,9},{9,8},{10,11... | collective-permute-start | bytes 344072 | tf_op jit(solution)/shard_map/ppermute | solution.py:500

commit v11 on v10

--- a/solution.py
+++ b/solution.py
@@ -197,10 +197,11 @@
         copy_tiles([((source, (unit, i)), (target, (start + unit, i))) for i in range(source.shape[1])])
 
 
-def hand_out(packed, outs):
+def hand_out(packed, outs, groups):
     me = lax.axis_index("lev")
-    for k, out in enumerate(outs):
-        copy_units(packed.at[me ^ k], out)
+    for group, out in zip(groups, outs):
+        for place, k in enumerate(group):
+            copy_units(packed.at[me ^ k], out, place * packed.shape[1])
 
 
 def own_coefficients(rows, joined, winds, cx, cy):
@@ -224,8 +225,8 @@
             target[level, at + q, :, tile(j)] = part
 
 
-def interior_kernel(count, rows, state, joined, *refs):
-    outs, (first, cx, cy), refs = refs[:count], refs[count:count + 3], refs[count + 3:]
+def interior_kernel(count, rows, groups, state, joined, *refs):
+    outs, (first, cx, cy), refs = refs[:len(groups)], refs[len(groups):len(groups) + 3], refs[len(groups) + 3:]
     halos, (packed, winds, swept, inter, west, flux) = refs[:-6], refs[-6:]
     levels, nlon = state.shape[0], state.shape[3]
     nj = nlon // LANES
@@ -254,11 +255,11 @@
         pack_block(done, packed, group, count, lane)
 
     lon_pass(work_last, swept, coef_x, inter, west, flux, lane, send)
-    hand_out(packed, outs)
+    hand_out(packed, outs, groups)
 
 
 def edge_kernel(count, rows, slot, joint, state, first_round, second_round, first, cx, cy, *refs):
-    others = refs[:joint]
+    others = refs[:len(joint)]
     outs, (packed, beyond, swept, edge, inter, west, flux) = refs[-7 - count:-7], refs[-7:]
     nlon = state.shape[3]
     nj = nlon // LANES
@@ -323,9 +324,11 @@
     lon_pass(listed(ends), swept, coef_x, inter, west, flux, lane, keep_edge)
     lat_pass(1, nj, ends_last, cell_first, coef_y, put_last)
     lon_pass(listed(ends_last), swept, coef_x, inter, west, flux, lane, send)
-    hand_out(packed, outs)
-    for other in others:
-        copy_units(other, outs[1], packed.shape[1])
+    hand_out(packed, outs, [(k,) for k in range(count)])
+    place = packed.shape[1]
+    for other, (begin, size) in zip(others, joint):
+        copy_units(other.at[pl.ds(begin, size)], outs[1], place)
+        place += size
 
 
 def weights_kernel(weights, source, out):
@@ -343,8 +346,9 @@
             out[k, row] = total
 
 
-def remap_kernel(count, plan, numbers, counts, *refs):
-    chunks, (weights, *ready, out, levels, result, sems) = refs[:len(plan)], refs[len(plan):]
+def remap_kernel(count, plan, numbers, whole, counts, *refs):
+    chunks, weights, ready, (out, levels, result, sems) = refs[:len(plan)], refs[len(plan)], refs[len(plan) + 1:-4], refs[-4:]
+    ready = ready if whole else ()
     me = lax.axis_index("lev")
     targets, _, _, width = result.shape
     _, mains, tail, per, _ = packed_sizes(width * count, count)
@@ -366,8 +370,8 @@
             start = start + jnp.where(e < d, counts[e], 0)
         return jnp.where(slot < counts[d], start + slot, targets)
 
-    for (k, units), chunk in zip(plan, chunks):
-        for unit, (slot, number) in enumerate(units):
+    for units, chunk in zip(plan, chunks):
+        for unit, (k, slot, number) in enumerate(units):
             if number in numbers:
                 at = numbers.index(number)
                 copy_tiles([((chunk, (unit, i)), (levels, (level_of(k, slot), at, i))) for i in range(chunk.shape[1])])
@@ -475,23 +479,26 @@
     coef = f32(3, depth, held, nlon)
     swept = vmem(depth, rows - 2 * REACH, number, nlon)
     stage = vmem(depth * (rows - 2 * REACH), number, nlon)
+    chips = tuple(range(2, count, 2))
+    groups = ((0,), (1,)) + tuple((k, k ^ 1) for k in chips)
+    inner_units = depth * inner
     result = call(
-        functools.partial(interior_kernel, count, rows),
-        [f32(*box(depth * inner))] * count + [f32(depth, rows - 2 * REACH, number, nlon), coef, coef] + [halo] * (2 * depth - 2),
-        (state, joined), scratch=[vmem(*box(depth * inner, count)), vmem(2, depth, held, nlon), swept, stage, stage, stage],
+        functools.partial(interior_kernel, count, rows, groups),
+        [f32(*box(len(group) * inner_units)) for group in groups]
+        + [f32(depth, rows - 2 * REACH, number, nlon), coef, coef] + [halo] * (2 * depth - 2),
+        (state, joined), scratch=[vmem(*box(inner_units, count)), vmem(2, depth, held, nlon), swept, stage, stage, stage],
         cost=cost(1, 1))
-    middle, (first, cx, cy), sent = result[:count], result[count:count + 3], result[count + 3:]
+    middle, (first, cx, cy), sent = result[:len(groups)], result[len(groups):len(groups) + 3], result[len(groups) + 3:]
     rounds += [beside(sent[2 * i:2 * i + 2]) for i in range(depth - 1)]
-    plan, chunks = [], []
     swept = vmem(1, 2 * HALO, number, nlon)
     stage = vmem(2 * HALO, number, nlon)
 
     def edge(slot, joint, after):
-        args = (state, *rounds[slot], first, cx, cy, *joint, *after)
-        units = 2 + (joint[0].shape[0] if joint else 0)
+        args = (state, *rounds[slot], first, cx, cy, *(chunk for chunk, _ in joint), *after)
+        parts = tuple(part for _, part in joint)
         return call(
-            functools.partial(edge_kernel, count, rows, slot, len(joint)),
-            [f32(*box(units if k == 1 else 2)) for k in range(count)], args,
+            functools.partial(edge_kernel, count, rows, slot, parts),
+            [f32(*box(2 + sum(size for _, size in parts) if k == 1 else 2)) for k in range(count)], args,
             specs=[VMEM] * (len(args) - len(after)) + [ANY] * len(after),
             scratch=[vmem(*box(2, count)), vmem(3, 2, SUB, nlon), swept, swept, stage, stage, stage],
             cost=cost(60 * tracers.size, 8 * tracers.size))
@@ -499,25 +506,15 @@
     def swapped(sent, k):
         return lax.ppermute(sent, "lev", [(i, i ^ k) for i in range(count)])
 
-    partners = range(count - 1, 1, -1)
-    units = tuple((slot, 1 + b) for slot in range(depth) for b in range(inner))
-    plan += [(k, units) for k in partners] + [(0, units)]
-    chunks += [swapped(middle[k], k) for k in partners] + [middle[0]]
-    after, joint = (taps,), (middle[1],)
-    for slot in range(depth):
-        own = ((slot, 0), (slot, blocks - 1))
-        done = edge(slot, joint, after)
-        plan += [(k, own) for k in partners] + [(0, own), (1, own + units if joint else own)]
-        chunks += [swapped(done[k], k) for k in partners] + [done[0], swapped(done[1], 1)]
-        if slot == 0:
-            after, joint, early = (done[0], *chunks[:len(partners)]), (), len(chunks)
-
-    def remap(part, numbers, height, ready):
-        args = (level_counts, *chunks[:part], taps, *ready)
+    def units_of(k, places):
+        return tuple((k, slot, block) for slot, block in places)
+
+    def remap(listed, numbers, height, ready, after=()):
+        args = (level_counts, *(chunk for _, chunk in listed), taps, *ready, *after)
         return pl.pallas_call(
-            functools.partial(remap_kernel, count, tuple(plan[:part]), numbers),
+            functools.partial(remap_kernel, count, tuple(units for units, _ in listed), numbers, bool(ready)),
             out_shape=f32(targets, height, number, width),
-            in_specs=[SMEM] + [VMEM] * (len(args) - 1),
+            in_specs=[SMEM] + [VMEM] * (len(args) - 1 - len(after)) + [ANY] * len(after),
             out_specs=ANY,
             scratch_shapes=[
                 vmem(targets + 1, len(numbers), size, SUB, LANES),
@@ -528,8 +525,29 @@
             cost_estimate=cost(1, 1),
         )(*args)
 
-    middle_rows = remap(early, tuple(range(1, blocks - 1)), inner * BLOCK, ())
-    out = remap(len(chunks), (0, blocks - 1), rows, (middle_rows,))
+    places = tuple((slot, 1 + b) for slot in range(depth) for b in range(inner))
+    passing = tuple((None, None, None) for _ in places)
+    arrived = [swapped(sent_on, k) for sent_on, k in zip(middle[2:], chips)]
+    middle_chunks = [(units_of(k, places) + passing, chunk) for k, chunk in zip(chips, arrived)]
+    middle_chunks.append((units_of(0, places), middle[0]))
+    joint, joint_units, after = [(middle[1], (0, inner_units))], units_of(1, places), (taps,)
+    edge_chunks, far = [], []
+    for slot in range(depth):
+        own = ((slot, 0), (slot, blocks - 1))
+        done = edge(slot, joint, after)
+        crossing = [(units_of(k, own), swapped(done[k], k)) for k in range(count - 1, 1, -1)]
+        beside_me = (units_of(1, own) + joint_units, swapped(done[1], 1))
+        edge_chunks += crossing + [(units_of(0, own), done[0]), beside_me]
+        if slot + 1 < depth:
+            far += [chunk for _, chunk in crossing]
+        middle_chunks.append(beside_me)
+        if slot == 0:
+            for k, chunk in zip(chips, arrived):
+                chunk, _ = lax.optimization_barrier((chunk, done[0]))
+                middle_chunks.append((units_of(k ^ 1, places), swapped(chunk[inner_units:], 1)))
+        joint, joint_units, after = [], (), (done[0], beside_me[1])
+    middle_rows = remap(middle_chunks, tuple(range(1, blocks - 1)), inner * BLOCK, (), far)
+    out = remap(edge_chunks, (0, blocks - 1), rows, (middle_rows,))
     return jnp.transpose(out, (2, 0, 1, 3))
 
 

time: 33.5 us -> 35.8 us (1.069)
  waiting for transfers between devices: 4.76 us -> 8.57 us
  starting transfers between devices: 13.9 us -> 12.3 us
    ppermute x8, waiting for transfers between devices: 4.75 us -> 8.56 us  [swapped(): return lax.ppermute(sent, 'lev', [(i, i ^ k) for i in range(count)])]
    ppermute x8, starting transfers between devices: 7.59 us -> 6.02 us  [swapped(): return lax.ppermute(sent, 'lev', [(i, i ^ k) for i in range(count)])]
  transfers between devices with their start and end apart: 12 -> 12, of which waited for: 3 -> 3; matrix products, arithmetic and copies ran while one was open for 0% -> 0% of each run, Pallas kernels for 30% -> 28%
where the time goes in v11:
time: 35.8 us; the launch traced here: 35.7 us
  starting transfers between devices  12.3 us (34%)
  Pallas kernels  12.1 us (34%)
  waiting for transfers between devices  8.57 us (24%)
  local copies, waits for them, and re-layouts  1.34 us (4%)
  other arithmetic  1.14 us (3%)
    pallas_call x5, Pallas kernels, call(): pl.pallas_call(kernel, out_shape=outs, in_specs=specs or [VMEM] * len(arg...  9.36 us
    ppermute x8, waiting for transfers between devices, swapped(): return lax.ppermute(sent, 'lev', [(i, i ^ k) for i in range(count)])  8.56 us
    ppermute x2, starting transfers between devices, beside(): lax.ppermute(sent[0], 'lat', [(i, i ^ 1) for i in range(bands)])  6.31 us
    ppermute x8, starting transfers between devices, swapped(): return lax.ppermute(sent, 'lev', [(i, i ^ k) for i in range(count)])  6.02 us
    pallas_call x2, Pallas kernels, remap(): pl.pallas_call(functools.partial(remap_kernel, count, tuple((units for un...  2.78 us
    unnamed x8, local copies, waits for them, and re-layouts  1.33 us
    concatenate x1, other arithmetic, shards(): jnp.concatenate([jnp.transpose(wind_x, (1, 0, 2)), jnp.transpose(wind_y,...  1.14 us
  transfers between devices with their start and end apart: 12, of which 3 were waited for; matrix products, arithmetic and copies ran while one was open for 0% of the time, Pallas kernels for 28%

profile of v11, /device:TPU:0, one launch (start us, length us, event | category | flops | bytes accessed | tf_op | source)
XLA Modules:
  0.0 35.7 jit_solution(422659254849840711)
XLA Ops:
  0.0 1.1 %pad_maximum_fusion.winds.joined = f32[36,2,1152]{2,1,0:T(2,128)S(1)} fusion(f32[18,2,1152]{2,1,0:T(2,128)} %bitcast.13, f32[18,2,1152]{2,1,0:T(2,128)} %bitcast.14), kind=kLoop, calls=%fused_computation | loop fusion | flops 82944 | bytes 663552 | tf_op jit(solution)/shard_map/concatenate | solution.py:452
  1.1 0.0 copy-start
  1.2 1.3 %copy-done = f32[8,2,18,1152]{3,1,2,0:T(2,128)S(1)} copy-done((f32[8,2,18,1152]{3,1,2,0:T(2,128)S(1)}, f32[8,2,18,1152]{3,1,2,0:T(2,128)}, u32[]{:S(2)}) %copy-start) | copy-done | bytes 1327128
  2.5 0.0 copy-start.1
  2.5 0.0 copy-start.2
  2.5 0.2 shard_map.64
  2.7 3.1 %collective-permute-start = (f32[7,8,1152]{2,1,0:T(8,128)S(1)}, f32[7,8,1152]{2,1,0:T(8,128)S(1)}, u32[]{:S(2)}, u32[]{:S(2)}) collective-permute-start(f32[7,8,1152]{2,1,0:T(8,128)S(1)} %get-tuple-element.26), channel_id=1, source_target_pairs={{0,4},{4,0},{8,12},{12,8},{1,5},{5,1},{9,13},{13,9},{2,6},{6,2},{1... | collective-permute-start | bytes 774152 | tf_op jit(solution)/shard_map/ppermute | solution.py:463
  5.8 0.0 collective-permute-start.1
  5.8 3.8 %shard_map.65 = (f32[2,14,8,128]{3,2,1,0:T(8,128)S(1)}, f32[2,14,8,128]{3,2,1,0:T(8,128)S(1)}, f32[4,14,8,128]{3,2,1,0:T(8,128)S(1)}, f32[2,12,8,1152]{3,2,1,0:T...) custom-call(f32[2,18,8,1152]{3,2,1,0:T(8,128)S(1)} %get-tuple-elemen, ...), custom_call_target="tpu_custom_call" | custom-call | flops 1 | bytes 1 | tf_op jit(solution)/shard_map/pallas_call | solution.py:423
  9.6 3.2 %collective-permute-start.5 = (f32[7,8,1152]{2,1,0:T(8,128)S(1)}, f32[7,8,1152]{2,1,0:T(8,128)S(1)}, u32[]{:S(2)}, u32[]{:S(2)}) collective-permute-start(f32[7,8,1152]{2,1,0:T(8,128)S(1)} %get-tuple-element.36), channel_id=1, source_target_pairs={{0,4},{4,0},{8,12},{12,8},{1,5},{5,1},{9,13},{13,9},{2,6},{6,2},{1... | collective-permute-start | bytes 774152 | tf_op jit(solution)/shard_map/ppermute | solution.py:463
  12.9 0.0 collective-permute-start.6
  12.9 1.5 %collective-permute-start.10 = (f32[4,14,8,128]{3,2,1,0:T(8,128)S(1)}, f32[4,14,8,128]{3,2,1,0:T(8,128)S(1)}, u32[]{:S(2)}, u32[]{:S(2)}) collective-permute-start(f32[4,14,8,128]{3,2,1,0:T(8,128)S(1)} %get-tuple-element.42), channel_id=1, source_target_pairs={{0,2},{1,3},{2,0},{3,1},{4,6},{5,7},{6,4},{7,5},{8,10},{9,11},{10,... | collective-permute-start | bytes 688136 | tf_op jit(solution)/shard_map/ppermute | solution.py:507
  14.4 0.0 copy-done.1
  14.4 0.0 copy-done.2
  14.4 0.2 shard_map.66.refs_1_.refs_5_.refs_8_
  14.6 0.0 collective-permute-done.first_round
  14.6 0.0 collective-permute-done.1.second_round
  14.6 2.6 %shard_map.67 = (f32[2,14,8,128]{3,2,1,0:T(8,128)S(1)}, f32[4,14,8,128]{3,2,1,0:T(8,128)S(1)}, f32[2,14,8,128]{3,2,1,0:T(8,128)S(1)}, f32[2,14,8,128]{3,2,1,0:T(8,128)S(1)}) custom-call(f32[2,18,8,1152]{3,2,1,0:T(8,128)S(1)} %get-tuple-element.25.state, f32[7,8,1152]{2,1,0:T(8,128)S(1)} %collective-permute-done.first_round, ...), custom_call_target="tpu_custom_call" | custom-call | flops 19906560 | bytes 2654208 | tf_op jit(solution)/shard_map/pallas_call | solution.py:423
  17.1 0.3 collective-permute-start.4
  17.4 0.4 %collective-permute-start.2 = (f32[2,14,8,128]{3,2,1,0:T(8,128)S(1)}, f32[2,14,8,128]{3,2,1,0:T(8,128)S(1)}, u32[]{:S(2)}, u32[]{:S(2)}) collective-permute-start(f32[2,14,8,128]{3,2,1,0:T(8,128)S(1)} %get-tuple-element.32), channel_id=1, source_target_pairs={{0,3},{1,2},{2,1},{3,0},{4,7},{5,6},{6,5},{7,4},{8,11},{9,10},{10,... | collective-permute-start | bytes 344072 | tf_op jit(solution)/shard_map/ppermute | solution.py:507
  17.9 3.4 %collective-permute-done.10.refs_0_ = f32[4,14,8,128]{3,2,1,0:T(8,128)S(1)} collective-permute-done((f32[4,14,8,128]{3,2,1,0:T(8,128)S(1)}, f32[4,14,8,128]{3,2,1,0:T(8,128)S(1)}, u32[]{:S(2)}, u32[]{:S(2)}) %collective-permute-start.10) | collective-permute-done | bytes 229408 | tf_op jit(solution)/shard_map/ppermute | solution.py:507
  21.3 1.5 %collective-permute-start.3 = (f32[2,14,8,128]{3,2,1,0:T(8,128)S(1)}, f32[2,14,8,128]{3,2,1,0:T(8,128)S(1)}, u32[]{:S(2)}, u32[]{:S(2)}) collective-permute-start(f32[2,14,8,128]{3,2,1,0:T(8,128)S(1)} %get-tuple-element.33), channel_id=1, source_target_pairs={{0,2},{1,3},{2,0},{3,1},{4,6},{5,7},{6,4},{7,5},{8,10},{9,11},{10,... | collective-permute-start | bytes 344072 | tf_op jit(solution)/shard_map/ppermute | solution.py:507
  22.8 0.0 copy-start.3
  22.8 0.0 collective-permute-done.5.first_round
  22.8 0.1 collective-permute-start.11
  22.9 0.0 collective-permute-done.6.second_round
  22.9 0.0 collective-permute-done.4.refs_1_.refs_2_.refs_3_
  22.9 2.5 %shard_map.68 = (f32[2,14,8,128]{3,2,1,0:T(8,128)S(1)}, f32[2,14,8,128]{3,2,1,0:T(8,128)S(1)}, f32[2,14,8,128]{3,2,1,0:T(8,128)S(1)}, f32[2,14,8,128]{3,2,1,0:T(8,128)S(1)}) custom-call(f32[2,18,8,1152]{3,2,1,0:T(8,128)S(1)} %get-tuple-element.25.state, f32[7,8,1152]{2,1,0:T(8,128)S(1)} %collective-permute-done.5.first_round, ...), custom_call_target="tpu_custom_call" | custom-call | flops 19906560 | bytes 2654208 | tf_op jit(solution)/shard_map/pallas_call | solution.py:423
  25.4 0.5 %collective-permute-start.9 = (f32[2,14,8,128]{3,2,1,0:T(8,128)S(1)}, f32[2,14,8,128]{3,2,1,0:T(8,128)S(1)}, u32[]{:S(2)}, u32[]{:S(2)}) collective-permute-start(f32[2,14,8,128]{3,2,1,0:T(8,128)S(1)} %get-tuple-element.41), channel_id=1, source_target_pairs={{0,1},{1,0},{2,3},{3,2},{4,5},{5,4},{6,7},{7,6},{8,9},{9,8},{10,11... | collective-permute-start | bytes 344072 | tf_op jit(solution)/shard_map/ppermute | solution.py:507
  26.0 0.2 collective-permute-start.7
  26.2 0.0 collective-permute-done.2.refs_6_.refs_0_
  26.2 1.5 %collective-permute-start.8 = (f32[2,14,8,128]{3,2,1,0:T(8,128)S(1)}, f32[2,14,8,128]{3,2,1,0:T(8,128)S(1)}, u32[]{:S(2)}, u32[]{:S(2)}) collective-permute-start(f32[2,14,8,128]{3,2,1,0:T(8,128)S(1)} %get-tuple-element.39), channel_id=1, source_target_pairs={{0,2},{1,3},{2,0},{3,1},{4,6},{5,7},{6,4},{7,5},{8,10},{9,11},{10,... | collective-permute-start | bytes 344072 | tf_op jit(solution)/shard_map/ppermute | solution.py:507
  27.7 0.0 collective-permute-done.3.refs_7_.refs_1_
  27.7 0.0 collective-permute-done.11.refs_3_
  27.7 0.0 collective-permute-done.9.refs_4_.refs_7_
  27.7 0.0 copy-done.3
  27.7 1.0 %shard_map.69.refs_9_ = f32[6,6,8,288]{3,2,1,0:T(8,128)S(1)} custom-call(s32[4]{0:T(128)S(1)} %copy-done.3, f32[4,14,8,128]{3,2,1,0:T(8,128)S(1)} %collective-permute-done.10.refs_0_, f32[2,14,8,128]{3,2,1,0:T(8,128)S(1)} %get-tuple-element.43.refs_1_, f32[4,14,8,128]{3,2,1,0:T(8,128)S(1)} %collective-permute-done.4.refs_1_.refs_2_.refs_3_, ...), custom_call_target="tpu_custom_call" | custom-call | flops 1 | bytes 1 | tf_op jit(solution)/shard_map/pallas_call | solution.py:514
  28.7 2.4 %collective-permute-done.7.refs_4_ = f32[2,14,8,128]{3,2,1,0:T(8,128)S(1)} collective-permute-done((f32[2,14,8,128]{3,2,1,0:T(8,128)S(1)}, f32[2,14,8,128]{3,2,1,0:T(8,128)S(1)}, u32[]{:S(2)}, u32[]{:S(2)}) %collective-permute-start.7) | collective-permute-done | bytes 114720 | tf_op jit(solution)/shard_map/ppermute | solution.py:507
  31.2 2.7 %collective-permute-done.8.refs_5_ = f32[2,14,8,128]{3,2,1,0:T(8,128)S(1)} collective-permute-done((f32[2,14,8,128]{3,2,1,0:T(8,128)S(1)}, f32[2,14,8,128]{3,2,1,0:T(8,128)S(1)}, u32[]{:S(2)}, u32[]{:S(2)}) %collective-permute-start.8) | collective-permute-done | bytes 114720 | tf_op jit(solution)/shard_map/ppermute | solution.py:507
  33.9 1.8 %shard_map.70 = f32[6,18,8,288]{3,2,1,0:T(8,128)} custom-call(s32[4]{0:T(128)S(1)} %copy-done.3, f32[2,14,8,128]{3,2,1,0:T(8,128)S(1)} %collective-permute-done.2.refs_6_.refs_0_, f32[2,14,8,128]{3,2,1,0:T(8,128)S(1)} %collective-permute-done.3.refs_7_.refs_1_, f32[2,14,8,128]{3,2,1,0:T(8,128)S(1)} %get-tuple-element.34.refs_0_.refs_2_, ...), custom_call_target="tpu_custom_call" | custom-call | flops 1 | bytes 1 | tf_op jit(solution)/shard_map/pallas_call | solution.py:514
  (1 shorter events, 0.0 us)
Async XLA Ops:
  1.1 1.3 %copy-start = (f32[8,2,18,1152]{3,1,2,0:T(2,128)S(1)}, f32[8,2,18,1152]{3,1,2,0:T(2,128)}, u32[]{:S(2)}) copy-start(f32[8,2,18,1152]{3,1,2,0:T(2,128)} %param.6) | copy-start | bytes 3981316
  2.5 11.9 %copy-start.1 = (f32[4,6,18,288]{3,0,2,1:T(4,128)S(1)}, f32[4,6,18,288]{3,0,2,1:T(4,128)}, u32[]{:S(2)}) copy-start(f32[4,6,18,288]{3,0,2,1:T(4,128)} %param.11) | copy-start | bytes 1492996
  2.5 11.9 %copy-start.2 = (s32[6,18,288]{2,1,0:T(8,128)S(1)}, s32[6,18,288]{2,1,0:T(8,128)}, u32[]{:S(2)}) copy-start(s32[6,18,288]{2,1,0:T(8,128)} %source.1) | copy-start | bytes 373252
  2.7 11.9 %collective-permute-start = (f32[7,8,1152]{2,1,0:T(8,128)S(1)}, f32[7,8,1152]{2,1,0:T(8,128)S(1)}, u32[]{:S(2)}, u32[]{:S(2)}) collective-permute-start(f32[7,8,1152]{2,1,0:T(8,128)S(1)} %get-tuple-element.26), channel_id=1, source_target_pairs={{0,4},{4,0},{8,12},{12,8},{1,5},{5,1},{9,13},{13,9},{2,6},{6,2},{1... | collective-permute-start | bytes 774152 | tf_op jit(solution)/shard_map/ppermute | solution.py:463
  5.8 8.8 %collective-permute-start.1 = (f32[7,8,1152]{2,1,0:T(8,128)S(1)}, f32[7,8,1152]{2,1,0:T(8,128)S(1)}, u32[]{:S(2)}, u32[]{:S(2)}) collective-permute-start(f32[7,8,1152]{2,1,0:T(8,128)S(1)} %get-tuple-element.27), channel_id=1, source_target_pairs={{0,1},{1,0},{2,3},{3,2},{4,8},{5,9},{6,10},{7,11},{8,4},{9,5},{10,... | collective-permute-start | bytes 774152 | tf_op jit(solution)/shard_map/ppermute | solution.py:464
  9.6 13.1 %collective-permute-start.5 = (f32[7,8,1152]{2,1,0:T(8,128)S(1)}, f32[7,8,1152]{2,1,0:T(8,128)S(1)}, u32[]{:S(2)}, u32[]{:S(2)}) collective-permute-start(f32[7,8,1152]{2,1,0:T(8,128)S(1)} %get-tuple-element.36), channel_id=1, source_target_pairs={{0,4},{4,0},{8,12},{12,8},{1,5},{5,1},{9,13},{13,9},{2,6},{6,2},{1... | collective-permute-start | bytes 774152 | tf_op jit(solution)/shard_map/ppermute | solution.py:463
  12.9 10.0 %collective-permute-start.6 = (f32[7,8,1152]{2,1,0:T(8,128)S(1)}, f32[7,8,1152]{2,1,0:T(8,128)S(1)}, u32[]{:S(2)}, u32[]{:S(2)}) collective-permute-start(f32[7,8,1152]{2,1,0:T(8,128)S(1)} %get-tuple-element.37), channel_id=1, source_target_pairs={{0,1},{1,0},{2,3},{3,2},{4,8},{5,9},{6,10},{7,11},{8,4},{9,5},{10,... | collective-permute-start | bytes 774152 | tf_op jit(solution)/shard_map/ppermute | solution.py:464
  12.9 8.4 %collective-permute-start.10 = (f32[4,14,8,128]{3,2,1,0:T(8,128)S(1)}, f32[4,14,8,128]{3,2,1,0:T(8,128)S(1)}, u32[]{:S(2)}, u32[]{:S(2)}) collective-permute-start(f32[4,14,8,128]{3,2,1,0:T(8,128)S(1)} %get-tuple-element.42), channel_id=1, source_target_pairs={{0,2},{1,3},{2,0},{3,1},{4,6},{5,7},{6,4},{7,5},{8,10},{9,11},{10,... | collective-permute-start | bytes 688136 | tf_op jit(solution)/shard_map/ppermute | solution.py:507
  17.1 5.7 %collective-permute-start.4 = (f32[4,14,8,128]{3,2,1,0:T(8,128)S(1)}, f32[4,14,8,128]{3,2,1,0:T(8,128)S(1)}, u32[]{:S(2)}, u32[]{:S(2)}) collective-permute-start(f32[4,14,8,128]{3,2,1,0:T(8,128)S(1)} %get-tuple-element.35), channel_id=1, source_target_pairs={{0,1},{1,0},{2,3},{3,2},{4,5},{5,4},{6,7},{7,6},{8,9},{9,8},{10,11... | collective-permute-start | bytes 688136 | tf_op jit(solution)/shard_map/ppermute | solution.py:507
  17.4 8.8 %collective-permute-start.2 = (f32[2,14,8,128]{3,2,1,0:T(8,128)S(1)}, f32[2,14,8,128]{3,2,1,0:T(8,128)S(1)}, u32[]{:S(2)}, u32[]{:S(2)}) collective-permute-start(f32[2,14,8,128]{3,2,1,0:T(8,128)S(1)} %get-tuple-element.32), channel_id=1, source_target_pairs={{0,3},{1,2},{2,1},{3,0},{4,7},{5,6},{6,5},{7,4},{8,11},{9,10},{10,... | collective-permute-start | bytes 344072 | tf_op jit(solution)/shard_map/ppermute | solution.py:507
  21.3 6.4 %collective-permute-start.3 = (f32[2,14,8,128]{3,2,1,0:T(8,128)S(1)}, f32[2,14,8,128]{3,2,1,0:T(8,128)S(1)}, u32[]{:S(2)}, u32[]{:S(2)}) collective-permute-start(f32[2,14,8,128]{3,2,1,0:T(8,128)S(1)} %get-tuple-element.33), channel_id=1, source_target_pairs={{0,2},{1,3},{2,0},{3,1},{4,6},{5,7},{6,4},{7,5},{8,10},{9,11},{10,... | collective-permute-start | bytes 344072 | tf_op jit(solution)/shard_map/ppermute | solution.py:507
  22.8 4.9 %copy-start.3 = (s32[4]{0:T(128)S(1)}, s32[4]{0:T(128)}, u32[]{:S(2)}) copy-start(s32[4]{0:T(128)} %counts.3) | copy-start | bytes 52
  22.8 4.9 %collective-permute-start.11 = (f32[2,14,8,128]{3,2,1,0:T(8,128)S(1)}, f32[2,14,8,128]{3,2,1,0:T(8,128)S(1)}, u32[]{:S(2)}, u32[]{:S(2)}) collective-permute-start(f32[2,14,8,128]{3,2,1,0:T(8,128)S(1)} %slice.3), channel_id=1, source_target_pairs={{0,1},{1,0},{2,3},{3,2},{4,5},{5,4},{6,7},{7,6},{8,9},{9,8},{10,11... | collective-permute-start | bytes 344072 | tf_op jit(solution)/shard_map/ppermute | solution.py:507
  25.4 2.3 %collective-permute-start.9 = (f32[2,14,8,128]{3,2,1,0:T(8,128)S(1)}, f32[2,14,8,128]{3,2,1,0:T(8,128)S(1)}, u32[]{:S(2)}, u32[]{:S(2)}) collective-permute-start(f32[2,14,8,128]{3,2,1,0:T(8,128)S(1)} %get-tuple-element.41), channel_id=1, source_target_pairs={{0,1},{1,0},{2,3},{3,2},{4,5},{5,4},{6,7},{7,6},{8,9},{9,8},{10,11... | collective-permute-start | bytes 344072 | tf_op jit(solution)/shard_map/ppermute | solution.py:507
  26.0 5.2 %collective-permute-start.7 = (f32[2,14,8,128]{3,2,1,0:T(8,128)S(1)}, f32[2,14,8,128]{3,2,1,0:T(8,128)S(1)}, u32[]{:S(2)}, u32[]{:S(2)}) collective-permute-start(f32[2,14,8,128]{3,2,1,0:T(8,128)S(1)} %get-tuple-element.38), channel_id=1, source_target_pairs={{0,3},{1,2},{2,1},{3,0},{4,7},{5,6},{6,5},{7,4},{8,11},{9,10},{10,... | collective-permute-start | bytes 344072 | tf_op jit(solution)/shard_map/ppermute | solution.py:507
  26.2 7.7 %collective-permute-start.8 = (f32[2,14,8,128]{3,2,1,0:T(8,128)S(1)}, f32[2,14,8,128]{3,2,1,0:T(8,128)S(1)}, u32[]{:S(2)}, u32[]{:S(2)}) collective-permute-start(f32[2,14,8,128]{3,2,1,0:T(8,128)S(1)} %get-tuple-element.39), channel_id=1, source_target_pairs={{0,2},{1,3},{2,0},{3,1},{4,6},{5,7},{6,4},{7,5},{8,10},{9,11},{10,... | collective-permute-start | bytes 344072 | tf_op jit(solution)/shard_map/ppermute | solution.py:507

commit v12 on v11

--- a/solution.py
+++ b/solution.py
@@ -258,9 +258,9 @@
     hand_out(packed, outs, groups)
 
 
-def edge_kernel(count, rows, slot, joint, state, first_round, second_round, first, cx, cy, *refs):
+def edge_kernel(count, rows, groups, slot, joint, state, first_round, second_round, first, cx, cy, *refs):
     others = refs[:len(joint)]
-    outs, (packed, beyond, swept, edge, inter, west, flux) = refs[-7 - count:-7], refs[-7:]
+    outs, (packed, beyond, swept, edge, inter, west, flux) = refs[-7 - len(groups):-7], refs[-7:]
     nlon = state.shape[3]
     nj = nlon // LANES
     lane = lane_ids()
@@ -324,7 +324,7 @@
     lon_pass(listed(ends), swept, coef_x, inter, west, flux, lane, keep_edge)
     lat_pass(1, nj, ends_last, cell_first, coef_y, put_last)
     lon_pass(listed(ends_last), swept, coef_x, inter, west, flux, lane, send)
-    hand_out(packed, outs, [(k,) for k in range(count)])
+    hand_out(packed, outs, groups)
     place = packed.shape[1]
     for other, (begin, size) in zip(others, joint):
         copy_units(other.at[pl.ds(begin, size)], outs[1], place)
@@ -346,9 +346,8 @@
             out[k, row] = total
 
 
-def remap_kernel(count, plan, numbers, whole, counts, *refs):
-    chunks, weights, ready, (out, levels, result, sems) = refs[:len(plan)], refs[len(plan)], refs[len(plan) + 1:-4], refs[-4:]
-    ready = ready if whole else ()
+def remap_kernel(count, plan, numbers, counts, *refs):
+    chunks, weights, (out, levels, result, sems) = refs[:len(plan)], refs[len(plan)], refs[-4:]
     me = lax.axis_index("lev")
     targets, _, _, width = result.shape
     _, mains, tail, per, _ = packed_sizes(width * count, count)
@@ -358,10 +357,6 @@
         copy = pltpu.make_async_copy(source, target, sems.at[len(copies)])
         copy.start()
         copies.append(copy)
-
-    if ready:
-        others = [n for n in range(out.shape[1] // BLOCK) if n not in numbers]
-        leave(ready[0], out.at[:, pl.ds(others[0] * BLOCK, len(others) * BLOCK)])
 
     def level_of(k, slot):
         d = me ^ k
@@ -398,12 +393,13 @@
                         term = jnp.broadcast_to(weights[k, row, j:j + 1, lanes], (SUB, wide)) * values[level][:, :wide]
                         total = term if total is None else total + term
                     result[k, at * BLOCK + q, :, lanes] = total
-        if ready:
-            leave(result.at[:, pl.ds(at * BLOCK, BLOCK)], out.at[:, pl.ds(number * BLOCK, BLOCK)])
-    if not ready:
-        leave(result, out)
+        leave(result.at[:, pl.ds(at * BLOCK, BLOCK)], out.at[:, pl.ds(number * BLOCK, BLOCK)])
     for copy in copies:
         copy.wait()
+
+
+def mark_kernel(*refs):
+    refs[-1][...] = jnp.zeros((SUB, LANES), jnp.float32)
 
 
 def tiles_of(array):
@@ -493,12 +489,13 @@
     swept = vmem(1, 2 * HALO, number, nlon)
     stage = vmem(2 * HALO, number, nlon)
 
-    def edge(slot, joint, after):
+    def edge(slot, groups, joint, after):
         args = (state, *rounds[slot], first, cx, cy, *(chunk for chunk, _ in joint), *after)
         parts = tuple(part for _, part in joint)
+        units = [2 * len(group) + (sum(size for _, size in parts) if group == (1,) else 0) for group in groups]
         return call(
-            functools.partial(edge_kernel, count, rows, slot, parts),
-            [f32(*box(2 + sum(size for _, size in parts) if k == 1 else 2)) for k in range(count)], args,
+            functools.partial(edge_kernel, count, rows, groups, slot, parts),
+            [f32(*box(n)) for n in units], args,
             specs=[VMEM] * (len(args) - len(after)) + [ANY] * len(after),
             scratch=[vmem(*box(2, count)), vmem(3, 2, SUB, nlon), swept, swept, stage, stage, stage],
             cost=cost(60 * tracers.size, 8 * tracers.size))
@@ -509,45 +506,46 @@
     def units_of(k, places):
         return tuple((k, slot, block) for slot, block in places)
 
-    def remap(listed, numbers, height, ready, after=()):
-        args = (level_counts, *(chunk for _, chunk in listed), taps, *ready, *after)
+    def remap(listed, after):
+        args = (level_counts, *(chunk for _, chunk in listed), taps, *after)
         return pl.pallas_call(
-            functools.partial(remap_kernel, count, tuple(units for units, _ in listed), numbers, bool(ready)),
-            out_shape=f32(targets, height, number, width),
+            functools.partial(remap_kernel, count, tuple(units for units, _ in listed), tuple(range(blocks))),
+            out_shape=f32(targets, rows, number, width),
             in_specs=[SMEM] + [VMEM] * (len(args) - 1 - len(after)) + [ANY] * len(after),
             out_specs=ANY,
             scratch_shapes=[
-                vmem(targets + 1, len(numbers), size, SUB, LANES),
-                vmem(targets, len(numbers) * BLOCK, number, width),
-                pltpu.SemaphoreType.DMA((len(numbers) + 1,)),
+                vmem(targets + 1, blocks, size, SUB, LANES),
+                vmem(targets, rows, number, width),
+                pltpu.SemaphoreType.DMA((blocks,)),
             ],
             compiler_params=pltpu.CompilerParams(vmem_limit_bytes=16 << 20),
             cost_estimate=cost(1, 1),
         )(*args)
 
+    def mark(chunks):
+        return pl.pallas_call(
+            mark_kernel, out_shape=f32(SUB, LANES), in_specs=[ANY] * len(chunks), out_specs=VMEM, cost_estimate=cost(1, 1),
+        )(*chunks)
+
     places = tuple((slot, 1 + b) for slot in range(depth) for b in range(inner))
     passing = tuple((None, None, None) for _ in places)
-    arrived = [swapped(sent_on, k) for sent_on, k in zip(middle[2:], chips)]
-    middle_chunks = [(units_of(k, places) + passing, chunk) for k, chunk in zip(chips, arrived)]
-    middle_chunks.append((units_of(0, places), middle[0]))
-    joint, joint_units, after = [(middle[1], (0, inner_units))], units_of(1, places), (taps,)
-    edge_chunks, far = [], []
+    arrived = [swapped(chunk, k) for k, chunk in zip(chips, middle[2:])]
+    listed = [(units_of(k, places) + passing, chunk) for k, chunk in zip(chips, arrived)]
+    listed.append((units_of(0, places), middle[0]))
+    beside_me = [(units_of(1, places), middle[1])]
+    after, marks = (taps,), []
     for slot in range(depth):
         own = ((slot, 0), (slot, blocks - 1))
-        done = edge(slot, joint, after)
+        done = edge(slot, tuple((k,) for k in range(count)), [], after)
         crossing = [(units_of(k, own), swapped(done[k], k)) for k in range(count - 1, 1, -1)]
-        beside_me = (units_of(1, own) + joint_units, swapped(done[1], 1))
-        edge_chunks += crossing + [(units_of(0, own), done[0]), beside_me]
-        if slot + 1 < depth:
-            far += [chunk for _, chunk in crossing]
-        middle_chunks.append(beside_me)
-        if slot == 0:
-            for k, chunk in zip(chips, arrived):
-                chunk, _ = lax.optimization_barrier((chunk, done[0]))
-                middle_chunks.append((units_of(k ^ 1, places), swapped(chunk[inner_units:], 1)))
-        joint, joint_units, after = [], (), (done[0], beside_me[1])
-    middle_rows = remap(middle_chunks, tuple(range(1, blocks - 1)), inner * BLOCK, (), far)
-    out = remap(edge_chunks, (0, blocks - 1), rows, (middle_rows,))
+        listed += crossing + [(units_of(0, own), done[0])]
+        beside_me.append((units_of(1, own), done[1]))
+        marks.append(mark([chunk for _, chunk in crossing]))
+        after = (done[0], *arrived)
+    beside_me += [(units_of(k ^ 1, places), chunk) for k, chunk in zip(chips, arrived)]
+    waiting = lax.optimization_barrier((*(chunk for _, chunk in beside_me), done[0]))
+    listed += [(units, swapped(chunk[chunk.shape[0] - len(units):], 1)) for (units, _), chunk in zip(beside_me, waiting)]
+    out = remap(listed, marks)
     return jnp.transpose(out, (2, 0, 1, 3))
 
 

time: 35.8 us -> 40.2 us (1.12)
  local copies, waits for them, and re-layouts: 1.34 us -> 6.93 us
  waiting for transfers between devices: 8.57 us -> 6.94 us
    unnamed x8 -> x28, local copies, waits for them, and re-layouts: 1.33 us -> 6.92 us
    ppermute x8 -> x9, waiting for transfers between devices: 8.56 us -> 6.93 us  [swapped(): return lax.ppermute(sent, 'lev', [(i, i ^ k) for i in range(count)])]
    pallas_call x0 -> x2, Pallas kernels: none -> 1.18 us  [mark(): pl.pallas_call(mark_kernel, out_shape=f32(SUB, LANES), in_specs=[ANY] * l...]
    pallas_call x2 -> x1, Pallas kernels: 2.78 us -> 1.9 us  [remap(): pl.pallas_call(functools.partial(remap_kernel, count, tuple((units for un...]
    ppermute x8 -> x9, starting transfers between devices: 6.02 us -> 6.05 us  [swapped(): return lax.ppermute(sent, 'lev', [(i, i ^ k) for i in range(count)])]
  transfers between devices with their start and end apart: 12 -> 13, of which waited for: 3 -> 3; matrix products, arithmetic and copies ran while one was open for 0% -> 0% of each run, Pallas kernels for 28% -> 26%
where the time goes in v12:
time: 40.2 us; the launch traced here: 39.9 us
  Pallas kernels  12.4 us (31%)
  starting transfers between devices  12.4 us (31%)
  waiting for transfers between devices  6.94 us (17%)
  local copies, waits for them, and re-layouts  6.93 us (17%)
  other arithmetic  1.14 us (3%)
    pallas_call x5, Pallas kernels, call(): pl.pallas_call(kernel, out_shape=outs, in_specs=specs or [VMEM] * len(arg...  9.36 us
    ppermute x9, waiting for transfers between devices, swapped(): return lax.ppermute(sent, 'lev', [(i, i ^ k) for i in range(count)])  6.93 us
    unnamed x28, local copies, waits for them, and re-layouts  6.92 us
    ppermute x2, starting transfers between devices, beside(): lax.ppermute(sent[0], 'lat', [(i, i ^ 1) for i in range(bands)])  6.31 us
    ppermute x9, starting transfers between devices, swapped(): return lax.ppermute(sent, 'lev', [(i, i ^ k) for i in range(count)])  6.05 us
    pallas_call x1, Pallas kernels, remap(): pl.pallas_call(functools.partial(remap_kernel, count, tuple((units for un...  1.9 us
    pallas_call x2, Pallas kernels, mark(): pl.pallas_call(mark_kernel, out_shape=f32(SUB, LANES), in_specs=[ANY] * l...  1.18 us
    concatenate x1, other arithmetic, shards(): jnp.concatenate([jnp.transpose(wind_x, (1, 0, 2)), jnp.transpose(wind_y,...  1.14 us
  transfers between devices with their start and end apart: 13, of which 3 were waited for; matrix products, arithmetic and copies ran while one was open for 0% of the time, Pallas kernels for 26%

profile of v12, /device:TPU:0, one launch (start us, length us, event | category | flops | bytes accessed | tf_op | source)
XLA Modules:
  0.0 39.9 jit_solution(15046839855358588273)
XLA Ops:
  0.0 1.1 %pad_maximum_fusion.winds.joined = f32[36,2,1152]{2,1,0:T(2,128)S(1)} fusion(f32[18,2,1152]{2,1,0:T(2,128)} %bitcast.13, f32[18,2,1152]{2,1,0:T(2,128)} %bitcast.14), kind=kLoop, calls=%fused_computation | loop fusion | flops 82944 | bytes 663552 | tf_op jit(solution)/shard_map/concatenate | solution.py:448
  1.1 0.0 copy-start
  1.2 1.3 %copy-done = f32[8,2,18,1152]{3,1,2,0:T(2,128)S(1)} copy-done((f32[8,2,18,1152]{3,1,2,0:T(2,128)S(1)}, f32[8,2,18,1152]{3,1,2,0:T(2,128)}, u32[]{:S(2)}) %copy-start) | copy-done | bytes 1327128
  2.5 0.2 shard_map.64
  2.7 3.1 %collective-permute-start.1 = (f32[7,8,1152]{2,1,0:T(8,128)S(1)}, f32[7,8,1152]{2,1,0:T(8,128)S(1)}, u32[]{:S(2)}, u32[]{:S(2)}) collective-permute-start(f32[7,8,1152]{2,1,0:T(8,128)S(1)} %get-tuple-element.31), channel_id=1, source_target_pairs={{0,4},{4,0},{8,12},{12,8},{1,5},{5,1},{9,13},{13,9},{2,6},{6,2},{1... | collective-permute-start | bytes 774152 | tf_op jit(solution)/shard_map/ppermute | solution.py:459
  5.8 0.0 collective-permute-start.2
  5.8 3.8 %shard_map.65 = (f32[2,14,8,128]{3,2,1,0:T(8,128)S(1)}, f32[2,14,8,128]{3,2,1,0:T(8,128)S(1)}, f32[4,14,8,128]{3,2,1,0:T(8,128)S(1)}, f32[2,12,8,1152]{3,2,1,0:T...) custom-call(f32[2,18,8,1152]{3,2,1,0:T(8,128)S(1)} %get-tuple-elemen, ...), custom_call_target="tpu_custom_call" | custom-call | flops 1 | bytes 1 | tf_op jit(solution)/shard_map/pallas_call | solution.py:419
  9.6 3.2 %collective-permute-start.5 = (f32[7,8,1152]{2,1,0:T(8,128)S(1)}, f32[7,8,1152]{2,1,0:T(8,128)S(1)}, u32[]{:S(2)}, u32[]{:S(2)}) collective-permute-start(f32[7,8,1152]{2,1,0:T(8,128)S(1)} %get-tuple-element.39), channel_id=1, source_target_pairs={{0,4},{4,0},{8,12},{12,8},{1,5},{5,1},{9,13},{13,9},{2,6},{6,2},{1... | collective-permute-start | bytes 774152 | tf_op jit(solution)/shard_map/ppermute | solution.py:459
  12.9 0.0 collective-permute-start.6
  12.9 1.5 %collective-permute-start = (f32[4,14,8,128]{3,2,1,0:T(8,128)S(1)}, f32[4,14,8,128]{3,2,1,0:T(8,128)S(1)}, u32[]{:S(2)}, u32[]{:S(2)}) collective-permute-start(f32[4,14,8,128]{3,2,1,0:T(8,128)S(1)} %get-tuple-element.29), channel_id=1, source_target_pairs={{0,2},{1,3},{2,0},{3,1},{4,6},{5,7},{6,4},{7,5},{8,10},{9,11},{10,... | collective-permute-start | bytes 688136 | tf_op jit(solution)/shard_map/ppermute | solution.py:504
  14.4 0.0 copy-done.1
  14.4 0.0 copy-done.10
  14.4 0.2 shard_map.66.refs_0_.refs_12_
  14.6 0.0 collective-permute-done.1.first_round
  14.6 0.0 collective-permute-done.2.second_round
  14.6 2.6 %shard_map.67 = (f32[2,14,8,128]{3,2,1,0:T(8,128)S(1)}, f32[2,14,8,128]{3,2,1,0:T(8,128)S(1)}, f32[2,14,8,128]{3,2,1,0:T(8,128)S(1)}, f32[2,14,8,128]{3,2,1,0:T(8,128)S(1)}) custom-call(f32[2,18,8,1152]{3,2,1,0:T(8,128)S(1)} %get-tuple-element.28.state, f32[7,8,1152]{2,1,0:T(8,128)S(1)} %collective-permute-done.1.first_round, ...), custom_call_target="tpu_custom_call" | custom-call | flops 19906560 | bytes 2654208 | tf_op jit(solution)/shard_map/pallas_call | solution.py:419
  17.1 0.4 %collective-permute-start.3 = (f32[2,14,8,128]{3,2,1,0:T(8,128)S(1)}, f32[2,14,8,128]{3,2,1,0:T(8,128)S(1)}, u32[]{:S(2)}, u32[]{:S(2)}) collective-permute-start(f32[2,14,8,128]{3,2,1,0:T(8,128)S(1)} %get-tuple-element.36), channel_id=1, source_target_pairs={{0,3},{1,2},{2,1},{3,0},{4,7},{5,6},{6,5},{7,4},{8,11},{9,10},{10,... | collective-permute-start | bytes 344072 | tf_op jit(solution)/shard_map/ppermute | solution.py:504
  17.6 1.5 %collective-permute-start.4 = (f32[2,14,8,128]{3,2,1,0:T(8,128)S(1)}, f32[2,14,8,128]{3,2,1,0:T(8,128)S(1)}, u32[]{:S(2)}, u32[]{:S(2)}) collective-permute-start(f32[2,14,8,128]{3,2,1,0:T(8,128)S(1)} %get-tuple-element.37), channel_id=1, source_target_pairs={{0,2},{1,3},{2,0},{3,1},{4,6},{5,7},{6,4},{7,5},{8,10},{9,11},{10,... | collective-permute-start | bytes 344072 | tf_op jit(solution)/shard_map/ppermute | solution.py:504
  19.1 2.2 %collective-permute-done.refs_1_.refs_0_ = f32[4,14,8,128]{3,2,1,0:T(8,128)S(1)} collective-permute-done((f32[4,14,8,128]{3,2,1,0:T(8,128)S(1)}, f32[4,14,8,128]{3,2,1,0:T(8,128)S(1)}, u32[]{:S(2)}, u32[]{:S(2)}) %collective-permute-start) | collective-permute-done | bytes 229408 | tf_op jit(solution)/shard_map/ppermute | solution.py:504
  21.3 0.0 collective-permute-done.5.first_round
  21.3 0.0 collective-permute-done.6.second_round
  21.3 2.5 %shard_map.68 = (f32[2,14,8,128]{3,2,1,0:T(8,128)S(1)}, f32[2,14,8,128]{3,2,1,0:T(8,128)S(1)}, f32[2,14,8,128]{3,2,1,0:T(8,128)S(1)}, f32[2,14,8,128]{3,2,1,0:T(8,128)S(1)}) custom-call(f32[2,18,8,1152]{3,2,1,0:T(8,128)S(1)} %get-tuple-element.28.state, f32[7,8,1152]{2,1,0:T(8,128)S(1)} %collective-permute-done.5.first_round, ...), custom_call_target="tpu_custom_call" | custom-call | flops 19906560 | bytes 2654208 | tf_op jit(solution)/shard_map/pallas_call | solution.py:419
  23.8 0.5 %collective-permute-start.7 = (f32[2,14,8,128]{3,2,1,0:T(8,128)S(1)}, f32[2,14,8,128]{3,2,1,0:T(8,128)S(1)}, u32[]{:S(2)}, u32[]{:S(2)}) collective-permute-start(f32[2,14,8,128]{3,2,1,0:T(8,128)S(1)} %get-tuple-element.41), channel_id=1, source_target_pairs={{0,3},{1,2},{2,1},{3,0},{4,7},{5,6},{6,5},{7,4},{8,11},{9,10},{10,... | collective-permute-start | bytes 344072 | tf_op jit(solution)/shard_map/ppermute | solution.py:504
  24.4 1.2 %collective-permute-start.12 = (f32[2,14,8,128]{3,2,1,0:T(8,128)S(1)}, f32[2,14,8,128]{3,2,1,0:T(8,128)S(1)}, u32[]{:S(2)}, u32[]{:S(2)}) collective-permute-start(f32[2,14,8,128]{3,2,1,0:T(8,128)S(1)} %slice.3), channel_id=1, source_target_pairs={{0,1},{1,0},{2,3},{3,2},{4,5},{5,4},{6,7},{7,6},{8,9},{9,8},{10,11... | collective-permute-start | bytes 344072 | tf_op jit(solution)/shard_map/ppermute | solution.py:504
  25.6 0.1 collective-permute-start.9
  25.7 0.0 collective-permute-done.3.refs_0_.refs_2_
  25.7 0.5 %collective-permute-start.8 = (f32[2,14,8,128]{3,2,1,0:T(8,128)S(1)}, f32[2,14,8,128]{3,2,1,0:T(8,128)S(1)}, u32[]{:S(2)}, u32[]{:S(2)}) collective-permute-start(f32[2,14,8,128]{3,2,1,0:T(8,128)S(1)} %get-tuple-element.42), channel_id=1, source_target_pairs={{0,2},{1,3},{2,0},{3,1},{4,6},{5,7},{6,4},{7,5},{8,10},{9,11},{10,... | collective-permute-start | bytes 344072 | tf_op jit(solution)/shard_map/ppermute | solution.py:504
  26.2 0.0 collective-permute-done.4.refs_1_.refs_3_
  26.2 0.2 collective-permute-start.10
  26.4 2.9 %collective-permute-done.7.refs_0_.refs_5_ = f32[2,14,8,128]{3,2,1,0:T(8,128)S(1)} collective-permute-done((f32[2,14,8,128]{3,2,1,0:T(8,128)S(1)}, f32[2,14,8,128]{3,2,1,0:T(8,128)S(1)}, u32[]{:S(2)}, u32[]{:S(2)}) %collective-permute-start.7) | collective-permute-done | bytes 114720 | tf_op jit(solution)/shard_map/ppermute | solution.py:504
  29.3 0.1 collective-permute-start.11
  29.4 0.0 copy-done.2
  29.4 0.6 %shard_map.69.refs_13_ = f32[8,128]{1,0:T(8,128)} custom-call(f32[2,14,8,128]{3,2,1,0:T(8,128)} %copy-done.2, f32[2,14,8,128]{3,2,1,0:T(8,128)} %copy-done.4), custom_call_target="tpu_custom_call" | custom-call | flops 1 | bytes 1 | tf_op jit(solution)/shard_map/pallas_call | solution.py:526
  30.0 1.8 %collective-permute-done.8.refs_1_.refs_6_ = f32[2,14,8,128]{3,2,1,0:T(8,128)S(1)} collective-permute-done((f32[2,14,8,128]{3,2,1,0:T(8,128)S(1)}, f32[2,14,8,128]{3,2,1,0:T(8,128)S(1)}, u32[]{:S(2)}, u32[]{:S(2)}) %collective-permute-start.8) | collective-permute-done | bytes 114720 | tf_op jit(solution)/shard_map/ppermute | solution.py:504
  31.8 0.6 %copy-done.8 = f32[2,14,8,128]{3,2,1,0:T(8,128)} copy-done((f32[2,14,8,128]{3,2,1,0:T(8,128)}, f32[2,14,8,128]{3,2,1,0:T(8,128)S(1)}, u32[]{:S(2)}) %copy-start.8) | copy-done | bytes 114712
  32.4 0.6 %shard_map.70.refs_14_ = f32[8,128]{1,0:T(8,128)} custom-call(f32[2,14,8,128]{3,2,1,0:T(8,128)} %copy-done.6, f32[2,14,8,128]{3,2,1,0:T(8,128)} %copy-done.8), custom_call_target="tpu_custom_call" | custom-call | flops 1 | bytes 1 | tf_op jit(solution)/shard_map/pallas_call | solution.py:526
  33.0 0.0 collective-permute-done.12.refs_11_
  33.0 0.0 collective-permute-done.9.refs_8_
  33.0 0.0 collective-permute-done.10.refs_9_
  33.1 0.0 collective-permute-done.11.refs_10_
  33.1 0.0 copy-start.3
  33.1 0.9 %copy-done.3 = f32[2,14,8,128]{3,2,1,0:T(8,128)S(1)} copy-done((f32[2,14,8,128]{3,2,1,0:T(8,128)S(1)}, f32[2,14,8,128]{3,2,1,0:T(8,128)}, u32[]{:S(2)}) %copy-start.3) | copy-done | bytes 114712
  34.0 0.9 %copy-done.5 = f32[2,14,8,128]{3,2,1,0:T(8,128)S(1)} copy-done((f32[2,14,8,128]{3,2,1,0:T(8,128)S(1)}, f32[2,14,8,128]{3,2,1,0:T(8,128)}, u32[]{:S(2)}) %copy-start.5) | copy-done | bytes 114712
  34.9 0.9 %copy-done.7 = f32[2,14,8,128]{3,2,1,0:T(8,128)S(1)} copy-done((f32[2,14,8,128]{3,2,1,0:T(8,128)S(1)}, f32[2,14,8,128]{3,2,1,0:T(8,128)}, u32[]{:S(2)}) %copy-start.7) | copy-done | bytes 114712
  35.8 0.9 %copy-done.9 = f32[2,14,8,128]{3,2,1,0:T(8,128)S(1)} copy-done((f32[2,14,8,128]{3,2,1,0:T(8,128)S(1)}, f32[2,14,8,128]{3,2,1,0:T(8,128)}, u32[]{:S(2)}) %copy-start.9) | copy-done | bytes 114712
  36.7 0.7 %copy-done.11 = f32[8,128]{1,0:T(8,128)S(1)} copy-done((f32[8,128]{1,0:T(8,128)S(1)}, f32[8,128]{1,0:T(8,128)}, u32[]{:S(2)}) %copy-start.11) | copy-done | bytes 4120
  37.3 0.7 %copy-done.12 = f32[8,128]{1,0:T(8,128)S(1)} copy-done((f32[8,128]{1,0:T(8,128)S(1)}, f32[8,128]{1,0:T(8,128)}, u32[]{:S(2)}) %copy-start.12) | copy-done | bytes 4120
  38.0 1.9 %shard_map.71 = f32[6,18,8,288]{3,2,1,0:T(8,128)} custom-call(s32[4]{0:T(128)S(1)} %copy-done.13, f32[4,14,8,128]{3,2,1,0:T(8,128)S(1)} %collective-permute-done.refs_1_.refs_0_, f32[2,14,8,128]{3,2,1,0:T(8,128)S(1)} %get-tuple-element.30.refs_1_, f32[2,14,8,128]{3,2,1,0:T(8,128)S(1)} %copy-done.3, f32[2,14,8,128]{3,2,1,0:T(8,128)S(1)} %copy-done.5, ...), custom_call_target="tpu_custom_call" | custom-call | flops 1 | bytes 1 | tf_op jit(solution)/shard_map/pallas_call | solution.py:511
  (16 shorter events, 0.0 us)
Async XLA Ops:
  1.1 1.3 %copy-start = (f32[8,2,18,1152]{3,1,2,0:T(2,128)S(1)}, f32[8,2,18,1152]{3,1,2,0:T(2,128)}, u32[]{:S(2)}) copy-start(f32[8,2,18,1152]{3,1,2,0:T(2,128)} %param.6) | copy-start | bytes 3981316
  2.5 11.9 %copy-start.1 = (f32[4,6,18,288]{3,0,2,1:T(4,128)S(1)}, f32[4,6,18,288]{3,0,2,1:T(4,128)}, u32[]{:S(2)}) copy-start(f32[4,6,18,288]{3,0,2,1:T(4,128)} %param.11) | copy-start | bytes 1492996
  2.5 11.9 %copy-start.10 = (s32[6,18,288]{2,1,0:T(8,128)S(1)}, s32[6,18,288]{2,1,0:T(8,128)}, u32[]{:S(2)}) copy-start(s32[6,18,288]{2,1,0:T(8,128)} %source.1) | copy-start | bytes 373252
  2.7 11.9 %collective-permute-start.1 = (f32[7,8,1152]{2,1,0:T(8,128)S(1)}, f32[7,8,1152]{2,1,0:T(8,128)S(1)}, u32[]{:S(2)}, u32[]{:S(2)}) collective-permute-start(f32[7,8,1152]{2,1,0:T(8,128)S(1)} %get-tuple-element.31), channel_id=1, source_target_pairs={{0,4},{4,0},{8,12},{12,8},{1,5},{5,1},{9,13},{13,9},{2,6},{6,2},{1... | collective-permute-start | bytes 774152 | tf_op jit(solution)/shard_map/ppermute | solution.py:459
  5.8 8.8 %collective-permute-start.2 = (f32[7,8,1152]{2,1,0:T(8,128)S(1)}, f32[7,8,1152]{2,1,0:T(8,128)S(1)}, u32[]{:S(2)}, u32[]{:S(2)}) collective-permute-start(f32[7,8,1152]{2,1,0:T(8,128)S(1)} %get-tuple-element.32), channel_id=1, source_target_pairs={{0,1},{1,0},{2,3},{3,2},{4,8},{5,9},{6,10},{7,11},{8,4},{9,5},{10,... | collective-permute-start | bytes 774152 | tf_op jit(solution)/shard_map/ppermute | solution.py:460
  9.6 11.6 %collective-permute-start.5 = (f32[7,8,1152]{2,1,0:T(8,128)S(1)}, f32[7,8,1152]{2,1,0:T(8,128)S(1)}, u32[]{:S(2)}, u32[]{:S(2)}) collective-permute-start(f32[7,8,1152]{2,1,0:T(8,128)S(1)} %get-tuple-element.39), channel_id=1, source_target_pairs={{0,4},{4,0},{8,12},{12,8},{1,5},{5,1},{9,13},{13,9},{2,6},{6,2},{1... | collective-permute-start | bytes 774152 | tf_op jit(solution)/shard_map/ppermute | solution.py:459
  12.9 8.4 %collective-permute-start.6 = (f32[7,8,1152]{2,1,0:T(8,128)S(1)}, f32[7,8,1152]{2,1,0:T(8,128)S(1)}, u32[]{:S(2)}, u32[]{:S(2)}) collective-permute-start(f32[7,8,1152]{2,1,0:T(8,128)S(1)} %get-tuple-element.40), channel_id=1, source_target_pairs={{0,1},{1,0},{2,3},{3,2},{4,8},{5,9},{6,10},{7,11},{8,4},{9,5},{10,... | collective-permute-start | bytes 774152 | tf_op jit(solution)/shard_map/ppermute | solution.py:460
  12.9 8.4 %collective-permute-start = (f32[4,14,8,128]{3,2,1,0:T(8,128)S(1)}, f32[4,14,8,128]{3,2,1,0:T(8,128)S(1)}, u32[]{:S(2)}, u32[]{:S(2)}) collective-permute-start(f32[4,14,8,128]{3,2,1,0:T(8,128)S(1)} %get-tuple-element.29), channel_id=1, source_target_pairs={{0,2},{1,3},{2,0},{3,1},{4,6},{5,7},{6,4},{7,5},{8,10},{9,11},{10,... | collective-permute-start | bytes 688136 | tf_op jit(solution)/shard_map/ppermute | solution.py:504
  17.1 8.5 %collective-permute-start.3 = (f32[2,14,8,128]{3,2,1,0:T(8,128)S(1)}, f32[2,14,8,128]{3,2,1,0:T(8,128)S(1)}, u32[]{:S(2)}, u32[]{:S(2)}) collective-permute-start(f32[2,14,8,128]{3,2,1,0:T(8,128)S(1)} %get-tuple-element.36), channel_id=1, source_target_pairs={{0,3},{1,2},{2,1},{3,0},{4,7},{5,6},{6,5},{7,4},{8,11},{9,10},{10,... | collective-permute-start | bytes 344072 | tf_op jit(solution)/shard_map/ppermute | solution.py:504
  17.6 8.6 %collective-permute-start.4 = (f32[2,14,8,128]{3,2,1,0:T(8,128)S(1)}, f32[2,14,8,128]{3,2,1,0:T(8,128)S(1)}, u32[]{:S(2)}, u32[]{:S(2)}) collective-permute-start(f32[2,14,8,128]{3,2,1,0:T(8,128)S(1)} %get-tuple-element.37), channel_id=1, source_target_pairs={{0,2},{1,3},{2,0},{3,1},{4,6},{5,7},{6,4},{7,5},{8,10},{9,11},{10,... | collective-permute-start | bytes 344072 | tf_op jit(solution)/shard_map/ppermute | solution.py:504
  21.3 11.8 %copy-start.13 = (s32[4]{0:T(128)S(1)}, s32[4]{0:T(128)}, u32[]{:S(2)}) copy-start(s32[4]{0:T(128)} %counts.1) | copy-start | bytes 52
  23.8 5.5 %collective-permute-start.7 = (f32[2,14,8,128]{3,2,1,0:T(8,128)S(1)}, f32[2,14,8,128]{3,2,1,0:T(8,128)S(1)}, u32[]{:S(2)}, u32[]{:S(2)}) collective-permute-start(f32[2,14,8,128]{3,2,1,0:T(8,128)S(1)} %get-tuple-element.41), channel_id=1, source_target_pairs={{0,3},{1,2},{2,1},{3,0},{4,7},{5,6},{6,5},{7,4},{8,11},{9,10},{10,... | collective-permute-start | bytes 344072 | tf_op jit(solution)/shard_map/ppermute | solution.py:504
  24.4 8.7 %collective-permute-start.12 = (f32[2,14,8,128]{3,2,1,0:T(8,128)S(1)}, f32[2,14,8,128]{3,2,1,0:T(8,128)S(1)}, u32[]{:S(2)}, u32[]{:S(2)}) collective-permute-start(f32[2,14,8,128]{3,2,1,0:T(8,128)S(1)} %slice.3), channel_id=1, source_target_pairs={{0,1},{1,0},{2,3},{3,2},{4,5},{5,4},{6,7},{7,6},{8,9},{9,8},{10,11... | collective-permute-start | bytes 344072 | tf_op jit(solution)/shard_map/ppermute | solution.py:504
  25.6 7.5 %collective-permute-start.9 = (f32[2,14,8,128]{3,2,1,0:T(8,128)S(1)}, f32[2,14,8,128]{3,2,1,0:T(8,128)S(1)}, u32[]{:S(2)}, u32[]{:S(2)}) collective-permute-start(f32[2,14,8,128]{3,2,1,0:T(8,128)S(1)} %get-tuple-element.47), channel_id=1, source_target_pairs={{0,1},{1,0},{2,3},{3,2},{4,5},{5,4},{6,7},{7,6},{8,9},{9,8},{10,11... | collective-permute-start | bytes 344072 | tf_op jit(solution)/shard_map/ppermute | solution.py:504
  25.7 3.8 %copy-start.2 = (f32[2,14,8,128]{3,2,1,0:T(8,128)}, f32[2,14,8,128]{3,2,1,0:T(8,128)S(1)}, u32[]{:S(2)}) copy-start(f32[2,14,8,128]{3,2,1,0:T(8,128)S(1)} %collective-permute-done.3.refs_0_.refs_2_) | copy-start | bytes 344068
  25.7 6.1 %collective-permute-start.8 = (f32[2,14,8,128]{3,2,1,0:T(8,128)S(1)}, f32[2,14,8,128]{3,2,1,0:T(8,128)S(1)}, u32[]{:S(2)}, u32[]{:S(2)}) collective-permute-start(f32[2,14,8,128]{3,2,1,0:T(8,128)S(1)} %get-tuple-element.42), channel_id=1, source_target_pairs={{0,2},{1,3},{2,0},{3,1},{4,6},{5,7},{6,4},{7,5},{8,10},{9,11},{10,... | collective-permute-start | bytes 344072 | tf_op jit(solution)/shard_map/ppermute | solution.py:504
  26.2 3.2 %copy-start.4 = (f32[2,14,8,128]{3,2,1,0:T(8,128)}, f32[2,14,8,128]{3,2,1,0:T(8,128)S(1)}, u32[]{:S(2)}) copy-start(f32[2,14,8,128]{3,2,1,0:T(8,128)S(1)} %collective-permute-done.4.refs_1_.refs_3_) | copy-start | bytes 344068
  26.2 6.8 %collective-permute-start.10 = (f32[2,14,8,128]{3,2,1,0:T(8,128)S(1)}, f32[2,14,8,128]{3,2,1,0:T(8,128)S(1)}, u32[]{:S(2)}, u32[]{:S(2)}) collective-permute-start(f32[2,14,8,128]{3,2,1,0:T(8,128)S(1)} %get-tuple-element.48), channel_id=1, source_target_pairs={{0,1},{1,0},{2,3},{3,2},{4,5},{5,4},{6,7},{7,6},{8,9},{9,8},{10,11... | collective-permute-start | bytes 344072 | tf_op jit(solution)/shard_map/ppermute | solution.py:504
  29.3 2.5 %copy-start.6 = (f32[2,14,8,128]{3,2,1,0:T(8,128)}, f32[2,14,8,128]{3,2,1,0:T(8,128)S(1)}, u32[]{:S(2)}) copy-start(f32[2,14,8,128]{3,2,1,0:T(8,128)S(1)} %collective-permute-done.7.refs_0_.refs_5_) | copy-start | bytes 344068
  29.3 3.8 %collective-permute-start.11 = (f32[2,14,8,128]{3,2,1,0:T(8,128)S(1)}, f32[2,14,8,128]{3,2,1,0:T(8,128)S(1)}, u32[]{:S(2)}, u32[]{:S(2)}) collective-permute-start(f32[2,14,8,128]{3,2,1,0:T(8,128)S(1)} %get-tuple-element.49), channel_id=1, source_target_pairs={{0,1},{1,0},{2,3},{3,2},{4,5},{5,4},{6,7},{7,6},{8,9},{9,8},{10,11... | collective-permute-start | bytes 344072 | tf_op jit(solution)/shard_map/ppermute | solution.py:504
  31.8 0.6 %copy-start.8 = (f32[2,14,8,128]{3,2,1,0:T(8,128)}, f32[2,14,8,128]{3,2,1,0:T(8,128)S(1)}, u32[]{:S(2)}) copy-start(f32[2,14,8,128]{3,2,1,0:T(8,128)S(1)} %collective-permute-done.8.refs_1_.refs_6_) | copy-start | bytes 344068
  33.1 0.9 %copy-start.3 = (f32[2,14,8,128]{3,2,1,0:T(8,128)S(1)}, f32[2,14,8,128]{3,2,1,0:T(8,128)}, u32[]{:S(2)}) copy-start(f32[2,14,8,128]{3,2,1,0:T(8,128)} %copy-done.2) | copy-start | bytes 344068
  34.0 0.9 %copy-start.5 = (f32[2,14,8,128]{3,2,1,0:T(8,128)S(1)}, f32[2,14,8,128]{3,2,1,0:T(8,128)}, u32[]{:S(2)}) copy-start(f32[2,14,8,128]{3,2,1,0:T(8,128)} %copy-done.4) | copy-start | bytes 344068
  34.9 0.9 %copy-start.7 = (f32[2,14,8,128]{3,2,1,0:T(8,128)S(1)}, f32[2,14,8,128]{3,2,1,0:T(8,128)}, u32[]{:S(2)}) copy-start(f32[2,14,8,128]{3,2,1,0:T(8,128)} %copy-done.6) | copy-start | bytes 344068
  35.8 0.9 %copy-start.9 = (f32[2,14,8,128]{3,2,1,0:T(8,128)S(1)}, f32[2,14,8,128]{3,2,1,0:T(8,128)}, u32[]{:S(2)}) copy-start(f32[2,14,8,128]{3,2,1,0:T(8,128)} %copy-done.8) | copy-start | bytes 344068
  36.7 0.7 %copy-start.11 = (f32[8,128]{1,0:T(8,128)S(1)}, f32[8,128]{1,0:T(8,128)}, u32[]{:S(2)}) copy-start(f32[8,128]{1,0:T(8,128)} %shard_map.69.refs_13_) | copy-start | bytes 12292
  37.3 0.7 %copy-start.12 = (f32[8,128]{1,0:T(8,128)S(1)}, f32[8,128]{1,0:T(8,128)}, u32[]{:S(2)}) copy-start(f32[8,128]{1,0:T(8,128)} %shard_map.70.refs_14_) | copy-start | bytes 12292

commit v13 on v12

--- a/solution.py
+++ b/solution.py
@@ -525,6 +525,7 @@
     def mark(chunks):
         return pl.pallas_call(
             mark_kernel, out_shape=f32(SUB, LANES), in_specs=[ANY] * len(chunks), out_specs=VMEM, cost_estimate=cost(1, 1),
+            compiler_params=pltpu.CompilerParams(vmem_limit_bytes=1 << 20),
         )(*chunks)
 
     places = tuple((slot, 1 + b) for slot in range(depth) for b in range(inner))

time: 40.2 us -> 33.9 us (0.84)
  local copies, waits for them, and re-layouts: 6.93 us -> 1.34 us
  Pallas kernels: 12.4 us -> 11.3 us
  waiting for transfers between devices: 6.94 us -> 7.53 us
    unnamed x28 -> x8, local copies, waits for them, and re-layouts: 6.92 us -> 1.33 us
    pallas_call x2, Pallas kernels: 1.18 us -> 0.01 us  [mark(): pl.pallas_call(mark_kernel, out_shape=f32(SUB, LANES), in_specs=[ANY] * l...]
    ppermute x9, waiting for transfers between devices: 6.93 us -> 7.52 us  [swapped(): return lax.ppermute(sent, 'lev', [(i, i ^ k) for i in range(count)])]
  transfers between devices with their start and end apart: 13 -> 13, of which waited for: 3 -> 3; matrix products, arithmetic and copies ran while one was open for 0% -> 0% of each run, Pallas kernels for 26% -> 27%
where the time goes in v13:
time: 33.9 us; the launch traced here: 33.8 us
  starting transfers between devices  12.4 us (37%)
  Pallas kernels  11.3 us (33%)
  waiting for transfers between devices  7.53 us (22%)
  local copies, waits for them, and re-layouts  1.34 us (4%)
  other arithmetic  1.14 us (3%)
    pallas_call x5, Pallas kernels, call(): pl.pallas_call(kernel, out_shape=outs, in_specs=specs or [VMEM] * len(arg...  9.36 us
    ppermute x9, waiting for transfers between devices, swapped(): return lax.ppermute(sent, 'lev', [(i, i ^ k) for i in range(count)])  7.52 us
    ppermute x2, starting transfers between devices, beside(): lax.ppermute(sent[0], 'lat', [(i, i ^ 1) for i in range(bands)])  6.31 us
    ppermute x9, starting transfers between devices, swapped(): return lax.ppermute(sent, 'lev', [(i, i ^ k) for i in range(count)])  6.05 us
    pallas_call x1, Pallas kernels, remap(): pl.pallas_call(functools.partial(remap_kernel, count, tuple((units for un...  1.94 us
    unnamed x8, local copies, waits for them, and re-layouts  1.33 us
    concatenate x1, other arithmetic, shards(): jnp.concatenate([jnp.transpose(wind_x, (1, 0, 2)), jnp.transpose(wind_y,...  1.14 us
  transfers between devices with their start and end apart: 13, of which 3 were waited for; matrix products, arithmetic and copies ran while one was open for 0% of the time, Pallas kernels for 27%

profile of v13, /device:TPU:0, one launch (start us, length us, event | category | flops | bytes accessed | tf_op | source)
XLA Modules:
  0.0 33.8 jit_solution(6425654053862466718)
XLA Ops:
  0.0 1.1 %pad_maximum_fusion.winds.joined = f32[36,2,1152]{2,1,0:T(2,128)S(1)} fusion(f32[18,2,1152]{2,1,0:T(2,128)} %bitcast.13, f32[18,2,1152]{2,1,0:T(2,128)} %bitcast.14), kind=kLoop, calls=%fused_computation | loop fusion | flops 82944 | bytes 663552 | tf_op jit(solution)/shard_map/concatenate | solution.py:448
  1.1 0.0 copy-start
  1.2 1.3 %copy-done = f32[8,2,18,1152]{3,1,2,0:T(2,128)S(1)} copy-done((f32[8,2,18,1152]{3,1,2,0:T(2,128)S(1)}, f32[8,2,18,1152]{3,1,2,0:T(2,128)}, u32[]{:S(2)}) %copy-start) | copy-done | bytes 1327128
  2.5 0.0 copy-start.1
  2.5 0.0 copy-start.2
  2.5 0.2 shard_map.64
  2.7 3.1 %collective-permute-start.1 = (f32[7,8,1152]{2,1,0:T(8,128)S(1)}, f32[7,8,1152]{2,1,0:T(8,128)S(1)}, u32[]{:S(2)}, u32[]{:S(2)}) collective-permute-start(f32[7,8,1152]{2,1,0:T(8,128)S(1)} %get-tuple-element.31), channel_id=1, source_target_pairs={{0,4},{4,0},{8,12},{12,8},{1,5},{5,1},{9,13},{13,9},{2,6},{6,2},{1... | collective-permute-start | bytes 774152 | tf_op jit(solution)/shard_map/ppermute | solution.py:459
  5.8 0.0 collective-permute-start.2
  5.8 3.8 %shard_map.65 = (f32[2,14,8,128]{3,2,1,0:T(8,128)S(1)}, f32[2,14,8,128]{3,2,1,0:T(8,128)S(1)}, f32[4,14,8,128]{3,2,1,0:T(8,128)S(1)}, f32[2,12,8,1152]{3,2,1,0:T...) custom-call(f32[2,18,8,1152]{3,2,1,0:T(8,128)S(1)} %get-tuple-elemen, ...), custom_call_target="tpu_custom_call" | custom-call | flops 1 | bytes 1 | tf_op jit(solution)/shard_map/pallas_call | solution.py:419
  9.6 3.2 %collective-permute-start.5 = (f32[7,8,1152]{2,1,0:T(8,128)S(1)}, f32[7,8,1152]{2,1,0:T(8,128)S(1)}, u32[]{:S(2)}, u32[]{:S(2)}) collective-permute-start(f32[7,8,1152]{2,1,0:T(8,128)S(1)} %get-tuple-element.39), channel_id=1, source_target_pairs={{0,4},{4,0},{8,12},{12,8},{1,5},{5,1},{9,13},{13,9},{2,6},{6,2},{1... | collective-permute-start | bytes 774152 | tf_op jit(solution)/shard_map/ppermute | solution.py:459
  12.9 0.0 collective-permute-start.6
  12.9 1.5 %collective-permute-start = (f32[4,14,8,128]{3,2,1,0:T(8,128)S(1)}, f32[4,14,8,128]{3,2,1,0:T(8,128)S(1)}, u32[]{:S(2)}, u32[]{:S(2)}) collective-permute-start(f32[4,14,8,128]{3,2,1,0:T(8,128)S(1)} %get-tuple-element.29), channel_id=1, source_target_pairs={{0,2},{1,3},{2,0},{3,1},{4,6},{5,7},{6,4},{7,5},{8,10},{9,11},{10,... | collective-permute-start | bytes 688136 | tf_op jit(solution)/shard_map/ppermute | solution.py:504
  14.4 0.0 copy-done.1
  14.4 0.0 copy-done.2
  14.4 0.2 shard_map.66.refs_0_.refs_12_
  14.6 0.0 collective-permute-done.1.first_round
  14.6 0.0 collective-permute-done.2.second_round
  14.6 2.6 %shard_map.67 = (f32[2,14,8,128]{3,2,1,0:T(8,128)S(1)}, f32[2,14,8,128]{3,2,1,0:T(8,128)S(1)}, f32[2,14,8,128]{3,2,1,0:T(8,128)S(1)}, f32[2,14,8,128]{3,2,1,0:T(8,128)S(1)}) custom-call(f32[2,18,8,1152]{3,2,1,0:T(8,128)S(1)} %get-tuple-element.28.state, f32[7,8,1152]{2,1,0:T(8,128)S(1)} %collective-permute-done.1.first_round, ...), custom_call_target="tpu_custom_call" | custom-call | flops 19906560 | bytes 2654208 | tf_op jit(solution)/shard_map/pallas_call | solution.py:419
  17.1 0.4 %collective-permute-start.3 = (f32[2,14,8,128]{3,2,1,0:T(8,128)S(1)}, f32[2,14,8,128]{3,2,1,0:T(8,128)S(1)}, u32[]{:S(2)}, u32[]{:S(2)}) collective-permute-start(f32[2,14,8,128]{3,2,1,0:T(8,128)S(1)} %get-tuple-element.36), channel_id=1, source_target_pairs={{0,3},{1,2},{2,1},{3,0},{4,7},{5,6},{6,5},{7,4},{8,11},{9,10},{10,... | collective-permute-start | bytes 344072 | tf_op jit(solution)/shard_map/ppermute | solution.py:504
  17.6 1.5 %collective-permute-start.4 = (f32[2,14,8,128]{3,2,1,0:T(8,128)S(1)}, f32[2,14,8,128]{3,2,1,0:T(8,128)S(1)}, u32[]{:S(2)}, u32[]{:S(2)}) collective-permute-start(f32[2,14,8,128]{3,2,1,0:T(8,128)S(1)} %get-tuple-element.37), channel_id=1, source_target_pairs={{0,2},{1,3},{2,0},{3,1},{4,6},{5,7},{6,4},{7,5},{8,10},{9,11},{10,... | collective-permute-start | bytes 344072 | tf_op jit(solution)/shard_map/ppermute | solution.py:504
  19.1 2.2 %collective-permute-done.refs_1_.refs_0_ = f32[4,14,8,128]{3,2,1,0:T(8,128)S(1)} collective-permute-done((f32[4,14,8,128]{3,2,1,0:T(8,128)S(1)}, f32[4,14,8,128]{3,2,1,0:T(8,128)S(1)}, u32[]{:S(2)}, u32[]{:S(2)}) %collective-permute-start) | collective-permute-done | bytes 229408 | tf_op jit(solution)/shard_map/ppermute | solution.py:504
  21.3 0.0 collective-permute-done.5.first_round
  21.3 0.0 collective-permute-done.6.second_round
  21.3 0.0 copy-start.3
  21.3 2.5 %shard_map.68 = (f32[2,14,8,128]{3,2,1,0:T(8,128)S(1)}, f32[2,14,8,128]{3,2,1,0:T(8,128)S(1)}, f32[2,14,8,128]{3,2,1,0:T(8,128)S(1)}, f32[2,14,8,128]{3,2,1,0:T(8,128)S(1)}) custom-call(f32[2,18,8,1152]{3,2,1,0:T(8,128)S(1)} %get-tuple-element.28.state, f32[7,8,1152]{2,1,0:T(8,128)S(1)} %collective-permute-done.5.first_round, ...), custom_call_target="tpu_custom_call" | custom-call | flops 19906560 | bytes 2654208 | tf_op jit(solution)/shard_map/pallas_call | solution.py:419
  23.8 0.5 %collective-permute-start.7 = (f32[2,14,8,128]{3,2,1,0:T(8,128)S(1)}, f32[2,14,8,128]{3,2,1,0:T(8,128)S(1)}, u32[]{:S(2)}, u32[]{:S(2)}) collective-permute-start(f32[2,14,8,128]{3,2,1,0:T(8,128)S(1)} %get-tuple-element.41), channel_id=1, source_target_pairs={{0,3},{1,2},{2,1},{3,0},{4,7},{5,6},{6,5},{7,4},{8,11},{9,10},{10,... | collective-permute-start | bytes 344072 | tf_op jit(solution)/shard_map/ppermute | solution.py:504
  24.4 1.2 %collective-permute-start.12 = (f32[2,14,8,128]{3,2,1,0:T(8,128)S(1)}, f32[2,14,8,128]{3,2,1,0:T(8,128)S(1)}, u32[]{:S(2)}, u32[]{:S(2)}) collective-permute-start(f32[2,14,8,128]{3,2,1,0:T(8,128)S(1)} %slice.3), channel_id=1, source_target_pairs={{0,1},{1,0},{2,3},{3,2},{4,5},{5,4},{6,7},{7,6},{8,9},{9,8},{10,11... | collective-permute-start | bytes 344072 | tf_op jit(solution)/shard_map/ppermute | solution.py:504
  25.6 0.1 collective-permute-start.9
  25.7 0.0 collective-permute-done.3.refs_0_.refs_2_
  25.7 0.5 %collective-permute-start.8 = (f32[2,14,8,128]{3,2,1,0:T(8,128)S(1)}, f32[2,14,8,128]{3,2,1,0:T(8,128)S(1)}, u32[]{:S(2)}, u32[]{:S(2)}) collective-permute-start(f32[2,14,8,128]{3,2,1,0:T(8,128)S(1)} %get-tuple-element.42), channel_id=1, source_target_pairs={{0,2},{1,3},{2,0},{3,1},{4,6},{5,7},{6,4},{7,5},{8,10},{9,11},{10,... | collective-permute-start | bytes 344072 | tf_op jit(solution)/shard_map/ppermute | solution.py:504
  26.2 0.0 collective-permute-done.4.refs_1_.refs_3_
  26.2 0.2 collective-permute-start.10
  26.4 2.9 %collective-permute-done.7.refs_0_.refs_5_ = f32[2,14,8,128]{3,2,1,0:T(8,128)S(1)} collective-permute-done((f32[2,14,8,128]{3,2,1,0:T(8,128)S(1)}, f32[2,14,8,128]{3,2,1,0:T(8,128)S(1)}, u32[]{:S(2)}, u32[]{:S(2)}) %collective-permute-start.7) | collective-permute-done | bytes 114720 | tf_op jit(solution)/shard_map/ppermute | solution.py:504
  29.3 0.1 collective-permute-start.11
  29.4 2.4 %collective-permute-done.8.refs_1_.refs_6_ = f32[2,14,8,128]{3,2,1,0:T(8,128)S(1)} collective-permute-done((f32[2,14,8,128]{3,2,1,0:T(8,128)S(1)}, f32[2,14,8,128]{3,2,1,0:T(8,128)S(1)}, u32[]{:S(2)}, u32[]{:S(2)}) %collective-permute-start.8) | collective-permute-done | bytes 114720 | tf_op jit(solution)/shard_map/ppermute | solution.py:504
  31.8 0.0 collective-permute-done.12.refs_11_
  31.8 0.0 collective-permute-done.9.refs_8_
  31.8 0.0 collective-permute-done.10.refs_9_
  31.8 0.0 collective-permute-done.11.refs_10_
  31.8 0.0 copy-done.3
  31.8 1.9 %shard_map.71 = f32[6,18,8,288]{3,2,1,0:T(8,128)} custom-call(s32[4]{0:T(128)S(1)} %copy-done.3, f32[4,14,8,128]{3,2,1,0:T(8,128)S(1)} %collective-permute-done.refs_1_.refs_0_, f32[2,14,8,128]{3,2,1,0:T(8,128)S(1)} %get-tuple-element.30.refs_1_, f32[2,14,8,128]{3,2,1,0:T(8,128)S(1)} %collective-permute-done.3.refs_0_.refs_2_, ...), custom_call_target="tpu_custom_call" | custom-call | flops 1 | bytes 1 | tf_op jit(solution)/shard_map/pallas_call | solution.py:511
  (3 shorter events, 0.0 us)
Async XLA Ops:
  1.1 1.3 %copy-start = (f32[8,2,18,1152]{3,1,2,0:T(2,128)S(1)}, f32[8,2,18,1152]{3,1,2,0:T(2,128)}, u32[]{:S(2)}) copy-start(f32[8,2,18,1152]{3,1,2,0:T(2,128)} %param.6) | copy-start | bytes 3981316
  2.5 11.9 %copy-start.1 = (f32[4,6,18,288]{3,0,2,1:T(4,128)S(1)}, f32[4,6,18,288]{3,0,2,1:T(4,128)}, u32[]{:S(2)}) copy-start(f32[4,6,18,288]{3,0,2,1:T(4,128)} %param.11) | copy-start | bytes 1492996
  2.5 11.9 %copy-start.2 = (s32[6,18,288]{2,1,0:T(8,128)S(1)}, s32[6,18,288]{2,1,0:T(8,128)}, u32[]{:S(2)}) copy-start(s32[6,18,288]{2,1,0:T(8,128)} %source.1) | copy-start | bytes 373252
  2.7 11.9 %collective-permute-start.1 = (f32[7,8,1152]{2,1,0:T(8,128)S(1)}, f32[7,8,1152]{2,1,0:T(8,128)S(1)}, u32[]{:S(2)}, u32[]{:S(2)}) collective-permute-start(f32[7,8,1152]{2,1,0:T(8,128)S(1)} %get-tuple-element.31), channel_id=1, source_target_pairs={{0,4},{4,0},{8,12},{12,8},{1,5},{5,1},{9,13},{13,9},{2,6},{6,2},{1... | collective-permute-start | bytes 774152 | tf_op jit(solution)/shard_map/ppermute | solution.py:459
  5.8 8.8 %collective-permute-start.2 = (f32[7,8,1152]{2,1,0:T(8,128)S(1)}, f32[7,8,1152]{2,1,0:T(8,128)S(1)}, u32[]{:S(2)}, u32[]{:S(2)}) collective-permute-start(f32[7,8,1152]{2,1,0:T(8,128)S(1)} %get-tuple-element.32), channel_id=1, source_target_pairs={{0,1},{1,0},{2,3},{3,2},{4,8},{5,9},{6,10},{7,11},{8,4},{9,5},{10,... | collective-permute-start | bytes 774152 | tf_op jit(solution)/shard_map/ppermute | solution.py:460
  9.6 11.6 %collective-permute-start.5 = (f32[7,8,1152]{2,1,0:T(8,128)S(1)}, f32[7,8,1152]{2,1,0:T(8,128)S(1)}, u32[]{:S(2)}, u32[]{:S(2)}) collective-permute-start(f32[7,8,1152]{2,1,0:T(8,128)S(1)} %get-tuple-element.39), channel_id=1, source_target_pairs={{0,4},{4,0},{8,12},{12,8},{1,5},{5,1},{9,13},{13,9},{2,6},{6,2},{1... | collective-permute-start | bytes 774152 | tf_op jit(solution)/shard_map/ppermute | solution.py:459
  12.9 8.4 %collective-permute-start.6 = (f32[7,8,1152]{2,1,0:T(8,128)S(1)}, f32[7,8,1152]{2,1,0:T(8,128)S(1)}, u32[]{:S(2)}, u32[]{:S(2)}) collective-permute-start(f32[7,8,1152]{2,1,0:T(8,128)S(1)} %get-tuple-element.40), channel_id=1, source_target_pairs={{0,1},{1,0},{2,3},{3,2},{4,8},{5,9},{6,10},{7,11},{8,4},{9,5},{10,... | collective-permute-start | bytes 774152 | tf_op jit(solution)/shard_map/ppermute | solution.py:460
  12.9 8.4 %collective-permute-start = (f32[4,14,8,128]{3,2,1,0:T(8,128)S(1)}, f32[4,14,8,128]{3,2,1,0:T(8,128)S(1)}, u32[]{:S(2)}, u32[]{:S(2)}) collective-permute-start(f32[4,14,8,128]{3,2,1,0:T(8,128)S(1)} %get-tuple-element.29), channel_id=1, source_target_pairs={{0,2},{1,3},{2,0},{3,1},{4,6},{5,7},{6,4},{7,5},{8,10},{9,11},{10,... | collective-permute-start | bytes 688136 | tf_op jit(solution)/shard_map/ppermute | solution.py:504
  17.1 8.5 %collective-permute-start.3 = (f32[2,14,8,128]{3,2,1,0:T(8,128)S(1)}, f32[2,14,8,128]{3,2,1,0:T(8,128)S(1)}, u32[]{:S(2)}, u32[]{:S(2)}) collective-permute-start(f32[2,14,8,128]{3,2,1,0:T(8,128)S(1)} %get-tuple-element.36), channel_id=1, source_target_pairs={{0,3},{1,2},{2,1},{3,0},{4,7},{5,6},{6,5},{7,4},{8,11},{9,10},{10,... | collective-permute-start | bytes 344072 | tf_op jit(solution)/shard_map/ppermute | solution.py:504
  17.6 8.6 %collective-permute-start.4 = (f32[2,14,8,128]{3,2,1,0:T(8,128)S(1)}, f32[2,14,8,128]{3,2,1,0:T(8,128)S(1)}, u32[]{:S(2)}, u32[]{:S(2)}) collective-permute-start(f32[2,14,8,128]{3,2,1,0:T(8,128)S(1)} %get-tuple-element.37), channel_id=1, source_target_pairs={{0,2},{1,3},{2,0},{3,1},{4,6},{5,7},{6,4},{7,5},{8,10},{9,11},{10,... | collective-permute-start | bytes 344072 | tf_op jit(solution)/shard_map/ppermute | solution.py:504
  21.3 10.6 %copy-start.3 = (s32[4]{0:T(128)S(1)}, s32[4]{0:T(128)}, u32[]{:S(2)}) copy-start(s32[4]{0:T(128)} %counts.1) | copy-start | bytes 52
  23.8 5.5 %collective-permute-start.7 = (f32[2,14,8,128]{3,2,1,0:T(8,128)S(1)}, f32[2,14,8,128]{3,2,1,0:T(8,128)S(1)}, u32[]{:S(2)}, u32[]{:S(2)}) collective-permute-start(f32[2,14,8,128]{3,2,1,0:T(8,128)S(1)} %get-tuple-element.41), channel_id=1, source_target_pairs={{0,3},{1,2},{2,1},{3,0},{4,7},{5,6},{6,5},{7,4},{8,11},{9,10},{10,... | collective-permute-start | bytes 344072 | tf_op jit(solution)/shard_map/ppermute | solution.py:504
  24.4 7.4 %collective-permute-start.12 = (f32[2,14,8,128]{3,2,1,0:T(8,128)S(1)}, f32[2,14,8,128]{3,2,1,0:T(8,128)S(1)}, u32[]{:S(2)}, u32[]{:S(2)}) collective-permute-start(f32[2,14,8,128]{3,2,1,0:T(8,128)S(1)} %slice.3), channel_id=1, source_target_pairs={{0,1},{1,0},{2,3},{3,2},{4,5},{5,4},{6,7},{7,6},{8,9},{9,8},{10,11... | collective-permute-start | bytes 344072 | tf_op jit(solution)/shard_map/ppermute | solution.py:504
  25.6 6.2 %collective-permute-start.9 = (f32[2,14,8,128]{3,2,1,0:T(8,128)S(1)}, f32[2,14,8,128]{3,2,1,0:T(8,128)S(1)}, u32[]{:S(2)}, u32[]{:S(2)}) collective-permute-start(f32[2,14,8,128]{3,2,1,0:T(8,128)S(1)} %get-tuple-element.47), channel_id=1, source_target_pairs={{0,1},{1,0},{2,3},{3,2},{4,5},{5,4},{6,7},{7,6},{8,9},{9,8},{10,11... | collective-permute-start | bytes 344072 | tf_op jit(solution)/shard_map/ppermute | solution.py:504
  25.7 6.1 %collective-permute-start.8 = (f32[2,14,8,128]{3,2,1,0:T(8,128)S(1)}, f32[2,14,8,128]{3,2,1,0:T(8,128)S(1)}, u32[]{:S(2)}, u32[]{:S(2)}) collective-permute-start(f32[2,14,8,128]{3,2,1,0:T(8,128)S(1)} %get-tuple-element.42), channel_id=1, source_target_pairs={{0,2},{1,3},{2,0},{3,1},{4,6},{5,7},{6,4},{7,5},{8,10},{9,11},{10,... | collective-permute-start | bytes 344072 | tf_op jit(solution)/shard_map/ppermute | solution.py:504
  26.2 5.6 %collective-permute-start.10 = (f32[2,14,8,128]{3,2,1,0:T(8,128)S(1)}, f32[2,14,8,128]{3,2,1,0:T(8,128)S(1)}, u32[]{:S(2)}, u32[]{:S(2)}) collective-permute-start(f32[2,14,8,128]{3,2,1,0:T(8,128)S(1)} %get-tuple-element.48), channel_id=1, source_target_pairs={{0,1},{1,0},{2,3},{3,2},{4,5},{5,4},{6,7},{7,6},{8,9},{9,8},{10,11... | collective-permute-start | bytes 344072 | tf_op jit(solution)/shard_map/ppermute | solution.py:504
  29.3 2.5 %collective-permute-start.11 = (f32[2,14,8,128]{3,2,1,0:T(8,128)S(1)}, f32[2,14,8,128]{3,2,1,0:T(8,128)S(1)}, u32[]{:S(2)}, u32[]{:S(2)}) collective-permute-start(f32[2,14,8,128]{3,2,1,0:T(8,128)S(1)} %get-tuple-element.49), channel_id=1, source_target_pairs={{0,1},{1,0},{2,3},{3,2},{4,5},{5,4},{6,7},{7,6},{8,9},{9,8},{10,11... | collective-permute-start | bytes 344072 | tf_op jit(solution)/shard_map/ppermute | solution.py:504

commit v14 on v13

--- a/solution.py
+++ b/solution.py
@@ -542,7 +542,7 @@
         listed += crossing + [(units_of(0, own), done[0])]
         beside_me.append((units_of(1, own), done[1]))
         marks.append(mark([chunk for _, chunk in crossing]))
-        after = (done[0], *arrived)
+        after = (done[0],)
     beside_me += [(units_of(k ^ 1, places), chunk) for k, chunk in zip(chips, arrived)]
     waiting = lax.optimization_barrier((*(chunk for _, chunk in beside_me), done[0]))
     listed += [(units, swapped(chunk[chunk.shape[0] - len(units):], 1)) for (units, _), chunk in zip(beside_me, waiting)]

time: 33.9 us -> 32.9 us (0.971)
  waiting for transfers between devices: 7.53 us -> 5.72 us
  starting transfers between devices: 12.4 us -> 13.1 us
    ppermute x9, waiting for transfers between devices: 7.52 us -> 5.71 us  [swapped(): return lax.ppermute(sent, 'lev', [(i, i ^ k) for i in range(count)])]
    ppermute x9, starting transfers between devices: 6.05 us -> 6.77 us  [swapped(): return lax.ppermute(sent, 'lev', [(i, i ^ k) for i in range(count)])]
  transfers between devices with their start and end apart: 13 -> 13, of which waited for: 3 -> 3; matrix products, arithmetic and copies ran while one was open for 0% -> 0% of each run, Pallas kernels for 27% -> 28%
where the time goes in v14:
time: 32.9 us; the launch traced here: 32.7 us
  starting transfers between devices  13.1 us (40%)
  Pallas kernels  11.3 us (34%)
  waiting for transfers between devices  5.72 us (17%)
  local copies, waits for them, and re-layouts  1.34 us (4%)
  other arithmetic  1.14 us (3%)
    pallas_call x5, Pallas kernels, call(): pl.pallas_call(kernel, out_shape=outs, in_specs=specs or [VMEM] * len(arg...  9.36 us
    ppermute x9, starting transfers between devices, swapped(): return lax.ppermute(sent, 'lev', [(i, i ^ k) for i in range(count)])  6.77 us
    ppermute x2, starting transfers between devices, beside(): lax.ppermute(sent[0], 'lat', [(i, i ^ 1) for i in range(bands)])  6.31 us
    ppermute x9, waiting for transfers between devices, swapped(): return lax.ppermute(sent, 'lev', [(i, i ^ k) for i in range(count)])  5.71 us
    pallas_call x1, Pallas kernels, remap(): pl.pallas_call(functools.partial(remap_kernel, count, tuple((units for un...  1.94 us
    unnamed x8, local copies, waits for them, and re-layouts  1.33 us
    concatenate x1, other arithmetic, shards(): jnp.concatenate([jnp.transpose(wind_x, (1, 0, 2)), jnp.transpose(wind_y,...  1.14 us
  transfers between devices with their start and end apart: 13, of which 3 were waited for; matrix products, arithmetic and copies ran while one was open for 0% of the time, Pallas kernels for 28%

profile of v14, /device:TPU:0, one launch (start us, length us, event | category | flops | bytes accessed | tf_op | source)
XLA Modules:
  0.0 32.7 jit_solution(6051577151123570980)
XLA Ops:
  0.0 1.1 %pad_maximum_fusion.winds.joined = f32[36,2,1152]{2,1,0:T(2,128)S(1)} fusion(f32[18,2,1152]{2,1,0:T(2,128)} %bitcast.13, f32[18,2,1152]{2,1,0:T(2,128)} %bitcast.14), kind=kLoop, calls=%fused_computation | loop fusion | flops 82944 | bytes 663552 | tf_op jit(solution)/shard_map/concatenate | solution.py:448
  1.1 0.0 copy-start
  1.2 1.3 %copy-done = f32[8,2,18,1152]{3,1,2,0:T(2,128)S(1)} copy-done((f32[8,2,18,1152]{3,1,2,0:T(2,128)S(1)}, f32[8,2,18,1152]{3,1,2,0:T(2,128)}, u32[]{:S(2)}) %copy-start) | copy-done | bytes 1327128
  2.5 0.0 copy-start.1
  2.5 0.0 copy-start.2
  2.5 0.2 shard_map.64
  2.7 3.1 %collective-permute-start.1 = (f32[7,8,1152]{2,1,0:T(8,128)S(1)}, f32[7,8,1152]{2,1,0:T(8,128)S(1)}, u32[]{:S(2)}, u32[]{:S(2)}) collective-permute-start(f32[7,8,1152]{2,1,0:T(8,128)S(1)} %get-tuple-element.31), channel_id=1, source_target_pairs={{0,4},{4,0},{8,12},{12,8},{1,5},{5,1},{9,13},{13,9},{2,6},{6,2},{1... | collective-permute-start | bytes 774152 | tf_op jit(solution)/shard_map/ppermute | solution.py:459
  5.8 0.0 collective-permute-start.2
  5.8 3.8 %shard_map.65 = (f32[2,14,8,128]{3,2,1,0:T(8,128)S(1)}, f32[2,14,8,128]{3,2,1,0:T(8,128)S(1)}, f32[4,14,8,128]{3,2,1,0:T(8,128)S(1)}, f32[2,12,8,1152]{3,2,1,0:T...) custom-call(f32[2,18,8,1152]{3,2,1,0:T(8,128)S(1)} %get-tuple-elemen, ...), custom_call_target="tpu_custom_call" | custom-call | flops 1 | bytes 1 | tf_op jit(solution)/shard_map/pallas_call | solution.py:419
  9.6 3.2 %collective-permute-start.5 = (f32[7,8,1152]{2,1,0:T(8,128)S(1)}, f32[7,8,1152]{2,1,0:T(8,128)S(1)}, u32[]{:S(2)}, u32[]{:S(2)}) collective-permute-start(f32[7,8,1152]{2,1,0:T(8,128)S(1)} %get-tuple-element.39), channel_id=1, source_target_pairs={{0,4},{4,0},{8,12},{12,8},{1,5},{5,1},{9,13},{13,9},{2,6},{6,2},{1... | collective-permute-start | bytes 774152 | tf_op jit(solution)/shard_map/ppermute | solution.py:459
  12.9 0.0 collective-permute-start.6
  12.9 1.5 %collective-permute-start = (f32[4,14,8,128]{3,2,1,0:T(8,128)S(1)}, f32[4,14,8,128]{3,2,1,0:T(8,128)S(1)}, u32[]{:S(2)}, u32[]{:S(2)}) collective-permute-start(f32[4,14,8,128]{3,2,1,0:T(8,128)S(1)} %get-tuple-element.29), channel_id=1, source_target_pairs={{0,2},{1,3},{2,0},{3,1},{4,6},{5,7},{6,4},{7,5},{8,10},{9,11},{10,... | collective-permute-start | bytes 688136 | tf_op jit(solution)/shard_map/ppermute | solution.py:504
  14.4 0.0 copy-done.1
  14.4 0.0 copy-done.2
  14.4 0.2 shard_map.66.refs_0_.refs_12_
  14.6 0.0 collective-permute-done.1.first_round
  14.6 0.0 collective-permute-done.2.second_round
  14.6 2.6 %shard_map.67 = (f32[2,14,8,128]{3,2,1,0:T(8,128)S(1)}, f32[2,14,8,128]{3,2,1,0:T(8,128)S(1)}, f32[2,14,8,128]{3,2,1,0:T(8,128)S(1)}, f32[2,14,8,128]{3,2,1,0:T(8,128)S(1)}) custom-call(f32[2,18,8,1152]{3,2,1,0:T(8,128)S(1)} %get-tuple-element.28.state, f32[7,8,1152]{2,1,0:T(8,128)S(1)} %collective-permute-done.1.first_round, ...), custom_call_target="tpu_custom_call" | custom-call | flops 19906560 | bytes 2654208 | tf_op jit(solution)/shard_map/pallas_call | solution.py:419
  17.1 0.4 %collective-permute-start.3 = (f32[2,14,8,128]{3,2,1,0:T(8,128)S(1)}, f32[2,14,8,128]{3,2,1,0:T(8,128)S(1)}, u32[]{:S(2)}, u32[]{:S(2)}) collective-permute-start(f32[2,14,8,128]{3,2,1,0:T(8,128)S(1)} %get-tuple-element.36), channel_id=1, source_target_pairs={{0,3},{1,2},{2,1},{3,0},{4,7},{5,6},{6,5},{7,4},{8,11},{9,10},{10,... | collective-permute-start | bytes 344072 | tf_op jit(solution)/shard_map/ppermute | solution.py:504
  17.6 1.5 %collective-permute-start.4 = (f32[2,14,8,128]{3,2,1,0:T(8,128)S(1)}, f32[2,14,8,128]{3,2,1,0:T(8,128)S(1)}, u32[]{:S(2)}, u32[]{:S(2)}) collective-permute-start(f32[2,14,8,128]{3,2,1,0:T(8,128)S(1)} %get-tuple-element.37), channel_id=1, source_target_pairs={{0,2},{1,3},{2,0},{3,1},{4,6},{5,7},{6,4},{7,5},{8,10},{9,11},{10,... | collective-permute-start | bytes 344072 | tf_op jit(solution)/shard_map/ppermute | solution.py:504
  19.1 0.0 collective-permute-done.5.first_round
  19.1 0.0 collective-permute-done.6.second_round
  19.1 0.0 copy-start.3
  19.1 2.5 %shard_map.68 = (f32[2,14,8,128]{3,2,1,0:T(8,128)S(1)}, f32[2,14,8,128]{3,2,1,0:T(8,128)S(1)}, f32[2,14,8,128]{3,2,1,0:T(8,128)S(1)}, f32[2,14,8,128]{3,2,1,0:T(8,128)S(1)}) custom-call(f32[2,18,8,1152]{3,2,1,0:T(8,128)S(1)} %get-tuple-element.28.state, f32[7,8,1152]{2,1,0:T(8,128)S(1)} %collective-permute-done.5.first_round, ...), custom_call_target="tpu_custom_call" | custom-call | flops 19906560 | bytes 2654208 | tf_op jit(solution)/shard_map/pallas_call | solution.py:419
  21.6 0.2 collective-permute-start.7
  21.9 0.0 collective-permute-done.refs_0_
  21.9 1.0 %collective-permute-start.12 = (f32[2,14,8,128]{3,2,1,0:T(8,128)S(1)}, f32[2,14,8,128]{3,2,1,0:T(8,128)S(1)}, u32[]{:S(2)}, u32[]{:S(2)}) collective-permute-start(f32[2,14,8,128]{3,2,1,0:T(8,128)S(1)} %slice.3), channel_id=1, source_target_pairs={{0,1},{1,0},{2,3},{3,2},{4,5},{5,4},{6,7},{7,6},{8,9},{9,8},{10,11... | collective-permute-start | bytes 344072 | tf_op jit(solution)/shard_map/ppermute | solution.py:504
  22.8 0.1 collective-permute-start.9
  22.9 0.0 collective-permute-done.3.refs_0_.refs_2_
  22.9 1.5 %collective-permute-start.8 = (f32[2,14,8,128]{3,2,1,0:T(8,128)S(1)}, f32[2,14,8,128]{3,2,1,0:T(8,128)S(1)}, u32[]{:S(2)}, u32[]{:S(2)}) collective-permute-start(f32[2,14,8,128]{3,2,1,0:T(8,128)S(1)} %get-tuple-element.42), channel_id=1, source_target_pairs={{0,2},{1,3},{2,0},{3,1},{4,6},{5,7},{6,4},{7,5},{8,10},{9,11},{10,... | collective-permute-start | bytes 344072 | tf_op jit(solution)/shard_map/ppermute | solution.py:504
  24.4 1.7 %collective-permute-done.4.refs_1_.refs_3_ = f32[2,14,8,128]{3,2,1,0:T(8,128)S(1)} collective-permute-done((f32[2,14,8,128]{3,2,1,0:T(8,128)S(1)}, f32[2,14,8,128]{3,2,1,0:T(8,128)S(1)}, u32[]{:S(2)}, u32[]{:S(2)}) %collective-permute-start.4) | collective-permute-done | bytes 114720 | tf_op jit(solution)/shard_map/ppermute | solution.py:504
  26.2 0.0 collective-permute-start.10
  26.2 1.7 %collective-permute-done.7.refs_0_.refs_5_ = f32[2,14,8,128]{3,2,1,0:T(8,128)S(1)} collective-permute-done((f32[2,14,8,128]{3,2,1,0:T(8,128)S(1)}, f32[2,14,8,128]{3,2,1,0:T(8,128)S(1)}, u32[]{:S(2)}, u32[]{:S(2)}) %collective-permute-start.7) | collective-permute-done | bytes 114720 | tf_op jit(solution)/shard_map/ppermute | solution.py:504
  27.9 0.6 %collective-permute-start.11 = (f32[2,14,8,128]{3,2,1,0:T(8,128)S(1)}, f32[2,14,8,128]{3,2,1,0:T(8,128)S(1)}, u32[]{:S(2)}, u32[]{:S(2)}) collective-permute-start(f32[2,14,8,128]{3,2,1,0:T(8,128)S(1)} %get-tuple-element.49), channel_id=1, source_target_pairs={{0,1},{1,0},{2,3},{3,2},{4,5},{5,4},{6,7},{7,6},{8,9},{9,8},{10,11... | collective-permute-start | bytes 344072 | tf_op jit(solution)/shard_map/ppermute | solution.py:504
  28.5 2.2 %collective-permute-done.8.refs_1_.refs_6_ = f32[2,14,8,128]{3,2,1,0:T(8,128)S(1)} collective-permute-done((f32[2,14,8,128]{3,2,1,0:T(8,128)S(1)}, f32[2,14,8,128]{3,2,1,0:T(8,128)S(1)}, u32[]{:S(2)}, u32[]{:S(2)}) %collective-permute-start.8) | collective-permute-done | bytes 114720 | tf_op jit(solution)/shard_map/ppermute | solution.py:504
  30.7 0.0 collective-permute-done.12.refs_11_
  30.7 0.0 collective-permute-done.9.refs_8_
  30.7 0.0 collective-permute-done.10.refs_9_
  30.7 0.0 collective-permute-done.11.refs_10_
  30.7 0.0 copy-done.3
  30.8 1.9 %shard_map.71 = f32[6,18,8,288]{3,2,1,0:T(8,128)} custom-call(s32[4]{0:T(128)S(1)} %copy-done.3, f32[4,14,8,128]{3,2,1,0:T(8,128)S(1)} %collective-permute-done.refs_0_, f32[2,14,8,128]{3,2,1,0:T(8,128)S(1)} %get-tuple-element.30.refs_1_, f32[2,14,8,128]{3,2,1,0:T(8,128)S(1)} %collective-permute-done.3.refs_0_.refs_2_, ...), custom_call_target="tpu_custom_call" | custom-call | flops 1 | bytes 1 | tf_op jit(solution)/shard_map/pallas_call | solution.py:511
  (3 shorter events, 0.0 us)
Async XLA Ops:
  1.1 1.3 %copy-start = (f32[8,2,18,1152]{3,1,2,0:T(2,128)S(1)}, f32[8,2,18,1152]{3,1,2,0:T(2,128)}, u32[]{:S(2)}) copy-start(f32[8,2,18,1152]{3,1,2,0:T(2,128)} %param.6) | copy-start | bytes 3981316
  2.5 11.9 %copy-start.1 = (f32[4,6,18,288]{3,0,2,1:T(4,128)S(1)}, f32[4,6,18,288]{3,0,2,1:T(4,128)}, u32[]{:S(2)}) copy-start(f32[4,6,18,288]{3,0,2,1:T(4,128)} %param.11) | copy-start | bytes 1492996
  2.5 11.9 %copy-start.2 = (s32[6,18,288]{2,1,0:T(8,128)S(1)}, s32[6,18,288]{2,1,0:T(8,128)}, u32[]{:S(2)}) copy-start(s32[6,18,288]{2,1,0:T(8,128)} %source.1) | copy-start | bytes 373252
  2.7 11.9 %collective-permute-start.1 = (f32[7,8,1152]{2,1,0:T(8,128)S(1)}, f32[7,8,1152]{2,1,0:T(8,128)S(1)}, u32[]{:S(2)}, u32[]{:S(2)}) collective-permute-start(f32[7,8,1152]{2,1,0:T(8,128)S(1)} %get-tuple-element.31), channel_id=1, source_target_pairs={{0,4},{4,0},{8,12},{12,8},{1,5},{5,1},{9,13},{13,9},{2,6},{6,2},{1... | collective-permute-start | bytes 774152 | tf_op jit(solution)/shard_map/ppermute | solution.py:459
  5.8 8.8 %collective-permute-start.2 = (f32[7,8,1152]{2,1,0:T(8,128)S(1)}, f32[7,8,1152]{2,1,0:T(8,128)S(1)}, u32[]{:S(2)}, u32[]{:S(2)}) collective-permute-start(f32[7,8,1152]{2,1,0:T(8,128)S(1)} %get-tuple-element.32), channel_id=1, source_target_pairs={{0,1},{1,0},{2,3},{3,2},{4,8},{5,9},{6,10},{7,11},{8,4},{9,5},{10,... | collective-permute-start | bytes 774152 | tf_op jit(solution)/shard_map/ppermute | solution.py:460
  9.6 9.4 %collective-permute-start.5 = (f32[7,8,1152]{2,1,0:T(8,128)S(1)}, f32[7,8,1152]{2,1,0:T(8,128)S(1)}, u32[]{:S(2)}, u32[]{:S(2)}) collective-permute-start(f32[7,8,1152]{2,1,0:T(8,128)S(1)} %get-tuple-element.39), channel_id=1, source_target_pairs={{0,4},{4,0},{8,12},{12,8},{1,5},{5,1},{9,13},{13,9},{2,6},{6,2},{1... | collective-permute-start | bytes 774152 | tf_op jit(solution)/shard_map/ppermute | solution.py:459
  12.9 6.2 %collective-permute-start.6 = (f32[7,8,1152]{2,1,0:T(8,128)S(1)}, f32[7,8,1152]{2,1,0:T(8,128)S(1)}, u32[]{:S(2)}, u32[]{:S(2)}) collective-permute-start(f32[7,8,1152]{2,1,0:T(8,128)S(1)} %get-tuple-element.40), channel_id=1, source_target_pairs={{0,1},{1,0},{2,3},{3,2},{4,8},{5,9},{6,10},{7,11},{8,4},{9,5},{10,... | collective-permute-start | bytes 774152 | tf_op jit(solution)/shard_map/ppermute | solution.py:460
  12.9 9.0 %collective-permute-start = (f32[4,14,8,128]{3,2,1,0:T(8,128)S(1)}, f32[4,14,8,128]{3,2,1,0:T(8,128)S(1)}, u32[]{:S(2)}, u32[]{:S(2)}) collective-permute-start(f32[4,14,8,128]{3,2,1,0:T(8,128)S(1)} %get-tuple-element.29), channel_id=1, source_target_pairs={{0,2},{1,3},{2,0},{3,1},{4,6},{5,7},{6,4},{7,5},{8,10},{9,11},{10,... | collective-permute-start | bytes 688136 | tf_op jit(solution)/shard_map/ppermute | solution.py:504
  17.1 5.8 %collective-permute-start.3 = (f32[2,14,8,128]{3,2,1,0:T(8,128)S(1)}, f32[2,14,8,128]{3,2,1,0:T(8,128)S(1)}, u32[]{:S(2)}, u32[]{:S(2)}) collective-permute-start(f32[2,14,8,128]{3,2,1,0:T(8,128)S(1)} %get-tuple-element.36), channel_id=1, source_target_pairs={{0,3},{1,2},{2,1},{3,0},{4,7},{5,6},{6,5},{7,4},{8,11},{9,10},{10,... | collective-permute-start | bytes 344072 | tf_op jit(solution)/shard_map/ppermute | solution.py:504
  17.6 8.6 %collective-permute-start.4 = (f32[2,14,8,128]{3,2,1,0:T(8,128)S(1)}, f32[2,14,8,128]{3,2,1,0:T(8,128)S(1)}, u32[]{:S(2)}, u32[]{:S(2)}) collective-permute-start(f32[2,14,8,128]{3,2,1,0:T(8,128)S(1)} %get-tuple-element.37), channel_id=1, source_target_pairs={{0,2},{1,3},{2,0},{3,1},{4,6},{5,7},{6,4},{7,5},{8,10},{9,11},{10,... | collective-permute-start | bytes 344072 | tf_op jit(solution)/shard_map/ppermute | solution.py:504
  19.1 11.7 %copy-start.3 = (s32[4]{0:T(128)S(1)}, s32[4]{0:T(128)}, u32[]{:S(2)}) copy-start(s32[4]{0:T(128)} %counts.1) | copy-start | bytes 52
  21.6 6.2 %collective-permute-start.7 = (f32[2,14,8,128]{3,2,1,0:T(8,128)S(1)}, f32[2,14,8,128]{3,2,1,0:T(8,128)S(1)}, u32[]{:S(2)}, u32[]{:S(2)}) collective-permute-start(f32[2,14,8,128]{3,2,1,0:T(8,128)S(1)} %get-tuple-element.41), channel_id=1, source_target_pairs={{0,3},{1,2},{2,1},{3,0},{4,7},{5,6},{6,5},{7,4},{8,11},{9,10},{10,... | collective-permute-start | bytes 344072 | tf_op jit(solution)/shard_map/ppermute | solution.py:504
  21.9 8.8 %collective-permute-start.12 = (f32[2,14,8,128]{3,2,1,0:T(8,128)S(1)}, f32[2,14,8,128]{3,2,1,0:T(8,128)S(1)}, u32[]{:S(2)}, u32[]{:S(2)}) collective-permute-start(f32[2,14,8,128]{3,2,1,0:T(8,128)S(1)} %slice.3), channel_id=1, source_target_pairs={{0,1},{1,0},{2,3},{3,2},{4,5},{5,4},{6,7},{7,6},{8,9},{9,8},{10,11... | collective-permute-start | bytes 344072 | tf_op jit(solution)/shard_map/ppermute | solution.py:504
  22.8 7.9 %collective-permute-start.9 = (f32[2,14,8,128]{3,2,1,0:T(8,128)S(1)}, f32[2,14,8,128]{3,2,1,0:T(8,128)S(1)}, u32[]{:S(2)}, u32[]{:S(2)}) collective-permute-start(f32[2,14,8,128]{3,2,1,0:T(8,128)S(1)} %get-tuple-element.47), channel_id=1, source_target_pairs={{0,1},{1,0},{2,3},{3,2},{4,5},{5,4},{6,7},{7,6},{8,9},{9,8},{10,11... | collective-permute-start | bytes 344072 | tf_op jit(solution)/shard_map/ppermute | solution.py:504
  22.9 7.8 %collective-permute-start.8 = (f32[2,14,8,128]{3,2,1,0:T(8,128)S(1)}, f32[2,14,8,128]{3,2,1,0:T(8,128)S(1)}, u32[]{:S(2)}, u32[]{:S(2)}) collective-permute-start(f32[2,14,8,128]{3,2,1,0:T(8,128)S(1)} %get-tuple-element.42), channel_id=1, source_target_pairs={{0,2},{1,3},{2,0},{3,1},{4,6},{5,7},{6,4},{7,5},{8,10},{9,11},{10,... | collective-permute-start | bytes 344072 | tf_op jit(solution)/shard_map/ppermute | solution.py:504
  26.2 4.5 %collective-permute-start.10 = (f32[2,14,8,128]{3,2,1,0:T(8,128)S(1)}, f32[2,14,8,128]{3,2,1,0:T(8,128)S(1)}, u32[]{:S(2)}, u32[]{:S(2)}) collective-permute-start(f32[2,14,8,128]{3,2,1,0:T(8,128)S(1)} %get-tuple-element.48), channel_id=1, source_target_pairs={{0,1},{1,0},{2,3},{3,2},{4,5},{5,4},{6,7},{7,6},{8,9},{9,8},{10,11... | collective-permute-start | bytes 344072 | tf_op jit(solution)/shard_map/ppermute | solution.py:504
  27.9 2.9 %collective-permute-start.11 = (f32[2,14,8,128]{3,2,1,0:T(8,128)S(1)}, f32[2,14,8,128]{3,2,1,0:T(8,128)S(1)}, u32[]{:S(2)}, u32[]{:S(2)}) collective-permute-start(f32[2,14,8,128]{3,2,1,0:T(8,128)S(1)} %get-tuple-element.49), channel_id=1, source_target_pairs={{0,1},{1,0},{2,3},{3,2},{4,5},{5,4},{6,7},{7,6},{8,9},{9,8},{10,11... | collective-permute-start | bytes 344072 | tf_op jit(solution)/shard_map/ppermute | solution.py:504

commit v15 on v14

--- a/solution.py
+++ b/solution.py
@@ -48,9 +48,11 @@
 def packed_sizes(nlon, count):
     width = nlon // count
     mains, tail = width // LANES, width % LANES
-    per = LANES // tail if tail else 1
-    tails = -(-BLOCK // per) if tail else 0
-    return width, mains, tail, per, BLOCK * mains + tails
+    return width, mains, tail, LANES // tail if tail else 1
+
+
+def packed_tiles(units, mains, tail, per):
+    return units * BLOCK * mains + (-(-units * BLOCK // per) if tail else 0)
 
 
 def fill_halos(rows, slot, state, winds, first_round, second_round):
@@ -164,9 +166,9 @@
             finish(g - 2, [update((g - 2) * BLOCK + q) for q in range(BLOCK)])
 
 
-def pack_block(block, packed, unit, count, lane):
+def pack_block(block, packed, unit, units, count, lane):
     nlon = len(block[0]) * LANES
-    width, mains, tail, per, size = packed_sizes(nlon, count)
+    width, mains, tail, per = packed_sizes(nlon, count)
     for d in range(count):
         j0, off = (d * width) // LANES, (d * width) % LANES
         for q, tiles in enumerate(block):
@@ -174,16 +176,36 @@
                       for m in range(mains + (1 if off else 0))]
             for m in range(mains):
                 whole = jnp.where(lane < LANES - off, turned[m], turned[m + 1]) if off else turned[m]
-                packed[d, unit, q * mains + m] = whole
+                packed[d, (unit * BLOCK + q) * mains + m] = whole
         if tail:
-            for g in range(-(-BLOCK // per)):
-                total = None
-                for place in range(min(per, BLOCK - g * per)):
-                    shift = (place * tail - off) % LANES
-                    source = block[g * per + place][j0 + mains]
-                    moved = pltpu.roll(source, shift, 1) if shift else source
-                    total = moved if total is None else jnp.where(lane < place * tail, total, moved)
-                packed[d, unit, BLOCK * mains + g] = total
+            totals = {}
+            for q, tiles in enumerate(block):
+                at, place = divmod(unit * BLOCK + q, per)
+                at += units * BLOCK * mains
+                shift = (place * tail - off) % LANES
+                moved = pltpu.roll(tiles[j0 + mains], shift, 1) if shift else tiles[j0 + mains]
+                if place:
+                    before = totals[at] if at in totals else packed[d, at]
+                    moved = jnp.where(lane < place * tail, before, moved)
+                totals[at] = moved
+            for at, total in totals.items():
+                packed[d, at] = total
+
+
+def unpack_unit(chunk, place, unit, units, target, lead, mains, tail, per, lane):
+    copy_tiles([((chunk, (place, unit * BLOCK * mains + i)), (target, lead + (i,))) for i in range(BLOCK * mains)])
+    totals = {}
+    for q in range(BLOCK if tail else 0):
+        at, there = divmod(unit * BLOCK + q, per)
+        to, here = divmod(q, per)
+        shift = (here - there) * tail % LANES
+        if to in totals and totals[to][1:] == (at, shift):
+            continue
+        source = chunk[place, units * BLOCK * mains + at]
+        moved = pltpu.roll(source, shift, 1) if shift else source
+        totals[to] = (jnp.where(lane < here * tail, totals[to][0], moved) if to in totals else moved, at, shift)
+    for to, (total, _, _) in totals.items():
+        target[lead + (BLOCK * mains + to,)] = total
 
 
 def copy_tiles(pairs):
@@ -192,16 +214,11 @@
         target[at] = value
 
 
-def copy_units(source, target, start=0):
-    for unit in range(source.shape[0]):
-        copy_tiles([((source, (unit, i)), (target, (start + unit, i))) for i in range(source.shape[1])])
-
-
 def hand_out(packed, outs, groups):
     me = lax.axis_index("lev")
     for group, out in zip(groups, outs):
         for place, k in enumerate(group):
-            copy_units(packed.at[me ^ k], out, place * packed.shape[1])
+            copy_tiles([((packed, (me ^ k, i)), (out, (place, i))) for i in range(packed.shape[1])])
 
 
 def own_coefficients(rows, joined, winds, cx, cy):
@@ -252,14 +269,13 @@
     work_last = [(level, row, row - REACH) for level in range(levels) for row in range(HALO, rows - HALO)]
 
     def send(group, done):
-        pack_block(done, packed, group, count, lane)
+        pack_block(done, packed, group, len(work_last) // BLOCK, count, lane)
 
     lon_pass(work_last, swept, coef_x, inter, west, flux, lane, send)
     hand_out(packed, outs, groups)
 
 
-def edge_kernel(count, rows, groups, slot, joint, state, first_round, second_round, first, cx, cy, *refs):
-    others = refs[:len(joint)]
+def edge_kernel(count, rows, groups, slot, state, first_round, second_round, first, cx, cy, *refs):
     outs, (packed, beyond, swept, edge, inter, west, flux) = refs[-7 - len(groups):-7], refs[-7:]
     nlon = state.shape[3]
     nj = nlon // LANES
@@ -318,17 +334,13 @@
         put_rows(edge, 0, group * BLOCK, done)
 
     def send(group, done):
-        pack_block(done, packed, group, count, lane)
+        pack_block(done, packed, group, len(ends_last), count, lane)
 
     lat_pass(1, nj, ends, cell, coef_y, put)
     lon_pass(listed(ends), swept, coef_x, inter, west, flux, lane, keep_edge)
     lat_pass(1, nj, ends_last, cell_first, coef_y, put_last)
     lon_pass(listed(ends_last), swept, coef_x, inter, west, flux, lane, send)
     hand_out(packed, outs, groups)
-    place = packed.shape[1]
-    for other, (begin, size) in zip(others, joint):
-        copy_units(other.at[pl.ds(begin, size)], outs[1], place)
-        place += size
 
 
 def weights_kernel(weights, source, out):
@@ -350,7 +362,8 @@
     chunks, weights, (out, levels, result, sems) = refs[:len(plan)], refs[len(plan)], refs[-4:]
     me = lax.axis_index("lev")
     targets, _, _, width = result.shape
-    _, mains, tail, per, _ = packed_sizes(width * count, count)
+    _, mains, tail, per = packed_sizes(width * count, count)
+    lane = lane_ids()
     copies = []
 
     def leave(source, target):
@@ -367,9 +380,8 @@
 
     for units, chunk in zip(plan, chunks):
         for unit, (k, slot, number) in enumerate(units):
-            if number in numbers:
-                at = numbers.index(number)
-                copy_tiles([((chunk, (unit, i)), (levels, (level_of(k, slot), at, i))) for i in range(chunk.shape[1])])
+            lead = (level_of(k, slot), numbers.index(number))
+            unpack_unit(chunk, 0, unit, len(units), levels, lead, mains, tail, per, lane)
 
     for at, number in enumerate(numbers):
         for q in range(BLOCK):
@@ -393,7 +405,8 @@
                         term = jnp.broadcast_to(weights[k, row, j:j + 1, lanes], (SUB, wide)) * values[level][:, :wide]
                         total = term if total is None else total + term
                     result[k, at * BLOCK + q, :, lanes] = total
-        leave(result.at[:, pl.ds(at * BLOCK, BLOCK)], out.at[:, pl.ds(number * BLOCK, BLOCK)])
+        for k in range(targets):
+            leave(result.at[k, pl.ds(at * BLOCK, BLOCK)], out.at[k, pl.ds(number * BLOCK, BLOCK)])
     for copy in copies:
         copy.wait()
 
@@ -440,7 +453,7 @@
     bands = lax.axis_size("lat")
     number, depth, rows, nlon = tracers.shape
     targets, _, width = source_level.shape
-    size = packed_sizes(nlon, count)[-1]
+    mains, tail, per = packed_sizes(nlon, count)[1:]
     blocks = rows // BLOCK
     inner = (rows - 2 * HALO) // BLOCK
 
@@ -465,8 +478,8 @@
         (jnp.transpose(remap_weight, (1, 2, 0, 3)), source_level),
         cost=cost(1, 1))
 
-    def box(units, *lead):
-        return lead + (units, size, SUB, LANES)
+    def box(places, units):
+        return places, packed_tiles(units, mains, tail, per), SUB, LANES
 
     def vmem(*shape):
         return pltpu.VMEM(shape, jnp.float32)
@@ -480,24 +493,22 @@
     inner_units = depth * inner
     result = call(
         functools.partial(interior_kernel, count, rows, groups),
-        [f32(*box(len(group) * inner_units)) for group in groups]
+        [f32(*box(len(group), inner_units)) for group in groups]
         + [f32(depth, rows - 2 * REACH, number, nlon), coef, coef] + [halo] * (2 * depth - 2),
-        (state, joined), scratch=[vmem(*box(inner_units, count)), vmem(2, depth, held, nlon), swept, stage, stage, stage],
+        (state, joined), scratch=[vmem(*box(count, inner_units)), vmem(2, depth, held, nlon), swept, stage, stage, stage],
         cost=cost(1, 1))
     middle, (first, cx, cy), sent = result[:len(groups)], result[len(groups):len(groups) + 3], result[len(groups) + 3:]
     rounds += [beside(sent[2 * i:2 * i + 2]) for i in range(depth - 1)]
     swept = vmem(1, 2 * HALO, number, nlon)
     stage = vmem(2 * HALO, number, nlon)
 
-    def edge(slot, groups, joint, after):
-        args = (state, *rounds[slot], first, cx, cy, *(chunk for chunk, _ in joint), *after)
-        parts = tuple(part for _, part in joint)
-        units = [2 * len(group) + (sum(size for _, size in parts) if group == (1,) else 0) for group in groups]
+    def edge(slot, groups, after):
+        args = (state, *rounds[slot], first, cx, cy, *after)
         return call(
-            functools.partial(edge_kernel, count, rows, groups, slot, parts),
-            [f32(*box(n)) for n in units], args,
+            functools.partial(edge_kernel, count, rows, groups, slot),
+            [f32(*box(len(group), 2)) for group in groups], args,
             specs=[VMEM] * (len(args) - len(after)) + [ANY] * len(after),
-            scratch=[vmem(*box(2, count)), vmem(3, 2, SUB, nlon), swept, swept, stage, stage, stage],
+            scratch=[vmem(*box(count, 2)), vmem(3, 2, SUB, nlon), swept, swept, stage, stage, stage],
             cost=cost(60 * tracers.size, 8 * tracers.size))
 
     def swapped(sent, k):
@@ -514,9 +525,9 @@
             in_specs=[SMEM] + [VMEM] * (len(args) - 1 - len(after)) + [ANY] * len(after),
             out_specs=ANY,
             scratch_shapes=[
-                vmem(targets + 1, blocks, size, SUB, LANES),
+                vmem(targets + 1, blocks, packed_tiles(1, mains, tail, per), SUB, LANES),
                 vmem(targets, rows, number, width),
-                pltpu.SemaphoreType.DMA((blocks,)),
+                pltpu.SemaphoreType.DMA((blocks * targets,)),
             ],
             compiler_params=pltpu.CompilerParams(vmem_limit_bytes=16 << 20),
             cost_estimate=cost(1, 1),
@@ -529,15 +540,14 @@
         )(*chunks)
 
     places = tuple((slot, 1 + b) for slot in range(depth) for b in range(inner))
-    passing = tuple((None, None, None) for _ in places)
     arrived = [swapped(chunk, k) for k, chunk in zip(chips, middle[2:])]
-    listed = [(units_of(k, places) + passing, chunk) for k, chunk in zip(chips, arrived)]
+    listed = [(units_of(k, places), chunk) for k, chunk in zip(chips, arrived)]
     listed.append((units_of(0, places), middle[0]))
     beside_me = [(units_of(1, places), middle[1])]
     after, marks = (taps,), []
     for slot in range(depth):
         own = ((slot, 0), (slot, blocks - 1))
-        done = edge(slot, tuple((k,) for k in range(count)), [], after)
+        done = edge(slot, tuple((k,) for k in range(count)), after)
         crossing = [(units_of(k, own), swapped(done[k], k)) for k in range(count - 1, 1, -1)]
         listed += crossing + [(units_of(0, own), done[0])]
         beside_me.append((units_of(1, own), done[1]))
@@ -545,7 +555,7 @@
         after = (done[0],)
     beside_me += [(units_of(k ^ 1, places), chunk) for k, chunk in zip(chips, arrived)]
     waiting = lax.optimization_barrier((*(chunk for _, chunk in beside_me), done[0]))
-    listed += [(units, swapped(chunk[chunk.shape[0] - len(units):], 1)) for (units, _), chunk in zip(beside_me, waiting)]
+    listed += [(units, swapped(chunk[-1:], 1)) for (units, _), chunk in zip(beside_me, waiting)]
     out = remap(listed, marks)
     return jnp.transpose(out, (2, 0, 1, 3))
 

time: 32.9 us -> 32.5 us (0.988)
  no operation moved by 1% of the time
where the time goes in v15:
time: 32.5 us; the launch traced here: 32.3 us
  starting transfers between devices  12.8 us (39%)
  Pallas kernels  11.5 us (35%)
  waiting for transfers between devices  5.43 us (17%)
  local copies, waits for them, and re-layouts  1.34 us (4%)
  other arithmetic  1.14 us (4%)
    pallas_call x5, Pallas kernels, call(): pl.pallas_call(kernel, out_shape=outs, in_specs=specs or [VMEM] * len(arg...  9.37 us
    ppermute x9, starting transfers between devices, swapped(): return lax.ppermute(sent, 'lev', [(i, i ^ k) for i in range(count)])  6.53 us
    ppermute x2, starting transfers between devices, beside(): lax.ppermute(sent[0], 'lat', [(i, i ^ 1) for i in range(bands)])  6.31 us
    ppermute x9, waiting for transfers between devices, swapped(): return lax.ppermute(sent, 'lev', [(i, i ^ k) for i in range(count)])  5.42 us
    pallas_call x1, Pallas kernels, remap(): pl.pallas_call(functools.partial(remap_kernel, count, tuple((units for un...  2.09 us
    unnamed x8, local copies, waits for them, and re-layouts  1.33 us
    concatenate x1, other arithmetic, shards(): jnp.concatenate([jnp.transpose(wind_x, (1, 0, 2)), jnp.transpose(wind_y,...  1.14 us
  transfers between devices with their start and end apart: 13, of which 3 were waited for; matrix products, arithmetic and copies ran while one was open for 0% of the time, Pallas kernels for 28%

profile of v15, /device:TPU:0, one launch (start us, length us, event | category | flops | bytes accessed | tf_op | source)
XLA Modules:
  0.0 32.3 jit_solution(7304562434714197162)
XLA Ops:
  0.0 1.1 %pad_maximum_fusion.winds.joined = f32[36,2,1152]{2,1,0:T(2,128)S(1)} fusion(f32[18,2,1152]{2,1,0:T(2,128)} %bitcast.13, f32[18,2,1152]{2,1,0:T(2,128)} %bitcast.14), kind=kLoop, calls=%fused_computation | loop fusion | flops 82944 | bytes 663552 | tf_op jit(solution)/shard_map/concatenate | solution.py:461
  1.1 0.0 copy-start
  1.2 1.3 %copy-done = f32[8,2,18,1152]{3,1,2,0:T(2,128)S(1)} copy-done((f32[8,2,18,1152]{3,1,2,0:T(2,128)S(1)}, f32[8,2,18,1152]{3,1,2,0:T(2,128)}, u32[]{:S(2)}) %copy-start) | copy-done | bytes 1327128
  2.5 0.0 copy-start.1
  2.5 0.0 copy-start.2
  2.5 0.2 shard_map.64
  2.7 3.1 %collective-permute-start.1 = (f32[7,8,1152]{2,1,0:T(8,128)S(1)}, f32[7,8,1152]{2,1,0:T(8,128)S(1)}, u32[]{:S(2)}, u32[]{:S(2)}) collective-permute-start(f32[7,8,1152]{2,1,0:T(8,128)S(1)} %get-tuple-element.31), channel_id=1, source_target_pairs={{0,4},{4,0},{8,12},{12,8},{1,5},{5,1},{9,13},{13,9},{2,6},{6,2},{1... | collective-permute-start | bytes 774152 | tf_op jit(solution)/shard_map/ppermute | solution.py:472
  5.8 0.0 collective-permute-start.2
  5.8 3.8 %shard_map.65 = (f32[1,27,8,128]{3,2,1,0:T(8,128)S(1)}, f32[1,27,8,128]{3,2,1,0:T(8,128)S(1)}, f32[2,27,8,128]{3,2,1,0:T(8,128)S(1)}, f32[2,12,8,1152]{3,2,1,0:T...) custom-call(f32[2,18,8,1152]{3,2,1,0:T(8,128)S(1)} %get-tuple-elemen, ...), custom_call_target="tpu_custom_call" | custom-call | flops 1 | bytes 1 | tf_op jit(solution)/shard_map/pallas_call | solution.py:432
  9.6 3.2 %collective-permute-start.5 = (f32[7,8,1152]{2,1,0:T(8,128)S(1)}, f32[7,8,1152]{2,1,0:T(8,128)S(1)}, u32[]{:S(2)}, u32[]{:S(2)}) collective-permute-start(f32[7,8,1152]{2,1,0:T(8,128)S(1)} %get-tuple-element.39), channel_id=1, source_target_pairs={{0,4},{4,0},{8,12},{12,8},{1,5},{5,1},{9,13},{13,9},{2,6},{6,2},{1... | collective-permute-start | bytes 774152 | tf_op jit(solution)/shard_map/ppermute | solution.py:472
  12.9 0.0 collective-permute-start.6
  12.9 1.5 %collective-permute-start = (f32[2,27,8,128]{3,2,1,0:T(8,128)S(1)}, f32[2,27,8,128]{3,2,1,0:T(8,128)S(1)}, u32[]{:S(2)}, u32[]{:S(2)}) collective-permute-start(f32[2,27,8,128]{3,2,1,0:T(8,128)S(1)} %get-tuple-element.29), channel_id=1, source_target_pairs={{0,2},{1,3},{2,0},{3,1},{4,6},{5,7},{6,4},{7,5},{8,10},{9,11},{10,... | collective-permute-start | bytes 663560 | tf_op jit(solution)/shard_map/ppermute | solution.py:515
  14.4 0.0 copy-done.1
  14.4 0.0 copy-done.2
  14.4 0.2 shard_map.66.refs_0_.refs_12_
  14.6 0.0 collective-permute-done.1.first_round
  14.6 0.0 collective-permute-done.2.second_round
  14.6 2.6 %shard_map.67 = (f32[1,27,8,128]{3,2,1,0:T(8,128)S(1)}, f32[1,27,8,128]{3,2,1,0:T(8,128)S(1)}, f32[1,27,8,128]{3,2,1,0:T(8,128)S(1)}, f32[1,27,8,128]{3,2,1,0:T(8,128)S(1)}) custom-call(f32[2,18,8,1152]{3,2,1,0:T(8,128)S(1)} %get-tuple-element.28.state, f32[7,8,1152]{2,1,0:T(8,128)S(1)} %collective-permute-done.1.first_round, ...), custom_call_target="tpu_custom_call" | custom-call | flops 19906560 | bytes 2654208 | tf_op jit(solution)/shard_map/pallas_call | solution.py:432
  17.1 0.4 %collective-permute-start.3 = (f32[1,27,8,128]{3,2,1,0:T(8,128)S(1)}, f32[1,27,8,128]{3,2,1,0:T(8,128)S(1)}, u32[]{:S(2)}, u32[]{:S(2)}) collective-permute-start(f32[1,27,8,128]{3,2,1,0:T(8,128)S(1)} %get-tuple-element.36), channel_id=1, source_target_pairs={{0,3},{1,2},{2,1},{3,0},{4,7},{5,6},{6,5},{7,4},{8,11},{9,10},{10,... | collective-permute-start | bytes 331784 | tf_op jit(solution)/shard_map/ppermute | solution.py:515
  17.6 1.5 %collective-permute-start.4 = (f32[1,27,8,128]{3,2,1,0:T(8,128)S(1)}, f32[1,27,8,128]{3,2,1,0:T(8,128)S(1)}, u32[]{:S(2)}, u32[]{:S(2)}) collective-permute-start(f32[1,27,8,128]{3,2,1,0:T(8,128)S(1)} %get-tuple-element.37), channel_id=1, source_target_pairs={{0,2},{1,3},{2,0},{3,1},{4,6},{5,7},{6,4},{7,5},{8,10},{9,11},{10,... | collective-permute-start | bytes 331784 | tf_op jit(solution)/shard_map/ppermute | solution.py:515
  19.1 0.0 collective-permute-done.5.first_round
  19.1 0.0 collective-permute-done.6.second_round
  19.1 0.0 copy-start.3
  19.1 2.6 %shard_map.68 = (f32[1,27,8,128]{3,2,1,0:T(8,128)S(1)}, f32[1,27,8,128]{3,2,1,0:T(8,128)S(1)}, f32[1,27,8,128]{3,2,1,0:T(8,128)S(1)}, f32[1,27,8,128]{3,2,1,0:T(8,128)S(1)}) custom-call(f32[2,18,8,1152]{3,2,1,0:T(8,128)S(1)} %get-tuple-element.28.state, f32[7,8,1152]{2,1,0:T(8,128)S(1)} %collective-permute-done.5.first_round, ...), custom_call_target="tpu_custom_call" | custom-call | flops 19906560 | bytes 2654208 | tf_op jit(solution)/shard_map/pallas_call | solution.py:432
  21.6 0.2 collective-permute-start.7
  21.9 0.0 collective-permute-done.refs_0_
  21.9 1.0 %collective-permute-start.12 = (f32[1,27,8,128]{3,2,1,0:T(8,128)S(1)}, f32[1,27,8,128]{3,2,1,0:T(8,128)S(1)}, u32[]{:S(2)}, u32[]{:S(2)}) collective-permute-start(f32[1,27,8,128]{3,2,1,0:T(8,128)S(1)} %slice.3), channel_id=1, source_target_pairs={{0,1},{1,0},{2,3},{3,2},{4,5},{5,4},{6,7},{7,6},{8,9},{9,8},{10,11... | collective-permute-start | bytes 331784 | tf_op jit(solution)/shard_map/ppermute | solution.py:515
  22.8 0.1 collective-permute-start.9
  22.9 0.0 collective-permute-done.3.refs_0_.refs_2_
  22.9 1.2 %collective-permute-start.8 = (f32[1,27,8,128]{3,2,1,0:T(8,128)S(1)}, f32[1,27,8,128]{3,2,1,0:T(8,128)S(1)}, u32[]{:S(2)}, u32[]{:S(2)}) collective-permute-start(f32[1,27,8,128]{3,2,1,0:T(8,128)S(1)} %get-tuple-element.42), channel_id=1, source_target_pairs={{0,2},{1,3},{2,0},{3,1},{4,6},{5,7},{6,4},{7,5},{8,10},{9,11},{10,... | collective-permute-start | bytes 331784 | tf_op jit(solution)/shard_map/ppermute | solution.py:515
  24.2 1.7 %collective-permute-done.4.refs_1_.refs_3_ = f32[1,27,8,128]{3,2,1,0:T(8,128)S(1)} collective-permute-done((f32[1,27,8,128]{3,2,1,0:T(8,128)S(1)}, f32[1,27,8,128]{3,2,1,0:T(8,128)S(1)}, u32[]{:S(2)}, u32[]{:S(2)}) %collective-permute-start.4) | collective-permute-done | bytes 110624 | tf_op jit(solution)/shard_map/ppermute | solution.py:515
  25.8 0.0 collective-permute-start.10
  25.8 1.6 %collective-permute-done.7.refs_0_.refs_5_ = f32[1,27,8,128]{3,2,1,0:T(8,128)S(1)} collective-permute-done((f32[1,27,8,128]{3,2,1,0:T(8,128)S(1)}, f32[1,27,8,128]{3,2,1,0:T(8,128)S(1)}, u32[]{:S(2)}, u32[]{:S(2)}) %collective-permute-start.7) | collective-permute-done | bytes 110624 | tf_op jit(solution)/shard_map/ppermute | solution.py:515
  27.4 0.6 %collective-permute-start.11 = (f32[1,27,8,128]{3,2,1,0:T(8,128)S(1)}, f32[1,27,8,128]{3,2,1,0:T(8,128)S(1)}, u32[]{:S(2)}, u32[]{:S(2)}) collective-permute-start(f32[1,27,8,128]{3,2,1,0:T(8,128)S(1)} %get-tuple-element.49), channel_id=1, source_target_pairs={{0,1},{1,0},{2,3},{3,2},{4,5},{5,4},{6,7},{7,6},{8,9},{9,8},{10,11... | collective-permute-start | bytes 331784 | tf_op jit(solution)/shard_map/ppermute | solution.py:515
  28.0 2.2 %collective-permute-done.8.refs_1_.refs_6_ = f32[1,27,8,128]{3,2,1,0:T(8,128)S(1)} collective-permute-done((f32[1,27,8,128]{3,2,1,0:T(8,128)S(1)}, f32[1,27,8,128]{3,2,1,0:T(8,128)S(1)}, u32[]{:S(2)}, u32[]{:S(2)}) %collective-permute-start.8) | collective-permute-done | bytes 110624 | tf_op jit(solution)/shard_map/ppermute | solution.py:515
  30.2 0.0 collective-permute-done.12.refs_11_
  30.2 0.0 collective-permute-done.9.refs_8_
  30.2 0.0 collective-permute-done.10.refs_9_
  30.2 0.0 collective-permute-done.11.refs_10_
  30.2 0.0 copy-done.3
  30.2 2.1 %shard_map.71 = f32[6,18,8,288]{3,2,1,0:T(8,128)} custom-call(s32[4]{0:T(128)S(1)} %copy-done.3, f32[2,27,8,128]{3,2,1,0:T(8,128)S(1)} %collective-permute-done.refs_0_, f32[1,27,8,128]{3,2,1,0:T(8,128)S(1)} %get-tuple-element.30.refs_1_, f32[1,27,8,128]{3,2,1,0:T(8,128)S(1)} %collective-permute-done.3.refs_0_.refs_2_, ...), custom_call_target="tpu_custom_call" | custom-call | flops 1 | bytes 1 | tf_op jit(solution)/shard_map/pallas_call | solution.py:522
  (3 shorter events, 0.0 us)
Async XLA Ops:
  1.1 1.3 %copy-start = (f32[8,2,18,1152]{3,1,2,0:T(2,128)S(1)}, f32[8,2,18,1152]{3,1,2,0:T(2,128)}, u32[]{:S(2)}) copy-start(f32[8,2,18,1152]{3,1,2,0:T(2,128)} %param.6) | copy-start | bytes 3981316
  2.5 11.9 %copy-start.1 = (f32[4,6,18,288]{3,0,2,1:T(4,128)S(1)}, f32[4,6,18,288]{3,0,2,1:T(4,128)}, u32[]{:S(2)}) copy-start(f32[4,6,18,288]{3,0,2,1:T(4,128)} %param.11) | copy-start | bytes 1492996
  2.5 11.9 %copy-start.2 = (s32[6,18,288]{2,1,0:T(8,128)S(1)}, s32[6,18,288]{2,1,0:T(8,128)}, u32[]{:S(2)}) copy-start(s32[6,18,288]{2,1,0:T(8,128)} %source.1) | copy-start | bytes 373252
  2.7 11.9 %collective-permute-start.1 = (f32[7,8,1152]{2,1,0:T(8,128)S(1)}, f32[7,8,1152]{2,1,0:T(8,128)S(1)}, u32[]{:S(2)}, u32[]{:S(2)}) collective-permute-start(f32[7,8,1152]{2,1,0:T(8,128)S(1)} %get-tuple-element.31), channel_id=1, source_target_pairs={{0,4},{4,0},{8,12},{12,8},{1,5},{5,1},{9,13},{13,9},{2,6},{6,2},{1... | collective-permute-start | bytes 774152 | tf_op jit(solution)/shard_map/ppermute | solution.py:472
  5.8 8.8 %collective-permute-start.2 = (f32[7,8,1152]{2,1,0:T(8,128)S(1)}, f32[7,8,1152]{2,1,0:T(8,128)S(1)}, u32[]{:S(2)}, u32[]{:S(2)}) collective-permute-start(f32[7,8,1152]{2,1,0:T(8,128)S(1)} %get-tuple-element.32), channel_id=1, source_target_pairs={{0,1},{1,0},{2,3},{3,2},{4,8},{5,9},{6,10},{7,11},{8,4},{9,5},{10,... | collective-permute-start | bytes 774152 | tf_op jit(solution)/shard_map/ppermute | solution.py:473
  9.6 9.4 %collective-permute-start.5 = (f32[7,8,1152]{2,1,0:T(8,128)S(1)}, f32[7,8,1152]{2,1,0:T(8,128)S(1)}, u32[]{:S(2)}, u32[]{:S(2)}) collective-permute-start(f32[7,8,1152]{2,1,0:T(8,128)S(1)} %get-tuple-element.39), channel_id=1, source_target_pairs={{0,4},{4,0},{8,12},{12,8},{1,5},{5,1},{9,13},{13,9},{2,6},{6,2},{1... | collective-permute-start | bytes 774152 | tf_op jit(solution)/shard_map/ppermute | solution.py:472
  12.9 6.2 %collective-permute-start.6 = (f32[7,8,1152]{2,1,0:T(8,128)S(1)}, f32[7,8,1152]{2,1,0:T(8,128)S(1)}, u32[]{:S(2)}, u32[]{:S(2)}) collective-permute-start(f32[7,8,1152]{2,1,0:T(8,128)S(1)} %get-tuple-element.40), channel_id=1, source_target_pairs={{0,1},{1,0},{2,3},{3,2},{4,8},{5,9},{6,10},{7,11},{8,4},{9,5},{10,... | collective-permute-start | bytes 774152 | tf_op jit(solution)/shard_map/ppermute | solution.py:473
  12.9 9.0 %collective-permute-start = (f32[2,27,8,128]{3,2,1,0:T(8,128)S(1)}, f32[2,27,8,128]{3,2,1,0:T(8,128)S(1)}, u32[]{:S(2)}, u32[]{:S(2)}) collective-permute-start(f32[2,27,8,128]{3,2,1,0:T(8,128)S(1)} %get-tuple-element.29), channel_id=1, source_target_pairs={{0,2},{1,3},{2,0},{3,1},{4,6},{5,7},{6,4},{7,5},{8,10},{9,11},{10,... | collective-permute-start | bytes 663560 | tf_op jit(solution)/shard_map/ppermute | solution.py:515
  17.1 5.8 %collective-permute-start.3 = (f32[1,27,8,128]{3,2,1,0:T(8,128)S(1)}, f32[1,27,8,128]{3,2,1,0:T(8,128)S(1)}, u32[]{:S(2)}, u32[]{:S(2)}) collective-permute-start(f32[1,27,8,128]{3,2,1,0:T(8,128)S(1)} %get-tuple-element.36), channel_id=1, source_target_pairs={{0,3},{1,2},{2,1},{3,0},{4,7},{5,6},{6,5},{7,4},{8,11},{9,10},{10,... | collective-permute-start | bytes 331784 | tf_op jit(solution)/shard_map/ppermute | solution.py:515
  17.6 8.2 %collective-permute-start.4 = (f32[1,27,8,128]{3,2,1,0:T(8,128)S(1)}, f32[1,27,8,128]{3,2,1,0:T(8,128)S(1)}, u32[]{:S(2)}, u32[]{:S(2)}) collective-permute-start(f32[1,27,8,128]{3,2,1,0:T(8,128)S(1)} %get-tuple-element.37), channel_id=1, source_target_pairs={{0,2},{1,3},{2,0},{3,1},{4,6},{5,7},{6,4},{7,5},{8,10},{9,11},{10,... | collective-permute-start | bytes 331784 | tf_op jit(solution)/shard_map/ppermute | solution.py:515
  19.1 11.1 %copy-start.3 = (s32[4]{0:T(128)S(1)}, s32[4]{0:T(128)}, u32[]{:S(2)}) copy-start(s32[4]{0:T(128)} %counts.1) | copy-start | bytes 52
  21.6 5.8 %collective-permute-start.7 = (f32[1,27,8,128]{3,2,1,0:T(8,128)S(1)}, f32[1,27,8,128]{3,2,1,0:T(8,128)S(1)}, u32[]{:S(2)}, u32[]{:S(2)}) collective-permute-start(f32[1,27,8,128]{3,2,1,0:T(8,128)S(1)} %get-tuple-element.41), channel_id=1, source_target_pairs={{0,3},{1,2},{2,1},{3,0},{4,7},{5,6},{6,5},{7,4},{8,11},{9,10},{10,... | collective-permute-start | bytes 331784 | tf_op jit(solution)/shard_map/ppermute | solution.py:515
  21.9 8.3 %collective-permute-start.12 = (f32[1,27,8,128]{3,2,1,0:T(8,128)S(1)}, f32[1,27,8,128]{3,2,1,0:T(8,128)S(1)}, u32[]{:S(2)}, u32[]{:S(2)}) collective-permute-start(f32[1,27,8,128]{3,2,1,0:T(8,128)S(1)} %slice.3), channel_id=1, source_target_pairs={{0,1},{1,0},{2,3},{3,2},{4,5},{5,4},{6,7},{7,6},{8,9},{9,8},{10,11... | collective-permute-start | bytes 331784 | tf_op jit(solution)/shard_map/ppermute | solution.py:515
  22.8 7.3 %collective-permute-start.9 = (f32[1,27,8,128]{3,2,1,0:T(8,128)S(1)}, f32[1,27,8,128]{3,2,1,0:T(8,128)S(1)}, u32[]{:S(2)}, u32[]{:S(2)}) collective-permute-start(f32[1,27,8,128]{3,2,1,0:T(8,128)S(1)} %get-tuple-element.47), channel_id=1, source_target_pairs={{0,1},{1,0},{2,3},{3,2},{4,5},{5,4},{6,7},{7,6},{8,9},{9,8},{10,11... | collective-permute-start | bytes 331784 | tf_op jit(solution)/shard_map/ppermute | solution.py:515
  22.9 7.3 %collective-permute-start.8 = (f32[1,27,8,128]{3,2,1,0:T(8,128)S(1)}, f32[1,27,8,128]{3,2,1,0:T(8,128)S(1)}, u32[]{:S(2)}, u32[]{:S(2)}) collective-permute-start(f32[1,27,8,128]{3,2,1,0:T(8,128)S(1)} %get-tuple-element.42), channel_id=1, source_target_pairs={{0,2},{1,3},{2,0},{3,1},{4,6},{5,7},{6,4},{7,5},{8,10},{9,11},{10,... | collective-permute-start | bytes 331784 | tf_op jit(solution)/shard_map/ppermute | solution.py:515
  25.8 4.4 %collective-permute-start.10 = (f32[1,27,8,128]{3,2,1,0:T(8,128)S(1)}, f32[1,27,8,128]{3,2,1,0:T(8,128)S(1)}, u32[]{:S(2)}, u32[]{:S(2)}) collective-permute-start(f32[1,27,8,128]{3,2,1,0:T(8,128)S(1)} %get-tuple-element.48), channel_id=1, source_target_pairs={{0,1},{1,0},{2,3},{3,2},{4,5},{5,4},{6,7},{7,6},{8,9},{9,8},{10,11... | collective-permute-start | bytes 331784 | tf_op jit(solution)/shard_map/ppermute | solution.py:515
  27.4 2.8 %collective-permute-start.11 = (f32[1,27,8,128]{3,2,1,0:T(8,128)S(1)}, f32[1,27,8,128]{3,2,1,0:T(8,128)S(1)}, u32[]{:S(2)}, u32[]{:S(2)}) collective-permute-start(f32[1,27,8,128]{3,2,1,0:T(8,128)S(1)} %get-tuple-element.49), channel_id=1, source_target_pairs={{0,1},{1,0},{2,3},{3,2},{4,5},{5,4},{6,7},{7,6},{8,9},{9,8},{10,11... | collective-permute-start | bytes 331784 | tf_op jit(solution)/shard_map/ppermute | solution.py:515

commit v16 on v15

--- a/solution.py
+++ b/solution.py
@@ -72,7 +72,7 @@
             target[HALO, REACH + q:REACH + q + 1, :] = scaled(winds[rows + row_y + q, slot:slot + 1, :])
 
 
-def prep_kernel(rows, tracers, winds, state, first_round, second_round):
+def prep_kernel(rows, tracers, winds, state, *halos):
     levels, nlon = state.shape[0], state.shape[3]
     nj = nlon // LANES
     row_stride = nj * levels
@@ -86,7 +86,8 @@
         return 0
 
     lax.fori_loop(0, rows, body, 0)
-    fill_halos(rows, 0, state, winds, first_round, second_round)
+    for slot in range(levels):
+        fill_halos(rows, slot, state, winds, *halos[2 * slot:2 * slot + 2])
 
 
 def lat_pass(levels, nj, ranges, cell, coef, store):
@@ -243,13 +244,10 @@
 
 
 def interior_kernel(count, rows, groups, state, joined, *refs):
-    outs, (first, cx, cy), refs = refs[:len(groups)], refs[len(groups):len(groups) + 3], refs[len(groups) + 3:]
-    halos, (packed, winds, swept, inter, west, flux) = refs[:-6], refs[-6:]
+    outs, (first, cx, cy, packed, winds, swept, inter, west, flux) = refs[:len(groups)], refs[len(groups):]
     levels, nlon = state.shape[0], state.shape[3]
     nj = nlon // LANES
     lane = lane_ids()
-    for slot in range(1, levels):
-        fill_halos(rows, slot, state, joined, *halos[2 * slot - 2:2 * slot])
     own_coefficients(rows, joined, winds, cx, cy)
     coef_x = lambda i, level, r, lanes: cx[i, level, r:r + 1, lanes]
     coef_y = lambda i, level, f, lanes: cy[i, level, f:f + 1, lanes]
@@ -462,7 +460,7 @@
     halo = f32(HALO + 1, number, nlon)
     state, *sent = call(
         functools.partial(prep_kernel, rows),
-        [f32(depth, rows, number, nlon), halo, halo], (raw, joined),
+        [f32(depth, rows, number, nlon)] + [halo] * (2 * depth), (raw, joined),
         cost=cost(1, 1))
     second = {i: ((i - 1) ^ 1) + 1 for i in range(1, bands - 1)}
     second_pairs = [(i * count + d, second[i] * count + d if i in second else i * count + (d ^ 1))
@@ -472,7 +470,7 @@
         return [lax.ppermute(sent[0], "lat", [(i, i ^ 1) for i in range(bands)]),
                 lax.ppermute(sent[1], ("lat", "lev"), second_pairs)]
 
-    rounds = [beside(sent)]
+    rounds = [beside(sent[2 * slot:2 * slot + 2]) for slot in range(depth)]
     taps = call(
         weights_kernel, f32(targets, rows, SUB, width),
         (jnp.transpose(remap_weight, (1, 2, 0, 3)), source_level),
@@ -494,11 +492,10 @@
     result = call(
         functools.partial(interior_kernel, count, rows, groups),
         [f32(*box(len(group), inner_units)) for group in groups]
-        + [f32(depth, rows - 2 * REACH, number, nlon), coef, coef] + [halo] * (2 * depth - 2),
+        + [f32(depth, rows - 2 * REACH, number, nlon), coef, coef],
         (state, joined), scratch=[vmem(*box(count, inner_units)), vmem(2, depth, held, nlon), swept, stage, stage, stage],
         cost=cost(1, 1))
-    middle, (first, cx, cy), sent = result[:len(groups)], result[len(groups):len(groups) + 3], result[len(groups) + 3:]
-    rounds += [beside(sent[2 * i:2 * i + 2]) for i in range(depth - 1)]
+    middle, (first, cx, cy) = result[:len(groups)], result[len(groups):]
     swept = vmem(1, 2 * HALO, number, nlon)
     stage = vmem(2 * HALO, number, nlon)
 

time: 32.5 us -> 32.5 us (level)
  no operation moved by 1% of the time
where the time goes in v16:
time: 32.5 us; the launch traced here: 32.3 us
  starting transfers between devices  12.6 us (39%)
  Pallas kernels  11.5 us (35%)
  waiting for transfers between devices  5.66 us (17%)
  local copies, waits for them, and re-layouts  1.34 us (4%)
  other arithmetic  1.14 us (4%)
    pallas_call x5, Pallas kernels, call(): pl.pallas_call(kernel, out_shape=outs, in_specs=specs or [VMEM] * len(arg...  9.39 us
    ppermute x9, starting transfers between devices, swapped(): return lax.ppermute(sent, 'lev', [(i, i ^ k) for i in range(count)])  6.35 us
    ppermute x2, starting transfers between devices, beside(): lax.ppermute(sent[0], 'lat', [(i, i ^ 1) for i in range(bands)])  6.24 us
    ppermute x9, waiting for transfers between devices, swapped(): return lax.ppermute(sent, 'lev', [(i, i ^ k) for i in range(count)])  5.65 us
    pallas_call x1, Pallas kernels, remap(): pl.pallas_call(functools.partial(remap_kernel, count, tuple((units for un...  2.1 us
    unnamed x8, local copies, waits for them, and re-layouts  1.33 us
    concatenate x1, other arithmetic, shards(): jnp.concatenate([jnp.transpose(wind_x, (1, 0, 2)), jnp.transpose(wind_y,...  1.14 us
  transfers between devices with their start and end apart: 13, of which 3 were waited for; matrix products, arithmetic and copies ran while one was open for 0% of the time, Pallas kernels for 28%

profile of v16, /device:TPU:0, one launch (start us, length us, event | category | flops | bytes accessed | tf_op | source)
XLA Modules:
  0.0 32.3 jit_solution(3419843762581269806)
XLA Ops:
  0.0 1.1 %pad_maximum_fusion.winds.joined = f32[36,2,1152]{2,1,0:T(2,128)S(1)} fusion(f32[18,2,1152]{2,1,0:T(2,128)} %bitcast.13, f32[18,2,1152]{2,1,0:T(2,128)} %bitcast.14), kind=kLoop, calls=%fused_computation | loop fusion | flops 82944 | bytes 663552 | tf_op jit(solution)/shard_map/concatenate | solution.py:459
  1.1 0.0 copy-start
  1.2 1.3 %copy-done = f32[8,2,18,1152]{3,1,2,0:T(2,128)S(1)} copy-done((f32[8,2,18,1152]{3,1,2,0:T(2,128)S(1)}, f32[8,2,18,1152]{3,1,2,0:T(2,128)}, u32[]{:S(2)}) %copy-start) | copy-done | bytes 1327128
  2.5 0.0 copy-start.1
  2.5 0.0 copy-start.2
  2.5 0.3 shard_map.64
  2.7 3.1 %collective-permute-start.1 = (f32[7,8,1152]{2,1,0:T(8,128)S(1)}, f32[7,8,1152]{2,1,0:T(8,128)S(1)}, u32[]{:S(2)}, u32[]{:S(2)}) collective-permute-start(f32[7,8,1152]{2,1,0:T(8,128)S(1)} %get-tuple-element.31), channel_id=1, source_target_pairs={{0,4},{4,0},{8,12},{12,8},{1,5},{5,1},{9,13},{13,9},{2,6},{6,2},{1... | collective-permute-start | bytes 774152 | tf_op jit(solution)/shard_map/ppermute | solution.py:470
  5.8 0.0 collective-permute-start.2
  5.8 3.1 %collective-permute-start.5 = (f32[7,8,1152]{2,1,0:T(8,128)S(1)}, f32[7,8,1152]{2,1,0:T(8,128)S(1)}, u32[]{:S(2)}, u32[]{:S(2)}) collective-permute-start(f32[7,8,1152]{2,1,0:T(8,128)S(1)} %get-tuple-element.39), channel_id=1, source_target_pairs={{0,4},{4,0},{8,12},{12,8},{1,5},{5,1},{9,13},{13,9},{2,6},{6,2},{1... | collective-permute-start | bytes 774152 | tf_op jit(solution)/shard_map/ppermute | solution.py:470
  9.0 0.0 collective-permute-start.6
  9.0 3.8 %shard_map.65 = (f32[1,27,8,128]{3,2,1,0:T(8,128)S(1)}, f32[1,27,8,128]{3,2,1,0:T(8,128)S(1)}, f32[2,27,8,128]{3,2,1,0:T(8,128)S(1)}, f32[2,12,8,1152]{3,2,1,0:T...) custom-call(f32[2,18,8,1152]{3,2,1,0:T(8,128)S(1)} %get-tuple-element.28.state, ...), custom_call_target="tpu_custom_call" | custom-call | flops 1 | bytes 1 | tf_op jit(solution)/shard_map/pallas_call | solution.py:430
  12.8 1.6 %collective-permute-start = (f32[2,27,8,128]{3,2,1,0:T(8,128)S(1)}, f32[2,27,8,128]{3,2,1,0:T(8,128)S(1)}, u32[]{:S(2)}, u32[]{:S(2)}) collective-permute-start(f32[2,27,8,128]{3,2,1,0:T(8,128)S(1)} %get-tuple-element.29), channel_id=1, source_target_pairs={{0,2},{1,3},{2,0},{3,1},{4,6},{5,7},{6,4},{7,5},{8,10},{9,11},{10,... | collective-permute-start | bytes 663560 | tf_op jit(solution)/shard_map/ppermute | solution.py:512
  14.4 0.0 copy-done.1
  14.4 0.0 copy-done.2
  14.4 0.2 shard_map.66.refs_0_.refs_12_
  14.6 0.0 collective-permute-done.1.first_round
  14.6 0.0 collective-permute-done.2.second_round
  14.6 2.6 %shard_map.67 = (f32[1,27,8,128]{3,2,1,0:T(8,128)S(1)}, f32[1,27,8,128]{3,2,1,0:T(8,128)S(1)}, f32[1,27,8,128]{3,2,1,0:T(8,128)S(1)}, f32[1,27,8,128]{3,2,1,0:T(8,128)S(1)}) custom-call(f32[2,18,8,1152]{3,2,1,0:T(8,128)S(1)} %get-tuple-element.28.state, f32[7,8,1152]{2,1,0:T(8,128)S(1)} %collective-permute-done.1.first_round, ...), custom_call_target="tpu_custom_call" | custom-call | flops 19906560 | bytes 2654208 | tf_op jit(solution)/shard_map/pallas_call | solution.py:430
  17.2 0.4 %collective-permute-start.3 = (f32[1,27,8,128]{3,2,1,0:T(8,128)S(1)}, f32[1,27,8,128]{3,2,1,0:T(8,128)S(1)}, u32[]{:S(2)}, u32[]{:S(2)}) collective-permute-start(f32[1,27,8,128]{3,2,1,0:T(8,128)S(1)} %get-tuple-element.36), channel_id=1, source_target_pairs={{0,3},{1,2},{2,1},{3,0},{4,7},{5,6},{6,5},{7,4},{8,11},{9,10},{10,... | collective-permute-start | bytes 331784 | tf_op jit(solution)/shard_map/ppermute | solution.py:512
  17.6 1.5 %collective-permute-start.4 = (f32[1,27,8,128]{3,2,1,0:T(8,128)S(1)}, f32[1,27,8,128]{3,2,1,0:T(8,128)S(1)}, u32[]{:S(2)}, u32[]{:S(2)}) collective-permute-start(f32[1,27,8,128]{3,2,1,0:T(8,128)S(1)} %get-tuple-element.37), channel_id=1, source_target_pairs={{0,2},{1,3},{2,0},{3,1},{4,6},{5,7},{6,4},{7,5},{8,10},{9,11},{10,... | collective-permute-start | bytes 331784 | tf_op jit(solution)/shard_map/ppermute | solution.py:512
  19.1 0.0 collective-permute-done.5.first_round
  19.1 0.0 collective-permute-done.6.second_round
  19.1 0.0 copy-start.3
  19.1 2.6 %shard_map.68 = (f32[1,27,8,128]{3,2,1,0:T(8,128)S(1)}, f32[1,27,8,128]{3,2,1,0:T(8,128)S(1)}, f32[1,27,8,128]{3,2,1,0:T(8,128)S(1)}, f32[1,27,8,128]{3,2,1,0:T(8,128)S(1)}) custom-call(f32[2,18,8,1152]{3,2,1,0:T(8,128)S(1)} %get-tuple-element.28.state, f32[7,8,1152]{2,1,0:T(8,128)S(1)} %collective-permute-done.5.first_round, ...), custom_call_target="tpu_custom_call" | custom-call | flops 19906560 | bytes 2654208 | tf_op jit(solution)/shard_map/pallas_call | solution.py:430
  21.7 0.2 collective-permute-start.7
  21.9 1.5 %collective-permute-start.8 = (f32[1,27,8,128]{3,2,1,0:T(8,128)S(1)}, f32[1,27,8,128]{3,2,1,0:T(8,128)S(1)}, u32[]{:S(2)}, u32[]{:S(2)}) collective-permute-start(f32[1,27,8,128]{3,2,1,0:T(8,128)S(1)} %get-tuple-element.42), channel_id=1, source_target_pairs={{0,2},{1,3},{2,0},{3,1},{4,6},{5,7},{6,4},{7,5},{8,10},{9,11},{10,... | collective-permute-start | bytes 331784 | tf_op jit(solution)/shard_map/ppermute | solution.py:512
  23.4 0.0 collective-permute-done.refs_0_
  23.4 0.3 collective-permute-start.12
  23.7 0.0 collective-permute-done.3.refs_0_.refs_2_
  23.7 0.3 collective-permute-start.9
  24.0 1.9 %collective-permute-done.4.refs_1_.refs_3_ = f32[1,27,8,128]{3,2,1,0:T(8,128)S(1)} collective-permute-done((f32[1,27,8,128]{3,2,1,0:T(8,128)S(1)}, f32[1,27,8,128]{3,2,1,0:T(8,128)S(1)}, u32[]{:S(2)}, u32[]{:S(2)}) %collective-permute-start.4) | collective-permute-done | bytes 110624 | tf_op jit(solution)/shard_map/ppermute | solution.py:512
  25.8 0.0 collective-permute-start.10
  25.8 1.6 %collective-permute-done.7.refs_0_.refs_5_ = f32[1,27,8,128]{3,2,1,0:T(8,128)S(1)} collective-permute-done((f32[1,27,8,128]{3,2,1,0:T(8,128)S(1)}, f32[1,27,8,128]{3,2,1,0:T(8,128)S(1)}, u32[]{:S(2)}, u32[]{:S(2)}) %collective-permute-start.7) | collective-permute-done | bytes 110624 | tf_op jit(solution)/shard_map/ppermute | solution.py:512
  27.4 0.6 %collective-permute-start.11 = (f32[1,27,8,128]{3,2,1,0:T(8,128)S(1)}, f32[1,27,8,128]{3,2,1,0:T(8,128)S(1)}, u32[]{:S(2)}, u32[]{:S(2)}) collective-permute-start(f32[1,27,8,128]{3,2,1,0:T(8,128)S(1)} %get-tuple-element.49), channel_id=1, source_target_pairs={{0,1},{1,0},{2,3},{3,2},{4,5},{5,4},{6,7},{7,6},{8,9},{9,8},{10,11... | collective-permute-start | bytes 331784 | tf_op jit(solution)/shard_map/ppermute | solution.py:512
  28.0 2.2 %collective-permute-done.8.refs_1_.refs_6_ = f32[1,27,8,128]{3,2,1,0:T(8,128)S(1)} collective-permute-done((f32[1,27,8,128]{3,2,1,0:T(8,128)S(1)}, f32[1,27,8,128]{3,2,1,0:T(8,128)S(1)}, u32[]{:S(2)}, u32[]{:S(2)}) %collective-permute-start.8) | collective-permute-done | bytes 110624 | tf_op jit(solution)/shard_map/ppermute | solution.py:512
  30.2 0.0 collective-permute-done.12.refs_11_
  30.2 0.0 collective-permute-done.9.refs_8_
  30.2 0.0 collective-permute-done.10.refs_9_
  30.2 0.0 collective-permute-done.11.refs_10_
  30.2 0.0 copy-done.3
  30.2 2.1 %shard_map.71 = f32[6,18,8,288]{3,2,1,0:T(8,128)} custom-call(s32[4]{0:T(128)S(1)} %copy-done.3, f32[2,27,8,128]{3,2,1,0:T(8,128)S(1)} %collective-permute-done.refs_0_, f32[1,27,8,128]{3,2,1,0:T(8,128)S(1)} %get-tuple-element.30.refs_1_, f32[1,27,8,128]{3,2,1,0:T(8,128)S(1)} %collective-permute-done.3.refs_0_.refs_2_, ...), custom_call_target="tpu_custom_call" | custom-call | flops 1 | bytes 1 | tf_op jit(solution)/shard_map/pallas_call | solution.py:519
  (3 shorter events, 0.0 us)
Async XLA Ops:
  1.1 1.3 %copy-start = (f32[8,2,18,1152]{3,1,2,0:T(2,128)S(1)}, f32[8,2,18,1152]{3,1,2,0:T(2,128)}, u32[]{:S(2)}) copy-start(f32[8,2,18,1152]{3,1,2,0:T(2,128)} %param.6) | copy-start | bytes 3981316
  2.5 11.9 %copy-start.1 = (f32[4,6,18,288]{3,0,2,1:T(4,128)S(1)}, f32[4,6,18,288]{3,0,2,1:T(4,128)}, u32[]{:S(2)}) copy-start(f32[4,6,18,288]{3,0,2,1:T(4,128)} %param.11) | copy-start | bytes 1492996
  2.5 11.9 %copy-start.2 = (s32[6,18,288]{2,1,0:T(8,128)S(1)}, s32[6,18,288]{2,1,0:T(8,128)}, u32[]{:S(2)}) copy-start(s32[6,18,288]{2,1,0:T(8,128)} %source.1) | copy-start | bytes 373252
  2.7 11.8 %collective-permute-start.1 = (f32[7,8,1152]{2,1,0:T(8,128)S(1)}, f32[7,8,1152]{2,1,0:T(8,128)S(1)}, u32[]{:S(2)}, u32[]{:S(2)}) collective-permute-start(f32[7,8,1152]{2,1,0:T(8,128)S(1)} %get-tuple-element.31), channel_id=1, source_target_pairs={{0,4},{4,0},{8,12},{12,8},{1,5},{5,1},{9,13},{13,9},{2,6},{6,2},{1... | collective-permute-start | bytes 774152 | tf_op jit(solution)/shard_map/ppermute | solution.py:470
  5.8 8.7 %collective-permute-start.2 = (f32[7,8,1152]{2,1,0:T(8,128)S(1)}, f32[7,8,1152]{2,1,0:T(8,128)S(1)}, u32[]{:S(2)}, u32[]{:S(2)}) collective-permute-start(f32[7,8,1152]{2,1,0:T(8,128)S(1)} %get-tuple-element.32), channel_id=1, source_target_pairs={{0,1},{1,0},{2,3},{3,2},{4,8},{5,9},{6,10},{7,11},{8,4},{9,5},{10,... | collective-permute-start | bytes 774152 | tf_op jit(solution)/shard_map/ppermute | solution.py:471
  5.8 13.3 %collective-permute-start.5 = (f32[7,8,1152]{2,1,0:T(8,128)S(1)}, f32[7,8,1152]{2,1,0:T(8,128)S(1)}, u32[]{:S(2)}, u32[]{:S(2)}) collective-permute-start(f32[7,8,1152]{2,1,0:T(8,128)S(1)} %get-tuple-element.39), channel_id=1, source_target_pairs={{0,4},{4,0},{8,12},{12,8},{1,5},{5,1},{9,13},{13,9},{2,6},{6,2},{1... | collective-permute-start | bytes 774152 | tf_op jit(solution)/shard_map/ppermute | solution.py:470
  9.0 10.1 %collective-permute-start.6 = (f32[7,8,1152]{2,1,0:T(8,128)S(1)}, f32[7,8,1152]{2,1,0:T(8,128)S(1)}, u32[]{:S(2)}, u32[]{:S(2)}) collective-permute-start(f32[7,8,1152]{2,1,0:T(8,128)S(1)} %get-tuple-element.40), channel_id=1, source_target_pairs={{0,1},{1,0},{2,3},{3,2},{4,8},{5,9},{6,10},{7,11},{8,4},{9,5},{10,... | collective-permute-start | bytes 774152 | tf_op jit(solution)/shard_map/ppermute | solution.py:471
  12.8 10.6 %collective-permute-start = (f32[2,27,8,128]{3,2,1,0:T(8,128)S(1)}, f32[2,27,8,128]{3,2,1,0:T(8,128)S(1)}, u32[]{:S(2)}, u32[]{:S(2)}) collective-permute-start(f32[2,27,8,128]{3,2,1,0:T(8,128)S(1)} %get-tuple-element.29), channel_id=1, source_target_pairs={{0,2},{1,3},{2,0},{3,1},{4,6},{5,7},{6,4},{7,5},{8,10},{9,11},{10,... | collective-permute-start | bytes 663560 | tf_op jit(solution)/shard_map/ppermute | solution.py:512
  17.2 6.5 %collective-permute-start.3 = (f32[1,27,8,128]{3,2,1,0:T(8,128)S(1)}, f32[1,27,8,128]{3,2,1,0:T(8,128)S(1)}, u32[]{:S(2)}, u32[]{:S(2)}) collective-permute-start(f32[1,27,8,128]{3,2,1,0:T(8,128)S(1)} %get-tuple-element.36), channel_id=1, source_target_pairs={{0,3},{1,2},{2,1},{3,0},{4,7},{5,6},{6,5},{7,4},{8,11},{9,10},{10,... | collective-permute-start | bytes 331784 | tf_op jit(solution)/shard_map/ppermute | solution.py:512
  17.6 8.2 %collective-permute-start.4 = (f32[1,27,8,128]{3,2,1,0:T(8,128)S(1)}, f32[1,27,8,128]{3,2,1,0:T(8,128)S(1)}, u32[]{:S(2)}, u32[]{:S(2)}) collective-permute-start(f32[1,27,8,128]{3,2,1,0:T(8,128)S(1)} %get-tuple-element.37), channel_id=1, source_target_pairs={{0,2},{1,3},{2,0},{3,1},{4,6},{5,7},{6,4},{7,5},{8,10},{9,11},{10,... | collective-permute-start | bytes 331784 | tf_op jit(solution)/shard_map/ppermute | solution.py:512
  19.1 11.1 %copy-start.3 = (s32[4]{0:T(128)S(1)}, s32[4]{0:T(128)}, u32[]{:S(2)}) copy-start(s32[4]{0:T(128)} %counts.1) | copy-start | bytes 52
  21.7 5.8 %collective-permute-start.7 = (f32[1,27,8,128]{3,2,1,0:T(8,128)S(1)}, f32[1,27,8,128]{3,2,1,0:T(8,128)S(1)}, u32[]{:S(2)}, u32[]{:S(2)}) collective-permute-start(f32[1,27,8,128]{3,2,1,0:T(8,128)S(1)} %get-tuple-element.41), channel_id=1, source_target_pairs={{0,3},{1,2},{2,1},{3,0},{4,7},{5,6},{6,5},{7,4},{8,11},{9,10},{10,... | collective-permute-start | bytes 331784 | tf_op jit(solution)/shard_map/ppermute | solution.py:512
  21.9 8.3 %collective-permute-start.8 = (f32[1,27,8,128]{3,2,1,0:T(8,128)S(1)}, f32[1,27,8,128]{3,2,1,0:T(8,128)S(1)}, u32[]{:S(2)}, u32[]{:S(2)}) collective-permute-start(f32[1,27,8,128]{3,2,1,0:T(8,128)S(1)} %get-tuple-element.42), channel_id=1, source_target_pairs={{0,2},{1,3},{2,0},{3,1},{4,6},{5,7},{6,4},{7,5},{8,10},{9,11},{10,... | collective-permute-start | bytes 331784 | tf_op jit(solution)/shard_map/ppermute | solution.py:512
  23.4 6.8 %collective-permute-start.12 = (f32[1,27,8,128]{3,2,1,0:T(8,128)S(1)}, f32[1,27,8,128]{3,2,1,0:T(8,128)S(1)}, u32[]{:S(2)}, u32[]{:S(2)}) collective-permute-start(f32[1,27,8,128]{3,2,1,0:T(8,128)S(1)} %slice.3), channel_id=1, source_target_pairs={{0,1},{1,0},{2,3},{3,2},{4,5},{5,4},{6,7},{7,6},{8,9},{9,8},{10,11... | collective-permute-start | bytes 331784 | tf_op jit(solution)/shard_map/ppermute | solution.py:512
  23.7 6.5 %collective-permute-start.9 = (f32[1,27,8,128]{3,2,1,0:T(8,128)S(1)}, f32[1,27,8,128]{3,2,1,0:T(8,128)S(1)}, u32[]{:S(2)}, u32[]{:S(2)}) collective-permute-start(f32[1,27,8,128]{3,2,1,0:T(8,128)S(1)} %get-tuple-element.47), channel_id=1, source_target_pairs={{0,1},{1,0},{2,3},{3,2},{4,5},{5,4},{6,7},{7,6},{8,9},{9,8},{10,11... | collective-permute-start | bytes 331784 | tf_op jit(solution)/shard_map/ppermute | solution.py:512
  25.8 4.4 %collective-permute-start.10 = (f32[1,27,8,128]{3,2,1,0:T(8,128)S(1)}, f32[1,27,8,128]{3,2,1,0:T(8,128)S(1)}, u32[]{:S(2)}, u32[]{:S(2)}) collective-permute-start(f32[1,27,8,128]{3,2,1,0:T(8,128)S(1)} %get-tuple-element.48), channel_id=1, source_target_pairs={{0,1},{1,0},{2,3},{3,2},{4,5},{5,4},{6,7},{7,6},{8,9},{9,8},{10,11... | collective-permute-start | bytes 331784 | tf_op jit(solution)/shard_map/ppermute | solution.py:512
  27.4 2.8 %collective-permute-start.11 = (f32[1,27,8,128]{3,2,1,0:T(8,128)S(1)}, f32[1,27,8,128]{3,2,1,0:T(8,128)S(1)}, u32[]{:S(2)}, u32[]{:S(2)}) collective-permute-start(f32[1,27,8,128]{3,2,1,0:T(8,128)S(1)} %get-tuple-element.49), channel_id=1, source_target_pairs={{0,1},{1,0},{2,3},{3,2},{4,5},{5,4},{6,7},{7,6},{8,9},{9,8},{10,11... | collective-permute-start | bytes 331784 | tf_op jit(solution)/shard_map/ppermute | solution.py:512

commit v17 on v15

--- a/solution.py
+++ b/solution.py
@@ -13,6 +13,7 @@
 REACH = 3
 HALO = REACH * SUBSTEPS
 BLOCK = 6
+LAG = 3
 LANES = 128
 SUB = 8
 
@@ -154,42 +155,36 @@
         e1 = from_east(here, lane)
         return [swept[level, at, :, tile(j)] - (e1[j] - here[j]) for j in each]
 
-    groups = len(work) // BLOCK
-    for g in range(groups + 2):
-        if g < groups:
-            for q in range(BLOCK):
-                interfaces(g * BLOCK + q)
-        if 1 <= g <= groups:
-            for q in range(BLOCK):
-                fluxes((g - 1) * BLOCK + q)
-        if g >= 2:
-            finish(g - 2, [update((g - 2) * BLOCK + q) for q in range(BLOCK)])
-
-
-def pack_block(block, packed, unit, units, count, lane):
-    nlon = len(block[0]) * LANES
-    width, mains, tail, per = packed_sizes(nlon, count)
-    for d in range(count):
-        j0, off = (d * width) // LANES, (d * width) % LANES
-        for q, tiles in enumerate(block):
+    for n in range(len(work) + 2 * LAG):
+        if n < len(work):
+            interfaces(n)
+        if LAG <= n < len(work) + LAG:
+            fluxes(n - LAG)
+        if n >= 2 * LAG:
+            finish(n - 2 * LAG, update(n - 2 * LAG))
+
+
+def packer(packed, rows, count, lane):
+    tails = {}
+
+    def pack(n, tiles):
+        width, mains, tail, per = packed_sizes(len(tiles) * LANES, count)
+        for d in range(count):
+            j0, off = (d * width) // LANES, (d * width) % LANES
             turned = [pltpu.roll(tiles[j0 + m], LANES - off, 1) if off else tiles[j0 + m]
                       for m in range(mains + (1 if off else 0))]
             for m in range(mains):
                 whole = jnp.where(lane < LANES - off, turned[m], turned[m + 1]) if off else turned[m]
-                packed[d, (unit * BLOCK + q) * mains + m] = whole
-        if tail:
-            totals = {}
-            for q, tiles in enumerate(block):
-                at, place = divmod(unit * BLOCK + q, per)
-                at += units * BLOCK * mains
+                packed[d, n * mains + m] = whole
+            if tail:
+                at, place = divmod(n, per)
                 shift = (place * tail - off) % LANES
                 moved = pltpu.roll(tiles[j0 + mains], shift, 1) if shift else tiles[j0 + mains]
-                if place:
-                    before = totals[at] if at in totals else packed[d, at]
-                    moved = jnp.where(lane < place * tail, before, moved)
-                totals[at] = moved
-            for at, total in totals.items():
-                packed[d, at] = total
+                tails[d] = jnp.where(lane < place * tail, tails[d], moved) if place else moved
+                if place == per - 1 or n == rows - 1:
+                    packed[d, rows * mains + at] = tails[d]
+
+    return pack
 
 
 def unpack_unit(chunk, place, unit, units, target, lead, mains, tail, per, lane):
@@ -236,10 +231,9 @@
                     target[p, level, :, tile(j)] = parts[p]
 
 
-def put_rows(target, level, at, rows):
-    for q, row in enumerate(rows):
-        for j, part in enumerate(row):
-            target[level, at + q, :, tile(j)] = part
+def put_row(target, level, at, row):
+    for j, part in enumerate(row):
+        target[level, at, :, tile(j)] = part
 
 
 def interior_kernel(count, rows, groups, state, joined, *refs):
@@ -260,18 +254,15 @@
     lat_pass(levels, nj, [(REACH, rows - REACH)], lambda level, r, lanes: state[level, r, :, lanes], coef_y, put)
     work = [(level, row, row - REACH) for level in range(levels) for row in range(REACH, rows - REACH)]
 
-    def keep_first(group, done):
-        level, _, at = work[group * BLOCK]
-        put_rows(first, level, at, done)
+    def keep_first(n, done):
+        level, _, at = work[n]
+        put_row(first, level, at, done)
 
     lon_pass(work, swept, coef_x, inter, west, flux, lane, keep_first)
     lat_pass(levels, nj, [(HALO, rows - HALO)], lambda level, r, lanes: first[level, r - REACH, :, lanes], coef_y, put)
     work_last = [(level, row, row - REACH) for level in range(levels) for row in range(HALO, rows - HALO)]
 
-    def send(group, done):
-        pack_block(done, packed, group, len(work_last) // BLOCK, count, lane)
-
-    lon_pass(work_last, swept, coef_x, inter, west, flux, lane, send)
+    lon_pass(work_last, swept, coef_x, inter, west, flux, lane, packer(packed, len(work_last), count, lane))
     hand_out(packed, outs, groups)
 
 
@@ -330,16 +321,13 @@
     def listed(ranges):
         return [(0, row, place(row, ranges)) for a, b in ranges for row in range(a, b)]
 
-    def keep_edge(group, done):
-        put_rows(edge, 0, group * BLOCK, done)
-
-    def send(group, done):
-        pack_block(done, packed, group, len(ends_last), count, lane)
+    def keep_edge(n, done):
+        put_row(edge, 0, n, done)
 
     lat_pass(1, nj, ends, cell, coef_y, put)
     lon_pass(listed(ends), swept, coef_x, inter, west, flux, lane, keep_edge)
     lat_pass(1, nj, ends_last, cell_first, coef_y, put_last)
-    lon_pass(listed(ends_last), swept, coef_x, inter, west, flux, lane, send)
+    lon_pass(listed(ends_last), swept, coef_x, inter, west, flux, lane, packer(packed, 2 * HALO, count, lane))
     hand_out(packed, outs, groups)
 
 
@@ -405,8 +393,7 @@
                         term = jnp.broadcast_to(weights[k, row, j:j + 1, lanes], (SUB, wide)) * values[level][:, :wide]
                         total = term if total is None else total + term
                     result[k, at * BLOCK + q, :, lanes] = total
-        for k in range(targets):
-            leave(result.at[k, pl.ds(at * BLOCK, BLOCK)], out.at[k, pl.ds(number * BLOCK, BLOCK)])
+            leave(result.at[:, pl.ds(at * BLOCK + q, 1)], out.at[:, pl.ds(row, 1)])
     for copy in copies:
         copy.wait()
 
@@ -527,7 +514,7 @@
             scratch_shapes=[
                 vmem(targets + 1, blocks, packed_tiles(1, mains, tail, per), SUB, LANES),
                 vmem(targets, rows, number, width),
-                pltpu.SemaphoreType.DMA((blocks * targets,)),
+                pltpu.SemaphoreType.DMA((rows,)),
             ],
             compiler_params=pltpu.CompilerParams(vmem_limit_bytes=16 << 20),
             cost_estimate=cost(1, 1),

time: 32.5 us -> 32.8 us (level)
  Pallas kernels: 11.5 us -> 12.6 us
  starting transfers between devices: 12.8 us -> 12.3 us
    pallas_call x5, Pallas kernels: 9.37 us -> 10.6 us  [call(): pl.pallas_call(kernel, out_shape=outs, in_specs=specs or [VMEM] * len(arg...]
    ppermute x9, starting transfers between devices: 6.53 us -> 5.96 us  [swapped(): return lax.ppermute(sent, 'lev', [(i, i ^ k) for i in range(count)])]
  transfers between devices with their start and end apart: 13 -> 13, of which waited for: 3 -> 3; matrix products, arithmetic and copies ran while one was open for 0% -> 0% of each run, Pallas kernels for 28% -> 32%
where the time goes in v17:
time: 32.8 us; the launch traced here: 32.7 us
  Pallas kernels  12.6 us (38%)
  starting transfers between devices  12.3 us (38%)
  waiting for transfers between devices  5.25 us (16%)
  local copies, waits for them, and re-layouts  1.34 us (4%)
  other arithmetic  1.14 us (3%)
    pallas_call x5, Pallas kernels, call(): pl.pallas_call(kernel, out_shape=outs, in_specs=specs or [VMEM] * len(arg...  10.6 us
    ppermute x2, starting transfers between devices, beside(): lax.ppermute(sent[0], 'lat', [(i, i ^ 1) for i in range(bands)])  6.31 us
    ppermute x9, starting transfers between devices, swapped(): return lax.ppermute(sent, 'lev', [(i, i ^ k) for i in range(count)])  5.96 us
    ppermute x9, waiting for transfers between devices, swapped(): return lax.ppermute(sent, 'lev', [(i, i ^ k) for i in range(count)])  5.24 us
    pallas_call x1, Pallas kernels, remap(): pl.pallas_call(functools.partial(remap_kernel, count, tuple((units for un...  1.99 us
    unnamed x8, local copies, waits for them, and re-layouts  1.33 us
    concatenate x1, other arithmetic, shards(): jnp.concatenate([jnp.transpose(wind_x, (1, 0, 2)), jnp.transpose(wind_y,...  1.14 us
  transfers between devices with their start and end apart: 13, of which 3 were waited for; matrix products, arithmetic and copies ran while one was open for 0% of the time, Pallas kernels for 32%

profile of v17, /device:TPU:0, one launch (start us, length us, event | category | flops | bytes accessed | tf_op | source)
XLA Modules:
  0.0 32.7 jit_solution(13703870574036703148)
XLA Ops:
  0.0 1.1 %pad_maximum_fusion.winds.joined = f32[36,2,1152]{2,1,0:T(2,128)S(1)} fusion(f32[18,2,1152]{2,1,0:T(2,128)} %bitcast.13, f32[18,2,1152]{2,1,0:T(2,128)} %bitcast.14), kind=kLoop, calls=%fused_computation | loop fusion | flops 82944 | bytes 663552 | tf_op jit(solution)/shard_map/concatenate | solution.py:448
  1.1 0.0 copy-start
  1.2 1.3 %copy-done = f32[8,2,18,1152]{3,1,2,0:T(2,128)S(1)} copy-done((f32[8,2,18,1152]{3,1,2,0:T(2,128)S(1)}, f32[8,2,18,1152]{3,1,2,0:T(2,128)}, u32[]{:S(2)}) %copy-start) | copy-done | bytes 1327128
  2.5 0.0 copy-start.1
  2.5 0.0 copy-start.2
  2.5 0.2 shard_map.64
  2.7 3.1 %collective-permute-start.1 = (f32[7,8,1152]{2,1,0:T(8,128)S(1)}, f32[7,8,1152]{2,1,0:T(8,128)S(1)}, u32[]{:S(2)}, u32[]{:S(2)}) collective-permute-start(f32[7,8,1152]{2,1,0:T(8,128)S(1)} %get-tuple-element.31), channel_id=1, source_target_pairs={{0,4},{4,0},{8,12},{12,8},{1,5},{5,1},{9,13},{13,9},{2,6},{6,2},{1... | collective-permute-start | bytes 774152 | tf_op jit(solution)/shard_map/ppermute | solution.py:459
  5.8 0.0 collective-permute-start.2
  5.8 4.2 %shard_map.65 = (f32[1,27,8,128]{3,2,1,0:T(8,128)S(1)}, f32[1,27,8,128]{3,2,1,0:T(8,128)S(1)}, f32[2,27,8,128]{3,2,1,0:T(8,128)S(1)}, f32[2,12,8,1152]{3,2,1,0:T...) custom-call(f32[2,18,8,1152]{3,2,1,0:T(8,128)S(1)} %get-tuple-elemen, ...), custom_call_target="tpu_custom_call" | custom-call | flops 1 | bytes 1 | tf_op jit(solution)/shard_map/pallas_call | solution.py:419
  10.0 3.2 %collective-permute-start.5 = (f32[7,8,1152]{2,1,0:T(8,128)S(1)}, f32[7,8,1152]{2,1,0:T(8,128)S(1)}, u32[]{:S(2)}, u32[]{:S(2)}) collective-permute-start(f32[7,8,1152]{2,1,0:T(8,128)S(1)} %get-tuple-element.39), channel_id=1, source_target_pairs={{0,4},{4,0},{8,12},{12,8},{1,5},{5,1},{9,13},{13,9},{2,6},{6,2},{1... | collective-permute-start | bytes 774152 | tf_op jit(solution)/shard_map/ppermute | solution.py:459
  13.2 0.0 collective-permute-start.6
  13.2 1.5 %collective-permute-start = (f32[2,27,8,128]{3,2,1,0:T(8,128)S(1)}, f32[2,27,8,128]{3,2,1,0:T(8,128)S(1)}, u32[]{:S(2)}, u32[]{:S(2)}) collective-permute-start(f32[2,27,8,128]{3,2,1,0:T(8,128)S(1)} %get-tuple-element.29), channel_id=1, source_target_pairs={{0,2},{1,3},{2,0},{3,1},{4,6},{5,7},{6,4},{7,5},{8,10},{9,11},{10,... | collective-permute-start | bytes 663560 | tf_op jit(solution)/shard_map/ppermute | solution.py:502
  14.7 0.0 copy-done.1
  14.7 0.0 copy-done.2
  14.8 0.2 shard_map.66.refs_0_.refs_12_
  14.9 0.0 collective-permute-done.1.first_round
  15.0 0.0 collective-permute-done.2.second_round
  15.0 3.0 %shard_map.67 = (f32[1,27,8,128]{3,2,1,0:T(8,128)S(1)}, f32[1,27,8,128]{3,2,1,0:T(8,128)S(1)}, f32[1,27,8,128]{3,2,1,0:T(8,128)S(1)}, f32[1,27,8,128]{3,2,1,0:T(8,128)S(1)}) custom-call(f32[2,18,8,1152]{3,2,1,0:T(8,128)S(1)} %get-tuple-element.28.state, f32[7,8,1152]{2,1,0:T(8,128)S(1)} %collective-permute-done.1.first_round, ...), custom_call_target="tpu_custom_call" | custom-call | flops 19906560 | bytes 2654208 | tf_op jit(solution)/shard_map/pallas_call | solution.py:419
  17.9 0.4 %collective-permute-start.3 = (f32[1,27,8,128]{3,2,1,0:T(8,128)S(1)}, f32[1,27,8,128]{3,2,1,0:T(8,128)S(1)}, u32[]{:S(2)}, u32[]{:S(2)}) collective-permute-start(f32[1,27,8,128]{3,2,1,0:T(8,128)S(1)} %get-tuple-element.36), channel_id=1, source_target_pairs={{0,3},{1,2},{2,1},{3,0},{4,7},{5,6},{6,5},{7,4},{8,11},{9,10},{10,... | collective-permute-start | bytes 331784 | tf_op jit(solution)/shard_map/ppermute | solution.py:502
  18.4 1.5 %collective-permute-start.4 = (f32[1,27,8,128]{3,2,1,0:T(8,128)S(1)}, f32[1,27,8,128]{3,2,1,0:T(8,128)S(1)}, u32[]{:S(2)}, u32[]{:S(2)}) collective-permute-start(f32[1,27,8,128]{3,2,1,0:T(8,128)S(1)} %get-tuple-element.37), channel_id=1, source_target_pairs={{0,2},{1,3},{2,0},{3,1},{4,6},{5,7},{6,4},{7,5},{8,10},{9,11},{10,... | collective-permute-start | bytes 331784 | tf_op jit(solution)/shard_map/ppermute | solution.py:502
  19.9 0.0 collective-permute-done.5.first_round
  19.9 0.0 collective-permute-done.6.second_round
  19.9 0.0 copy-start.3
  19.9 3.0 %shard_map.68 = (f32[1,27,8,128]{3,2,1,0:T(8,128)S(1)}, f32[1,27,8,128]{3,2,1,0:T(8,128)S(1)}, f32[1,27,8,128]{3,2,1,0:T(8,128)S(1)}, f32[1,27,8,128]{3,2,1,0:T(8,128)S(1)}) custom-call(f32[2,18,8,1152]{3,2,1,0:T(8,128)S(1)} %get-tuple-element.28.state, f32[7,8,1152]{2,1,0:T(8,128)S(1)} %collective-permute-done.5.first_round, ...), custom_call_target="tpu_custom_call" | custom-call | flops 19906560 | bytes 2654208 | tf_op jit(solution)/shard_map/pallas_call | solution.py:419
  22.9 0.2 collective-permute-start.7
  23.1 0.0 collective-permute-done.refs_0_
  23.1 0.6 %collective-permute-start.12 = (f32[1,27,8,128]{3,2,1,0:T(8,128)S(1)}, f32[1,27,8,128]{3,2,1,0:T(8,128)S(1)}, u32[]{:S(2)}, u32[]{:S(2)}) collective-permute-start(f32[1,27,8,128]{3,2,1,0:T(8,128)S(1)} %slice.3), channel_id=1, source_target_pairs={{0,1},{1,0},{2,3},{3,2},{4,5},{5,4},{6,7},{7,6},{8,9},{9,8},{10,11... | collective-permute-start | bytes 331784 | tf_op jit(solution)/shard_map/ppermute | solution.py:502
  23.7 0.1 collective-permute-start.9
  23.7 0.0 collective-permute-done.3.refs_0_.refs_2_
  23.7 1.5 %collective-permute-start.8 = (f32[1,27,8,128]{3,2,1,0:T(8,128)S(1)}, f32[1,27,8,128]{3,2,1,0:T(8,128)S(1)}, u32[]{:S(2)}, u32[]{:S(2)}) collective-permute-start(f32[1,27,8,128]{3,2,1,0:T(8,128)S(1)} %get-tuple-element.42), channel_id=1, source_target_pairs={{0,2},{1,3},{2,0},{3,1},{4,6},{5,7},{6,4},{7,5},{8,10},{9,11},{10,... | collective-permute-start | bytes 331784 | tf_op jit(solution)/shard_map/ppermute | solution.py:502
  25.2 0.6 %collective-permute-done.4.refs_1_.refs_3_ = f32[1,27,8,128]{3,2,1,0:T(8,128)S(1)} collective-permute-done((f32[1,27,8,128]{3,2,1,0:T(8,128)S(1)}, f32[1,27,8,128]{3,2,1,0:T(8,128)S(1)}, u32[]{:S(2)}, u32[]{:S(2)}) %collective-permute-start.4) | collective-permute-done | bytes 110624 | tf_op jit(solution)/shard_map/ppermute | solution.py:502
  25.8 0.0 collective-permute-start.10
  25.8 2.3 %collective-permute-done.7.refs_0_.refs_5_ = f32[1,27,8,128]{3,2,1,0:T(8,128)S(1)} collective-permute-done((f32[1,27,8,128]{3,2,1,0:T(8,128)S(1)}, f32[1,27,8,128]{3,2,1,0:T(8,128)S(1)}, u32[]{:S(2)}, u32[]{:S(2)}) %collective-permute-start.7) | collective-permute-done | bytes 110624 | tf_op jit(solution)/shard_map/ppermute | solution.py:502
  28.1 0.2 collective-permute-start.11
  28.3 2.4 %collective-permute-done.8.refs_1_.refs_6_ = f32[1,27,8,128]{3,2,1,0:T(8,128)S(1)} collective-permute-done((f32[1,27,8,128]{3,2,1,0:T(8,128)S(1)}, f32[1,27,8,128]{3,2,1,0:T(8,128)S(1)}, u32[]{:S(2)}, u32[]{:S(2)}) %collective-permute-start.8) | collective-permute-done | bytes 110624 | tf_op jit(solution)/shard_map/ppermute | solution.py:502
  30.6 0.0 collective-permute-done.12.refs_11_
  30.7 0.0 collective-permute-done.9.refs_8_
  30.7 0.0 collective-permute-done.10.refs_9_
  30.7 0.0 collective-permute-done.11.refs_10_
  30.7 0.0 copy-done.3
  30.7 2.0 %shard_map.71 = f32[6,18,8,288]{3,2,1,0:T(8,128)} custom-call(s32[4]{0:T(128)S(1)} %copy-done.3, f32[2,27,8,128]{3,2,1,0:T(8,128)S(1)} %collective-permute-done.refs_0_, f32[1,27,8,128]{3,2,1,0:T(8,128)S(1)} %get-tuple-element.30.refs_1_, f32[1,27,8,128]{3,2,1,0:T(8,128)S(1)} %collective-permute-done.3.refs_0_.refs_2_, ...), custom_call_target="tpu_custom_call" | custom-call | flops 1 | bytes 1 | tf_op jit(solution)/shard_map/pallas_call | solution.py:509
  (3 shorter events, 0.0 us)
Async XLA Ops:
  1.1 1.3 %copy-start = (f32[8,2,18,1152]{3,1,2,0:T(2,128)S(1)}, f32[8,2,18,1152]{3,1,2,0:T(2,128)}, u32[]{:S(2)}) copy-start(f32[8,2,18,1152]{3,1,2,0:T(2,128)} %param.6) | copy-start | bytes 3981316
  2.5 12.3 %copy-start.1 = (f32[4,6,18,288]{3,0,2,1:T(4,128)S(1)}, f32[4,6,18,288]{3,0,2,1:T(4,128)}, u32[]{:S(2)}) copy-start(f32[4,6,18,288]{3,0,2,1:T(4,128)} %param.11) | copy-start | bytes 1492996
  2.5 12.3 %copy-start.2 = (s32[6,18,288]{2,1,0:T(8,128)S(1)}, s32[6,18,288]{2,1,0:T(8,128)}, u32[]{:S(2)}) copy-start(s32[6,18,288]{2,1,0:T(8,128)} %source.1) | copy-start | bytes 373252
  2.7 12.2 %collective-permute-start.1 = (f32[7,8,1152]{2,1,0:T(8,128)S(1)}, f32[7,8,1152]{2,1,0:T(8,128)S(1)}, u32[]{:S(2)}, u32[]{:S(2)}) collective-permute-start(f32[7,8,1152]{2,1,0:T(8,128)S(1)} %get-tuple-element.31), channel_id=1, source_target_pairs={{0,4},{4,0},{8,12},{12,8},{1,5},{5,1},{9,13},{13,9},{2,6},{6,2},{1... | collective-permute-start | bytes 774152 | tf_op jit(solution)/shard_map/ppermute | solution.py:459
  5.8 9.2 %collective-permute-start.2 = (f32[7,8,1152]{2,1,0:T(8,128)S(1)}, f32[7,8,1152]{2,1,0:T(8,128)S(1)}, u32[]{:S(2)}, u32[]{:S(2)}) collective-permute-start(f32[7,8,1152]{2,1,0:T(8,128)S(1)} %get-tuple-element.32), channel_id=1, source_target_pairs={{0,1},{1,0},{2,3},{3,2},{4,8},{5,9},{6,10},{7,11},{8,4},{9,5},{10,... | collective-permute-start | bytes 774152 | tf_op jit(solution)/shard_map/ppermute | solution.py:460
  10.0 9.8 %collective-permute-start.5 = (f32[7,8,1152]{2,1,0:T(8,128)S(1)}, f32[7,8,1152]{2,1,0:T(8,128)S(1)}, u32[]{:S(2)}, u32[]{:S(2)}) collective-permute-start(f32[7,8,1152]{2,1,0:T(8,128)S(1)} %get-tuple-element.39), channel_id=1, source_target_pairs={{0,4},{4,0},{8,12},{12,8},{1,5},{5,1},{9,13},{13,9},{2,6},{6,2},{1... | collective-permute-start | bytes 774152 | tf_op jit(solution)/shard_map/ppermute | solution.py:459
  13.2 6.6 %collective-permute-start.6 = (f32[7,8,1152]{2,1,0:T(8,128)S(1)}, f32[7,8,1152]{2,1,0:T(8,128)S(1)}, u32[]{:S(2)}, u32[]{:S(2)}) collective-permute-start(f32[7,8,1152]{2,1,0:T(8,128)S(1)} %get-tuple-element.40), channel_id=1, source_target_pairs={{0,1},{1,0},{2,3},{3,2},{4,8},{5,9},{6,10},{7,11},{8,4},{9,5},{10,... | collective-permute-start | bytes 774152 | tf_op jit(solution)/shard_map/ppermute | solution.py:460
  13.2 9.8 %collective-permute-start = (f32[2,27,8,128]{3,2,1,0:T(8,128)S(1)}, f32[2,27,8,128]{3,2,1,0:T(8,128)S(1)}, u32[]{:S(2)}, u32[]{:S(2)}) collective-permute-start(f32[2,27,8,128]{3,2,1,0:T(8,128)S(1)} %get-tuple-element.29), channel_id=1, source_target_pairs={{0,2},{1,3},{2,0},{3,1},{4,6},{5,7},{6,4},{7,5},{8,10},{9,11},{10,... | collective-permute-start | bytes 663560 | tf_op jit(solution)/shard_map/ppermute | solution.py:502
  17.9 5.8 %collective-permute-start.3 = (f32[1,27,8,128]{3,2,1,0:T(8,128)S(1)}, f32[1,27,8,128]{3,2,1,0:T(8,128)S(1)}, u32[]{:S(2)}, u32[]{:S(2)}) collective-permute-start(f32[1,27,8,128]{3,2,1,0:T(8,128)S(1)} %get-tuple-element.36), channel_id=1, source_target_pairs={{0,3},{1,2},{2,1},{3,0},{4,7},{5,6},{6,5},{7,4},{8,11},{9,10},{10,... | collective-permute-start | bytes 331784 | tf_op jit(solution)/shard_map/ppermute | solution.py:502
  18.4 7.5 %collective-permute-start.4 = (f32[1,27,8,128]{3,2,1,0:T(8,128)S(1)}, f32[1,27,8,128]{3,2,1,0:T(8,128)S(1)}, u32[]{:S(2)}, u32[]{:S(2)}) collective-permute-start(f32[1,27,8,128]{3,2,1,0:T(8,128)S(1)} %get-tuple-element.37), channel_id=1, source_target_pairs={{0,2},{1,3},{2,0},{3,1},{4,6},{5,7},{6,4},{7,5},{8,10},{9,11},{10,... | collective-permute-start | bytes 331784 | tf_op jit(solution)/shard_map/ppermute | solution.py:502
  19.9 10.8 %copy-start.3 = (s32[4]{0:T(128)S(1)}, s32[4]{0:T(128)}, u32[]{:S(2)}) copy-start(s32[4]{0:T(128)} %counts.1) | copy-start | bytes 52
  22.9 5.2 %collective-permute-start.7 = (f32[1,27,8,128]{3,2,1,0:T(8,128)S(1)}, f32[1,27,8,128]{3,2,1,0:T(8,128)S(1)}, u32[]{:S(2)}, u32[]{:S(2)}) collective-permute-start(f32[1,27,8,128]{3,2,1,0:T(8,128)S(1)} %get-tuple-element.41), channel_id=1, source_target_pairs={{0,3},{1,2},{2,1},{3,0},{4,7},{5,6},{6,5},{7,4},{8,11},{9,10},{10,... | collective-permute-start | bytes 331784 | tf_op jit(solution)/shard_map/ppermute | solution.py:502
  23.1 7.6 %collective-permute-start.12 = (f32[1,27,8,128]{3,2,1,0:T(8,128)S(1)}, f32[1,27,8,128]{3,2,1,0:T(8,128)S(1)}, u32[]{:S(2)}, u32[]{:S(2)}) collective-permute-start(f32[1,27,8,128]{3,2,1,0:T(8,128)S(1)} %slice.3), channel_id=1, source_target_pairs={{0,1},{1,0},{2,3},{3,2},{4,5},{5,4},{6,7},{7,6},{8,9},{9,8},{10,11... | collective-permute-start | bytes 331784 | tf_op jit(solution)/shard_map/ppermute | solution.py:502
  23.7 7.0 %collective-permute-start.9 = (f32[1,27,8,128]{3,2,1,0:T(8,128)S(1)}, f32[1,27,8,128]{3,2,1,0:T(8,128)S(1)}, u32[]{:S(2)}, u32[]{:S(2)}) collective-permute-start(f32[1,27,8,128]{3,2,1,0:T(8,128)S(1)} %get-tuple-element.47), channel_id=1, source_target_pairs={{0,1},{1,0},{2,3},{3,2},{4,5},{5,4},{6,7},{7,6},{8,9},{9,8},{10,11... | collective-permute-start | bytes 331784 | tf_op jit(solution)/shard_map/ppermute | solution.py:502
  23.7 6.9 %collective-permute-start.8 = (f32[1,27,8,128]{3,2,1,0:T(8,128)S(1)}, f32[1,27,8,128]{3,2,1,0:T(8,128)S(1)}, u32[]{:S(2)}, u32[]{:S(2)}) collective-permute-start(f32[1,27,8,128]{3,2,1,0:T(8,128)S(1)} %get-tuple-element.42), channel_id=1, source_target_pairs={{0,2},{1,3},{2,0},{3,1},{4,6},{5,7},{6,4},{7,5},{8,10},{9,11},{10,... | collective-permute-start | bytes 331784 | tf_op jit(solution)/shard_map/ppermute | solution.py:502
  25.8 4.8 %collective-permute-start.10 = (f32[1,27,8,128]{3,2,1,0:T(8,128)S(1)}, f32[1,27,8,128]{3,2,1,0:T(8,128)S(1)}, u32[]{:S(2)}, u32[]{:S(2)}) collective-permute-start(f32[1,27,8,128]{3,2,1,0:T(8,128)S(1)} %get-tuple-element.48), channel_id=1, source_target_pairs={{0,1},{1,0},{2,3},{3,2},{4,5},{5,4},{6,7},{7,6},{8,9},{9,8},{10,11... | collective-permute-start | bytes 331784 | tf_op jit(solution)/shard_map/ppermute | solution.py:502
  28.1 2.6 %collective-permute-start.11 = (f32[1,27,8,128]{3,2,1,0:T(8,128)S(1)}, f32[1,27,8,128]{3,2,1,0:T(8,128)S(1)}, u32[]{:S(2)}, u32[]{:S(2)}) collective-permute-start(f32[1,27,8,128]{3,2,1,0:T(8,128)S(1)} %get-tuple-element.49), channel_id=1, source_target_pairs={{0,1},{1,0},{2,3},{3,2},{4,5},{5,4},{6,7},{7,6},{8,9},{9,8},{10,11... | collective-permute-start | bytes 331784 | tf_op jit(solution)/shard_map/ppermute | solution.py:502

commit v18 on v15

--- a/solution.py
+++ b/solution.py
@@ -154,16 +154,12 @@
         e1 = from_east(here, lane)
         return [swept[level, at, :, tile(j)] - (e1[j] - here[j]) for j in each]
 
-    groups = len(work) // BLOCK
-    for g in range(groups + 2):
-        if g < groups:
-            for q in range(BLOCK):
-                interfaces(g * BLOCK + q)
-        if 1 <= g <= groups:
-            for q in range(BLOCK):
-                fluxes((g - 1) * BLOCK + q)
-        if g >= 2:
-            finish(g - 2, [update((g - 2) * BLOCK + q) for q in range(BLOCK)])
+    for n in range(len(work)):
+        interfaces(n)
+    for n in range(len(work)):
+        fluxes(n)
+    for g in range(len(work) // BLOCK):
+        finish(g, [update(g * BLOCK + q) for q in range(BLOCK)])
 
 
 def pack_block(block, packed, unit, units, count, lane):
@@ -405,8 +401,7 @@
                         term = jnp.broadcast_to(weights[k, row, j:j + 1, lanes], (SUB, wide)) * values[level][:, :wide]
                         total = term if total is None else total + term
                     result[k, at * BLOCK + q, :, lanes] = total
-        for k in range(targets):
-            leave(result.at[k, pl.ds(at * BLOCK, BLOCK)], out.at[k, pl.ds(number * BLOCK, BLOCK)])
+            leave(result.at[:, pl.ds(at * BLOCK + q, 1)], out.at[:, pl.ds(row, 1)])
     for copy in copies:
         copy.wait()
 
@@ -527,7 +522,7 @@
             scratch_shapes=[
                 vmem(targets + 1, blocks, packed_tiles(1, mains, tail, per), SUB, LANES),
                 vmem(targets, rows, number, width),
-                pltpu.SemaphoreType.DMA((blocks * targets,)),
+                pltpu.SemaphoreType.DMA((rows,)),
             ],
             compiler_params=pltpu.CompilerParams(vmem_limit_bytes=16 << 20),
             cost_estimate=cost(1, 1),

time: 32.5 us -> 32.4 us (level)
  no operation moved by 1% of the time
where the time goes in v18:
time: 32.4 us; the launch traced here: 32.2 us
  starting transfers between devices  12.8 us (40%)
  Pallas kernels  11.4 us (35%)
  waiting for transfers between devices  5.43 us (17%)
  local copies, waits for them, and re-layouts  1.34 us (4%)
  other arithmetic  1.14 us (4%)
    pallas_call x5, Pallas kernels, call(): pl.pallas_call(kernel, out_shape=outs, in_specs=specs or [VMEM] * len(arg...  9.39 us
    ppermute x9, starting transfers between devices, swapped(): return lax.ppermute(sent, 'lev', [(i, i ^ k) for i in range(count)])  6.53 us
    ppermute x2, starting transfers between devices, beside(): lax.ppermute(sent[0], 'lat', [(i, i ^ 1) for i in range(bands)])  6.31 us
    ppermute x9, waiting for transfers between devices, swapped(): return lax.ppermute(sent, 'lev', [(i, i ^ k) for i in range(count)])  5.42 us
    pallas_call x1, Pallas kernels, remap(): pl.pallas_call(functools.partial(remap_kernel, count, tuple((units for un...  1.99 us
    unnamed x8, local copies, waits for them, and re-layouts  1.33 us
    concatenate x1, other arithmetic, shards(): jnp.concatenate([jnp.transpose(wind_x, (1, 0, 2)), jnp.transpose(wind_y,...  1.14 us
  transfers between devices with their start and end apart: 13, of which 3 were waited for; matrix products, arithmetic and copies ran while one was open for 0% of the time, Pallas kernels for 28%

profile of v18, /device:TPU:0, one launch (start us, length us, event | category | flops | bytes accessed | tf_op | source)
XLA Modules:
  0.0 32.2 jit_solution(7414277220640112373)
XLA Ops:
  0.0 1.1 %pad_maximum_fusion.winds.joined = f32[36,2,1152]{2,1,0:T(2,128)S(1)} fusion(f32[18,2,1152]{2,1,0:T(2,128)} %bitcast.13, f32[18,2,1152]{2,1,0:T(2,128)} %bitcast.14), kind=kLoop, calls=%fused_computation | loop fusion | flops 82944 | bytes 663552 | tf_op jit(solution)/shard_map/concatenate | solution.py:456
  1.1 0.0 copy-start
  1.2 1.3 %copy-done = f32[8,2,18,1152]{3,1,2,0:T(2,128)S(1)} copy-done((f32[8,2,18,1152]{3,1,2,0:T(2,128)S(1)}, f32[8,2,18,1152]{3,1,2,0:T(2,128)}, u32[]{:S(2)}) %copy-start) | copy-done | bytes 1327128
  2.5 0.0 copy-start.1
  2.5 0.0 copy-start.2
  2.5 0.2 shard_map.64
  2.7 3.1 %collective-permute-start.1 = (f32[7,8,1152]{2,1,0:T(8,128)S(1)}, f32[7,8,1152]{2,1,0:T(8,128)S(1)}, u32[]{:S(2)}, u32[]{:S(2)}) collective-permute-start(f32[7,8,1152]{2,1,0:T(8,128)S(1)} %get-tuple-element.31), channel_id=1, source_target_pairs={{0,4},{4,0},{8,12},{12,8},{1,5},{5,1},{9,13},{13,9},{2,6},{6,2},{1... | collective-permute-start | bytes 774152 | tf_op jit(solution)/shard_map/ppermute | solution.py:467
  5.8 0.0 collective-permute-start.2
  5.8 3.9 %shard_map.65 = (f32[1,27,8,128]{3,2,1,0:T(8,128)S(1)}, f32[1,27,8,128]{3,2,1,0:T(8,128)S(1)}, f32[2,27,8,128]{3,2,1,0:T(8,128)S(1)}, f32[2,12,8,1152]{3,2,1,0:T...) custom-call(f32[2,18,8,1152]{3,2,1,0:T(8,128)S(1)} %get-tuple-elemen, ...), custom_call_target="tpu_custom_call" | custom-call | flops 1 | bytes 1 | tf_op jit(solution)/shard_map/pallas_call | solution.py:427
  9.7 3.2 %collective-permute-start.5 = (f32[7,8,1152]{2,1,0:T(8,128)S(1)}, f32[7,8,1152]{2,1,0:T(8,128)S(1)}, u32[]{:S(2)}, u32[]{:S(2)}) collective-permute-start(f32[7,8,1152]{2,1,0:T(8,128)S(1)} %get-tuple-element.39), channel_id=1, source_target_pairs={{0,4},{4,0},{8,12},{12,8},{1,5},{5,1},{9,13},{13,9},{2,6},{6,2},{1... | collective-permute-start | bytes 774152 | tf_op jit(solution)/shard_map/ppermute | solution.py:467
  12.9 0.0 collective-permute-start.6
  12.9 1.5 %collective-permute-start = (f32[2,27,8,128]{3,2,1,0:T(8,128)S(1)}, f32[2,27,8,128]{3,2,1,0:T(8,128)S(1)}, u32[]{:S(2)}, u32[]{:S(2)}) collective-permute-start(f32[2,27,8,128]{3,2,1,0:T(8,128)S(1)} %get-tuple-element.29), channel_id=1, source_target_pairs={{0,2},{1,3},{2,0},{3,1},{4,6},{5,7},{6,4},{7,5},{8,10},{9,11},{10,... | collective-permute-start | bytes 663560 | tf_op jit(solution)/shard_map/ppermute | solution.py:510
  14.4 0.0 copy-done.1
  14.4 0.0 copy-done.2
  14.4 0.2 shard_map.66.refs_0_.refs_12_
  14.6 0.0 collective-permute-done.1.first_round
  14.6 0.0 collective-permute-done.2.second_round
  14.6 2.6 %shard_map.67 = (f32[1,27,8,128]{3,2,1,0:T(8,128)S(1)}, f32[1,27,8,128]{3,2,1,0:T(8,128)S(1)}, f32[1,27,8,128]{3,2,1,0:T(8,128)S(1)}, f32[1,27,8,128]{3,2,1,0:T(8,128)S(1)}) custom-call(f32[2,18,8,1152]{3,2,1,0:T(8,128)S(1)} %get-tuple-element.28.state, f32[7,8,1152]{2,1,0:T(8,128)S(1)} %collective-permute-done.1.first_round, ...), custom_call_target="tpu_custom_call" | custom-call | flops 19906560 | bytes 2654208 | tf_op jit(solution)/shard_map/pallas_call | solution.py:427
  17.2 0.4 %collective-permute-start.3 = (f32[1,27,8,128]{3,2,1,0:T(8,128)S(1)}, f32[1,27,8,128]{3,2,1,0:T(8,128)S(1)}, u32[]{:S(2)}, u32[]{:S(2)}) collective-permute-start(f32[1,27,8,128]{3,2,1,0:T(8,128)S(1)} %get-tuple-element.36), channel_id=1, source_target_pairs={{0,3},{1,2},{2,1},{3,0},{4,7},{5,6},{6,5},{7,4},{8,11},{9,10},{10,... | collective-permute-start | bytes 331784 | tf_op jit(solution)/shard_map/ppermute | solution.py:510
  17.6 1.5 %collective-permute-start.4 = (f32[1,27,8,128]{3,2,1,0:T(8,128)S(1)}, f32[1,27,8,128]{3,2,1,0:T(8,128)S(1)}, u32[]{:S(2)}, u32[]{:S(2)}) collective-permute-start(f32[1,27,8,128]{3,2,1,0:T(8,128)S(1)} %get-tuple-element.37), channel_id=1, source_target_pairs={{0,2},{1,3},{2,0},{3,1},{4,6},{5,7},{6,4},{7,5},{8,10},{9,11},{10,... | collective-permute-start | bytes 331784 | tf_op jit(solution)/shard_map/ppermute | solution.py:510
  19.1 0.0 collective-permute-done.5.first_round
  19.1 0.0 collective-permute-done.6.second_round
  19.1 0.0 copy-start.3
  19.1 2.6 %shard_map.68 = (f32[1,27,8,128]{3,2,1,0:T(8,128)S(1)}, f32[1,27,8,128]{3,2,1,0:T(8,128)S(1)}, f32[1,27,8,128]{3,2,1,0:T(8,128)S(1)}, f32[1,27,8,128]{3,2,1,0:T(8,128)S(1)}) custom-call(f32[2,18,8,1152]{3,2,1,0:T(8,128)S(1)} %get-tuple-element.28.state, f32[7,8,1152]{2,1,0:T(8,128)S(1)} %collective-permute-done.5.first_round, ...), custom_call_target="tpu_custom_call" | custom-call | flops 19906560 | bytes 2654208 | tf_op jit(solution)/shard_map/pallas_call | solution.py:427
  21.7 0.2 collective-permute-start.7
  21.9 0.0 collective-permute-done.refs_0_
  21.9 1.0 %collective-permute-start.12 = (f32[1,27,8,128]{3,2,1,0:T(8,128)S(1)}, f32[1,27,8,128]{3,2,1,0:T(8,128)S(1)}, u32[]{:S(2)}, u32[]{:S(2)}) collective-permute-start(f32[1,27,8,128]{3,2,1,0:T(8,128)S(1)} %slice.3), channel_id=1, source_target_pairs={{0,1},{1,0},{2,3},{3,2},{4,5},{5,4},{6,7},{7,6},{8,9},{9,8},{10,11... | collective-permute-start | bytes 331784 | tf_op jit(solution)/shard_map/ppermute | solution.py:510
  22.9 0.1 collective-permute-start.9
  22.9 0.0 collective-permute-done.3.refs_0_.refs_2_
  22.9 1.2 %collective-permute-start.8 = (f32[1,27,8,128]{3,2,1,0:T(8,128)S(1)}, f32[1,27,8,128]{3,2,1,0:T(8,128)S(1)}, u32[]{:S(2)}, u32[]{:S(2)}) collective-permute-start(f32[1,27,8,128]{3,2,1,0:T(8,128)S(1)} %get-tuple-element.42), channel_id=1, source_target_pairs={{0,2},{1,3},{2,0},{3,1},{4,6},{5,7},{6,4},{7,5},{8,10},{9,11},{10,... | collective-permute-start | bytes 331784 | tf_op jit(solution)/shard_map/ppermute | solution.py:510
  24.2 1.7 %collective-permute-done.4.refs_1_.refs_3_ = f32[1,27,8,128]{3,2,1,0:T(8,128)S(1)} collective-permute-done((f32[1,27,8,128]{3,2,1,0:T(8,128)S(1)}, f32[1,27,8,128]{3,2,1,0:T(8,128)S(1)}, u32[]{:S(2)}, u32[]{:S(2)}) %collective-permute-start.4) | collective-permute-done | bytes 110624 | tf_op jit(solution)/shard_map/ppermute | solution.py:510
  25.8 0.0 collective-permute-start.10
  25.9 1.6 %collective-permute-done.7.refs_0_.refs_5_ = f32[1,27,8,128]{3,2,1,0:T(8,128)S(1)} collective-permute-done((f32[1,27,8,128]{3,2,1,0:T(8,128)S(1)}, f32[1,27,8,128]{3,2,1,0:T(8,128)S(1)}, u32[]{:S(2)}, u32[]{:S(2)}) %collective-permute-start.7) | collective-permute-done | bytes 110624 | tf_op jit(solution)/shard_map/ppermute | solution.py:510
  27.4 0.6 %collective-permute-start.11 = (f32[1,27,8,128]{3,2,1,0:T(8,128)S(1)}, f32[1,27,8,128]{3,2,1,0:T(8,128)S(1)}, u32[]{:S(2)}, u32[]{:S(2)}) collective-permute-start(f32[1,27,8,128]{3,2,1,0:T(8,128)S(1)} %get-tuple-element.49), channel_id=1, source_target_pairs={{0,1},{1,0},{2,3},{3,2},{4,5},{5,4},{6,7},{7,6},{8,9},{9,8},{10,11... | collective-permute-start | bytes 331784 | tf_op jit(solution)/shard_map/ppermute | solution.py:510
  28.0 2.2 %collective-permute-done.8.refs_1_.refs_6_ = f32[1,27,8,128]{3,2,1,0:T(8,128)S(1)} collective-permute-done((f32[1,27,8,128]{3,2,1,0:T(8,128)S(1)}, f32[1,27,8,128]{3,2,1,0:T(8,128)S(1)}, u32[]{:S(2)}, u32[]{:S(2)}) %collective-permute-start.8) | collective-permute-done | bytes 110624 | tf_op jit(solution)/shard_map/ppermute | solution.py:510
  30.2 0.0 collective-permute-done.12.refs_11_
  30.2 0.0 collective-permute-done.9.refs_8_
  30.2 0.0 collective-permute-done.10.refs_9_
  30.2 0.0 collective-permute-done.11.refs_10_
  30.2 0.0 copy-done.3
  30.2 2.0 %shard_map.71 = f32[6,18,8,288]{3,2,1,0:T(8,128)} custom-call(s32[4]{0:T(128)S(1)} %copy-done.3, f32[2,27,8,128]{3,2,1,0:T(8,128)S(1)} %collective-permute-done.refs_0_, f32[1,27,8,128]{3,2,1,0:T(8,128)S(1)} %get-tuple-element.30.refs_1_, f32[1,27,8,128]{3,2,1,0:T(8,128)S(1)} %collective-permute-done.3.refs_0_.refs_2_, ...), custom_call_target="tpu_custom_call" | custom-call | flops 1 | bytes 1 | tf_op jit(solution)/shard_map/pallas_call | solution.py:517
  (3 shorter events, 0.0 us)
Async XLA Ops:
  1.1 1.3 %copy-start = (f32[8,2,18,1152]{3,1,2,0:T(2,128)S(1)}, f32[8,2,18,1152]{3,1,2,0:T(2,128)}, u32[]{:S(2)}) copy-start(f32[8,2,18,1152]{3,1,2,0:T(2,128)} %param.6) | copy-start | bytes 3981316
  2.5 11.9 %copy-start.1 = (f32[4,6,18,288]{3,0,2,1:T(4,128)S(1)}, f32[4,6,18,288]{3,0,2,1:T(4,128)}, u32[]{:S(2)}) copy-start(f32[4,6,18,288]{3,0,2,1:T(4,128)} %param.11) | copy-start | bytes 1492996
  2.5 11.9 %copy-start.2 = (s32[6,18,288]{2,1,0:T(8,128)S(1)}, s32[6,18,288]{2,1,0:T(8,128)}, u32[]{:S(2)}) copy-start(s32[6,18,288]{2,1,0:T(8,128)} %source.1) | copy-start | bytes 373252
  2.7 11.9 %collective-permute-start.1 = (f32[7,8,1152]{2,1,0:T(8,128)S(1)}, f32[7,8,1152]{2,1,0:T(8,128)S(1)}, u32[]{:S(2)}, u32[]{:S(2)}) collective-permute-start(f32[7,8,1152]{2,1,0:T(8,128)S(1)} %get-tuple-element.31), channel_id=1, source_target_pairs={{0,4},{4,0},{8,12},{12,8},{1,5},{5,1},{9,13},{13,9},{2,6},{6,2},{1... | collective-permute-start | bytes 774152 | tf_op jit(solution)/shard_map/ppermute | solution.py:467
  5.8 8.8 %collective-permute-start.2 = (f32[7,8,1152]{2,1,0:T(8,128)S(1)}, f32[7,8,1152]{2,1,0:T(8,128)S(1)}, u32[]{:S(2)}, u32[]{:S(2)}) collective-permute-start(f32[7,8,1152]{2,1,0:T(8,128)S(1)} %get-tuple-element.32), channel_id=1, source_target_pairs={{0,1},{1,0},{2,3},{3,2},{4,8},{5,9},{6,10},{7,11},{8,4},{9,5},{10,... | collective-permute-start | bytes 774152 | tf_op jit(solution)/shard_map/ppermute | solution.py:468
  9.7 9.4 %collective-permute-start.5 = (f32[7,8,1152]{2,1,0:T(8,128)S(1)}, f32[7,8,1152]{2,1,0:T(8,128)S(1)}, u32[]{:S(2)}, u32[]{:S(2)}) collective-permute-start(f32[7,8,1152]{2,1,0:T(8,128)S(1)} %get-tuple-element.39), channel_id=1, source_target_pairs={{0,4},{4,0},{8,12},{12,8},{1,5},{5,1},{9,13},{13,9},{2,6},{6,2},{1... | collective-permute-start | bytes 774152 | tf_op jit(solution)/shard_map/ppermute | solution.py:467
  12.9 6.2 %collective-permute-start.6 = (f32[7,8,1152]{2,1,0:T(8,128)S(1)}, f32[7,8,1152]{2,1,0:T(8,128)S(1)}, u32[]{:S(2)}, u32[]{:S(2)}) collective-permute-start(f32[7,8,1152]{2,1,0:T(8,128)S(1)} %get-tuple-element.40), channel_id=1, source_target_pairs={{0,1},{1,0},{2,3},{3,2},{4,8},{5,9},{6,10},{7,11},{8,4},{9,5},{10,... | collective-permute-start | bytes 774152 | tf_op jit(solution)/shard_map/ppermute | solution.py:468
  12.9 9.0 %collective-permute-start = (f32[2,27,8,128]{3,2,1,0:T(8,128)S(1)}, f32[2,27,8,128]{3,2,1,0:T(8,128)S(1)}, u32[]{:S(2)}, u32[]{:S(2)}) collective-permute-start(f32[2,27,8,128]{3,2,1,0:T(8,128)S(1)} %get-tuple-element.29), channel_id=1, source_target_pairs={{0,2},{1,3},{2,0},{3,1},{4,6},{5,7},{6,4},{7,5},{8,10},{9,11},{10,... | collective-permute-start | bytes 663560 | tf_op jit(solution)/shard_map/ppermute | solution.py:510
  17.2 5.8 %collective-permute-start.3 = (f32[1,27,8,128]{3,2,1,0:T(8,128)S(1)}, f32[1,27,8,128]{3,2,1,0:T(8,128)S(1)}, u32[]{:S(2)}, u32[]{:S(2)}) collective-permute-start(f32[1,27,8,128]{3,2,1,0:T(8,128)S(1)} %get-tuple-element.36), channel_id=1, source_target_pairs={{0,3},{1,2},{2,1},{3,0},{4,7},{5,6},{6,5},{7,4},{8,11},{9,10},{10,... | collective-permute-start | bytes 331784 | tf_op jit(solution)/shard_map/ppermute | solution.py:510
  17.6 8.2 %collective-permute-start.4 = (f32[1,27,8,128]{3,2,1,0:T(8,128)S(1)}, f32[1,27,8,128]{3,2,1,0:T(8,128)S(1)}, u32[]{:S(2)}, u32[]{:S(2)}) collective-permute-start(f32[1,27,8,128]{3,2,1,0:T(8,128)S(1)} %get-tuple-element.37), channel_id=1, source_target_pairs={{0,2},{1,3},{2,0},{3,1},{4,6},{5,7},{6,4},{7,5},{8,10},{9,11},{10,... | collective-permute-start | bytes 331784 | tf_op jit(solution)/shard_map/ppermute | solution.py:510
  19.1 11.1 %copy-start.3 = (s32[4]{0:T(128)S(1)}, s32[4]{0:T(128)}, u32[]{:S(2)}) copy-start(s32[4]{0:T(128)} %counts.1) | copy-start | bytes 52
  21.7 5.8 %collective-permute-start.7 = (f32[1,27,8,128]{3,2,1,0:T(8,128)S(1)}, f32[1,27,8,128]{3,2,1,0:T(8,128)S(1)}, u32[]{:S(2)}, u32[]{:S(2)}) collective-permute-start(f32[1,27,8,128]{3,2,1,0:T(8,128)S(1)} %get-tuple-element.41), channel_id=1, source_target_pairs={{0,3},{1,2},{2,1},{3,0},{4,7},{5,6},{6,5},{7,4},{8,11},{9,10},{10,... | collective-permute-start | bytes 331784 | tf_op jit(solution)/shard_map/ppermute | solution.py:510
  21.9 8.3 %collective-permute-start.12 = (f32[1,27,8,128]{3,2,1,0:T(8,128)S(1)}, f32[1,27,8,128]{3,2,1,0:T(8,128)S(1)}, u32[]{:S(2)}, u32[]{:S(2)}) collective-permute-start(f32[1,27,8,128]{3,2,1,0:T(8,128)S(1)} %slice.3), channel_id=1, source_target_pairs={{0,1},{1,0},{2,3},{3,2},{4,5},{5,4},{6,7},{7,6},{8,9},{9,8},{10,11... | collective-permute-start | bytes 331784 | tf_op jit(solution)/shard_map/ppermute | solution.py:510
  22.9 7.3 %collective-permute-start.9 = (f32[1,27,8,128]{3,2,1,0:T(8,128)S(1)}, f32[1,27,8,128]{3,2,1,0:T(8,128)S(1)}, u32[]{:S(2)}, u32[]{:S(2)}) collective-permute-start(f32[1,27,8,128]{3,2,1,0:T(8,128)S(1)} %get-tuple-element.47), channel_id=1, source_target_pairs={{0,1},{1,0},{2,3},{3,2},{4,5},{5,4},{6,7},{7,6},{8,9},{9,8},{10,11... | collective-permute-start | bytes 331784 | tf_op jit(solution)/shard_map/ppermute | solution.py:510
  22.9 7.3 %collective-permute-start.8 = (f32[1,27,8,128]{3,2,1,0:T(8,128)S(1)}, f32[1,27,8,128]{3,2,1,0:T(8,128)S(1)}, u32[]{:S(2)}, u32[]{:S(2)}) collective-permute-start(f32[1,27,8,128]{3,2,1,0:T(8,128)S(1)} %get-tuple-element.42), channel_id=1, source_target_pairs={{0,2},{1,3},{2,0},{3,1},{4,6},{5,7},{6,4},{7,5},{8,10},{9,11},{10,... | collective-permute-start | bytes 331784 | tf_op jit(solution)/shard_map/ppermute | solution.py:510
  25.8 4.4 %collective-permute-start.10 = (f32[1,27,8,128]{3,2,1,0:T(8,128)S(1)}, f32[1,27,8,128]{3,2,1,0:T(8,128)S(1)}, u32[]{:S(2)}, u32[]{:S(2)}) collective-permute-start(f32[1,27,8,128]{3,2,1,0:T(8,128)S(1)} %get-tuple-element.48), channel_id=1, source_target_pairs={{0,1},{1,0},{2,3},{3,2},{4,5},{5,4},{6,7},{7,6},{8,9},{9,8},{10,11... | collective-permute-start | bytes 331784 | tf_op jit(solution)/shard_map/ppermute | solution.py:510
  27.4 2.8 %collective-permute-start.11 = (f32[1,27,8,128]{3,2,1,0:T(8,128)S(1)}, f32[1,27,8,128]{3,2,1,0:T(8,128)S(1)}, u32[]{:S(2)}, u32[]{:S(2)}) collective-permute-start(f32[1,27,8,128]{3,2,1,0:T(8,128)S(1)} %get-tuple-element.49), channel_id=1, source_target_pairs={{0,1},{1,0},{2,3},{3,2},{4,5},{5,4},{6,7},{7,6},{8,9},{9,8},{10,11... | collective-permute-start | bytes 331784 | tf_op jit(solution)/shard_map/ppermute | solution.py:510

commit v19 on v18

--- a/solution.py
+++ b/solution.py
@@ -92,14 +92,13 @@
 def lat_pass(levels, nj, ranges, cell, coef, store):
     group = 3 if nj % 3 == 0 else 1
 
-    def body(i, _):
-        level = i // (nj // group)
-        results = []
-        for u in range(group):
-            lanes = pl.ds(pl.multiple_of(((i % (nj // group)) * group + u) * LANES, LANES), LANES)
-            results += [(level, row, lanes, value) for row, value in one(level, lanes)]
-        for result in results:
-            store(*result)
+    def body(level, _):
+        for start in range(0, nj, group):
+            results = []
+            for j in range(start, start + group):
+                results += [(level, row, tile(j), value) for row, value in one(level, tile(j))]
+            for result in results:
+                store(*result)
         return 0
 
     def one(level, lanes):
@@ -118,7 +117,7 @@
                     results.append((f - 1, a[f - 1] - (flux[f] - flux[f - 1])))
         return results
 
-    lax.fori_loop(0, levels * nj // group, body, 0)
+    lax.fori_loop(0, levels, body, 0)
 
 
 def tile(j):

time: 32.4 us -> 32.2 us (level)
  Pallas kernels: 11.4 us -> 10.7 us
  starting transfers between devices: 12.8 us -> 13.3 us
    pallas_call x5, Pallas kernels: 9.39 us -> 8.68 us  [call(): pl.pallas_call(kernel, out_shape=outs, in_specs=specs or [VMEM] * len(arg...]
    ppermute x9, starting transfers between devices: 6.53 us -> 7.02 us  [swapped(): return lax.ppermute(sent, 'lev', [(i, i ^ k) for i in range(count)])]
  transfers between devices with their start and end apart: 13 -> 13, of which waited for: 3 -> 3; matrix products, arithmetic and copies ran while one was open for 0% -> 0% of each run, Pallas kernels for 28% -> 26%
where the time goes in v19:
time: 32.2 us; the launch traced here: 32.1 us
  starting transfers between devices  13.3 us (41%)
  Pallas kernels  10.7 us (33%)
  waiting for transfers between devices  5.46 us (17%)
  local copies, waits for them, and re-layouts  1.34 us (4%)
  other arithmetic  1.14 us (4%)
    pallas_call x5, Pallas kernels, call(): pl.pallas_call(kernel, out_shape=outs, in_specs=specs or [VMEM] * len(arg...  8.68 us
    ppermute x9, starting transfers between devices, swapped(): return lax.ppermute(sent, 'lev', [(i, i ^ k) for i in range(count)])  7.02 us
    ppermute x2, starting transfers between devices, beside(): lax.ppermute(sent[0], 'lat', [(i, i ^ 1) for i in range(bands)])  6.31 us
    ppermute x9, waiting for transfers between devices, swapped(): return lax.ppermute(sent, 'lev', [(i, i ^ k) for i in range(count)])  5.45 us
    pallas_call x1, Pallas kernels, remap(): pl.pallas_call(functools.partial(remap_kernel, count, tuple((units for un...  1.99 us
    unnamed x8, local copies, waits for them, and re-layouts  1.33 us
    concatenate x1, other arithmetic, shards(): jnp.concatenate([jnp.transpose(wind_x, (1, 0, 2)), jnp.transpose(wind_y,...  1.14 us
  transfers between devices with their start and end apart: 13, of which 3 were waited for; matrix products, arithmetic and copies ran while one was open for 0% of the time, Pallas kernels for 26%

profile of v19, /device:TPU:0, one launch (start us, length us, event | category | flops | bytes accessed | tf_op | source)
XLA Modules:
  0.0 32.1 jit_solution(16832744693815327280)
XLA Ops:
  0.0 1.1 %pad_maximum_fusion.winds.joined = f32[36,2,1152]{2,1,0:T(2,128)S(1)} fusion(f32[18,2,1152]{2,1,0:T(2,128)} %bitcast.13, f32[18,2,1152]{2,1,0:T(2,128)} %bitcast.14), kind=kLoop, calls=%fused_computation | loop fusion | flops 82944 | bytes 663552 | tf_op jit(solution)/shard_map/concatenate | solution.py:455
  1.1 0.0 copy-start
  1.2 1.3 %copy-done = f32[8,2,18,1152]{3,1,2,0:T(2,128)S(1)} copy-done((f32[8,2,18,1152]{3,1,2,0:T(2,128)S(1)}, f32[8,2,18,1152]{3,1,2,0:T(2,128)}, u32[]{:S(2)}) %copy-start) | copy-done | bytes 1327128
  2.5 0.0 copy-start.1
  2.5 0.0 copy-start.2
  2.5 0.2 shard_map.64
  2.7 3.1 %collective-permute-start.1 = (f32[7,8,1152]{2,1,0:T(8,128)S(1)}, f32[7,8,1152]{2,1,0:T(8,128)S(1)}, u32[]{:S(2)}, u32[]{:S(2)}) collective-permute-start(f32[7,8,1152]{2,1,0:T(8,128)S(1)} %get-tuple-element.31), channel_id=1, source_target_pairs={{0,4},{4,0},{8,12},{12,8},{1,5},{5,1},{9,13},{13,9},{2,6},{6,2},{1... | collective-permute-start | bytes 774152 | tf_op jit(solution)/shard_map/ppermute | solution.py:466
  5.8 0.0 collective-permute-start.2
  5.8 3.7 %shard_map.65 = (f32[1,27,8,128]{3,2,1,0:T(8,128)S(1)}, f32[1,27,8,128]{3,2,1,0:T(8,128)S(1)}, f32[2,27,8,128]{3,2,1,0:T(8,128)S(1)}, f32[2,12,8,1152]{3,2,1,0:T...) custom-call(f32[2,18,8,1152]{3,2,1,0:T(8,128)S(1)} %get-tuple-elemen, ...), custom_call_target="tpu_custom_call" | custom-call | flops 1 | bytes 1 | tf_op jit(solution)/shard_map/pallas_call | solution.py:426
  9.5 3.2 %collective-permute-start.5 = (f32[7,8,1152]{2,1,0:T(8,128)S(1)}, f32[7,8,1152]{2,1,0:T(8,128)S(1)}, u32[]{:S(2)}, u32[]{:S(2)}) collective-permute-start(f32[7,8,1152]{2,1,0:T(8,128)S(1)} %get-tuple-element.39), channel_id=1, source_target_pairs={{0,4},{4,0},{8,12},{12,8},{1,5},{5,1},{9,13},{13,9},{2,6},{6,2},{1... | collective-permute-start | bytes 774152 | tf_op jit(solution)/shard_map/ppermute | solution.py:466
  12.7 0.0 collective-permute-start.6
  12.7 1.5 %collective-permute-start = (f32[2,27,8,128]{3,2,1,0:T(8,128)S(1)}, f32[2,27,8,128]{3,2,1,0:T(8,128)S(1)}, u32[]{:S(2)}, u32[]{:S(2)}) collective-permute-start(f32[2,27,8,128]{3,2,1,0:T(8,128)S(1)} %get-tuple-element.29), channel_id=1, source_target_pairs={{0,2},{1,3},{2,0},{3,1},{4,6},{5,7},{6,4},{7,5},{8,10},{9,11},{10,... | collective-permute-start | bytes 663560 | tf_op jit(solution)/shard_map/ppermute | solution.py:509
  14.2 0.0 copy-done.1
  14.2 0.0 copy-done.2
  14.2 0.2 shard_map.66.refs_0_.refs_12_
  14.4 0.0 collective-permute-done.1.first_round
  14.4 0.0 collective-permute-done.2.second_round
  14.4 2.3 %shard_map.67 = (f32[1,27,8,128]{3,2,1,0:T(8,128)S(1)}, f32[1,27,8,128]{3,2,1,0:T(8,128)S(1)}, f32[1,27,8,128]{3,2,1,0:T(8,128)S(1)}, f32[1,27,8,128]{3,2,1,0:T(8,128)S(1)}) custom-call(f32[2,18,8,1152]{3,2,1,0:T(8,128)S(1)} %get-tuple-element.28.state, f32[7,8,1152]{2,1,0:T(8,128)S(1)} %collective-permute-done.1.first_round, ...), custom_call_target="tpu_custom_call" | custom-call | flops 19906560 | bytes 2654208 | tf_op jit(solution)/shard_map/pallas_call | solution.py:426
  16.7 0.4 %collective-permute-start.3 = (f32[1,27,8,128]{3,2,1,0:T(8,128)S(1)}, f32[1,27,8,128]{3,2,1,0:T(8,128)S(1)}, u32[]{:S(2)}, u32[]{:S(2)}) collective-permute-start(f32[1,27,8,128]{3,2,1,0:T(8,128)S(1)} %get-tuple-element.36), channel_id=1, source_target_pairs={{0,3},{1,2},{2,1},{3,0},{4,7},{5,6},{6,5},{7,4},{8,11},{9,10},{10,... | collective-permute-start | bytes 331784 | tf_op jit(solution)/shard_map/ppermute | solution.py:509
  17.2 1.5 %collective-permute-start.4 = (f32[1,27,8,128]{3,2,1,0:T(8,128)S(1)}, f32[1,27,8,128]{3,2,1,0:T(8,128)S(1)}, u32[]{:S(2)}, u32[]{:S(2)}) collective-permute-start(f32[1,27,8,128]{3,2,1,0:T(8,128)S(1)} %get-tuple-element.37), channel_id=1, source_target_pairs={{0,2},{1,3},{2,0},{3,1},{4,6},{5,7},{6,4},{7,5},{8,10},{9,11},{10,... | collective-permute-start | bytes 331784 | tf_op jit(solution)/shard_map/ppermute | solution.py:509
  18.7 0.0 collective-permute-done.5.first_round
  18.7 0.0 collective-permute-done.6.second_round
  18.7 0.0 copy-start.3
  18.7 2.3 %shard_map.68 = (f32[1,27,8,128]{3,2,1,0:T(8,128)S(1)}, f32[1,27,8,128]{3,2,1,0:T(8,128)S(1)}, f32[1,27,8,128]{3,2,1,0:T(8,128)S(1)}, f32[1,27,8,128]{3,2,1,0:T(8,128)S(1)}) custom-call(f32[2,18,8,1152]{3,2,1,0:T(8,128)S(1)} %get-tuple-element.28.state, f32[7,8,1152]{2,1,0:T(8,128)S(1)} %collective-permute-done.5.first_round, ...), custom_call_target="tpu_custom_call" | custom-call | flops 19906560 | bytes 2654208 | tf_op jit(solution)/shard_map/pallas_call | solution.py:426
  21.0 0.2 collective-permute-start.7
  21.2 0.0 collective-permute-done.refs_0_
  21.2 1.2 %collective-permute-start.12 = (f32[1,27,8,128]{3,2,1,0:T(8,128)S(1)}, f32[1,27,8,128]{3,2,1,0:T(8,128)S(1)}, u32[]{:S(2)}, u32[]{:S(2)}) collective-permute-start(f32[1,27,8,128]{3,2,1,0:T(8,128)S(1)} %slice.3), channel_id=1, source_target_pairs={{0,1},{1,0},{2,3},{3,2},{4,5},{5,4},{6,7},{7,6},{8,9},{9,8},{10,11... | collective-permute-start | bytes 331784 | tf_op jit(solution)/shard_map/ppermute | solution.py:509
  22.4 0.1 collective-permute-start.9
  22.5 0.0 collective-permute-done.3.refs_0_.refs_2_
  22.5 1.5 %collective-permute-start.8 = (f32[1,27,8,128]{3,2,1,0:T(8,128)S(1)}, f32[1,27,8,128]{3,2,1,0:T(8,128)S(1)}, u32[]{:S(2)}, u32[]{:S(2)}) collective-permute-start(f32[1,27,8,128]{3,2,1,0:T(8,128)S(1)} %get-tuple-element.42), channel_id=1, source_target_pairs={{0,2},{1,3},{2,0},{3,1},{4,6},{5,7},{6,4},{7,5},{8,10},{9,11},{10,... | collective-permute-start | bytes 331784 | tf_op jit(solution)/shard_map/ppermute | solution.py:509
  24.0 1.7 %collective-permute-done.4.refs_1_.refs_3_ = f32[1,27,8,128]{3,2,1,0:T(8,128)S(1)} collective-permute-done((f32[1,27,8,128]{3,2,1,0:T(8,128)S(1)}, f32[1,27,8,128]{3,2,1,0:T(8,128)S(1)}, u32[]{:S(2)}, u32[]{:S(2)}) %collective-permute-start.4) | collective-permute-done | bytes 110624 | tf_op jit(solution)/shard_map/ppermute | solution.py:509
  25.7 0.0 collective-permute-start.10
  25.7 1.6 %collective-permute-done.7.refs_0_.refs_5_ = f32[1,27,8,128]{3,2,1,0:T(8,128)S(1)} collective-permute-done((f32[1,27,8,128]{3,2,1,0:T(8,128)S(1)}, f32[1,27,8,128]{3,2,1,0:T(8,128)S(1)}, u32[]{:S(2)}, u32[]{:S(2)}) %collective-permute-start.7) | collective-permute-done | bytes 110624 | tf_op jit(solution)/shard_map/ppermute | solution.py:509
  27.3 0.6 %collective-permute-start.11 = (f32[1,27,8,128]{3,2,1,0:T(8,128)S(1)}, f32[1,27,8,128]{3,2,1,0:T(8,128)S(1)}, u32[]{:S(2)}, u32[]{:S(2)}) collective-permute-start(f32[1,27,8,128]{3,2,1,0:T(8,128)S(1)} %get-tuple-element.49), channel_id=1, source_target_pairs={{0,1},{1,0},{2,3},{3,2},{4,5},{5,4},{6,7},{7,6},{8,9},{9,8},{10,11... | collective-permute-start | bytes 331784 | tf_op jit(solution)/shard_map/ppermute | solution.py:509
  27.9 2.2 %collective-permute-done.8.refs_1_.refs_6_ = f32[1,27,8,128]{3,2,1,0:T(8,128)S(1)} collective-permute-done((f32[1,27,8,128]{3,2,1,0:T(8,128)S(1)}, f32[1,27,8,128]{3,2,1,0:T(8,128)S(1)}, u32[]{:S(2)}, u32[]{:S(2)}) %collective-permute-start.8) | collective-permute-done | bytes 110624 | tf_op jit(solution)/shard_map/ppermute | solution.py:509
  30.0 0.0 collective-permute-done.12.refs_11_
  30.0 0.0 collective-permute-done.9.refs_8_
  30.0 0.0 collective-permute-done.10.refs_9_
  30.0 0.0 collective-permute-done.11.refs_10_
  30.1 0.0 copy-done.3
  30.1 2.0 %shard_map.71 = f32[6,18,8,288]{3,2,1,0:T(8,128)} custom-call(s32[4]{0:T(128)S(1)} %copy-done.3, f32[2,27,8,128]{3,2,1,0:T(8,128)S(1)} %collective-permute-done.refs_0_, f32[1,27,8,128]{3,2,1,0:T(8,128)S(1)} %get-tuple-element.30.refs_1_, f32[1,27,8,128]{3,2,1,0:T(8,128)S(1)} %collective-permute-done.3.refs_0_.refs_2_, ...), custom_call_target="tpu_custom_call" | custom-call | flops 1 | bytes 1 | tf_op jit(solution)/shard_map/pallas_call | solution.py:516
  (3 shorter events, 0.0 us)
Async XLA Ops:
  1.1 1.3 %copy-start = (f32[8,2,18,1152]{3,1,2,0:T(2,128)S(1)}, f32[8,2,18,1152]{3,1,2,0:T(2,128)}, u32[]{:S(2)}) copy-start(f32[8,2,18,1152]{3,1,2,0:T(2,128)} %param.6) | copy-start | bytes 3981316
  2.5 11.7 %copy-start.1 = (f32[4,6,18,288]{3,0,2,1:T(4,128)S(1)}, f32[4,6,18,288]{3,0,2,1:T(4,128)}, u32[]{:S(2)}) copy-start(f32[4,6,18,288]{3,0,2,1:T(4,128)} %param.11) | copy-start | bytes 1492996
  2.5 11.7 %copy-start.2 = (s32[6,18,288]{2,1,0:T(8,128)S(1)}, s32[6,18,288]{2,1,0:T(8,128)}, u32[]{:S(2)}) copy-start(s32[6,18,288]{2,1,0:T(8,128)} %source.1) | copy-start | bytes 373252
  2.7 11.7 %collective-permute-start.1 = (f32[7,8,1152]{2,1,0:T(8,128)S(1)}, f32[7,8,1152]{2,1,0:T(8,128)S(1)}, u32[]{:S(2)}, u32[]{:S(2)}) collective-permute-start(f32[7,8,1152]{2,1,0:T(8,128)S(1)} %get-tuple-element.31), channel_id=1, source_target_pairs={{0,4},{4,0},{8,12},{12,8},{1,5},{5,1},{9,13},{13,9},{2,6},{6,2},{1... | collective-permute-start | bytes 774152 | tf_op jit(solution)/shard_map/ppermute | solution.py:466
  5.8 8.6 %collective-permute-start.2 = (f32[7,8,1152]{2,1,0:T(8,128)S(1)}, f32[7,8,1152]{2,1,0:T(8,128)S(1)}, u32[]{:S(2)}, u32[]{:S(2)}) collective-permute-start(f32[7,8,1152]{2,1,0:T(8,128)S(1)} %get-tuple-element.32), channel_id=1, source_target_pairs={{0,1},{1,0},{2,3},{3,2},{4,8},{5,9},{6,10},{7,11},{8,4},{9,5},{10,... | collective-permute-start | bytes 774152 | tf_op jit(solution)/shard_map/ppermute | solution.py:467
  9.5 9.2 %collective-permute-start.5 = (f32[7,8,1152]{2,1,0:T(8,128)S(1)}, f32[7,8,1152]{2,1,0:T(8,128)S(1)}, u32[]{:S(2)}, u32[]{:S(2)}) collective-permute-start(f32[7,8,1152]{2,1,0:T(8,128)S(1)} %get-tuple-element.39), channel_id=1, source_target_pairs={{0,4},{4,0},{8,12},{12,8},{1,5},{5,1},{9,13},{13,9},{2,6},{6,2},{1... | collective-permute-start | bytes 774152 | tf_op jit(solution)/shard_map/ppermute | solution.py:466
  12.7 6.0 %collective-permute-start.6 = (f32[7,8,1152]{2,1,0:T(8,128)S(1)}, f32[7,8,1152]{2,1,0:T(8,128)S(1)}, u32[]{:S(2)}, u32[]{:S(2)}) collective-permute-start(f32[7,8,1152]{2,1,0:T(8,128)S(1)} %get-tuple-element.40), channel_id=1, source_target_pairs={{0,1},{1,0},{2,3},{3,2},{4,8},{5,9},{6,10},{7,11},{8,4},{9,5},{10,... | collective-permute-start | bytes 774152 | tf_op jit(solution)/shard_map/ppermute | solution.py:467
  12.7 8.5 %collective-permute-start = (f32[2,27,8,128]{3,2,1,0:T(8,128)S(1)}, f32[2,27,8,128]{3,2,1,0:T(8,128)S(1)}, u32[]{:S(2)}, u32[]{:S(2)}) collective-permute-start(f32[2,27,8,128]{3,2,1,0:T(8,128)S(1)} %get-tuple-element.29), channel_id=1, source_target_pairs={{0,2},{1,3},{2,0},{3,1},{4,6},{5,7},{6,4},{7,5},{8,10},{9,11},{10,... | collective-permute-start | bytes 663560 | tf_op jit(solution)/shard_map/ppermute | solution.py:509
  16.7 5.8 %collective-permute-start.3 = (f32[1,27,8,128]{3,2,1,0:T(8,128)S(1)}, f32[1,27,8,128]{3,2,1,0:T(8,128)S(1)}, u32[]{:S(2)}, u32[]{:S(2)}) collective-permute-start(f32[1,27,8,128]{3,2,1,0:T(8,128)S(1)} %get-tuple-element.36), channel_id=1, source_target_pairs={{0,3},{1,2},{2,1},{3,0},{4,7},{5,6},{6,5},{7,4},{8,11},{9,10},{10,... | collective-permute-start | bytes 331784 | tf_op jit(solution)/shard_map/ppermute | solution.py:509
  17.2 8.5 %collective-permute-start.4 = (f32[1,27,8,128]{3,2,1,0:T(8,128)S(1)}, f32[1,27,8,128]{3,2,1,0:T(8,128)S(1)}, u32[]{:S(2)}, u32[]{:S(2)}) collective-permute-start(f32[1,27,8,128]{3,2,1,0:T(8,128)S(1)} %get-tuple-element.37), channel_id=1, source_target_pairs={{0,2},{1,3},{2,0},{3,1},{4,6},{5,7},{6,4},{7,5},{8,10},{9,11},{10,... | collective-permute-start | bytes 331784 | tf_op jit(solution)/shard_map/ppermute | solution.py:509
  18.7 11.4 %copy-start.3 = (s32[4]{0:T(128)S(1)}, s32[4]{0:T(128)}, u32[]{:S(2)}) copy-start(s32[4]{0:T(128)} %counts.1) | copy-start | bytes 52
  21.0 6.3 %collective-permute-start.7 = (f32[1,27,8,128]{3,2,1,0:T(8,128)S(1)}, f32[1,27,8,128]{3,2,1,0:T(8,128)S(1)}, u32[]{:S(2)}, u32[]{:S(2)}) collective-permute-start(f32[1,27,8,128]{3,2,1,0:T(8,128)S(1)} %get-tuple-element.41), channel_id=1, source_target_pairs={{0,3},{1,2},{2,1},{3,0},{4,7},{5,6},{6,5},{7,4},{8,11},{9,10},{10,... | collective-permute-start | bytes 331784 | tf_op jit(solution)/shard_map/ppermute | solution.py:509
  21.2 8.8 %collective-permute-start.12 = (f32[1,27,8,128]{3,2,1,0:T(8,128)S(1)}, f32[1,27,8,128]{3,2,1,0:T(8,128)S(1)}, u32[]{:S(2)}, u32[]{:S(2)}) collective-permute-start(f32[1,27,8,128]{3,2,1,0:T(8,128)S(1)} %slice.3), channel_id=1, source_target_pairs={{0,1},{1,0},{2,3},{3,2},{4,5},{5,4},{6,7},{7,6},{8,9},{9,8},{10,11... | collective-permute-start | bytes 331784 | tf_op jit(solution)/shard_map/ppermute | solution.py:509
  22.4 7.6 %collective-permute-start.9 = (f32[1,27,8,128]{3,2,1,0:T(8,128)S(1)}, f32[1,27,8,128]{3,2,1,0:T(8,128)S(1)}, u32[]{:S(2)}, u32[]{:S(2)}) collective-permute-start(f32[1,27,8,128]{3,2,1,0:T(8,128)S(1)} %get-tuple-element.47), channel_id=1, source_target_pairs={{0,1},{1,0},{2,3},{3,2},{4,5},{5,4},{6,7},{7,6},{8,9},{9,8},{10,11... | collective-permute-start | bytes 331784 | tf_op jit(solution)/shard_map/ppermute | solution.py:509
  22.5 7.5 %collective-permute-start.8 = (f32[1,27,8,128]{3,2,1,0:T(8,128)S(1)}, f32[1,27,8,128]{3,2,1,0:T(8,128)S(1)}, u32[]{:S(2)}, u32[]{:S(2)}) collective-permute-start(f32[1,27,8,128]{3,2,1,0:T(8,128)S(1)} %get-tuple-element.42), channel_id=1, source_target_pairs={{0,2},{1,3},{2,0},{3,1},{4,6},{5,7},{6,4},{7,5},{8,10},{9,11},{10,... | collective-permute-start | bytes 331784 | tf_op jit(solution)/shard_map/ppermute | solution.py:509
  25.7 4.4 %collective-permute-start.10 = (f32[1,27,8,128]{3,2,1,0:T(8,128)S(1)}, f32[1,27,8,128]{3,2,1,0:T(8,128)S(1)}, u32[]{:S(2)}, u32[]{:S(2)}) collective-permute-start(f32[1,27,8,128]{3,2,1,0:T(8,128)S(1)} %get-tuple-element.48), channel_id=1, source_target_pairs={{0,1},{1,0},{2,3},{3,2},{4,5},{5,4},{6,7},{7,6},{8,9},{9,8},{10,11... | collective-permute-start | bytes 331784 | tf_op jit(solution)/shard_map/ppermute | solution.py:509
  27.3 2.8 %collective-permute-start.11 = (f32[1,27,8,128]{3,2,1,0:T(8,128)S(1)}, f32[1,27,8,128]{3,2,1,0:T(8,128)S(1)}, u32[]{:S(2)}, u32[]{:S(2)}) collective-permute-start(f32[1,27,8,128]{3,2,1,0:T(8,128)S(1)} %get-tuple-element.49), channel_id=1, source_target_pairs={{0,1},{1,0},{2,3},{3,2},{4,5},{5,4},{6,7},{7,6},{8,9},{9,8},{10,11... | collective-permute-start | bytes 331784 | tf_op jit(solution)/shard_map/ppermute | solution.py:509

commit v20 on v19

--- a/solution.py
+++ b/solution.py
@@ -72,7 +72,7 @@
             target[HALO, REACH + q:REACH + q + 1, :] = scaled(winds[rows + row_y + q, slot:slot + 1, :])
 
 
-def prep_kernel(rows, tracers, winds, state, first_round, second_round):
+def prep_kernel(rows, tracers, winds, state, *halos):
     levels, nlon = state.shape[0], state.shape[3]
     nj = nlon // LANES
     row_stride = nj * levels
@@ -86,7 +86,8 @@
         return 0
 
     lax.fori_loop(0, rows, body, 0)
-    fill_halos(rows, 0, state, winds, first_round, second_round)
+    for slot in range(levels):
+        fill_halos(rows, slot, state, winds, *halos[2 * slot:2 * slot + 2])
 
 
 def lat_pass(levels, nj, ranges, cell, coef, store):
@@ -238,13 +239,10 @@
 
 
 def interior_kernel(count, rows, groups, state, joined, *refs):
-    outs, (first, cx, cy), refs = refs[:len(groups)], refs[len(groups):len(groups) + 3], refs[len(groups) + 3:]
-    halos, (packed, winds, swept, inter, west, flux) = refs[:-6], refs[-6:]
+    outs, (first, cx, cy, packed, winds, swept, inter, west, flux) = refs[:len(groups)], refs[len(groups):]
     levels, nlon = state.shape[0], state.shape[3]
     nj = nlon // LANES
     lane = lane_ids()
-    for slot in range(1, levels):
-        fill_halos(rows, slot, state, joined, *halos[2 * slot - 2:2 * slot])
     own_coefficients(rows, joined, winds, cx, cy)
     coef_x = lambda i, level, r, lanes: cx[i, level, r:r + 1, lanes]
     coef_y = lambda i, level, f, lanes: cy[i, level, f:f + 1, lanes]
@@ -456,7 +454,7 @@
     halo = f32(HALO + 1, number, nlon)
     state, *sent = call(
         functools.partial(prep_kernel, rows),
-        [f32(depth, rows, number, nlon), halo, halo], (raw, joined),
+        [f32(depth, rows, number, nlon)] + [halo] * (2 * depth), (raw, joined),
         cost=cost(1, 1))
     second = {i: ((i - 1) ^ 1) + 1 for i in range(1, bands - 1)}
     second_pairs = [(i * count + d, second[i] * count + d if i in second else i * count + (d ^ 1))
@@ -466,7 +464,7 @@
         return [lax.ppermute(sent[0], "lat", [(i, i ^ 1) for i in range(bands)]),
                 lax.ppermute(sent[1], ("lat", "lev"), second_pairs)]
 
-    rounds = [beside(sent)]
+    rounds = [beside(sent[2 * slot:2 * slot + 2]) for slot in range(depth)]
     taps = call(
         weights_kernel, f32(targets, rows, SUB, width),
         (jnp.transpose(remap_weight, (1, 2, 0, 3)), source_level),
@@ -488,11 +486,10 @@
     result = call(
         functools.partial(interior_kernel, count, rows, groups),
         [f32(*box(len(group), inner_units)) for group in groups]
-        + [f32(depth, rows - 2 * REACH, number, nlon), coef, coef] + [halo] * (2 * depth - 2),
+        + [f32(depth, rows - 2 * REACH, number, nlon), coef, coef],
         (state, joined), scratch=[vmem(*box(count, inner_units)), vmem(2, depth, held, nlon), swept, stage, stage, stage],
         cost=cost(1, 1))
-    middle, (first, cx, cy), sent = result[:len(groups)], result[len(groups):len(groups) + 3], result[len(groups) + 3:]
-    rounds += [beside(sent[2 * i:2 * i + 2]) for i in range(depth - 1)]
+    middle, (first, cx, cy) = result[:len(groups)], result[len(groups):]
     swept = vmem(1, 2 * HALO, number, nlon)
     stage = vmem(2 * HALO, number, nlon)
 

time: 32.2 us -> 32.2 us (level)
  waiting for transfers between devices: 5.46 us -> 6.18 us
  starting transfers between devices: 13.3 us -> 12.6 us
    ppermute x9, waiting for transfers between devices: 5.45 us -> 6.17 us  [swapped(): return lax.ppermute(sent, 'lev', [(i, i ^ k) for i in range(count)])]
    ppermute x9, starting transfers between devices: 7.02 us -> 6.35 us  [swapped(): return lax.ppermute(sent, 'lev', [(i, i ^ k) for i in range(count)])]
where the time goes in v20:
time: 32.2 us; the launch traced here: 32.1 us
  starting transfers between devices  12.6 us (39%)
  Pallas kernels  10.7 us (33%)
  waiting for transfers between devices  6.18 us (19%)
  local copies, waits for them, and re-layouts  1.34 us (4%)
  other arithmetic  1.14 us (4%)
    pallas_call x5, Pallas kernels, call(): pl.pallas_call(kernel, out_shape=outs, in_specs=specs or [VMEM] * len(arg...  8.71 us
    ppermute x9, starting transfers between devices, swapped(): return lax.ppermute(sent, 'lev', [(i, i ^ k) for i in range(count)])  6.35 us
    ppermute x2, starting transfers between devices, beside(): lax.ppermute(sent[0], 'lat', [(i, i ^ 1) for i in range(bands)])  6.24 us
    ppermute x9, waiting for transfers between devices, swapped(): return lax.ppermute(sent, 'lev', [(i, i ^ k) for i in range(count)])  6.17 us
    pallas_call x1, Pallas kernels, remap(): pl.pallas_call(functools.partial(remap_kernel, count, tuple((units for un...  1.99 us
    unnamed x8, local copies, waits for them, and re-layouts  1.33 us
    concatenate x1, other arithmetic, shards(): jnp.concatenate([jnp.transpose(wind_x, (1, 0, 2)), jnp.transpose(wind_y,...  1.14 us
  transfers between devices with their start and end apart: 13, of which 3 were waited for; matrix products, arithmetic and copies ran while one was open for 0% of the time, Pallas kernels for 26%

profile of v20, /device:TPU:0, one launch (start us, length us, event | category | flops | bytes accessed | tf_op | source)
XLA Modules:
  0.0 32.1 jit_solution(672330757903307268)
XLA Ops:
  0.0 1.1 %pad_maximum_fusion.winds.joined = f32[36,2,1152]{2,1,0:T(2,128)S(1)} fusion(f32[18,2,1152]{2,1,0:T(2,128)} %bitcast.13, f32[18,2,1152]{2,1,0:T(2,128)} %bitcast.14), kind=kLoop, calls=%fused_computation | loop fusion | flops 82944 | bytes 663552 | tf_op jit(solution)/shard_map/concatenate | solution.py:453
  1.1 0.0 copy-start
  1.2 1.3 %copy-done = f32[8,2,18,1152]{3,1,2,0:T(2,128)S(1)} copy-done((f32[8,2,18,1152]{3,1,2,0:T(2,128)S(1)}, f32[8,2,18,1152]{3,1,2,0:T(2,128)}, u32[]{:S(2)}) %copy-start) | copy-done | bytes 1327128
  2.5 0.0 copy-start.1
  2.5 0.0 copy-start.2
  2.5 0.3 shard_map.64
  2.7 3.1 %collective-permute-start.1 = (f32[7,8,1152]{2,1,0:T(8,128)S(1)}, f32[7,8,1152]{2,1,0:T(8,128)S(1)}, u32[]{:S(2)}, u32[]{:S(2)}) collective-permute-start(f32[7,8,1152]{2,1,0:T(8,128)S(1)} %get-tuple-element.31), channel_id=1, source_target_pairs={{0,4},{4,0},{8,12},{12,8},{1,5},{5,1},{9,13},{13,9},{2,6},{6,2},{1... | collective-permute-start | bytes 774152 | tf_op jit(solution)/shard_map/ppermute | solution.py:464
  5.8 0.0 collective-permute-start.2
  5.8 3.1 %collective-permute-start.5 = (f32[7,8,1152]{2,1,0:T(8,128)S(1)}, f32[7,8,1152]{2,1,0:T(8,128)S(1)}, u32[]{:S(2)}, u32[]{:S(2)}) collective-permute-start(f32[7,8,1152]{2,1,0:T(8,128)S(1)} %get-tuple-element.39), channel_id=1, source_target_pairs={{0,4},{4,0},{8,12},{12,8},{1,5},{5,1},{9,13},{13,9},{2,6},{6,2},{1... | collective-permute-start | bytes 774152 | tf_op jit(solution)/shard_map/ppermute | solution.py:464
  9.0 0.0 collective-permute-start.6
  9.0 3.6 %shard_map.65 = (f32[1,27,8,128]{3,2,1,0:T(8,128)S(1)}, f32[1,27,8,128]{3,2,1,0:T(8,128)S(1)}, f32[2,27,8,128]{3,2,1,0:T(8,128)S(1)}, f32[2,12,8,1152]{3,2,1,0:T...) custom-call(f32[2,18,8,1152]{3,2,1,0:T(8,128)S(1)} %get-tuple-element.28.state, ...), custom_call_target="tpu_custom_call" | custom-call | flops 1 | bytes 1 | tf_op jit(solution)/shard_map/pallas_call | solution.py:424
  12.6 1.6 %collective-permute-start = (f32[2,27,8,128]{3,2,1,0:T(8,128)S(1)}, f32[2,27,8,128]{3,2,1,0:T(8,128)S(1)}, u32[]{:S(2)}, u32[]{:S(2)}) collective-permute-start(f32[2,27,8,128]{3,2,1,0:T(8,128)S(1)} %get-tuple-element.29), channel_id=1, source_target_pairs={{0,2},{1,3},{2,0},{3,1},{4,6},{5,7},{6,4},{7,5},{8,10},{9,11},{10,... | collective-permute-start | bytes 663560 | tf_op jit(solution)/shard_map/ppermute | solution.py:506
  14.2 0.0 copy-done.1
  14.2 0.0 copy-done.2
  14.2 0.2 shard_map.66.refs_0_.refs_12_
  14.4 0.0 collective-permute-done.1.first_round
  14.4 0.0 collective-permute-done.2.second_round
  14.4 2.3 %shard_map.67 = (f32[1,27,8,128]{3,2,1,0:T(8,128)S(1)}, f32[1,27,8,128]{3,2,1,0:T(8,128)S(1)}, f32[1,27,8,128]{3,2,1,0:T(8,128)S(1)}, f32[1,27,8,128]{3,2,1,0:T(8,128)S(1)}) custom-call(f32[2,18,8,1152]{3,2,1,0:T(8,128)S(1)} %get-tuple-element.28.state, f32[7,8,1152]{2,1,0:T(8,128)S(1)} %collective-permute-done.1.first_round, ...), custom_call_target="tpu_custom_call" | custom-call | flops 19906560 | bytes 2654208 | tf_op jit(solution)/shard_map/pallas_call | solution.py:424
  16.7 0.4 %collective-permute-start.3 = (f32[1,27,8,128]{3,2,1,0:T(8,128)S(1)}, f32[1,27,8,128]{3,2,1,0:T(8,128)S(1)}, u32[]{:S(2)}, u32[]{:S(2)}) collective-permute-start(f32[1,27,8,128]{3,2,1,0:T(8,128)S(1)} %get-tuple-element.36), channel_id=1, source_target_pairs={{0,3},{1,2},{2,1},{3,0},{4,7},{5,6},{6,5},{7,4},{8,11},{9,10},{10,... | collective-permute-start | bytes 331784 | tf_op jit(solution)/shard_map/ppermute | solution.py:506
  17.2 1.5 %collective-permute-start.4 = (f32[1,27,8,128]{3,2,1,0:T(8,128)S(1)}, f32[1,27,8,128]{3,2,1,0:T(8,128)S(1)}, u32[]{:S(2)}, u32[]{:S(2)}) collective-permute-start(f32[1,27,8,128]{3,2,1,0:T(8,128)S(1)} %get-tuple-element.37), channel_id=1, source_target_pairs={{0,2},{1,3},{2,0},{3,1},{4,6},{5,7},{6,4},{7,5},{8,10},{9,11},{10,... | collective-permute-start | bytes 331784 | tf_op jit(solution)/shard_map/ppermute | solution.py:506
  18.7 0.0 collective-permute-done.5.first_round
  18.7 0.0 collective-permute-done.6.second_round
  18.7 0.0 copy-start.3
  18.7 2.3 %shard_map.68 = (f32[1,27,8,128]{3,2,1,0:T(8,128)S(1)}, f32[1,27,8,128]{3,2,1,0:T(8,128)S(1)}, f32[1,27,8,128]{3,2,1,0:T(8,128)S(1)}, f32[1,27,8,128]{3,2,1,0:T(8,128)S(1)}) custom-call(f32[2,18,8,1152]{3,2,1,0:T(8,128)S(1)} %get-tuple-element.28.state, f32[7,8,1152]{2,1,0:T(8,128)S(1)} %collective-permute-done.5.first_round, ...), custom_call_target="tpu_custom_call" | custom-call | flops 19906560 | bytes 2654208 | tf_op jit(solution)/shard_map/pallas_call | solution.py:424
  21.0 0.2 collective-permute-start.7
  21.2 1.5 %collective-permute-start.8 = (f32[1,27,8,128]{3,2,1,0:T(8,128)S(1)}, f32[1,27,8,128]{3,2,1,0:T(8,128)S(1)}, u32[]{:S(2)}, u32[]{:S(2)}) collective-permute-start(f32[1,27,8,128]{3,2,1,0:T(8,128)S(1)} %get-tuple-element.42), channel_id=1, source_target_pairs={{0,2},{1,3},{2,0},{3,1},{4,6},{5,7},{6,4},{7,5},{8,10},{9,11},{10,... | collective-permute-start | bytes 331784 | tf_op jit(solution)/shard_map/ppermute | solution.py:506
  22.7 0.0 collective-permute-done.refs_0_
  22.7 0.3 collective-permute-start.12
  23.0 0.0 collective-permute-done.3.refs_0_.refs_2_
  23.0 0.3 collective-permute-start.9
  23.3 2.4 %collective-permute-done.4.refs_1_.refs_3_ = f32[1,27,8,128]{3,2,1,0:T(8,128)S(1)} collective-permute-done((f32[1,27,8,128]{3,2,1,0:T(8,128)S(1)}, f32[1,27,8,128]{3,2,1,0:T(8,128)S(1)}, u32[]{:S(2)}, u32[]{:S(2)}) %collective-permute-start.4) | collective-permute-done | bytes 110624 | tf_op jit(solution)/shard_map/ppermute | solution.py:506
  25.7 0.0 collective-permute-start.10
  25.7 1.6 %collective-permute-done.7.refs_0_.refs_5_ = f32[1,27,8,128]{3,2,1,0:T(8,128)S(1)} collective-permute-done((f32[1,27,8,128]{3,2,1,0:T(8,128)S(1)}, f32[1,27,8,128]{3,2,1,0:T(8,128)S(1)}, u32[]{:S(2)}, u32[]{:S(2)}) %collective-permute-start.7) | collective-permute-done | bytes 110624 | tf_op jit(solution)/shard_map/ppermute | solution.py:506
  27.3 0.6 %collective-permute-start.11 = (f32[1,27,8,128]{3,2,1,0:T(8,128)S(1)}, f32[1,27,8,128]{3,2,1,0:T(8,128)S(1)}, u32[]{:S(2)}, u32[]{:S(2)}) collective-permute-start(f32[1,27,8,128]{3,2,1,0:T(8,128)S(1)} %get-tuple-element.49), channel_id=1, source_target_pairs={{0,1},{1,0},{2,3},{3,2},{4,5},{5,4},{6,7},{7,6},{8,9},{9,8},{10,11... | collective-permute-start | bytes 331784 | tf_op jit(solution)/shard_map/ppermute | solution.py:506
  27.9 2.2 %collective-permute-done.8.refs_1_.refs_6_ = f32[1,27,8,128]{3,2,1,0:T(8,128)S(1)} collective-permute-done((f32[1,27,8,128]{3,2,1,0:T(8,128)S(1)}, f32[1,27,8,128]{3,2,1,0:T(8,128)S(1)}, u32[]{:S(2)}, u32[]{:S(2)}) %collective-permute-start.8) | collective-permute-done | bytes 110624 | tf_op jit(solution)/shard_map/ppermute | solution.py:506
  30.0 0.0 collective-permute-done.12.refs_11_
  30.0 0.0 collective-permute-done.9.refs_8_
  30.0 0.0 collective-permute-done.10.refs_9_
  30.1 0.0 collective-permute-done.11.refs_10_
  30.1 0.0 copy-done.3
  30.1 2.0 %shard_map.71 = f32[6,18,8,288]{3,2,1,0:T(8,128)} custom-call(s32[4]{0:T(128)S(1)} %copy-done.3, f32[2,27,8,128]{3,2,1,0:T(8,128)S(1)} %collective-permute-done.refs_0_, f32[1,27,8,128]{3,2,1,0:T(8,128)S(1)} %get-tuple-element.30.refs_1_, f32[1,27,8,128]{3,2,1,0:T(8,128)S(1)} %collective-permute-done.3.refs_0_.refs_2_, ...), custom_call_target="tpu_custom_call" | custom-call | flops 1 | bytes 1 | tf_op jit(solution)/shard_map/pallas_call | solution.py:513
  (3 shorter events, 0.0 us)
Async XLA Ops:
  1.1 1.3 %copy-start = (f32[8,2,18,1152]{3,1,2,0:T(2,128)S(1)}, f32[8,2,18,1152]{3,1,2,0:T(2,128)}, u32[]{:S(2)}) copy-start(f32[8,2,18,1152]{3,1,2,0:T(2,128)} %param.6) | copy-start | bytes 3981316
  2.5 11.7 %copy-start.1 = (f32[4,6,18,288]{3,0,2,1:T(4,128)S(1)}, f32[4,6,18,288]{3,0,2,1:T(4,128)}, u32[]{:S(2)}) copy-start(f32[4,6,18,288]{3,0,2,1:T(4,128)} %param.11) | copy-start | bytes 1492996
  2.5 11.7 %copy-start.2 = (s32[6,18,288]{2,1,0:T(8,128)S(1)}, s32[6,18,288]{2,1,0:T(8,128)}, u32[]{:S(2)}) copy-start(s32[6,18,288]{2,1,0:T(8,128)} %source.1) | copy-start | bytes 373252
  2.7 11.7 %collective-permute-start.1 = (f32[7,8,1152]{2,1,0:T(8,128)S(1)}, f32[7,8,1152]{2,1,0:T(8,128)S(1)}, u32[]{:S(2)}, u32[]{:S(2)}) collective-permute-start(f32[7,8,1152]{2,1,0:T(8,128)S(1)} %get-tuple-element.31), channel_id=1, source_target_pairs={{0,4},{4,0},{8,12},{12,8},{1,5},{5,1},{9,13},{13,9},{2,6},{6,2},{1... | collective-permute-start | bytes 774152 | tf_op jit(solution)/shard_map/ppermute | solution.py:464
  5.8 8.6 %collective-permute-start.2 = (f32[7,8,1152]{2,1,0:T(8,128)S(1)}, f32[7,8,1152]{2,1,0:T(8,128)S(1)}, u32[]{:S(2)}, u32[]{:S(2)}) collective-permute-start(f32[7,8,1152]{2,1,0:T(8,128)S(1)} %get-tuple-element.32), channel_id=1, source_target_pairs={{0,1},{1,0},{2,3},{3,2},{4,8},{5,9},{6,10},{7,11},{8,4},{9,5},{10,... | collective-permute-start | bytes 774152 | tf_op jit(solution)/shard_map/ppermute | solution.py:465
  5.8 12.8 %collective-permute-start.5 = (f32[7,8,1152]{2,1,0:T(8,128)S(1)}, f32[7,8,1152]{2,1,0:T(8,128)S(1)}, u32[]{:S(2)}, u32[]{:S(2)}) collective-permute-start(f32[7,8,1152]{2,1,0:T(8,128)S(1)} %get-tuple-element.39), channel_id=1, source_target_pairs={{0,4},{4,0},{8,12},{12,8},{1,5},{5,1},{9,13},{13,9},{2,6},{6,2},{1... | collective-permute-start | bytes 774152 | tf_op jit(solution)/shard_map/ppermute | solution.py:464
  9.0 9.7 %collective-permute-start.6 = (f32[7,8,1152]{2,1,0:T(8,128)S(1)}, f32[7,8,1152]{2,1,0:T(8,128)S(1)}, u32[]{:S(2)}, u32[]{:S(2)}) collective-permute-start(f32[7,8,1152]{2,1,0:T(8,128)S(1)} %get-tuple-element.40), channel_id=1, source_target_pairs={{0,1},{1,0},{2,3},{3,2},{4,8},{5,9},{6,10},{7,11},{8,4},{9,5},{10,... | collective-permute-start | bytes 774152 | tf_op jit(solution)/shard_map/ppermute | solution.py:465
  12.6 10.0 %collective-permute-start = (f32[2,27,8,128]{3,2,1,0:T(8,128)S(1)}, f32[2,27,8,128]{3,2,1,0:T(8,128)S(1)}, u32[]{:S(2)}, u32[]{:S(2)}) collective-permute-start(f32[2,27,8,128]{3,2,1,0:T(8,128)S(1)} %get-tuple-element.29), channel_id=1, source_target_pairs={{0,2},{1,3},{2,0},{3,1},{4,6},{5,7},{6,4},{7,5},{8,10},{9,11},{10,... | collective-permute-start | bytes 663560 | tf_op jit(solution)/shard_map/ppermute | solution.py:506
  16.7 6.3 %collective-permute-start.3 = (f32[1,27,8,128]{3,2,1,0:T(8,128)S(1)}, f32[1,27,8,128]{3,2,1,0:T(8,128)S(1)}, u32[]{:S(2)}, u32[]{:S(2)}) collective-permute-start(f32[1,27,8,128]{3,2,1,0:T(8,128)S(1)} %get-tuple-element.36), channel_id=1, source_target_pairs={{0,3},{1,2},{2,1},{3,0},{4,7},{5,6},{6,5},{7,4},{8,11},{9,10},{10,... | collective-permute-start | bytes 331784 | tf_op jit(solution)/shard_map/ppermute | solution.py:506
  17.2 8.5 %collective-permute-start.4 = (f32[1,27,8,128]{3,2,1,0:T(8,128)S(1)}, f32[1,27,8,128]{3,2,1,0:T(8,128)S(1)}, u32[]{:S(2)}, u32[]{:S(2)}) collective-permute-start(f32[1,27,8,128]{3,2,1,0:T(8,128)S(1)} %get-tuple-element.37), channel_id=1, source_target_pairs={{0,2},{1,3},{2,0},{3,1},{4,6},{5,7},{6,4},{7,5},{8,10},{9,11},{10,... | collective-permute-start | bytes 331784 | tf_op jit(solution)/shard_map/ppermute | solution.py:506
  18.7 11.4 %copy-start.3 = (s32[4]{0:T(128)S(1)}, s32[4]{0:T(128)}, u32[]{:S(2)}) copy-start(s32[4]{0:T(128)} %counts.1) | copy-start | bytes 52
  21.0 6.3 %collective-permute-start.7 = (f32[1,27,8,128]{3,2,1,0:T(8,128)S(1)}, f32[1,27,8,128]{3,2,1,0:T(8,128)S(1)}, u32[]{:S(2)}, u32[]{:S(2)}) collective-permute-start(f32[1,27,8,128]{3,2,1,0:T(8,128)S(1)} %get-tuple-element.41), channel_id=1, source_target_pairs={{0,3},{1,2},{2,1},{3,0},{4,7},{5,6},{6,5},{7,4},{8,11},{9,10},{10,... | collective-permute-start | bytes 331784 | tf_op jit(solution)/shard_map/ppermute | solution.py:506
  21.2 8.8 %collective-permute-start.8 = (f32[1,27,8,128]{3,2,1,0:T(8,128)S(1)}, f32[1,27,8,128]{3,2,1,0:T(8,128)S(1)}, u32[]{:S(2)}, u32[]{:S(2)}) collective-permute-start(f32[1,27,8,128]{3,2,1,0:T(8,128)S(1)} %get-tuple-element.42), channel_id=1, source_target_pairs={{0,2},{1,3},{2,0},{3,1},{4,6},{5,7},{6,4},{7,5},{8,10},{9,11},{10,... | collective-permute-start | bytes 331784 | tf_op jit(solution)/shard_map/ppermute | solution.py:506
  22.7 7.3 %collective-permute-start.12 = (f32[1,27,8,128]{3,2,1,0:T(8,128)S(1)}, f32[1,27,8,128]{3,2,1,0:T(8,128)S(1)}, u32[]{:S(2)}, u32[]{:S(2)}) collective-permute-start(f32[1,27,8,128]{3,2,1,0:T(8,128)S(1)} %slice.3), channel_id=1, source_target_pairs={{0,1},{1,0},{2,3},{3,2},{4,5},{5,4},{6,7},{7,6},{8,9},{9,8},{10,11... | collective-permute-start | bytes 331784 | tf_op jit(solution)/shard_map/ppermute | solution.py:506
  23.0 7.0 %collective-permute-start.9 = (f32[1,27,8,128]{3,2,1,0:T(8,128)S(1)}, f32[1,27,8,128]{3,2,1,0:T(8,128)S(1)}, u32[]{:S(2)}, u32[]{:S(2)}) collective-permute-start(f32[1,27,8,128]{3,2,1,0:T(8,128)S(1)} %get-tuple-element.47), channel_id=1, source_target_pairs={{0,1},{1,0},{2,3},{3,2},{4,5},{5,4},{6,7},{7,6},{8,9},{9,8},{10,11... | collective-permute-start | bytes 331784 | tf_op jit(solution)/shard_map/ppermute | solution.py:506
  25.7 4.4 %collective-permute-start.10 = (f32[1,27,8,128]{3,2,1,0:T(8,128)S(1)}, f32[1,27,8,128]{3,2,1,0:T(8,128)S(1)}, u32[]{:S(2)}, u32[]{:S(2)}) collective-permute-start(f32[1,27,8,128]{3,2,1,0:T(8,128)S(1)} %get-tuple-element.48), channel_id=1, source_target_pairs={{0,1},{1,0},{2,3},{3,2},{4,5},{5,4},{6,7},{7,6},{8,9},{9,8},{10,11... | collective-permute-start | bytes 331784 | tf_op jit(solution)/shard_map/ppermute | solution.py:506
  27.3 2.8 %collective-permute-start.11 = (f32[1,27,8,128]{3,2,1,0:T(8,128)S(1)}, f32[1,27,8,128]{3,2,1,0:T(8,128)S(1)}, u32[]{:S(2)}, u32[]{:S(2)}) collective-permute-start(f32[1,27,8,128]{3,2,1,0:T(8,128)S(1)} %get-tuple-element.49), channel_id=1, source_target_pairs={{0,1},{1,0},{2,3},{3,2},{4,5},{5,4},{6,7},{7,6},{8,9},{9,8},{10,11... | collective-permute-start | bytes 331784 | tf_op jit(solution)/shard_map/ppermute | solution.py:506
